TPU v7x, 32 devices: a whole 2x2x4 slice. The times are simulated.
32 devices in a mesh: grp: 2 (over core), gx: 8 (over z, x), gy: 2 (over y).
Axes of the slice: x: 2, y: 2, z: 4, core: 2. Of those that a mesh axis runs over, the one named last changes fastest.
Arguments:
- les_velocity: float32 [256, 32, 3, 512], P('gx', 'gy', None, 'grp'), may hold values from -6 to 6
- mean_mach: float32 [128, 32], P('gx', 'gy'), may hold values from 0.2 to 0.6
- transfer_tiles: bfloat16 [64, 2, 2, 64, 64], P('gx', 'gy'), may hold values from -0.75 to 0.75
- intersection_offset: int32 [64], P('gx'), may hold values from -1 to 1, as said below
- acoustic_state: float32 [128, 32, 4, 512], P('gx', 'gy', None, 'grp'), may hold values from -6 to 6
Outputs:
- acoustic_out: float32 [128, 32, 4, 512], P('gx', 'gy', None, 'grp')
Inputs may be any that keep to these rules, and one draw needn't show every extreme that they name: `intersection_offset`: each value is -1 or 1. The first block of every gx shard has -1 and the last has 1, except that the first two blocks of the grid have 1 and the last two have -1.
All inputs are finite; a program needn't handle non-finite values.
Results may differ from a plain program's by a relative error of at most 0.018.
Values sent between devices are 32-bit elements; how exact they have to be, the bound alone decides.
No kernel may reach another device: no remote copies, remote signals or barrier semaphores. Data moves between devices by JAX's collectives and lax.ppermute only.
A program may use at most 128 MiB of HBM per device.

v0:
```python
import jax
import jax.numpy as jnp
from jax import lax
from jax.sharding import PartitionSpec as P

STEPS = 2


eddy_step = 0.1
viscosity = 0.5
wave_step = 0.2
filter_weight = 0.2
derivative_weights = (0.770882380518, -0.166705904415, 0.02084314277)
filter_taps = (0.28739284246, -0.226146951809, 0.10630357877, -0.023853048191)
unit_moves = ((1, 0, 0), (0, 1, 0), (0, 0, 1))


def padded_2(block, sides, width):
    for axis, dim in sides:
        count = lax.axis_size(axis)
        forward = [(i, i + 1) for i in range(count - 1)]
        backward = [(target, source) for source, target in forward]
        low = lax.ppermute(
            lax.slice_in_dim(block, block.shape[dim] - width, None, axis=dim), axis, forward
        )
        high = lax.ppermute(lax.slice_in_dim(block, 0, width, axis=dim), axis, backward)
        block = jnp.concatenate([low, block, high], axis=dim)
    return block


def shifted(array, axis, by):
    length = lax.axis_size(axis)
    pairs = [(i, i + by) for i in range(length) if 0 <= i + by < length]
    return lax.ppermute(array, axis, pairs)


def window(array, along_x, along_y, along_z, margin):
    return array[
        margin + along_x : array.shape[0] - margin + along_x,
        margin + along_y : array.shape[1] - margin + along_y,
        :,
        margin + along_z : array.shape[3] - margin + along_z,
    ]


def eddy_terms(velocity):
    padded = padded_2(velocity, (("grp", 3), ("gx", 0), ("gy", 1)), 1)
    center = window(padded, 0, 0, 0, 1)
    grads = []
    laplace = -6.0 * center
    for move in unit_moves:
        ahead = window(padded, move[0], move[1], move[2], 1)
        behind = window(padded, -move[0], -move[1], -move[2], 1)
        grads.append(0.5 * (ahead - behind))
        laplace = laplace + ahead + behind
    vort_x = grads[1][:, :, 2] - grads[2][:, :, 1]
    vort_y = grads[2][:, :, 0] - grads[0][:, :, 2]
    vort_z = grads[0][:, :, 1] - grads[1][:, :, 0]
    lamb = jnp.stack(
        [
            vort_y * center[:, :, 2] - vort_z * center[:, :, 1],
            vort_z * center[:, :, 0] - vort_x * center[:, :, 2],
            vort_x * center[:, :, 1] - vort_y * center[:, :, 0],
        ],
        axis=2,
    )
    return (lamb, laplace)


def derivative(padded, move):
    total = None
    for index in range(3):
        reach = index + 1
        ahead = window(padded, reach * move[0], reach * move[1], reach * move[2], 3)
        behind = window(padded, -reach * move[0], -reach * move[1], -reach * move[2], 3)
        term = derivative_weights[index] * (ahead - behind)
        total = term if total is None else total + term
    return total


def rate(padded, mach, source):
    grads = [derivative(padded, move) for move in unit_moves]
    convect = mach[:, :, None, None] * grads[0]
    pressure_rate = -(convect[:, :, 0] + grads[0][:, :, 1] + grads[1][:, :, 2] + grads[2][:, :, 3])
    x_rate = -(convect[:, :, 1] + grads[0][:, :, 0]) - source[:, :, 0]
    y_rate = -(convect[:, :, 2] + grads[1][:, :, 0]) - source[:, :, 1]
    z_rate = -(convect[:, :, 3] + grads[2][:, :, 0]) - source[:, :, 2]
    return jnp.stack([pressure_rate, x_rate, y_rate, z_rate], axis=2)


def smooth(padded):
    center = window(padded, 0, 0, 0, 3)
    total = 3.0 * filter_taps[0] * center
    for move in unit_moves:
        for index in range(1, 4):
            ahead = window(padded, index * move[0], index * move[1], index * move[2], 3)
            behind = window(padded, -index * move[0], -index * move[1], -index * move[2], 3)
            total = total + filter_taps[index] * (ahead + behind)
    return center - filter_weight * total


def shallow_rim(state):
    return padded_2(state, (("grp", 3), ("gx", 0), ("gy", 1)), 3)


def attach(own, from_lower, from_upper):
    own = own.at[0].add(from_lower)
    return own.at[-1].add(from_upper)


def body(les_velocity, mean_mach, transfer_tiles, intersection_offset, acoustic_state):
    cells_x, width_y, components, depth = les_velocity.shape
    wave_x = cells_x // 2
    tiles = transfer_tiles[:, 0].astype(jnp.float32)
    blocks = tiles.shape[0]
    plane = tiles.shape[2]
    bricks = blocks // 2
    slot = jnp.arange(blocks, dtype=jnp.int32) // 2 + 1 + intersection_offset
    onehot = (slot[:, None] == jnp.arange(bricks + 2, dtype=jnp.int32)[None, :]).astype(jnp.float32)
    velocity = les_velocity
    sources = []
    for step in range(STEPS):
        lamb, laplace = eddy_terms(velocity)
        terms = jnp.einsum(
            "bkpq,bpc->bkqc",
            tiles,
            lamb.reshape(blocks, plane, 3 * depth),
            precision=lax.Precision.HIGHEST,
            preferred_element_type=jnp.float32,
        )
        own = terms[:, 0].reshape(bricks, 2, plane, terms.shape[3]).sum(axis=1)
        spread = jnp.einsum("bs,bqc->sqc", onehot, terms[:, 1], precision=lax.Precision.HIGHEST)
        own, lower, upper = (own + spread[1:-1], spread[0], spread[-1])
        from_upper = shifted(lower, "gx", -1)
        from_lower = shifted(upper, "gx", 1)
        sources.append(attach(own, from_lower, from_upper).reshape(wave_x, width_y, 3, depth))
        if step + 1 < STEPS:
            velocity = velocity + eddy_step * (viscosity * laplace - lamb)
    state = acoustic_state
    for source in sources:
        first = rate(shallow_rim(state), mean_mach, source)
        middle = state + wave_step * first
        second = rate(shallow_rim(middle), mean_mach, source)
        updated = state + 0.5 * wave_step * (first + second)
        state = smooth(shallow_rim(updated))
    return state


def solution(mesh):
    placed = (
        P("gx", "gy", None, "grp"),
        P("gx", "gy"),
        P("gx", "gy", None, None, None),
        P("gx"),
        P("gx", "gy", None, "grp"),
    )
    return jax.shard_map(
        body, mesh=mesh, in_specs=placed, out_specs=P("gx", "gy", None, "grp"), check_vma=False
    )
```

profile of v0, /device:TPU:6, one launch (start us, length us, event | category | flops | bytes accessed | tf_op | source)
XLA Modules:
  0.0 446.9 jit_solution(9971361645334212558)
XLA Ops:
  19.6 4.3 collective-permute-start.9
  28.2 4.8 %collective-permute-start.3 = (f32[3,16,4,262]{3,2,1,0:T(4,128)}, f32[3,16,4,262]{3,2,1,0:T(4,128)}, u32[]{:S(2)}, u32[]{:S(2)}) collective-permute-start(f32[3,16,4,262]{3,2,1,0:T(4,128)} %get-tuple-element.146), channel_id=1, source_target_pairs={{0,2},{2,4},{4,6},{6,8},{8,10},{10,12},{12,14},{1,3},{3,5},{5,7},{... | collective-permute-start | bytes 603656 | tf_op jit(solution)/shard_map/ppermute | solution.py:23
  34.2 6.3 %fusion.70 = f32[16,16,4,256]{3,2,1,0:T(4,128)} fusion(f32[16,16,4,256]{3,2,1,0:T(4,128)S(1)} %copy-done, f32[16,16,4,3]{3,2,1,0:T(4,128)} %collective-permute-done, f32[16,16,4,259]{3,2,1,0:T(4,128)S(1)} %constant_dynamic-update-slice_fusion), kind=kLoop, calls=%fused_computation.184 | loop fusion | flops 2883584 | bytes 5255168 | tf_op jit(solution)/shard_map/add | solution.py:77
  48.9 4.0 collective-permute-done.11
  53.0 3.8 subtract_multiply_fusion
  61.3 3.9 reshape.134
  73.5 3.6 multiply_add_fusion
  91.1 4.2 collective-permute-start.13
  99.8 4.8 %collective-permute-start.35 = (f32[1,16,3,258]{3,1,2,0:T(8,128)S(1)}, f32[1,16,3,258]{3,1,2,0:T(8,128)S(1)}, u32[]{:S(2)}, u32[]{:S(2)}) collective-permute-start(f32[1,16,3,258]{3,1,2,0:T(8,128)S(1)} %get-tuple-element.76), channel_id=1, source_target_pairs={{0,2},{2,4},{4,6},{6,8},{8,10},{10,12},{12,14},{1,3},{3,5},{5,7},{... | collective-permute-start | bytes 148616 | tf_op jit(solution)/shard_map/ppermute | solution.py:23
  109.6 4.4 pad_maximum_fusion.6
  114.0 4.7 %broadcast_multiply_fusion.3 = (f32[16,16,4,256]{3,2,1,0:T(4,128)}, f32[16,16,4,256]{3,2,1,0:T(4,128)}) fusion(f32[16,16]{1,0:T(8,128)S(1)} %copy-done.31, f32[19,16,4,262]{3,2,1,0:T(4,128)S(1)} %get-tuple-element.144, f32[19,16,4,262]{3,2,1,0:T(4,128)S(1)} %get-tuple-element.143), kind=kLoop, calls=%fused_computation.338 | loop fusion | flops 2359296 | bytes 8389632 | tf_op jit(solution)/shard_map/mul | solution.py:83
  125.8 4.5 %collective-permute-done.37 = f32[34,1,3,258]{3,0,2,1:T(8,128)S(1)} collective-permute-done((f32[34,1,3,258]{3,0,2,1:T(8,128)S(1)}, f32[34,1,3,258]{3,0,2,1:T(8,128)S(1)}, u32[]{:S(2)}, u32[]{:S(2)}) %collective-permute-start.37) | collective-permute-done | bytes 105296 | tf_op jit(solution)/shard_map/ppermute | solution.py:23
  130.5 3.9 fusion.1
  147.4 8.3 %pad_maximum_fusion = (f32[22,19,4,262]{3,2,1,0:T(4,128)S(1)}, f32[22,19,4,262]{3,2,1,0:T(4,128)S(1)}) fusion(f32[22,3,4,262]{3,2,1,0:T(4,128)} %collective-permute-done.4, f32[3,16,4,262]{3,2,1,0:T(4,128)} %collective-permute-done.2, f32[16,16,4,3]{3,2,1,0:T(4,128)} %collective-permute-done.1, f32[16,16,4,256]{3,2,1,0:T(4,128)S(1)} %copy-done, ...), kind=kLoop, calls=%fused_computation | loop fusion | flops 4380640 | bytes 5533440 | tf_op jit(solution)/shard_map/concatenate | solution.py:27
  167.8 3.9 collective-permute-start.39
  174.2 4.8 %collective-permute-start.17 = (f32[3,16,4,262]{3,2,1,0:T(4,128)S(1)}, f32[3,16,4,262]{3,2,1,0:T(4,128)S(1)}, u32[]{:S(2)}, u32[]{:S(2)}) collective-permute-start(f32[3,16,4,262]{3,2,1,0:T(4,128)S(1)} %get-tuple-element.138), channel_id=1, source_target_pairs={{0,2},{2,4},{4,6},{6,8},{8,10},{10,12},{12,14},{1,3},{3,5},{5,7},{... | collective-permute-start | bytes 603656 | tf_op jit(solution)/shard_map/ppermute | solution.py:23
  179.0 5.6 %fusion.60 = f32[16,16,4,256]{3,2,1,0:T(4,128)S(1)} fusion(f32[16,16,4,256]{3,2,1,0:T(4,128)S(1)} %multiply_add_fusion.2, f32[16,16,4,3]{3,2,1,0:T(4,128)S(1)} %collective-permute-done.14, f32[16,16,4,3]{3,2,1,0:T(4,128)S(1)} %collective-permute-done.15), kind=kLoop, calls=%fused_computation.174 | loop fusion | flops 3670016 | bytes 2121728 | tf_op jit(solution)/shard_map/add | solution.py:77
  184.8 7.4 %collective-permute-done.17 = f32[3,16,4,262]{3,2,1,0:T(4,128)S(1)} collective-permute-done((f32[3,16,4,262]{3,2,1,0:T(4,128)S(1)}, f32[3,16,4,262]{3,2,1,0:T(4,128)S(1)}, u32[]{:S(2)}, u32[]{:S(2)}) %collective-permute-start.17) | collective-permute-done | bytes 201248 | tf_op jit(solution)/shard_map/ppermute | solution.py:23
  198.5 3.7 broadcast_multiply_fusion.2
  203.1 4.1 collective-permute-done.19
  207.3 6.7 %pad_maximum_fusion.1 = (f32[22,19,4,262]{3,2,1,0:T(4,128)S(1)}, f32[22,19,4,262]{3,2,1,0:T(4,128)S(1)}) fusion(f32[22,3,4,262]{3,2,1,0:T(4,128)S(1)} %collective-permute-done.18, f32[3,16,4,262]{3,2,1,0:T(4,128)S(1)} %collective-permute-done.16, f32[16,16,4,3]{3,2,1,0:T(4,128)S(1)} %collective-permute-done.15, f32[16,16,4,256]{3,2,1,0:T(4,128)S(1)} %multiply_add_fusion.2, ...), kind=kLoop, calls=%fused_computation.2 | loop fusion | flops 4380640 | bytes 5533440 | tf_op jit(solution)/shard_map/concatenate | solution.py:27
  229.7 4.8 %collective-permute-start.23 = (f32[3,16,4,262]{3,2,1,0:T(4,128)S(1)}, f32[3,16,4,262]{3,2,1,0:T(4,128)S(1)}, u32[]{:S(2)}, u32[]{:S(2)}) collective-permute-start(f32[3,16,4,262]{3,2,1,0:T(4,128)S(1)} %get-tuple-element.129), channel_id=1, source_target_pairs={{0,2},{2,4},{4,6},{6,8},{8,10},{10,12},{12,14},{1,3},{3,5},{5,7},{... | collective-permute-start | bytes 603656 | tf_op jit(solution)/shard_map/ppermute | solution.py:23
  236.1 3.5 collective-permute-done.22
  239.7 6.2 %collective-permute-done.23 = f32[3,16,4,262]{3,2,1,0:T(4,128)S(1)} collective-permute-done((f32[3,16,4,262]{3,2,1,0:T(4,128)S(1)}, f32[3,16,4,262]{3,2,1,0:T(4,128)S(1)}, u32[]{:S(2)}, u32[]{:S(2)}) %collective-permute-start.23) | collective-permute-done | bytes 201248 | tf_op jit(solution)/shard_map/ppermute | solution.py:23
  252.2 4.6 %collective-permute-done.24 = f32[22,3,4,262]{3,2,1,0:T(4,128)S(1)} collective-permute-done((f32[22,3,4,262]{3,2,1,0:T(4,128)S(1)}, f32[22,3,4,262]{3,2,1,0:T(4,128)S(1)}, u32[]{:S(2)}, u32[]{:S(2)}) %collective-permute-start.24) | collective-permute-done | bytes 276704 | tf_op jit(solution)/shard_map/ppermute | solution.py:26
  256.8 4.1 collective-permute-done.25
  260.9 6.7 %pad_maximum_fusion.2 = (f32[22,19,4,262]{3,2,1,0:T(4,128)S(1)}, f32[22,19,4,262]{3,2,1,0:T(4,128)S(1)}) fusion(f32[22,3,4,262]{3,2,1,0:T(4,128)S(1)} %collective-permute-done.24, f32[3,16,4,262]{3,2,1,0:T(4,128)S(1)} %collective-permute-done.22, f32[16,16,4,3]{3,2,1,0:T(4,128)S(1)} %collective-permute-done.21, f32[16,16,4,256]{3,2,1,0:T(4,128)S(1)} %fusion.151, ...), kind=kLoop, calls=%fused_computation.4 | loop fusion | flops 4380640 | bytes 5533440 | tf_op jit(solution)/shard_map/concatenate | solution.py:27
  267.6 11.9 %fusion.49 = f32[16,16,4,256]{3,2,1,0:T(4,128)S(1)} fusion(f32[16,16,4,256]{3,2,1,0:T(4,128)S(1)} %fusion.151, f32[16,16,4,3]{3,2,1,0:T(4,128)S(1)} %collective-permute-done.20, f32[16,16,4,3]{3,2,1,0:T(4,128)S(1)} %collective-permute-done.21, f32[22,19,4,262]{3,2,1,0:T(4,128)S(1)} %get-tuple-element.96, f32[22,19,4,262]{3,2,1,0:T(4,128)S(1)} %get-tuple-element.95, ...), kind=kLoop, calls=%fused_computation.163 | loop fusion | flops 9437184 | bytes 14704640 | tf_op jit(solution)/shard_map/sub | solution.py:99
  289.1 4.8 %collective-permute-start.29 = (f32[3,16,4,262]{3,2,1,0:T(4,128)S(1)}, f32[3,16,4,262]{3,2,1,0:T(4,128)S(1)}, u32[]{:S(2)}, u32[]{:S(2)}) collective-permute-start(f32[3,16,4,262]{3,2,1,0:T(4,128)S(1)} %get-tuple-element.126), channel_id=1, source_target_pairs={{0,2},{2,4},{4,6},{6,8},{8,10},{10,12},{12,14},{1,3},{3,5},{5,7},{... | collective-permute-start | bytes 603656 | tf_op jit(solution)/shard_map/ppermute | solution.py:23
  294.0 5.2 %fusion.37 = f32[16,16,4,256]{3,2,1,0:T(4,128)S(1)} fusion(f32[16,16,4,256]{3,2,1,0:T(4,128)S(1)} %fusion.49, f32[16,16,4,3]{3,2,1,0:T(4,128)S(1)} %collective-permute-done.26, f32[16,16,4,3]{3,2,1,0:T(4,128)S(1)} %collective-permute-done.27), kind=kLoop, calls=%fused_computation.151 | loop fusion | flops 3670016 | bytes 2121728 | tf_op jit(solution)/shard_map/add | solution.py:77
  299.8 6.4 %collective-permute-done.29 = f32[3,16,4,262]{3,2,1,0:T(4,128)S(1)} collective-permute-done((f32[3,16,4,262]{3,2,1,0:T(4,128)S(1)}, f32[3,16,4,262]{3,2,1,0:T(4,128)S(1)}, u32[]{:S(2)}, u32[]{:S(2)}) %collective-permute-start.29) | collective-permute-done | bytes 201248 | tf_op jit(solution)/shard_map/ppermute | solution.py:23
  309.4 3.4 pad_maximum_fusion.9
  312.9 3.7 broadcast_multiply_fusion.1
  317.1 4.1 collective-permute-done.31
  321.3 6.7 %pad_maximum_fusion.3 = (f32[22,19,4,262]{3,2,1,0:T(4,128)S(1)}, f32[22,19,4,262]{3,2,1,0:T(4,128)S(1)}) fusion(f32[22,3,4,262]{3,2,1,0:T(4,128)S(1)} %collective-permute-done.30, f32[3,16,4,262]{3,2,1,0:T(4,128)S(1)} %collective-permute-done.28, f32[16,16,4,3]{3,2,1,0:T(4,128)S(1)} %collective-permute-done.27, f32[16,16,4,256]{3,2,1,0:T(4,128)S(1)} %fusion.49, ...), kind=kLoop, calls=%fused_computation.6 | loop fusion | flops 4380640 | bytes 5533440 | tf_op jit(solution)/shard_map/concatenate | solution.py:27
  342.4 4.8 %collective-permute-start.43 = (f32[3,16,4,262]{3,2,1,0:T(4,128)S(1)}, f32[3,16,4,262]{3,2,1,0:T(4,128)S(1)}, u32[]{:S(2)}, u32[]{:S(2)}) collective-permute-start(f32[3,16,4,262]{3,2,1,0:T(4,128)S(1)} %get-tuple-element.118), channel_id=1, source_target_pairs={{0,2},{2,4},{4,6},{6,8},{8,10},{10,12},{12,14},{1,3},{3,5},{5,7},{... | collective-permute-start | bytes 603656 | tf_op jit(solution)/shard_map/ppermute | solution.py:23
  347.3 5.3 %fusion.27 = f32[16,16,4,256]{3,2,1,0:T(4,128)S(1)} fusion(f32[16,16,4,256]{3,2,1,0:T(4,128)S(1)} %multiply_add_fusion.1, f32[16,16,4,3]{3,2,1,0:T(4,128)S(1)} %collective-permute-done.40, f32[16,16,4,3]{3,2,1,0:T(4,128)S(1)} %collective-permute-done.41), kind=kLoop, calls=%fused_computation.141 | loop fusion | flops 3670016 | bytes 2121728 | tf_op jit(solution)/shard_map/add | solution.py:77
  352.6 6.0 %collective-permute-done.43 = f32[3,16,4,262]{3,2,1,0:T(4,128)S(1)} collective-permute-done((f32[3,16,4,262]{3,2,1,0:T(4,128)S(1)}, f32[3,16,4,262]{3,2,1,0:T(4,128)S(1)}, u32[]{:S(2)}, u32[]{:S(2)}) %collective-permute-start.43) | collective-permute-done | bytes 201248 | tf_op jit(solution)/shard_map/ppermute | solution.py:23
  365.0 3.7 broadcast_multiply_fusion
  369.5 4.1 collective-permute-done.45
  373.7 6.7 %pad_maximum_fusion.4 = (f32[22,19,4,262]{3,2,1,0:T(4,128)S(1)}, f32[22,19,4,262]{3,2,1,0:T(4,128)S(1)}) fusion(f32[22,3,4,262]{3,2,1,0:T(4,128)S(1)} %collective-permute-done.44, f32[3,16,4,262]{3,2,1,0:T(4,128)S(1)} %collective-permute-done.42, f32[16,16,4,3]{3,2,1,0:T(4,128)S(1)} %collective-permute-done.41, f32[16,16,4,256]{3,2,1,0:T(4,128)S(1)} %multiply_add_fusion.1, ...), kind=kLoop, calls=%fused_computation.8 | loop fusion | flops 4380640 | bytes 5533440 | tf_op jit(solution)/shard_map/concatenate | solution.py:27
  396.1 4.8 %collective-permute-start.49 = (f32[3,16,4,262]{3,2,1,0:T(4,128)S(1)}, f32[3,16,4,262]{3,2,1,0:T(4,128)S(1)}, u32[]{:S(2)}, u32[]{:S(2)}) collective-permute-start(f32[3,16,4,262]{3,2,1,0:T(4,128)S(1)} %get-tuple-element.109), channel_id=1, source_target_pairs={{0,2},{2,4},{4,6},{6,8},{8,10},{10,12},{12,14},{1,3},{3,5},{5,7},{... | collective-permute-start | bytes 603656 | tf_op jit(solution)/shard_map/ppermute | solution.py:23
  400.9 5.2 %collective-permute-done.48 = f32[3,16,4,262]{3,2,1,0:T(4,128)S(1)} collective-permute-done((f32[3,16,4,262]{3,2,1,0:T(4,128)S(1)}, f32[3,16,4,262]{3,2,1,0:T(4,128)S(1)}, u32[]{:S(2)}, u32[]{:S(2)}) %collective-permute-start.48) | collective-permute-done | bytes 201248 | tf_op jit(solution)/shard_map/ppermute | solution.py:26
  406.1 6.2 %collective-permute-done.49 = f32[3,16,4,262]{3,2,1,0:T(4,128)S(1)} collective-permute-done((f32[3,16,4,262]{3,2,1,0:T(4,128)S(1)}, f32[3,16,4,262]{3,2,1,0:T(4,128)S(1)}, u32[]{:S(2)}, u32[]{:S(2)}) %collective-permute-start.49) | collective-permute-done | bytes 201248 | tf_op jit(solution)/shard_map/ppermute | solution.py:23
  418.6 4.6 %collective-permute-done.50 = f32[22,3,4,262]{3,2,1,0:T(4,128)S(1)} collective-permute-done((f32[22,3,4,262]{3,2,1,0:T(4,128)S(1)}, f32[22,3,4,262]{3,2,1,0:T(4,128)S(1)}, u32[]{:S(2)}, u32[]{:S(2)}) %collective-permute-start.50) | collective-permute-done | bytes 276704 | tf_op jit(solution)/shard_map/ppermute | solution.py:26
  423.2 4.1 collective-permute-done.51
  427.3 6.7 %pad_maximum_fusion.5 = (f32[22,19,4,262]{3,2,1,0:T(4,128)S(1)}, f32[22,19,4,262]{3,2,1,0:T(4,128)S(1)}) fusion(f32[22,3,4,262]{3,2,1,0:T(4,128)S(1)} %collective-permute-done.50, f32[3,16,4,262]{3,2,1,0:T(4,128)S(1)} %collective-permute-done.48, f32[16,16,4,3]{3,2,1,0:T(4,128)S(1)} %collective-permute-done.47, f32[16,16,4,256]{3,2,1,0:T(4,128)S(1)} %fusion.153, ...), kind=kLoop, calls=%fused_computation.10 | loop fusion | flops 4380640 | bytes 5533440 | tf_op jit(solution)/shard_map/concatenate | solution.py:27
  434.0 12.6 %fusion.16 = f32[16,16,4,256]{3,2,1,0:T(4,128)} fusion(f32[16,16,4,256]{3,2,1,0:T(4,128)S(1)} %fusion.153, f32[16,16,4,3]{3,2,1,0:T(4,128)S(1)} %collective-permute-done.46, f32[16,16,4,3]{3,2,1,0:T(4,128)S(1)} %collective-permute-done.47, f32[22,19,4,262]{3,2,1,0:T(4,128)S(1)} %get-tuple-element.84, f32[22,19,4,262]{3,2,1,0:T(4,128)S(1)} %get-tuple-element.83, ...), kind=kLoop, calls=%fused_computation.130 | loop fusion | flops 9437184 | bytes 14704640 | tf_op jit(solution)/shard_map/sub | solution.py:99
  (241 shorter events, 192.1 us)
Async XLA Ops:
  2.1 12.3 %collective-permute-start.6 = (f32[32,16,3,1]{0,1,3,2:T(8,128)S(1)}, f32[32,16,3,1]{0,1,3,2:T(8,128)S(1)}, u32[]{:S(2)}, u32[]{:S(2)}) collective-permute-start(f32[32,16,3,1]{0,1,3,2:T(8,128)S(1)} %copy.88), channel_id=1, source_target_pairs={{16,0},{17,1},{18,2},{19,3},{20,4},{21,5},{22,6},{23,7},{24,8},{25... | collective-permute-start | bytes 18440 | tf_op jit(solution)/shard_map/ppermute | solution.py:26
  3.8 11.0 %collective-permute-start.7 = (f32[32,16,3,1]{0,1,3,2:T(8,128)S(1)}, f32[32,16,3,1]{0,1,3,2:T(8,128)S(1)}, u32[]{:S(2)}, u32[]{:S(2)}) collective-permute-start(f32[32,16,3,1]{0,1,3,2:T(8,128)S(1)} %copy.89), channel_id=1, source_target_pairs={{0,16},{1,17},{2,18},{3,19},{4,20},{5,21},{6,22},{7,23},{8,24},{9,... | collective-permute-start | bytes 18440 | tf_op jit(solution)/shard_map/ppermute | solution.py:23
  8.3 15.6 %collective-permute-start = (f32[16,16,4,3]{3,2,1,0:T(4,128)}, f32[16,16,4,3]{3,2,1,0:T(4,128)}, u32[]{:S(2)}, u32[]{:S(2)}) collective-permute-start(f32[16,16,4,3]{3,2,1,0:T(4,128)} %get-tuple-element.166), channel_id=1, source_target_pairs={{0,16},{1,17},{2,18},{3,19},{4,20},{5,21},{6,22},{7,23},{8,24},{9,... | collective-permute-start | bytes 36872 | tf_op jit(solution)/shard_map/ppermute | solution.py:23
  10.4 13.5 %collective-permute-start.1 = (f32[16,16,4,3]{3,2,1,0:T(4,128)}, f32[16,16,4,3]{3,2,1,0:T(4,128)}, u32[]{:S(2)}, u32[]{:S(2)}) collective-permute-start(f32[16,16,4,3]{3,2,1,0:T(4,128)} %get-tuple-element.165), channel_id=1, source_target_pairs={{16,0},{17,1},{18,2},{19,3},{20,4},{21,5},{22,6},{23,7},{24,8},{25... | collective-permute-start | bytes 36872 | tf_op jit(solution)/shard_map/ppermute | solution.py:26
  17.0 23.5 %collective-permute-start.8 = (f32[1,16,3,258]{3,1,2,0:T(8,128)S(1)}, f32[1,16,3,258]{3,1,2,0:T(8,128)S(1)}, u32[]{:S(2)}, u32[]{:S(2)}) collective-permute-start(f32[1,16,3,258]{3,1,2,0:T(8,128)S(1)} %get-tuple-element.82), channel_id=1, source_target_pairs={{2,0},{4,2},{6,4},{8,6},{10,8},{12,10},{14,12},{3,1},{5,3},{7,5},{... | collective-permute-start | bytes 148616 | tf_op jit(solution)/shard_map/ppermute | solution.py:26
  19.6 20.9 %collective-permute-start.9 = (f32[1,16,3,258]{3,1,2,0:T(8,128)S(1)}, f32[1,16,3,258]{3,1,2,0:T(8,128)S(1)}, u32[]{:S(2)}, u32[]{:S(2)}) collective-permute-start(f32[1,16,3,258]{3,1,2,0:T(8,128)S(1)} %get-tuple-element.81), channel_id=1, source_target_pairs={{0,2},{2,4},{4,6},{6,8},{8,10},{10,12},{12,14},{1,3},{3,5},{5,7},{... | collective-permute-start | bytes 148616 | tf_op jit(solution)/shard_map/ppermute | solution.py:23
  26.2 73.5 %collective-permute-start.2 = (f32[3,16,4,262]{3,2,1,0:T(4,128)}, f32[3,16,4,262]{3,2,1,0:T(4,128)}, u32[]{:S(2)}, u32[]{:S(2)}) collective-permute-start(f32[3,16,4,262]{3,2,1,0:T(4,128)} %get-tuple-element.145), channel_id=1, source_target_pairs={{2,0},{4,2},{6,4},{8,6},{10,8},{12,10},{14,12},{3,1},{5,3},{7,5},{... | collective-permute-start | bytes 603656 | tf_op jit(solution)/shard_map/ppermute | solution.py:26
  28.2 76.5 %collective-permute-start.3 = (f32[3,16,4,262]{3,2,1,0:T(4,128)}, f32[3,16,4,262]{3,2,1,0:T(4,128)}, u32[]{:S(2)}, u32[]{:S(2)}) collective-permute-start(f32[3,16,4,262]{3,2,1,0:T(4,128)} %get-tuple-element.146), channel_id=1, source_target_pairs={{0,2},{2,4},{4,6},{6,8},{8,10},{10,12},{12,14},{1,3},{3,5},{5,7},{... | collective-permute-start | bytes 603656 | tf_op jit(solution)/shard_map/ppermute | solution.py:23
  41.4 7.3 %collective-permute-start.10 = (f32[34,1,3,258]{3,0,2,1:T(8,128)S(1)}, f32[34,1,3,258]{3,0,2,1:T(8,128)S(1)}, u32[]{:S(2)}, u32[]{:S(2)}) collective-permute-start(f32[34,1,3,258]{3,0,2,1:T(8,128)S(1)} %copy.62), channel_id=1, source_target_pairs={{1,0},{3,2},{5,4},{7,6},{9,8},{11,10},{13,12},{15,14},{17,16},{19,... | collective-permute-start | bytes 315800 | tf_op jit(solution)/shard_map/ppermute | solution.py:26
  43.9 9.0 %collective-permute-start.11 = (f32[34,1,3,258]{3,0,2,1:T(8,128)S(1)}, f32[34,1,3,258]{3,0,2,1:T(8,128)S(1)}, u32[]{:S(2)}, u32[]{:S(2)}) collective-permute-start(f32[34,1,3,258]{3,0,2,1:T(8,128)S(1)} %copy.64), channel_id=1, source_target_pairs={{0,1},{2,3},{4,5},{6,7},{8,9},{10,11},{12,13},{14,15},{16,17},{18,... | collective-permute-start | bytes 315800 | tf_op jit(solution)/shard_map/ppermute | solution.py:23
  79.8 11.3 %collective-permute-start.32 = (f32[32,16,3,1]{0,1,3,2:T(8,128)S(1)}, f32[32,16,3,1]{0,1,3,2:T(8,128)S(1)}, u32[]{:S(2)}, u32[]{:S(2)}) collective-permute-start(f32[32,16,3,1]{0,1,3,2:T(8,128)S(1)} %copy.71), channel_id=1, source_target_pairs={{16,0},{17,1},{18,2},{19,3},{20,4},{21,5},{22,6},{23,7},{24,8},{25... | collective-permute-start | bytes 18440 | tf_op jit(solution)/shard_map/ppermute | solution.py:26
  82.7 13.0 %collective-permute-start.33 = (f32[32,16,3,1]{0,1,3,2:T(8,128)S(1)}, f32[32,16,3,1]{0,1,3,2:T(8,128)S(1)}, u32[]{:S(2)}, u32[]{:S(2)}) collective-permute-start(f32[32,16,3,1]{0,1,3,2:T(8,128)S(1)} %copy.73), channel_id=1, source_target_pairs={{0,16},{1,17},{2,18},{3,19},{4,20},{5,21},{6,22},{7,23},{8,24},{9,... | collective-permute-start | bytes 18440 | tf_op jit(solution)/shard_map/ppermute | solution.py:23
  86.7 58.1 %collective-permute-start.12 = (f32[64,768]{1,0:T(8,128)}, f32[64,768]{1,0:T(8,128)}, u32[]{:S(2)}, u32[]{:S(2)}) collective-permute-start(f32[64,768]{1,0:T(8,128)} %bitcast.45), channel_id=1, source_target_pairs={{0,2},{2,4},{4,6},{6,8},{8,10},{10,12},{12,14},{1,3},{3,5},{5,7},{... | collective-permute-start | bytes 589832 | tf_op jit(solution)/shard_map/ppermute | solution.py:34
  91.1 54.9 %collective-permute-start.13 = (f32[64,768]{1,0:T(8,128)}, f32[64,768]{1,0:T(8,128)}, u32[]{:S(2)}, u32[]{:S(2)}) collective-permute-start(f32[64,768]{1,0:T(8,128)} %bitcast.47), channel_id=1, source_target_pairs={{2,0},{4,2},{6,4},{8,6},{10,8},{12,10},{14,12},{3,1},{5,3},{7,5},{... | collective-permute-start | bytes 589832 | tf_op jit(solution)/shard_map/ppermute | solution.py:34
  97.9 20.8 %collective-permute-start.34 = (f32[1,16,3,258]{3,1,2,0:T(8,128)S(1)}, f32[1,16,3,258]{3,1,2,0:T(8,128)S(1)}, u32[]{:S(2)}, u32[]{:S(2)}) collective-permute-start(f32[1,16,3,258]{3,1,2,0:T(8,128)S(1)} %get-tuple-element.75), channel_id=1, source_target_pairs={{2,0},{4,2},{6,4},{8,6},{10,8},{12,10},{14,12},{3,1},{5,3},{7,5},{... | collective-permute-start | bytes 148616 | tf_op jit(solution)/shard_map/ppermute | solution.py:26
  99.8 18.9 %collective-permute-start.35 = (f32[1,16,3,258]{3,1,2,0:T(8,128)S(1)}, f32[1,16,3,258]{3,1,2,0:T(8,128)S(1)}, u32[]{:S(2)}, u32[]{:S(2)}) collective-permute-start(f32[1,16,3,258]{3,1,2,0:T(8,128)S(1)} %get-tuple-element.76), channel_id=1, source_target_pairs={{0,2},{2,4},{4,6},{6,8},{8,10},{10,12},{12,14},{1,3},{3,5},{5,7},{... | collective-permute-start | bytes 148616 | tf_op jit(solution)/shard_map/ppermute | solution.py:23
  107.2 40.2 %collective-permute-start.4 = (f32[22,3,4,262]{3,2,1,0:T(4,128)}, f32[22,3,4,262]{3,2,1,0:T(4,128)}, u32[]{:S(2)}, u32[]{:S(2)}) collective-permute-start(f32[22,3,4,262]{3,2,1,0:T(4,128)} %get-tuple-element.105), channel_id=1, source_target_pairs={{1,0},{3,2},{5,4},{7,6},{9,8},{11,10},{13,12},{15,14},{17,16},{19,... | collective-permute-start | bytes 830024 | tf_op jit(solution)/shard_map/ppermute | solution.py:26
  119.6 4.3 collective-permute-start.36
  120.9 9.4 %collective-permute-start.37 = (f32[34,1,3,258]{3,0,2,1:T(8,128)S(1)}, f32[34,1,3,258]{3,0,2,1:T(8,128)S(1)}, u32[]{:S(2)}, u32[]{:S(2)}) collective-permute-start(f32[34,1,3,258]{3,0,2,1:T(8,128)S(1)} %copy.79), channel_id=1, source_target_pairs={{0,1},{2,3},{4,5},{6,7},{8,9},{10,11},{12,13},{14,15},{16,17},{18,... | collective-permute-start | bytes 315800 | tf_op jit(solution)/shard_map/ppermute | solution.py:23
  123.9 23.5 %collective-permute-start.5 = (f32[22,3,4,262]{3,2,1,0:T(4,128)}, f32[22,3,4,262]{3,2,1,0:T(4,128)}, u32[]{:S(2)}, u32[]{:S(2)}) collective-permute-start(f32[22,3,4,262]{3,2,1,0:T(4,128)} %get-tuple-element.106), channel_id=1, source_target_pairs={{0,1},{2,3},{4,5},{6,7},{8,9},{10,11},{12,13},{14,15},{16,17},{18,... | collective-permute-start | bytes 830024 | tf_op jit(solution)/shard_map/ppermute | solution.py:23
  162.7 9.0 %collective-permute-start.14 = (f32[16,16,4,3]{3,2,1,0:T(4,128)S(1)}, f32[16,16,4,3]{3,2,1,0:T(4,128)S(1)}, u32[]{:S(2)}, u32[]{:S(2)}) collective-permute-start(f32[16,16,4,3]{3,2,1,0:T(4,128)S(1)} %get-tuple-element.164), channel_id=1, source_target_pairs={{0,16},{1,17},{2,18},{3,19},{4,20},{5,21},{6,22},{7,23},{8,24},{9,... | collective-permute-start | bytes 36872 | tf_op jit(solution)/shard_map/ppermute | solution.py:23
  164.2 7.6 %collective-permute-start.15 = (f32[16,16,4,3]{3,2,1,0:T(4,128)S(1)}, f32[16,16,4,3]{3,2,1,0:T(4,128)S(1)}, u32[]{:S(2)}, u32[]{:S(2)}) collective-permute-start(f32[16,16,4,3]{3,2,1,0:T(4,128)S(1)} %get-tuple-element.163), channel_id=1, source_target_pairs={{16,0},{17,1},{18,2},{19,3},{20,4},{21,5},{22,6},{23,7},{24,8},{25... | collective-permute-start | bytes 36872 | tf_op jit(solution)/shard_map/ppermute | solution.py:26
  165.8 68.6 %collective-permute-start.38 = (f32[64,768]{1,0:T(8,128)S(1)}, f32[64,768]{1,0:T(8,128)S(1)}, u32[]{:S(2)}, u32[]{:S(2)}) collective-permute-start(f32[64,768]{1,0:T(8,128)S(1)} %bitcast.58), channel_id=1, source_target_pairs={{0,2},{2,4},{4,6},{6,8},{8,10},{10,12},{12,14},{1,3},{3,5},{5,7},{... | collective-permute-start | bytes 589832 | tf_op jit(solution)/shard_map/ppermute | solution.py:34
  167.8 115.7 %collective-permute-start.39 = (f32[64,768]{1,0:T(8,128)S(1)}, f32[64,768]{1,0:T(8,128)S(1)}, u32[]{:S(2)}, u32[]{:S(2)}) collective-permute-start(f32[64,768]{1,0:T(8,128)S(1)} %bitcast.57), channel_id=1, source_target_pairs={{2,0},{4,2},{6,4},{8,6},{10,8},{12,10},{14,12},{3,1},{5,3},{7,5},{... | collective-permute-start | bytes 589832 | tf_op jit(solution)/shard_map/ppermute | solution.py:34
  172.2 12.6 %collective-permute-start.16 = (f32[3,16,4,262]{3,2,1,0:T(4,128)S(1)}, f32[3,16,4,262]{3,2,1,0:T(4,128)S(1)}, u32[]{:S(2)}, u32[]{:S(2)}) collective-permute-start(f32[3,16,4,262]{3,2,1,0:T(4,128)S(1)} %get-tuple-element.137), channel_id=1, source_target_pairs={{2,0},{4,2},{6,4},{8,6},{10,8},{12,10},{14,12},{3,1},{5,3},{7,5},{... | collective-permute-start | bytes 603656 | tf_op jit(solution)/shard_map/ppermute | solution.py:26
  174.2 18.0 %collective-permute-start.17 = (f32[3,16,4,262]{3,2,1,0:T(4,128)S(1)}, f32[3,16,4,262]{3,2,1,0:T(4,128)S(1)}, u32[]{:S(2)}, u32[]{:S(2)}) collective-permute-start(f32[3,16,4,262]{3,2,1,0:T(4,128)S(1)} %get-tuple-element.138), channel_id=1, source_target_pairs={{0,2},{2,4},{4,6},{6,8},{8,10},{10,12},{12,14},{1,3},{3,5},{5,7},{... | collective-permute-start | bytes 603656 | tf_op jit(solution)/shard_map/ppermute | solution.py:23
  192.7 10.5 %collective-permute-start.18 = (f32[22,3,4,262]{3,2,1,0:T(4,128)S(1)}, f32[22,3,4,262]{3,2,1,0:T(4,128)S(1)}, u32[]{:S(2)}, u32[]{:S(2)}) collective-permute-start(f32[22,3,4,262]{3,2,1,0:T(4,128)S(1)} %get-tuple-element.101), channel_id=1, source_target_pairs={{1,0},{3,2},{5,4},{7,6},{9,8},{11,10},{13,12},{15,14},{17,16},{19,... | collective-permute-start | bytes 830024 | tf_op jit(solution)/shard_map/ppermute | solution.py:26
  194.1 13.1 %collective-permute-start.19 = (f32[22,3,4,262]{3,2,1,0:T(4,128)S(1)}, f32[22,3,4,262]{3,2,1,0:T(4,128)S(1)}, u32[]{:S(2)}, u32[]{:S(2)}) collective-permute-start(f32[22,3,4,262]{3,2,1,0:T(4,128)S(1)} %get-tuple-element.102), channel_id=1, source_target_pairs={{0,1},{2,3},{4,5},{6,7},{8,9},{10,11},{12,13},{14,15},{16,17},{18,... | collective-permute-start | bytes 830024 | tf_op jit(solution)/shard_map/ppermute | solution.py:23
  223.5 3.8 collective-permute-start.21
  227.7 11.9 %collective-permute-start.22 = (f32[3,16,4,262]{3,2,1,0:T(4,128)S(1)}, f32[3,16,4,262]{3,2,1,0:T(4,128)S(1)}, u32[]{:S(2)}, u32[]{:S(2)}) collective-permute-start(f32[3,16,4,262]{3,2,1,0:T(4,128)S(1)} %get-tuple-element.130), channel_id=1, source_target_pairs={{2,0},{4,2},{6,4},{8,6},{10,8},{12,10},{14,12},{3,1},{5,3},{7,5},{... | collective-permute-start | bytes 603656 | tf_op jit(solution)/shard_map/ppermute | solution.py:26
  229.7 16.2 %collective-permute-start.23 = (f32[3,16,4,262]{3,2,1,0:T(4,128)S(1)}, f32[3,16,4,262]{3,2,1,0:T(4,128)S(1)}, u32[]{:S(2)}, u32[]{:S(2)}) collective-permute-start(f32[3,16,4,262]{3,2,1,0:T(4,128)S(1)} %get-tuple-element.129), channel_id=1, source_target_pairs={{0,2},{2,4},{4,6},{6,8},{8,10},{10,12},{12,14},{1,3},{3,5},{5,7},{... | collective-permute-start | bytes 603656 | tf_op jit(solution)/shard_map/ppermute | solution.py:23
  246.4 10.4 %collective-permute-start.24 = (f32[22,3,4,262]{3,2,1,0:T(4,128)S(1)}, f32[22,3,4,262]{3,2,1,0:T(4,128)S(1)}, u32[]{:S(2)}, u32[]{:S(2)}) collective-permute-start(f32[22,3,4,262]{3,2,1,0:T(4,128)S(1)} %get-tuple-element.97), channel_id=1, source_target_pairs={{1,0},{3,2},{5,4},{7,6},{9,8},{11,10},{13,12},{15,14},{17,16},{19,... | collective-permute-start | bytes 830024 | tf_op jit(solution)/shard_map/ppermute | solution.py:26
  247.9 13.1 %collective-permute-start.25 = (f32[22,3,4,262]{3,2,1,0:T(4,128)S(1)}, f32[22,3,4,262]{3,2,1,0:T(4,128)S(1)}, u32[]{:S(2)}, u32[]{:S(2)}) collective-permute-start(f32[22,3,4,262]{3,2,1,0:T(4,128)S(1)} %get-tuple-element.98), channel_id=1, source_target_pairs={{0,1},{2,3},{4,5},{6,7},{8,9},{10,11},{12,13},{14,15},{16,17},{18,... | collective-permute-start | bytes 830024 | tf_op jit(solution)/shard_map/ppermute | solution.py:23
  280.9 5.8 %collective-permute-start.26 = (f32[16,16,4,3]{3,2,1,0:T(4,128)}, f32[16,16,4,3]{3,2,1,0:T(4,128)S(1)}, u32[]{:S(2)}, u32[]{:S(2)}) collective-permute-start(f32[16,16,4,3]{3,2,1,0:T(4,128)} %get-tuple-element.160), channel_id=1, source_target_pairs={{0,16},{1,17},{2,18},{3,19},{4,20},{5,21},{6,22},{7,23},{8,24},{9,... | collective-permute-start | bytes 36872 | tf_op jit(solution)/shard_map/ppermute | solution.py:23
  282.2 4.5 %collective-permute-start.27 = (f32[16,16,4,3]{3,2,1,0:T(4,128)}, f32[16,16,4,3]{3,2,1,0:T(4,128)S(1)}, u32[]{:S(2)}, u32[]{:S(2)}) collective-permute-start(f32[16,16,4,3]{3,2,1,0:T(4,128)} %get-tuple-element.159), channel_id=1, source_target_pairs={{16,0},{17,1},{18,2},{19,3},{20,4},{21,5},{22,6},{23,7},{24,8},{25... | collective-permute-start | bytes 36872 | tf_op jit(solution)/shard_map/ppermute | solution.py:26
  287.2 12.6 %collective-permute-start.28 = (f32[3,16,4,262]{3,2,1,0:T(4,128)S(1)}, f32[3,16,4,262]{3,2,1,0:T(4,128)S(1)}, u32[]{:S(2)}, u32[]{:S(2)}) collective-permute-start(f32[3,16,4,262]{3,2,1,0:T(4,128)S(1)} %get-tuple-element.125), channel_id=1, source_target_pairs={{2,0},{4,2},{6,4},{8,6},{10,8},{12,10},{14,12},{3,1},{5,3},{7,5},{... | collective-permute-start | bytes 603656 | tf_op jit(solution)/shard_map/ppermute | solution.py:26
  289.1 17.1 %collective-permute-start.29 = (f32[3,16,4,262]{3,2,1,0:T(4,128)S(1)}, f32[3,16,4,262]{3,2,1,0:T(4,128)S(1)}, u32[]{:S(2)}, u32[]{:S(2)}) collective-permute-start(f32[3,16,4,262]{3,2,1,0:T(4,128)S(1)} %get-tuple-element.126), channel_id=1, source_target_pairs={{0,2},{2,4},{4,6},{6,8},{8,10},{10,12},{12,14},{1,3},{3,5},{5,7},{... | collective-permute-start | bytes 603656 | tf_op jit(solution)/shard_map/ppermute | solution.py:23
  306.7 10.5 %collective-permute-start.30 = (f32[22,3,4,262]{3,2,1,0:T(4,128)S(1)}, f32[22,3,4,262]{3,2,1,0:T(4,128)S(1)}, u32[]{:S(2)}, u32[]{:S(2)}) collective-permute-start(f32[22,3,4,262]{3,2,1,0:T(4,128)S(1)} %get-tuple-element.93), channel_id=1, source_target_pairs={{1,0},{3,2},{5,4},{7,6},{9,8},{11,10},{13,12},{15,14},{17,16},{19,... | collective-permute-start | bytes 830024 | tf_op jit(solution)/shard_map/ppermute | solution.py:26
  308.1 13.1 %collective-permute-start.31 = (f32[22,3,4,262]{3,2,1,0:T(4,128)S(1)}, f32[22,3,4,262]{3,2,1,0:T(4,128)S(1)}, u32[]{:S(2)}, u32[]{:S(2)}) collective-permute-start(f32[22,3,4,262]{3,2,1,0:T(4,128)S(1)} %get-tuple-element.94), channel_id=1, source_target_pairs={{0,1},{2,3},{4,5},{6,7},{8,9},{10,11},{12,13},{14,15},{16,17},{18,... | collective-permute-start | bytes 830024 | tf_op jit(solution)/shard_map/ppermute | solution.py:23
  340.5 12.1 %collective-permute-start.42 = (f32[3,16,4,262]{3,2,1,0:T(4,128)S(1)}, f32[3,16,4,262]{3,2,1,0:T(4,128)S(1)}, u32[]{:S(2)}, u32[]{:S(2)}) collective-permute-start(f32[3,16,4,262]{3,2,1,0:T(4,128)S(1)} %get-tuple-element.117), channel_id=1, source_target_pairs={{2,0},{4,2},{6,4},{8,6},{10,8},{12,10},{14,12},{3,1},{5,3},{7,5},{... | collective-permute-start | bytes 603656 | tf_op jit(solution)/shard_map/ppermute | solution.py:26
  342.4 16.2 %collective-permute-start.43 = (f32[3,16,4,262]{3,2,1,0:T(4,128)S(1)}, f32[3,16,4,262]{3,2,1,0:T(4,128)S(1)}, u32[]{:S(2)}, u32[]{:S(2)}) collective-permute-start(f32[3,16,4,262]{3,2,1,0:T(4,128)S(1)} %get-tuple-element.118), channel_id=1, source_target_pairs={{0,2},{2,4},{4,6},{6,8},{8,10},{10,12},{12,14},{1,3},{3,5},{5,7},{... | collective-permute-start | bytes 603656 | tf_op jit(solution)/shard_map/ppermute | solution.py:23
  359.1 10.4 %collective-permute-start.44 = (f32[22,3,4,262]{3,2,1,0:T(4,128)S(1)}, f32[22,3,4,262]{3,2,1,0:T(4,128)S(1)}, u32[]{:S(2)}, u32[]{:S(2)}) collective-permute-start(f32[22,3,4,262]{3,2,1,0:T(4,128)S(1)} %get-tuple-element.89), channel_id=1, source_target_pairs={{1,0},{3,2},{5,4},{7,6},{9,8},{11,10},{13,12},{15,14},{17,16},{19,... | collective-permute-start | bytes 830024 | tf_op jit(solution)/shard_map/ppermute | solution.py:26
  360.6 13.1 %collective-permute-start.45 = (f32[22,3,4,262]{3,2,1,0:T(4,128)S(1)}, f32[22,3,4,262]{3,2,1,0:T(4,128)S(1)}, u32[]{:S(2)}, u32[]{:S(2)}) collective-permute-start(f32[22,3,4,262]{3,2,1,0:T(4,128)S(1)} %get-tuple-element.90), channel_id=1, source_target_pairs={{0,1},{2,3},{4,5},{6,7},{8,9},{10,11},{12,13},{14,15},{16,17},{18,... | collective-permute-start | bytes 830024 | tf_op jit(solution)/shard_map/ppermute | solution.py:23
  389.9 3.8 collective-permute-start.47
  394.1 11.9 %collective-permute-start.48 = (f32[3,16,4,262]{3,2,1,0:T(4,128)S(1)}, f32[3,16,4,262]{3,2,1,0:T(4,128)S(1)}, u32[]{:S(2)}, u32[]{:S(2)}) collective-permute-start(f32[3,16,4,262]{3,2,1,0:T(4,128)S(1)} %get-tuple-element.110), channel_id=1, source_target_pairs={{2,0},{4,2},{6,4},{8,6},{10,8},{12,10},{14,12},{3,1},{5,3},{7,5},{... | collective-permute-start | bytes 603656 | tf_op jit(solution)/shard_map/ppermute | solution.py:26
  396.1 16.2 %collective-permute-start.49 = (f32[3,16,4,262]{3,2,1,0:T(4,128)S(1)}, f32[3,16,4,262]{3,2,1,0:T(4,128)S(1)}, u32[]{:S(2)}, u32[]{:S(2)}) collective-permute-start(f32[3,16,4,262]{3,2,1,0:T(4,128)S(1)} %get-tuple-element.109), channel_id=1, source_target_pairs={{0,2},{2,4},{4,6},{6,8},{8,10},{10,12},{12,14},{1,3},{3,5},{5,7},{... | collective-permute-start | bytes 603656 | tf_op jit(solution)/shard_map/ppermute | solution.py:23
  412.8 10.4 %collective-permute-start.50 = (f32[22,3,4,262]{3,2,1,0:T(4,128)S(1)}, f32[22,3,4,262]{3,2,1,0:T(4,128)S(1)}, u32[]{:S(2)}, u32[]{:S(2)}) collective-permute-start(f32[22,3,4,262]{3,2,1,0:T(4,128)S(1)} %get-tuple-element.85), channel_id=1, source_target_pairs={{1,0},{3,2},{5,4},{7,6},{9,8},{11,10},{13,12},{15,14},{17,16},{19,... | collective-permute-start | bytes 830024 | tf_op jit(solution)/shard_map/ppermute | solution.py:26
  414.3 13.1 %collective-permute-start.51 = (f32[22,3,4,262]{3,2,1,0:T(4,128)S(1)}, f32[22,3,4,262]{3,2,1,0:T(4,128)S(1)}, u32[]{:S(2)}, u32[]{:S(2)}) collective-permute-start(f32[22,3,4,262]{3,2,1,0:T(4,128)S(1)} %get-tuple-element.86), channel_id=1, source_target_pairs={{0,1},{2,3},{4,5},{6,7},{8,9},{10,11},{12,13},{14,15},{16,17},{18,... | collective-permute-start | bytes 830024 | tf_op jit(solution)/shard_map/ppermute | solution.py:23
  (39 other events, 171.7 us)
where the time goes:
time: 454 us; the launch traced here: 447 us
  other arithmetic  188 us (41%)
  starting transfers between devices  117 us (26%)
  waiting for transfers between devices  93 us (20%)
  local copies, waits for them, and re-layouts  38 us (8%)
  matrix products  9.11 us (2%)
    concatenate x16, other arithmetic, padded_2(): block = jnp.concatenate([low, block, high], axis=dim)  64.6 us
    ppermute x24, starting transfers between devices, padded_2(): lax.ppermute(lax.slice_in_dim(block, block.shape[dim] - width, None, axis...  64.1 us
    ppermute x24, waiting for transfers between devices, padded_2(): lax.ppermute(lax.slice_in_dim(block, block.shape[dim] - width, None, axis...  61.8 us
    ppermute x24, starting transfers between devices, padded_2(): lax.ppermute(lax.slice_in_dim(block, 0, width, axis=dim), axis, backward)  39.9 us
    add x8, other arithmetic, derivative(): total = term if total is None else total + term  35.6 us
    ppermute x24, waiting for transfers between devices, padded_2(): lax.ppermute(lax.slice_in_dim(block, 0, width, axis=dim), axis, backward)  31.1 us
    sub x2, other arithmetic, smooth(): return center - filter_weight * total  24.6 us
    mul x4, other arithmetic, rate(): convect = mach[:, :, None, None] * grads[0]  15.8 us
  transfers between devices with their start and end apart: 52, of which 28 were waited for; matrix products, arithmetic and copies ran while one was open for 37% of the time, Pallas kernels for 0%

commit v1 on v0

v1 whole, which is shorter than its diff:
```python
import functools

import jax
import jax.numpy as jnp
from jax import lax
from jax.experimental import pallas as pl
from jax.experimental.pallas import tpu as pltpu
from jax.sharding import PartitionSpec as P

MOVED = True

eddy_step = 0.1
viscosity = 0.5
wave_step = 0.2
filter_weight = 0.2
deriv = (0.770882380518, -0.166705904415, 0.02084314277)
taps = (0.28739284246, -0.226146951809, 0.10630357877, -0.023853048191)

RATE_Y, RATE_Z = (0, 2), (0, 3)
ALL = (0, 1, 2, 3)
LANES = 128
VMEM = pl.BlockSpec(memory_space=pltpu.VMEM)
SMEM = pl.BlockSpec(memory_space=pltpu.SMEM)


def lane_ids(rows):
    return lax.broadcasted_iota(jnp.int32, (rows, LANES), 1)


def row_ids(lanes):
    return lax.broadcasted_iota(jnp.int32, (8, lanes), 0)


def call(body, outs, ins, scratch=(), smem=1, flops=1000000):
    shapes = [jax.ShapeDtypeStruct(s, jnp.float32) for s in outs]
    size = sum(o.size for o in shapes) + sum(i.size for i in ins)
    return pl.pallas_call(
        body,
        out_shape=shapes,
        in_specs=[SMEM] * smem + [VMEM] * (len(ins) - smem),
        out_specs=[VMEM] * len(shapes),
        scratch_shapes=list(scratch),
        compiler_params=pltpu.CompilerParams(vmem_limit_bytes=24 * 1024 * 1024),
        cost_estimate=pl.CostEstimate(flops=flops, bytes_accessed=4 * size, transcendentals=0),
    )(*ins)


def shift_tiles(tiles, left, right, by, lanes):
    out = []
    row = [left] + tiles + [right]
    for at in range(1, len(tiles) + 1):
        if by > 0:
            mixed = jnp.where(lanes < by, row[at + 1], row[at])
            out.append(pltpu.roll(mixed, LANES - by, 1))
        else:
            mixed = jnp.where(lanes >= LANES + by, row[at - 1], row[at])
            out.append(pltpu.roll(mixed, -by, 1))
    return out


def side_tiles(packed, at, group, reach, half):
    shift = lax.rem(2 * LANES - group * at - jnp.where(half == 1, reach, 0), LANES)
    tile = pltpu.roll(packed, shift, 1)
    zero = jnp.zeros_like(tile)
    return jnp.where(half == 1, tile, zero), jnp.where(half == 0, tile, zero)


def pack_z(src, dst, comps, layers, group, reach, half, put):
    rows, depth = src.shape[2], src.shape[3]
    lanes = lane_ids(rows)
    start = pl.multiple_of(jnp.where(half == 0, depth - LANES, 0), LANES)

    def step(i, acc):
        shift = lax.rem(group * i + jnp.where(half == 0, reach, 0), LANES)
        inside = (lanes >= group * i) & (lanes < group * (i + 1))
        return tuple(
            jnp.where(inside, pltpu.roll(src[put(c, i) + (slice(None), pl.ds(start, LANES))], shift, 1), a)
            for c, a in zip(comps, acc)
        )

    done = lax.fori_loop(0, layers, step, tuple(jnp.zeros((rows, LANES), jnp.float32) for _ in comps))
    for n, value in enumerate(done):
        dst[n] = value


def pack_state(o, inner, outer, ymsg, zmsg, ycomps, zcomps, info):
    pos, row, half = info[0], info[1], info[2]
    X, Y, Z = o.shape[1:]
    si = jnp.where(pos == 0, X - 3, 0)
    so = jnp.where(pos == 0, 0, X - 3)
    for c in range(4):
        for l in range(3):
            inner[3 * c + l] = o[c, si + l]
            outer[3 * c + l] = o[c, so + l]
    rows = row_ids(Z)
    ys = pl.multiple_of(jnp.where(row == 0, Y - 8, 0), 8)

    def normal(c, i):
        tile = o[c, i, pl.ds(ys, 8), :]
        return jnp.where(row == 0, pltpu.roll(tile, 4, 0), tile)

    def step(i, carry):
        for n in range(len(ycomps) // 2):
            first, second = normal(ycomps[2 * n], i), normal(ycomps[2 * n + 1], i)
            ymsg[n, i] = jnp.where(rows < 4, first, pltpu.roll(second, 4, 0))
        return carry

    lax.fori_loop(0, X, step, 0)
    pack_z(o, zmsg, zcomps, X, LANES // X, 3, half, lambda c, i: (c, i))


def fill(F, f, inner, outer, ymsg, ycomps, info):
    pos, row = info[0], info[1]
    X, Y, Z = f.shape[1:]
    hi = jnp.where(pos == 0, X + 3, 0)
    ho = jnp.where(pos == 0, 0, X + 3)
    for c in range(4):
        for l in range(3):
            F[c, hi + l, 8 : 8 + Y, :] = inner[3 * c + l]
            F[c, ho + l, 8 : 8 + Y, :] = outer[3 * c + l]

    def step(i, carry):
        for c in range(4):
            F[c, i + 3, 8 : 8 + Y, :] = f[c, i]
        for n, c in enumerate(ycomps):
            tile = ymsg[n // 2, i]
            turned = pltpu.roll(tile, 4, 0)
            if n % 2:
                tile, turned = turned, tile
            zero = jnp.zeros_like(tile)
            F[c, i + 3, 0:8, :] = jnp.where(row == 1, turned, zero)
            F[c, i + 3, 8 + Y : 16 + Y, :] = jnp.where(row == 0, tile, zero)
        return carry

    lax.fori_loop(0, X, step, 0)


def dx(F, c, i, Y, lane):
    return sum(deriv[j - 1] * (F[c, i + 3 + j, 8 : 8 + Y, lane] - F[c, i + 3 - j, 8 : 8 + Y, lane]) for j in (1, 2, 3))


def dy(F, c, i, Y, lane):
    return sum(
        deriv[j - 1] * (F[c, i + 3, 8 + j : 8 + Y + j, lane] - F[c, i + 3, 8 - j : 8 + Y - j, lane]) for j in (1, 2, 3)
    )


def z_neighbours(F, c, i, Y, Z, packed, half):
    lanes = lane_ids(Y)
    tiles = [F[c, i + 3, 8 : 8 + Y, pl.ds(t * LANES, LANES)] for t in range(Z // LANES)]
    left, right = side_tiles(packed, i, LANES // (F.shape[1] - 6), 3, half)
    return [
        (shift_tiles(tiles, left, right, j, lanes), shift_tiles(tiles, left, right, -j, lanes)) for j in (1, 2, 3)
    ]


def rate_loop(F, mach, source, zmsg, X, Y, Z, half, emit):
    def step(i, carry):
        zs = []
        for n, c in enumerate(RATE_Z):
            pairs = z_neighbours(F, c, i, Y, Z, zmsg[n], half)
            zs.append(
                [sum(deriv[j] * (pairs[j][0][t] - pairs[j][1][t]) for j in range(3)) for t in range(Z // LANES)]
            )
        for t in range(Z // LANES):
            lane = slice(t * LANES, (t + 1) * LANES)
            m = mach[i]
            gp, gu, gv, gw = (dx(F, c, i, Y, lane) for c in range(4))
            emit(0, i, lane, -(m * gp + gu + dy(F, 2, i, Y, lane) + zs[1][t]))
            emit(1, i, lane, -(m * gu + gp) - source(0, i, lane))
            emit(2, i, lane, -(m * gv + dy(F, 0, i, Y, lane)) - source(1, i, lane))
            emit(3, i, lane, -(m * gw + zs[0][t]) - source(2, i, lane))
        return carry

    lax.fori_loop(0, X, step, 0)


def source_of(S, Y):
    brick = S.shape[2] // Y

    def source(c, i, lane):
        return S[i // brick, c, pl.ds(pl.multiple_of(lax.rem(i, brick) * Y, 8), Y), lane]

    return source


def first_body(info, f, inner, outer, ymsg, zmsg, mach, own, t_in, t_out, o, S, n_in, n_out, ny, nz, F):
    X, Y, Z = f.shape[1:]
    bricks = own.shape[0]
    fill(F, f, inner, outer, ymsg, RATE_Y, info)
    at_in = jnp.where(info[0] == 0, bricks - 1, 0)
    at_out = jnp.where(info[0] == 0, 0, bricks - 1)
    S[...] = own[...]
    layers = own.shape[2] // Y
    for ref, at in ((t_in, at_in), (t_out, at_out)):
        for c in range(3):
            for l in range(layers):
                piece = (at, c, slice(l * Y, (l + 1) * Y))
                S[piece] = S[piece] + ref[c * layers + l]

    def emit(c, i, lane, value):
        o[c, i, :, lane] = f[c, i, :, lane] + wave_step * value

    rate_loop(F, mach, source_of(S, Y), zmsg, X, Y, Z, info[2], emit)
    pack_state(o, n_in, n_out, ny, nz, RATE_Y, RATE_Z, info)


def second_body(info, f, inner, outer, ymsg, zmsg, mach, S, state, *rest, extra):
    if extra:
        t_in, t_out, o, n_in, n_out, ny, nz, F = rest
        for n in range(t_in.shape[0]):
            n_in[12 + n] = t_in[n]
            n_out[12 + n] = t_out[n]
    else:
        o, n_in, n_out, ny, nz, F = rest
    X, Y, Z = f.shape[1:]
    fill(F, f, inner, outer, ymsg, RATE_Y, info)

    def emit(c, i, lane, value):
        o[c, i, :, lane] = 0.5 * (state[c, i, :, lane] + f[c, i, :, lane]) + (0.5 * wave_step) * value

    rate_loop(F, mach, source_of(S, Y), zmsg, X, Y, Z, info[2], emit)
    pack_state(o, n_in, n_out, ny, nz, ALL, ALL, info)


def smooth_body(info, f, inner, outer, ymsg, zmsg, o, *rest):
    F = rest[-1]
    X, Y, Z = f.shape[1:]
    fill(F, f, inner, outer, ymsg, ALL, info)

    def step(i, carry):
        for c in range(4):
            pairs = z_neighbours(F, c, i, Y, Z, zmsg[c], info[2])
            for t in range(Z // LANES):
                lane = slice(t * LANES, (t + 1) * LANES)
                center = F[c, i + 3, 8 : 8 + Y, lane]
                total = (1.0 - 3.0 * filter_weight * taps[0]) * center
                for j in (1, 2, 3):
                    beside = (
                        (F[c, i + 3 + j, 8 : 8 + Y, lane] + F[c, i + 3 - j, 8 : 8 + Y, lane])
                        + (F[c, i + 3, 8 + j : 8 + Y + j, lane] + F[c, i + 3, 8 - j : 8 + Y - j, lane])
                        + (pairs[j - 1][0][t] + pairs[j - 1][1][t])
                    )
                    total = total - (filter_weight * taps[j]) * beside
                o[c, i, :, lane] = total
        return carry

    lax.fori_loop(0, X, step, 0)
    if len(rest) > 1:
        pack_state(o, *rest[:4], RATE_Y, RATE_Z, info)


def pack_body(info, f, inner, outer, ymsg, zmsg):
    pack_state(f, inner, outer, ymsg, zmsg, RATE_Y, RATE_Z, info)


def pack_les(v, inner, outer, ymsg, zmsg, base, info):
    pos, row, half = info[0], info[1], info[2]
    X, _, Y, Z = v.shape
    si = jnp.where(pos == 0, X - 1, 0)
    so = jnp.where(pos == 0, 0, X - 1)
    rows = row_ids(Z)
    ys = pl.multiple_of(jnp.where(row == 0, Y - 8, 0), 8)
    for c in range(3):
        inner[base + c] = v[si, c]
        outer[base + c] = v[so, c]
        for n in range(X // 8):
            acc = jnp.zeros((8, Z), jnp.float32)
            for r in range(8):
                tile = v[8 * n + r, c, pl.ds(ys, 8), :]
                moved = jnp.where(row == 0, pltpu.roll(tile, (r + 1) % 8, 0), pltpu.roll(tile, r, 0) if r else tile)
                acc = jnp.where(rows == r, moved, acc)
            ymsg[c, n] = acc
    pack_z(v, zmsg, (0, 1, 2), X, LANES // X, 1, half, lambda c, i: (i, c))


def pack_les_body(info, v, inner, outer, ymsg, zmsg):
    pack_les(v, inner, outer, ymsg, zmsg, 0, info)


def les_body(info, offset, v, inner, outer, ymsg, zmsg, tiles, *rest, base, advance):
    if advance:
        v1, own, n_in, n_out, ny, nz, V, LB, ACC = rest
    else:
        own, n_in, n_out, V, LB, ACC = rest
    pos, row, half = info[0], info[1], info[2]
    X, _, Y, Z = v.shape
    blocks = LB.shape[1]
    wide = X // blocks
    plane = wide * Y
    bricks = own.shape[0]
    hi = jnp.where(pos == 0, X + 1, 0)
    ho = jnp.where(pos == 0, 0, X + 1)
    for c in range(3):
        V[c, hi, 8 : 8 + Y, :] = inner[base + c]
        V[c, ho, 8 : 8 + Y, :] = outer[base + c]
        for n in range(X // 8):
            tile = ymsg[c, n]
            zero = jnp.zeros_like(tile)
            for r in range(8):
                low = pltpu.roll(tile, 7 - r, 0) if r < 7 else tile
                high = pltpu.roll(tile, 8 - r, 0) if r else tile
                V[c, 8 * n + r + 1, 0:8, :] = jnp.where(row == 1, low, zero)
                V[c, 8 * n + r + 1, 8 + Y : 16 + Y, :] = jnp.where(row == 0, high, zero)

    def copy(i, carry):
        for c in range(3):
            V[c, i + 1, 8 : 8 + Y, :] = v[i, c]
        return carry

    lax.fori_loop(0, X, copy, 0)
    ACC[...] = jnp.zeros_like(ACC)
    lanes = lane_ids(Y)
    count = Z // LANES

    def step(i, carry):
        center = [[V[c, i + 1, 8 : 8 + Y, pl.ds(t * LANES, LANES)] for t in range(count)] for c in range(3)]
        ahead, behind = [], []
        for c in range(3 if advance else 2):
            left, right = side_tiles(zmsg[c], i, LANES // X, 1, half)
            ahead.append(shift_tiles(center[c], left, right, 1, lanes))
            behind.append(shift_tiles(center[c], left, right, -1, lanes))
        at = lax.rem(i, wide) * Y
        b = i // wide
        for t in range(count):
            lane = slice(t * LANES, (t + 1) * LANES)
            xa = [V[c, i + 2, 8 : 8 + Y, lane] for c in range(3)]
            xb = [V[c, i, 8 : 8 + Y, lane] for c in range(3)]
            ya = [V[c, i + 1, 9 : 9 + Y, lane] for c in range(3)]
            yb = [V[c, i + 1, 7 : 7 + Y, lane] for c in range(3)]
            u, w, q = center[0][t], center[1][t], center[2][t]
            vx = 0.5 * ((ya[2] - yb[2]) - (ahead[1][t] - behind[1][t]))
            vy = 0.5 * ((ahead[0][t] - behind[0][t]) - (xa[2] - xb[2]))
            vz = 0.5 * ((xa[1] - xb[1]) - (ya[0] - yb[0]))
            lamb = [vy * q - vz * w, vz * u - vx * q, vx * w - vy * u]
            for c in range(3):
                high = lamb[c].astype(jnp.bfloat16)
                low = (lamb[c] - high.astype(jnp.float32)).astype(jnp.bfloat16)
                LB[c, b, pl.ds(pl.multiple_of(at, 16), Y), lane] = high
                LB[c, b, pl.ds(pl.multiple_of(plane + at, 16), Y), lane] = low
                if advance:
                    laplace = -6.0 * center[c][t] + ((xa[c] + xb[c]) + (ya[c] + yb[c]) + (ahead[c][t] + behind[c][t]))
                    v1[i, c, :, lane] = center[c][t] + eddy_step * (viscosity * laplace - lamb[c])
        return carry

    lax.fori_loop(0, X, step, 0)

    def restrict(b, carry):
        tile = tiles[b].astype(jnp.bfloat16)
        m = b // 2 + 1
        to = m + offset[b]
        for c in range(3):
            both = jnp.dot(tile, LB[c, b], preferred_element_type=jnp.float32)
            ACC[m, c] = ACC[m, c] + both[:plane]
            ACC[to, c] = ACC[to, c] + both[plane:]
        return carry

    lax.fori_loop(0, blocks, restrict, 0)
    own[...] = ACC[1 : bricks + 1]
    ti = jnp.where(pos == 0, bricks + 1, 0)
    to = jnp.where(pos == 0, 0, bricks + 1)
    layers = plane // Y
    for c in range(3):
        for l in range(layers):
            n_in[c * layers + l] = ACC[ti, c, l * Y : (l + 1) * Y, :]
            n_out[c * layers + l] = ACC[to, c, l * Y : (l + 1) * Y, :]
    if advance:
        pack_les(v1, n_in, n_out, ny, nz, 3 * layers, info)


def solution(mesh):
    axes = mesh.axis_names
    sizes = [mesh.shape[a] for a in axes]
    gx = mesh.shape["gx"]

    def flat(**at):
        index = 0
        for axis, size in zip(axes, sizes):
            index = index * size + at[axis]
        return index

    cells = [(k, p, y, c) for k in range(gx // 2) for p in (0, 1) for y in range(mesh.shape["gy"]) for c in (0, 1)]

    def home(g, y, a):
        return flat(gx=2 * (g // 2) + a, gy=y, grp=g % 2)

    move = [(flat(gx=2 * k + p, gy=y, grp=c), home(2 * k + p, y, c)) for k, p, y, c in cells]
    back = [(target, source) for source, target in move]
    swap = [(0, 1), (1, 0)]
    even = [pair for k in range(gx // 2) for pair in ((2 * k, 2 * k + 1), (2 * k + 1, 2 * k))]
    odd = [pair for k in range(gx // 2 - 1) for pair in ((2 * k + 1, 2 * k + 2), (2 * k + 2, 2 * k + 1))]
    hop = [(home(s, y, a), home(d, y, a)) for s, d in odd for y in range(mesh.shape["gy"]) for a in (0, 1)]

    def send(inner, outer, ymsg, zmsg):
        if MOVED:
            outer = lax.ppermute(outer, axes, hop)
            zmsg = lax.ppermute(zmsg, "gx", even)
            ymsg = lax.ppermute(ymsg, "gy", swap)
            inner = lax.ppermute(inner, "grp", swap)
        else:
            outer = lax.ppermute(outer, "gx", odd)
            inner = lax.ppermute(inner, "gx", even)
            ymsg = lax.ppermute(ymsg, "gy", swap)
            zmsg = lax.ppermute(zmsg, "grp", swap)
        return inner, outer, ymsg, zmsg

    def body(les_velocity, mean_mach, transfer_tiles, intersection_offset, acoustic_state):
        X2, Y, _, Z = les_velocity.shape
        X = acoustic_state.shape[0]
        blocks, plane = transfer_tiles.shape[0], transfer_tiles.shape[-1]
        bricks = blocks // 2
        layers = plane // Y
        position, parity = lax.axis_index("grp"), lax.axis_index("gx") % 2
        if not MOVED:
            position, parity = parity, position
        info = jnp.stack([position, lax.axis_index("gy"), parity]).astype(jnp.int32)

        v = les_velocity.transpose(0, 2, 1, 3)
        state = acoustic_state.transpose(2, 0, 1, 3)
        tiles = transfer_tiles[:, 0].astype(jnp.float32).swapaxes(2, 3).reshape(blocks, 2 * plane, plane)
        mach, offset = mean_mach, intersection_offset
        if MOVED:
            v = lax.ppermute(v, axes, move)
            small = jnp.concatenate(
                [
                    tiles.reshape(-1, LANES),
                    jnp.pad(mach, ((0, 0), (0, LANES - Y))),
                    jnp.pad(offset.astype(jnp.float32)[None], ((0, 7), (0, LANES - blocks))),
                ]
            )
            small = lax.ppermute(small, axes, move)
            state = lax.ppermute(state, axes, move)
            tall = tiles.size // LANES
            tiles = small[:tall].reshape(blocks, 2 * plane, plane)
            mach = small[tall : tall + X, :Y]
            offset = small[tall + X, :blocks].astype(jnp.int32)
        tiles = jnp.concatenate([tiles, tiles], axis=2)
        mach = jnp.broadcast_to(mach[:, :, None], (X, Y, LANES))

        edge_x = (12, Y, Z)
        edge_y, edge_yy = (1, X, 8, Z), (2, X, 8, Z)
        edge_z, edge_zz = (2, Y, LANES), (4, Y, LANES)
        les_y, les_z = (3, X2 // 8, 8, Z), (3, Y, LANES)
        F = pltpu.VMEM((4, X + 6, Y + 16, Z), jnp.float32)
        les_scratch = [
            pltpu.VMEM((3, X2 + 2, Y + 16, Z), jnp.float32),
            pltpu.VMEM((3, blocks, 2 * plane, Z), jnp.bfloat16),
            pltpu.VMEM((bricks + 2, 3, plane, Z), jnp.float32),
        ]
        grid = state.shape
        own_shape = (bricks, 3, plane, Z)
        term = (3 * layers, Y, Z)

        les_edges = send(*call(pack_les_body, [(3, Y, Z), (3, Y, Z), les_y, les_z], [info, v]))
        state_edges = send(*call(pack_body, [edge_x, edge_x, edge_y, edge_z], [info, state]))
        with_terms = (3 * layers + 3, Y, Z)
        v1, own, *edges = call(
            functools.partial(les_body, base=0, advance=True),
            [v.shape, own_shape, with_terms, with_terms, les_y, les_z],
            [info, offset, v, *les_edges, tiles],
            les_scratch,
            smem=2,
            flops=4000000,
        )
        edges = send(*edges)
        middle, S, *middle_edges = call(
            first_body,
            [grid, own_shape, edge_x, edge_x, edge_y, edge_z],
            [info, state, *state_edges, mach, own, edges[0], edges[1]],
            [F],
            flops=4000000,
        )
        middle_edges = send(*middle_edges)
        own2, up2, down2 = call(
            functools.partial(les_body, base=3 * layers, advance=False),
            [own_shape, term, term],
            [info, offset, v1, *edges, tiles],
            les_scratch,
            smem=2,
            flops=4000000,
        )
        edge_t = (12 + 3 * layers, Y, Z)
        updated, *up_edges = call(
            functools.partial(second_body, extra=True),
            [grid, edge_t, edge_t, edge_yy, edge_zz],
            [info, middle, *middle_edges, mach, S, state, up2, down2],
            [F],
            flops=4000000,
        )
        up_edges = send(*up_edges)
        state, *state_edges = call(
            smooth_body, [grid, edge_x, edge_x, edge_y, edge_z], [info, updated, *up_edges], [F], flops=4000000
        )
        state_edges = send(*state_edges)
        middle, S, *middle_edges = call(
            first_body,
            [grid, own_shape, edge_x, edge_x, edge_y, edge_z],
            [info, state, *state_edges, mach, own2, up_edges[0][12:], up_edges[1][12:]],
            [F],
            flops=4000000,
        )
        middle_edges = send(*middle_edges)
        updated, *up_edges = call(
            functools.partial(second_body, extra=False),
            [grid, edge_x, edge_x, edge_yy, edge_zz],
            [info, middle, *middle_edges, mach, S, state],
            [F],
            flops=4000000,
        )
        up_edges = send(*up_edges)
        (state,) = call(smooth_body, [grid], [info, updated, *up_edges], [F], flops=4000000)
        if MOVED:
            state = lax.ppermute(state, axes, back)
        return state.transpose(1, 2, 0, 3)

    placed = (
        P("gx", "gy", None, "grp"),
        P("gx", "gy"),
        P("gx", "gy", None, None, None),
        P("gx"),
        P("gx", "gy", None, "grp"),
    )
    return jax.shard_map(body, mesh=mesh, in_specs=placed, out_specs=P("gx", "gy", None, "grp"), check_vma=False)
```

time: 454 us -> 181 us (0.40)
  the two profiles are of different devices: /device:TPU:6 before, /device:TPU:9 now
where the time goes in v1:
time: 181 us
  waiting for transfers between devices  59 us (33%)
  starting transfers between devices  57.1 us (32%)
  Pallas kernels  54.9 us (30%)
  local copies, waits for them, and re-layouts  7.38 us (4%)
  other arithmetic  1.84 us (1%)
    pallas_call x10, Pallas kernels, call(): pl.pallas_call(body, out_shape=shapes, in_specs=[SMEM] * smem + [VMEM] *...  54.9 us
    ppermute x8, starting transfers between devices, send(): outer = lax.ppermute(outer, axes, hop)  25.6 us
    ppermute x1, waiting for transfers between devices, body(): small = lax.ppermute(small, axes, move)  22.1 us
    ppermute x8, waiting for transfers between devices, send(): ymsg = lax.ppermute(ymsg, 'gy', swap)  12.9 us
    ppermute x1, waiting for transfers between devices, body(): state = lax.ppermute(state, axes, back)  12.5 us
    ppermute x8, starting transfers between devices, send(): zmsg = lax.ppermute(zmsg, 'gx', even)  11.6 us
    ppermute x8, waiting for transfers between devices, send(): zmsg = lax.ppermute(zmsg, 'gx', even)  10.8 us
    ppermute x8, starting transfers between devices, send(): ymsg = lax.ppermute(ymsg, 'gy', swap)  4.11 us
  transfers between devices with their start and end apart: 36, of which 15 were waited for; matrix products, arithmetic and copies ran while one was open for 4% of the time, Pallas kernels for 14%

profile of v1, /device:TPU:9, one launch (start us, length us, event | category | flops | bytes accessed | tf_op | source)
XLA Modules:
  0.0 180.6 jit_solution(12911966434622993230)
XLA Ops:
  0.0 3.8 %collective-permute-start.6 = (f32[32,3,16,256]{3,2,1,0:T(8,128)}, f32[32,3,16,256]{3,2,1,0:T(8,128)S(1)}, u32[]{:S(2)}, u32[]{:S(2)}) collective-permute-start(f32[32,3,16,256]{3,2,1,0:T(8,128)} %bitcast.20), channel_id=1, source_target_pairs={{0,0},{16,2},{1,1},{17,3},{2,16},{18,18},{3,17},{19,19},{4,4},{20,... | collective-permute-start | bytes 4718600 | tf_op jit(solution)/shard_map/ppermute | solution.py:423
  3.8 2.4 %copy.12 = f32[16,16,4,256]{3,1,0,2:T(8,128)} copy(f32[16,16,4,256]{3,2,1,0:T(4,128)} %param.9) | data formatting | bytes 2097152 | tf_op args[4]
  6.2 2.0 %collective-permute-start = (f32[4,16,16,256]{3,2,1,0:T(8,128)}, f32[4,16,16,256]{3,2,1,0:T(8,128)S(1)}, u32[]{:S(2)}, u32[]{:S(2)}) collective-permute-start(f32[4,16,16,256]{3,2,1,0:T(8,128)} %bitcast.18), channel_id=1, source_target_pairs={{0,0},{16,2},{1,1},{17,3},{2,16},{18,18},{3,17},{19,19},{4,4},{20,... | collective-permute-start | bytes 3145736 | tf_op jit(solution)/shard_map/ppermute | solution.py:432
  9.1 1.2 copy.9
  10.6 3.6 %collective-permute-start.5 = (f32[536,128]{1,0:T(8,128)S(1)}, f32[536,128]{1,0:T(8,128)}, u32[]{:S(2)}, u32[]{:S(2)}) collective-permute-start(f32[536,128]{1,0:T(8,128)S(1)} %select_maximum_fusion), channel_id=1, source_target_pairs={{0,0},{16,2},{1,1},{17,3},{2,16},{18,18},{3,17},{19,19},{4,4},{20,... | collective-permute-start | bytes 823304 | tf_op jit(solution)/shard_map/ppermute | solution.py:431
  14.3 22.1 %collective-permute-done.5 = f32[536,128]{1,0:T(8,128)} collective-permute-done((f32[536,128]{1,0:T(8,128)S(1)}, f32[536,128]{1,0:T(8,128)}, u32[]{:S(2)}, u32[]{:S(2)}) %collective-permute-start.5) | collective-permute-done | bytes 274464 | tf_op jit(solution)/shard_map/ppermute | solution.py:431
  38.2 3.1 %shard_map.56 = (f32[3,16,256]{2,1,0:T(8,128)S(1)}, f32[3,16,256]{2,1,0:T(8,128)S(1)}, f32[3,4,8,256]{3,2,1,0:T(8,128)S(1)}, f32[3,16,128]{2,1,0:T(8,128)S(1)}) custom-call(s32[3]{0:T(128)S(1)} %pad_add_fusion.info, f32[32,3,16,256]{3,2,1,0:T(8,128)S(1)} %collective-permute-done.6.v), custom_call_target="tpu_custom_call" | custom-call | flops 1000000 | bytes 1794060 | tf_op jit(solution)/shard_map/pallas_call | solution.py:37
  41.3 1.3 collective-permute-start.9
  42.5 3.6 %collective-permute-start.8 = (f32[3,16,256]{2,1,0:T(8,128)S(1)}, f32[3,16,256]{2,1,0:T(8,128)S(1)}, u32[]{:S(2)}, u32[]{:S(2)}) collective-permute-start(f32[3,16,256]{2,1,0:T(8,128)S(1)} %get-tuple-element.54), channel_id=1, source_target_pairs={{16,4},{18,6},{17,5},{19,7},{4,16},{6,18},{5,17},{7,19},{20,8},{22... | collective-permute-start | bytes 147464 | tf_op jit(solution)/shard_map/ppermute | solution.py:396
  46.1 1.7 collective-permute-start.10
  48.0 1.0 collective-permute-done.10.zmsg
  49.1 11.5 %shard_map.57 = (f32[32,3,16,256]{3,2,1,0:T(8,128)S(1)}, f32[4,3,64,256]{3,2,1,0:T(8,128)S(1)}, f32[15,16,256]{2,1,0:T(8,128)S(1)}, f32[15,16,256]{2,1,0:T(8,128...) custom-call(s32[3]{0:T(128)S(1)} %pad_add_fusion.info, s32[8]{0:T(128)S(1)} %fusion.1.offset, ...), custom_call_target="tpu_custom_call" | custom-call | flops 4000000 | bytes 5292076 | tf_op jit(solution)/shard_map/pallas_call | solution.py:37
  60.8 3.3 %collective-permute-start.12 = (f32[15,16,256]{2,1,0:T(8,128)S(1)}, f32[15,16,256]{2,1,0:T(8,128)S(1)}, u32[]{:S(2)}, u32[]{:S(2)}) collective-permute-start(f32[15,16,256]{2,1,0:T(8,128)S(1)} %get-tuple-element.59), channel_id=1, source_target_pairs={{16,4},{18,6},{17,5},{19,7},{4,16},{6,18},{5,17},{7,19},{20,8},{22... | collective-permute-start | bytes 737288 | tf_op jit(solution)/shard_map/ppermute | solution.py:396
  64.1 1.8 %shard_map.55 = (f32[12,16,256]{2,1,0:T(8,128)S(1)}, f32[12,16,256]{2,1,0:T(8,128)S(1)}, f32[1,16,8,256]{3,2,1,0:T(8,128)S(1)}, f32[2,16,128]{2,1,0:T(8,128)S(1)}) custom-call(s32[3]{0:T(128)S(1)} %pad_add_fusion.info, f32[4,16,16,256]{3,2,1,0:T(8,128)S(1)} %collective-permute-done.f.state), custom_call_target="tpu_custom_call" | custom-call | flops 1000000 | bytes 1589260 | tf_op jit(solution)/shard_map/pallas_call | solution.py:37
  66.0 3.3 %collective-permute-start.2 = (f32[12,16,256]{2,1,0:T(8,128)S(1)}, f32[12,16,256]{2,1,0:T(8,128)S(1)}, u32[]{:S(2)}, u32[]{:S(2)}) collective-permute-start(f32[12,16,256]{2,1,0:T(8,128)S(1)} %get-tuple-element.50), channel_id=1, source_target_pairs={{16,4},{18,6},{17,5},{19,7},{4,16},{6,18},{5,17},{7,19},{20,8},{22... | collective-permute-start | bytes 589832 | tf_op jit(solution)/shard_map/ppermute | solution.py:396
  69.4 1.8 collective-permute-start.4
  71.2 1.4 collective-permute-done.4.zmsg
  73.5 4.4 %collective-permute-done.3.ymsg = f32[1,16,8,256]{3,2,1,0:T(8,128)S(1)} collective-permute-done((f32[1,16,8,256]{3,2,1,0:T(8,128)S(1)}, f32[1,16,8,256]{3,2,1,0:T(8,128)S(1)}, u32[]{:S(2)}, u32[]{:S(2)}) %collective-permute-start.3) | collective-permute-done | bytes 131104 | tf_op jit(solution)/shard_map/ppermute | solution.py:398
  78.1 5.0 %shard_map.58 = (f32[4,16,16,256]{3,2,1,0:T(8,128)S(1)}, f32[4,3,64,256]{3,2,1,0:T(8,128)S(1)}, f32[12,16,256]{2,1,0:T(8,128)S(1)}, f32[12,16,256]{2,1,0:T(8,128...) custom-call(s32[3]{0:T(128)S(1)} %pad_add_fusion.info, ...), custom_call_target="tpu_custom_call" | custom-call | flops 4000000 | bytes 5373964 | tf_op jit(solution)/shard_map/pallas_call | solution.py:37
  83.7 2.1 %collective-permute-start.14 = (f32[12,16,256]{2,1,0:T(8,128)S(1)}, f32[12,16,256]{2,1,0:T(8,128)S(1)}, u32[]{:S(2)}, u32[]{:S(2)}) collective-permute-start(f32[12,16,256]{2,1,0:T(8,128)S(1)} %get-tuple-element.62), channel_id=1, source_target_pairs={{16,4},{18,6},{17,5},{19,7},{4,16},{6,18},{5,17},{7,19},{20,8},{22... | collective-permute-start | bytes 589832 | tf_op jit(solution)/shard_map/ppermute | solution.py:396
  86.0 1.2 collective-permute-start.17
  87.3 1.5 collective-permute-start.18
  88.8 1.5 collective-permute-done.18.zmsg
  90.3 1.5 collective-permute-start.16
  91.8 1.3 collective-permute-done.17.ymsg
  93.1 8.5 %shard_map.59 = (f32[4,3,64,256]{3,2,1,0:T(8,128)S(1)}, f32[12,16,256]{2,1,0:T(8,128)S(1)}, f32[12,16,256]{2,1,0:T(8,128)S(1)}) custom-call(s32[3]{0:T(128)S(1)} %pad_add_fusion.info, s32[8]{0:T(128)S(1)} %fusion.1.offset, f32[32,3,16,256]{3,2,1,0:T(8,128)S(1)} %get-tuple-element.66.v, f32[15,16,256]{2,1,0:T(8,128)S(1)} %collective-permute-done.11.t_in.inner, ...), custom_call_target="tpu_custom_call" | custom-call | flops 4000000 | bytes 3891244 | tf_op jit(solution)/shard_map/pallas_call | solution.py:37
  101.6 5.1 %shard_map.60 = (f32[4,16,16,256]{3,2,1,0:T(8,128)S(1)}, f32[24,16,256]{2,1,0:T(8,128)S(1)}, f32[24,16,256]{2,1,0:T(8,128)S(1)}, f32[2,16,8,256]{3,2,1,0:T(8,128)S(1)}, f32[4,16,128]{2,1,0:T(8,128)S(1)}) custom-call(s32[3]{0:T(128)S(1)} %pad_add_fusion.info, f32[4,16,16,256]{3,2,1,0:T(8,128)S(1)} %get-tuple-element.60.f, ...), custom_call_target="tpu_custom_call" | custom-call | flops 4000000 | bytes 6078476 | tf_op jit(solution)/shard_map/pallas_call | solution.py:37
  107.5 3.1 %collective-permute-start.20 = (f32[24,16,256]{2,1,0:T(8,128)S(1)}, f32[24,16,256]{2,1,0:T(8,128)S(1)}, u32[]{:S(2)}, u32[]{:S(2)}) collective-permute-start(f32[24,16,256]{2,1,0:T(8,128)S(1)} %get-tuple-element.73), channel_id=1, source_target_pairs={{16,4},{18,6},{17,5},{19,7},{4,16},{6,18},{5,17},{7,19},{20,8},{22... | collective-permute-start | bytes 1179656 | tf_op jit(solution)/shard_map/ppermute | solution.py:396
  110.8 1.3 collective-permute-start.22
  112.2 1.7 collective-permute-done.22.zmsg
  113.9 4.1 %collective-permute-done.21.ymsg = f32[2,16,8,256]{3,2,1,0:T(8,128)S(1)} collective-permute-done((f32[2,16,8,256]{3,2,1,0:T(8,128)S(1)}, f32[2,16,8,256]{3,2,1,0:T(8,128)S(1)}, u32[]{:S(2)}, u32[]{:S(2)}) %collective-permute-start.21) | collective-permute-done | bytes 262176 | tf_op jit(solution)/shard_map/ppermute | solution.py:398
  118.0 5.6 %shard_map.61 = (f32[4,16,16,256]{3,2,1,0:T(8,128)S(1)}, f32[12,16,256]{2,1,0:T(8,128)S(1)}, f32[12,16,256]{2,1,0:T(8,128)S(1)}, f32[1,16,8,256]{3,2,1,0:T(8,128)S(1)}, f32[2,16,128]{2,1,0:T(8,128)S(1)}) custom-call(s32[3]{0:T(128)S(1)} %pad_add_fusion.info, f32[4,16,16,256]{3,2,1,0:T(8,128)S(1)} %get-tuple-element.71.f, ...), custom_call_target="tpu_custom_call" | custom-call | flops 4000000 | bytes 3719180 | tf_op jit(solution)/shard_map/pallas_call | solution.py:37
  123.7 3.5 %collective-permute-start.24 = (f32[12,16,256]{2,1,0:T(8,128)S(1)}, f32[12,16,256]{2,1,0:T(8,128)S(1)}, u32[]{:S(2)}, u32[]{:S(2)}) collective-permute-start(f32[12,16,256]{2,1,0:T(8,128)S(1)} %get-tuple-element.78), channel_id=1, source_target_pairs={{16,4},{18,6},{17,5},{19,7},{4,16},{6,18},{5,17},{7,19},{20,8},{22... | collective-permute-start | bytes 589832 | tf_op jit(solution)/shard_map/ppermute | solution.py:396
  128.6 1.8 %collective-permute-done.26.zmsg = f32[2,16,128]{2,1,0:T(8,128)S(1)} collective-permute-done((f32[2,16,128]{2,1,0:T(8,128)S(1)}, f32[2,16,128]{2,1,0:T(8,128)S(1)}, u32[]{:S(2)}, u32[]{:S(2)}) %collective-permute-start.26) | collective-permute-done | bytes 16416 | tf_op jit(solution)/shard_map/ppermute | solution.py:397
  130.4 1.4 collective-permute-done.25.ymsg
  131.8 5.0 %shard_map.62 = (f32[4,16,16,256]{3,2,1,0:T(8,128)S(1)}, f32[4,3,64,256]{3,2,1,0:T(8,128)S(1)}, f32[12,16,256]{2,1,0:T(8,128)S(1)}, f32[12,16,256]{2,1,0:T(8,128...) custom-call(s32[3]{0:T(128)S(1)} %pad_add_fusion.info, ...), custom_call_target="tpu_custom_call" | custom-call | flops 4000000 | bytes 5275660 | tf_op jit(solution)/shard_map/pallas_call | solution.py:37
  136.9 3.3 %collective-permute-start.28 = (f32[12,16,256]{2,1,0:T(8,128)S(1)}, f32[12,16,256]{2,1,0:T(8,128)S(1)}, u32[]{:S(2)}, u32[]{:S(2)}) collective-permute-start(f32[12,16,256]{2,1,0:T(8,128)S(1)} %get-tuple-element.84), channel_id=1, source_target_pairs={{16,4},{18,6},{17,5},{19,7},{4,16},{6,18},{5,17},{7,19},{20,8},{22... | collective-permute-start | bytes 589832 | tf_op jit(solution)/shard_map/ppermute | solution.py:396
  140.5 1.2 collective-permute-start.30
  141.7 1.7 collective-permute-done.30.zmsg
  143.4 1.6 collective-permute-done.29.ymsg
  145.0 5.1 %shard_map.63 = (f32[4,16,16,256]{3,2,1,0:T(8,128)S(1)}, f32[12,16,256]{2,1,0:T(8,128)S(1)}, f32[12,16,256]{2,1,0:T(8,128)S(1)}, f32[2,16,8,256]{3,2,1,0:T(8,128)S(1)}, f32[4,16,128]{2,1,0:T(8,128)S(1)}) custom-call(s32[3]{0:T(128)S(1)} %pad_add_fusion.info, f32[4,16,16,256]{3,2,1,0:T(8,128)S(1)} %get-tuple-element.82.f, ...), custom_call_target="tpu_custom_call" | custom-call | flops 4000000 | bytes 5292044 | tf_op jit(solution)/shard_map/pallas_call | solution.py:37
  150.9 3.3 %collective-permute-start.32 = (f32[12,16,256]{2,1,0:T(8,128)S(1)}, f32[12,16,256]{2,1,0:T(8,128)S(1)}, u32[]{:S(2)}, u32[]{:S(2)}) collective-permute-start(f32[12,16,256]{2,1,0:T(8,128)S(1)} %get-tuple-element.90), channel_id=1, source_target_pairs={{16,4},{18,6},{17,5},{19,7},{4,16},{6,18},{5,17},{7,19},{20,8},{22... | collective-permute-start | bytes 589832 | tf_op jit(solution)/shard_map/ppermute | solution.py:396
  154.1 1.6 collective-permute-start.34
  155.8 1.6 collective-permute-done.34.zmsg
  158.2 4.3 %shard_map.64 = f32[4,16,16,256]{3,2,1,0:T(8,128)S(1)} custom-call(s32[3]{0:T(128)S(1)} %pad_add_fusion.info, f32[4,16,16,256]{3,2,1,0:T(8,128)S(1)} %get-tuple-element.88.f, f32[12,16,256]{2,1,0:T(8,128)S(1)} %collective-permute-done.31.inner, f32[12,16,256]{2,1,0:T(8,128)S(1)} %collective-permute-done.32.outer, ...), custom_call_target="tpu_custom_call" | custom-call | flops 4000000 | bytes 2785292 | tf_op jit(solution)/shard_map/pallas_call | solution.py:37
  162.4 4.0 %collective-permute-start.35 = (f32[4,16,16,256]{3,2,1,0:T(8,128)S(1)}, f32[4,16,16,256]{3,2,1,0:T(8,128)S(1)}, u32[]{:S(2)}, u32[]{:S(2)}) collective-permute-start(f32[4,16,16,256]{3,2,1,0:T(8,128)S(1)} %shard_map.64), channel_id=1, source_target_pairs={{0,0},{2,16},{1,1},{3,17},{16,2},{18,18},{17,3},{19,19},{4,4},{6,2... | collective-permute-start | bytes 3145736 | tf_op jit(solution)/shard_map/ppermute | solution.py:513
  166.4 12.5 %collective-permute-done.35 = f32[4,16,16,256]{3,2,1,0:T(8,128)S(1)} collective-permute-done((f32[4,16,16,256]{3,2,1,0:T(8,128)S(1)}, f32[4,16,16,256]{3,2,1,0:T(8,128)S(1)}, u32[]{:S(2)}, u32[]{:S(2)}) %collective-permute-start.35) | collective-permute-done | bytes 1048608 | tf_op jit(solution)/shard_map/ppermute | solution.py:513
  178.9 1.7 copy.10
  (56 shorter events, 9.6 us)
Async XLA Ops:
  0.0 8.3 %copy-start = (bf16[8,1,2,64,64]{4,3,2,1,0:T(8,128)(2,1)S(1)}, bf16[8,1,2,64,64]{4,3,2,1,0:T(8,128)(2,1)}, u32[]{:S(2)}) copy-start(bf16[8,1,2,64,64]{4,3,2,1,0:T(8,128)(2,1)} %param.7) | copy-start | bytes 393220
  0.0 38.2 %collective-permute-start.6 = (f32[32,3,16,256]{3,2,1,0:T(8,128)}, f32[32,3,16,256]{3,2,1,0:T(8,128)S(1)}, u32[]{:S(2)}, u32[]{:S(2)}) collective-permute-start(f32[32,3,16,256]{3,2,1,0:T(8,128)} %bitcast.20), channel_id=1, source_target_pairs={{0,0},{16,2},{1,1},{17,3},{2,16},{18,18},{3,17},{19,19},{4,4},{20,... | collective-permute-start | bytes 4718600 | tf_op jit(solution)/shard_map/ppermute | solution.py:423
  6.2 4.3 %copy-start.2 = (s32[8]{0:T(128)S(1)}, s32[8]{0:T(128)}, u32[]{:S(2)}) copy-start(s32[8]{0:T(128)} %param.8) | copy-start | bytes 100
  6.2 4.3 %copy-start.1 = (f32[16,16]{1,0:T(8,128)S(1)}, f32[16,16]{1,0:T(8,128)}, u32[]{:S(2)}) copy-start(f32[16,16]{1,0:T(8,128)} %param.6) | copy-start | bytes 3076
  6.2 57.9 %collective-permute-start = (f32[4,16,16,256]{3,2,1,0:T(8,128)}, f32[4,16,16,256]{3,2,1,0:T(8,128)S(1)}, u32[]{:S(2)}, u32[]{:S(2)}) collective-permute-start(f32[4,16,16,256]{3,2,1,0:T(8,128)} %bitcast.18), channel_id=1, source_target_pairs={{0,0},{16,2},{1,1},{17,3},{2,16},{18,18},{3,17},{19,19},{4,4},{20,... | collective-permute-start | bytes 3145736 | tf_op jit(solution)/shard_map/ppermute | solution.py:432
  10.6 25.8 %collective-permute-start.5 = (f32[536,128]{1,0:T(8,128)S(1)}, f32[536,128]{1,0:T(8,128)}, u32[]{:S(2)}, u32[]{:S(2)}) collective-permute-start(f32[536,128]{1,0:T(8,128)S(1)} %select_maximum_fusion), channel_id=1, source_target_pairs={{0,0},{16,2},{1,1},{17,3},{2,16},{18,18},{3,17},{19,19},{4,4},{20,... | collective-permute-start | bytes 823304 | tf_op jit(solution)/shard_map/ppermute | solution.py:431
  41.3 7.8 %collective-permute-start.9 = (f32[3,4,8,256]{3,2,1,0:T(8,128)S(1)}, f32[3,4,8,256]{3,2,1,0:T(8,128)S(1)}, u32[]{:S(2)}, u32[]{:S(2)}) collective-permute-start(f32[3,4,8,256]{3,2,1,0:T(8,128)S(1)} %get-tuple-element.55), channel_id=1, source_target_pairs={{0,1},{1,0},{2,3},{3,2},{4,5},{5,4},{6,7},{7,6},{8,9},{9,8},{10,11... | collective-permute-start | bytes 294920 | tf_op jit(solution)/shard_map/ppermute | solution.py:398
  42.5 6.5 %collective-permute-start.7 = (f32[3,16,256]{2,1,0:T(8,128)S(1)}, f32[3,16,256]{2,1,0:T(8,128)S(1)}, u32[]{:S(2)}, u32[]{:S(2)}) collective-permute-start(f32[3,16,256]{2,1,0:T(8,128)S(1)} %get-tuple-element.53), channel_id=1, source_target_pairs={{0,16},{16,0},{1,17},{17,1},{2,18},{18,2},{3,19},{19,3},{4,20},{20... | collective-permute-start | bytes 147464 | tf_op jit(solution)/shard_map/ppermute | solution.py:399
  42.5 6.5 %collective-permute-start.8 = (f32[3,16,256]{2,1,0:T(8,128)S(1)}, f32[3,16,256]{2,1,0:T(8,128)S(1)}, u32[]{:S(2)}, u32[]{:S(2)}) collective-permute-start(f32[3,16,256]{2,1,0:T(8,128)S(1)} %get-tuple-element.54), channel_id=1, source_target_pairs={{16,4},{18,6},{17,5},{19,7},{4,16},{6,18},{5,17},{7,19},{20,8},{22... | collective-permute-start | bytes 147464 | tf_op jit(solution)/shard_map/ppermute | solution.py:396
  46.1 2.9 %collective-permute-start.10 = (f32[3,16,128]{2,1,0:T(8,128)S(1)}, f32[3,16,128]{2,1,0:T(8,128)S(1)}, u32[]{:S(2)}, u32[]{:S(2)}) collective-permute-start(f32[3,16,128]{2,1,0:T(8,128)S(1)} %get-tuple-element.56), channel_id=1, source_target_pairs={{0,2},{2,0},{4,6},{6,4},{8,10},{10,8},{12,14},{14,12},{1,3},{3,1},... | collective-permute-start | bytes 73736 | tf_op jit(solution)/shard_map/ppermute | solution.py:397
  60.5 17.4 %collective-permute-start.11 = (f32[15,16,256]{2,1,0:T(8,128)S(1)}, f32[15,16,256]{2,1,0:T(8,128)S(1)}, u32[]{:S(2)}, u32[]{:S(2)}) collective-permute-start(f32[15,16,256]{2,1,0:T(8,128)S(1)} %get-tuple-element.58), channel_id=1, source_target_pairs={{0,16},{16,0},{1,17},{17,1},{2,18},{18,2},{3,19},{19,3},{4,20},{20... | collective-permute-start | bytes 737288 | tf_op jit(solution)/shard_map/ppermute | solution.py:399
  60.8 17.2 %collective-permute-start.12 = (f32[15,16,256]{2,1,0:T(8,128)S(1)}, f32[15,16,256]{2,1,0:T(8,128)S(1)}, u32[]{:S(2)}, u32[]{:S(2)}) collective-permute-start(f32[15,16,256]{2,1,0:T(8,128)S(1)} %get-tuple-element.59), channel_id=1, source_target_pairs={{16,4},{18,6},{17,5},{19,7},{4,16},{6,18},{5,17},{7,19},{20,8},{22... | collective-permute-start | bytes 737288 | tf_op jit(solution)/shard_map/ppermute | solution.py:396
  66.0 12.0 %collective-permute-start.1 = (f32[12,16,256]{2,1,0:T(8,128)S(1)}, f32[12,16,256]{2,1,0:T(8,128)S(1)}, u32[]{:S(2)}, u32[]{:S(2)}) collective-permute-start(f32[12,16,256]{2,1,0:T(8,128)S(1)} %get-tuple-element.49), channel_id=1, source_target_pairs={{0,16},{16,0},{1,17},{17,1},{2,18},{18,2},{3,19},{19,3},{4,20},{20... | collective-permute-start | bytes 589832 | tf_op jit(solution)/shard_map/ppermute | solution.py:399
  66.0 11.9 %collective-permute-start.2 = (f32[12,16,256]{2,1,0:T(8,128)S(1)}, f32[12,16,256]{2,1,0:T(8,128)S(1)}, u32[]{:S(2)}, u32[]{:S(2)}) collective-permute-start(f32[12,16,256]{2,1,0:T(8,128)S(1)} %get-tuple-element.50), channel_id=1, source_target_pairs={{16,4},{18,6},{17,5},{19,7},{4,16},{6,18},{5,17},{7,19},{20,8},{22... | collective-permute-start | bytes 589832 | tf_op jit(solution)/shard_map/ppermute | solution.py:396
  69.4 3.2 %collective-permute-start.4 = (f32[2,16,128]{2,1,0:T(8,128)S(1)}, f32[2,16,128]{2,1,0:T(8,128)S(1)}, u32[]{:S(2)}, u32[]{:S(2)}) collective-permute-start(f32[2,16,128]{2,1,0:T(8,128)S(1)} %get-tuple-element.52), channel_id=1, source_target_pairs={{0,2},{2,0},{4,6},{6,4},{8,10},{10,8},{12,14},{14,12},{1,3},{3,1},... | collective-permute-start | bytes 49160 | tf_op jit(solution)/shard_map/ppermute | solution.py:397
  72.6 5.3 %collective-permute-start.3 = (f32[1,16,8,256]{3,2,1,0:T(8,128)S(1)}, f32[1,16,8,256]{3,2,1,0:T(8,128)S(1)}, u32[]{:S(2)}, u32[]{:S(2)}) collective-permute-start(f32[1,16,8,256]{3,2,1,0:T(8,128)S(1)} %get-tuple-element.51), channel_id=1, source_target_pairs={{0,1},{1,0},{2,3},{3,2},{4,5},{5,4},{6,7},{7,6},{8,9},{9,8},{10,11... | collective-permute-start | bytes 393224 | tf_op jit(solution)/shard_map/ppermute | solution.py:398
  83.1 18.5 %collective-permute-start.13 = (f32[12,16,256]{2,1,0:T(8,128)S(1)}, f32[12,16,256]{2,1,0:T(8,128)S(1)}, u32[]{:S(2)}, u32[]{:S(2)}) collective-permute-start(f32[12,16,256]{2,1,0:T(8,128)S(1)} %get-tuple-element.61), channel_id=1, source_target_pairs={{0,16},{16,0},{1,17},{17,1},{2,18},{18,2},{3,19},{19,3},{4,20},{20... | collective-permute-start | bytes 589832 | tf_op jit(solution)/shard_map/ppermute | solution.py:399
  83.7 17.9 %collective-permute-start.14 = (f32[12,16,256]{2,1,0:T(8,128)S(1)}, f32[12,16,256]{2,1,0:T(8,128)S(1)}, u32[]{:S(2)}, u32[]{:S(2)}) collective-permute-start(f32[12,16,256]{2,1,0:T(8,128)S(1)} %get-tuple-element.62), channel_id=1, source_target_pairs={{16,4},{18,6},{17,5},{19,7},{4,16},{6,18},{5,17},{7,19},{20,8},{22... | collective-permute-start | bytes 589832 | tf_op jit(solution)/shard_map/ppermute | solution.py:396
  85.8 15.8 %collective-permute-start.15 = (f32[1,16,8,256]{3,2,1,0:T(8,128)S(1)}, f32[1,16,8,256]{3,2,1,0:T(8,128)S(1)}, u32[]{:S(2)}, u32[]{:S(2)}) collective-permute-start(f32[1,16,8,256]{3,2,1,0:T(8,128)S(1)} %get-tuple-element.63), channel_id=1, source_target_pairs={{0,1},{1,0},{2,3},{3,2},{4,5},{5,4},{6,7},{7,6},{8,9},{9,8},{10,11... | collective-permute-start | bytes 393224 | tf_op jit(solution)/shard_map/ppermute | solution.py:398
  86.0 7.1 %collective-permute-start.17 = (f32[3,4,8,256]{3,2,1,0:T(8,128)S(1)}, f32[3,4,8,256]{3,2,1,0:T(8,128)S(1)}, u32[]{:S(2)}, u32[]{:S(2)}) collective-permute-start(f32[3,4,8,256]{3,2,1,0:T(8,128)S(1)} %get-tuple-element.67), channel_id=1, source_target_pairs={{0,1},{1,0},{2,3},{3,2},{4,5},{5,4},{6,7},{7,6},{8,9},{9,8},{10,11... | collective-permute-start | bytes 294920 | tf_op jit(solution)/shard_map/ppermute | solution.py:398
  87.3 3.0 %collective-permute-start.18 = (f32[3,16,128]{2,1,0:T(8,128)S(1)}, f32[3,16,128]{2,1,0:T(8,128)S(1)}, u32[]{:S(2)}, u32[]{:S(2)}) collective-permute-start(f32[3,16,128]{2,1,0:T(8,128)S(1)} %get-tuple-element.68), channel_id=1, source_target_pairs={{0,2},{2,0},{4,6},{6,4},{8,10},{10,8},{12,14},{14,12},{1,3},{3,1},... | collective-permute-start | bytes 73736 | tf_op jit(solution)/shard_map/ppermute | solution.py:397
  90.3 11.3 %collective-permute-start.16 = (f32[2,16,128]{2,1,0:T(8,128)S(1)}, f32[2,16,128]{2,1,0:T(8,128)S(1)}, u32[]{:S(2)}, u32[]{:S(2)}) collective-permute-start(f32[2,16,128]{2,1,0:T(8,128)S(1)} %get-tuple-element.64), channel_id=1, source_target_pairs={{0,2},{2,0},{4,6},{6,4},{8,10},{10,8},{12,14},{14,12},{1,3},{3,1},... | collective-permute-start | bytes 49160 | tf_op jit(solution)/shard_map/ppermute | solution.py:397
  106.7 11.2 %collective-permute-start.19 = (f32[24,16,256]{2,1,0:T(8,128)S(1)}, f32[24,16,256]{2,1,0:T(8,128)S(1)}, u32[]{:S(2)}, u32[]{:S(2)}) collective-permute-start(f32[24,16,256]{2,1,0:T(8,128)S(1)} %get-tuple-element.72), channel_id=1, source_target_pairs={{0,16},{16,0},{1,17},{17,1},{2,18},{18,2},{3,19},{19,3},{4,20},{20... | collective-permute-start | bytes 1179656 | tf_op jit(solution)/shard_map/ppermute | solution.py:399
  107.5 10.5 %collective-permute-start.20 = (f32[24,16,256]{2,1,0:T(8,128)S(1)}, f32[24,16,256]{2,1,0:T(8,128)S(1)}, u32[]{:S(2)}, u32[]{:S(2)}) collective-permute-start(f32[24,16,256]{2,1,0:T(8,128)S(1)} %get-tuple-element.73), channel_id=1, source_target_pairs={{16,4},{18,6},{17,5},{19,7},{4,16},{6,18},{5,17},{7,19},{20,8},{22... | collective-permute-start | bytes 1179656 | tf_op jit(solution)/shard_map/ppermute | solution.py:396
  110.5 7.4 %collective-permute-start.21 = (f32[2,16,8,256]{3,2,1,0:T(8,128)S(1)}, f32[2,16,8,256]{3,2,1,0:T(8,128)S(1)}, u32[]{:S(2)}, u32[]{:S(2)}) collective-permute-start(f32[2,16,8,256]{3,2,1,0:T(8,128)S(1)} %get-tuple-element.74), channel_id=1, source_target_pairs={{0,1},{1,0},{2,3},{3,2},{4,5},{5,4},{6,7},{7,6},{8,9},{9,8},{10,11... | collective-permute-start | bytes 786440 | tf_op jit(solution)/shard_map/ppermute | solution.py:398
  110.8 3.1 %collective-permute-start.22 = (f32[4,16,128]{2,1,0:T(8,128)S(1)}, f32[4,16,128]{2,1,0:T(8,128)S(1)}, u32[]{:S(2)}, u32[]{:S(2)}) collective-permute-start(f32[4,16,128]{2,1,0:T(8,128)S(1)} %get-tuple-element.75), channel_id=1, source_target_pairs={{0,2},{2,0},{4,6},{6,4},{8,10},{10,8},{12,14},{14,12},{1,3},{3,1},... | collective-permute-start | bytes 98312 | tf_op jit(solution)/shard_map/ppermute | solution.py:397
  123.6 8.2 %collective-permute-start.23 = (f32[12,16,256]{2,1,0:T(8,128)S(1)}, f32[12,16,256]{2,1,0:T(8,128)S(1)}, u32[]{:S(2)}, u32[]{:S(2)}) collective-permute-start(f32[12,16,256]{2,1,0:T(8,128)S(1)} %get-tuple-element.77), channel_id=1, source_target_pairs={{0,16},{16,0},{1,17},{17,1},{2,18},{18,2},{3,19},{19,3},{4,20},{20... | collective-permute-start | bytes 589832 | tf_op jit(solution)/shard_map/ppermute | solution.py:399
  123.7 8.1 %collective-permute-start.24 = (f32[12,16,256]{2,1,0:T(8,128)S(1)}, f32[12,16,256]{2,1,0:T(8,128)S(1)}, u32[]{:S(2)}, u32[]{:S(2)}) collective-permute-start(f32[12,16,256]{2,1,0:T(8,128)S(1)} %get-tuple-element.78), channel_id=1, source_target_pairs={{16,4},{18,6},{17,5},{19,7},{4,16},{6,18},{5,17},{7,19},{20,8},{22... | collective-permute-start | bytes 589832 | tf_op jit(solution)/shard_map/ppermute | solution.py:396
  127.2 4.6 %collective-permute-start.25 = (f32[1,16,8,256]{3,2,1,0:T(8,128)S(1)}, f32[1,16,8,256]{3,2,1,0:T(8,128)S(1)}, u32[]{:S(2)}, u32[]{:S(2)}) collective-permute-start(f32[1,16,8,256]{3,2,1,0:T(8,128)S(1)} %get-tuple-element.79), channel_id=1, source_target_pairs={{0,1},{1,0},{2,3},{3,2},{4,5},{5,4},{6,7},{7,6},{8,9},{9,8},{10,11... | collective-permute-start | bytes 393224 | tf_op jit(solution)/shard_map/ppermute | solution.py:398
  127.5 2.9 %collective-permute-start.26 = (f32[2,16,128]{2,1,0:T(8,128)S(1)}, f32[2,16,128]{2,1,0:T(8,128)S(1)}, u32[]{:S(2)}, u32[]{:S(2)}) collective-permute-start(f32[2,16,128]{2,1,0:T(8,128)S(1)} %get-tuple-element.80), channel_id=1, source_target_pairs={{0,2},{2,0},{4,6},{6,4},{8,10},{10,8},{12,14},{14,12},{1,3},{3,1},... | collective-permute-start | bytes 49160 | tf_op jit(solution)/shard_map/ppermute | solution.py:397
  136.8 8.2 %collective-permute-start.27 = (f32[12,16,256]{2,1,0:T(8,128)S(1)}, f32[12,16,256]{2,1,0:T(8,128)S(1)}, u32[]{:S(2)}, u32[]{:S(2)}) collective-permute-start(f32[12,16,256]{2,1,0:T(8,128)S(1)} %get-tuple-element.83), channel_id=1, source_target_pairs={{0,16},{16,0},{1,17},{17,1},{2,18},{18,2},{3,19},{19,3},{4,20},{20... | collective-permute-start | bytes 589832 | tf_op jit(solution)/shard_map/ppermute | solution.py:399
  136.9 8.2 %collective-permute-start.28 = (f32[12,16,256]{2,1,0:T(8,128)S(1)}, f32[12,16,256]{2,1,0:T(8,128)S(1)}, u32[]{:S(2)}, u32[]{:S(2)}) collective-permute-start(f32[12,16,256]{2,1,0:T(8,128)S(1)} %get-tuple-element.84), channel_id=1, source_target_pairs={{16,4},{18,6},{17,5},{19,7},{4,16},{6,18},{5,17},{7,19},{20,8},{22... | collective-permute-start | bytes 589832 | tf_op jit(solution)/shard_map/ppermute | solution.py:396
  140.2 4.8 %collective-permute-start.29 = (f32[1,16,8,256]{3,2,1,0:T(8,128)S(1)}, f32[1,16,8,256]{3,2,1,0:T(8,128)S(1)}, u32[]{:S(2)}, u32[]{:S(2)}) collective-permute-start(f32[1,16,8,256]{3,2,1,0:T(8,128)S(1)} %get-tuple-element.85), channel_id=1, source_target_pairs={{0,1},{1,0},{2,3},{3,2},{4,5},{5,4},{6,7},{7,6},{8,9},{9,8},{10,11... | collective-permute-start | bytes 393224 | tf_op jit(solution)/shard_map/ppermute | solution.py:398
  140.5 2.9 %collective-permute-start.30 = (f32[2,16,128]{2,1,0:T(8,128)S(1)}, f32[2,16,128]{2,1,0:T(8,128)S(1)}, u32[]{:S(2)}, u32[]{:S(2)}) collective-permute-start(f32[2,16,128]{2,1,0:T(8,128)S(1)} %get-tuple-element.86), channel_id=1, source_target_pairs={{0,2},{2,0},{4,6},{6,4},{8,10},{10,8},{12,14},{14,12},{1,3},{3,1},... | collective-permute-start | bytes 49160 | tf_op jit(solution)/shard_map/ppermute | solution.py:397
  150.1 8.1 %collective-permute-start.33 = (f32[2,16,8,256]{3,2,1,0:T(8,128)S(1)}, f32[2,16,8,256]{3,2,1,0:T(8,128)S(1)}, u32[]{:S(2)}, u32[]{:S(2)}) collective-permute-start(f32[2,16,8,256]{3,2,1,0:T(8,128)S(1)} %get-tuple-element.91), channel_id=1, source_target_pairs={{0,1},{1,0},{2,3},{3,2},{4,5},{5,4},{6,7},{7,6},{8,9},{9,8},{10,11... | collective-permute-start | bytes 786440 | tf_op jit(solution)/shard_map/ppermute | solution.py:398
  150.3 7.1 %collective-permute-start.31 = (f32[12,16,256]{2,1,0:T(8,128)S(1)}, f32[12,16,256]{2,1,0:T(8,128)S(1)}, u32[]{:S(2)}, u32[]{:S(2)}) collective-permute-start(f32[12,16,256]{2,1,0:T(8,128)S(1)} %get-tuple-element.89), channel_id=1, source_target_pairs={{0,16},{16,0},{1,17},{17,1},{2,18},{18,2},{3,19},{19,3},{4,20},{20... | collective-permute-start | bytes 589832 | tf_op jit(solution)/shard_map/ppermute | solution.py:399
  150.9 7.3 %collective-permute-start.32 = (f32[12,16,256]{2,1,0:T(8,128)S(1)}, f32[12,16,256]{2,1,0:T(8,128)S(1)}, u32[]{:S(2)}, u32[]{:S(2)}) collective-permute-start(f32[12,16,256]{2,1,0:T(8,128)S(1)} %get-tuple-element.90), channel_id=1, source_target_pairs={{16,4},{18,6},{17,5},{19,7},{4,16},{6,18},{5,17},{7,19},{20,8},{22... | collective-permute-start | bytes 589832 | tf_op jit(solution)/shard_map/ppermute | solution.py:396
  154.1 3.2 %collective-permute-start.34 = (f32[4,16,128]{2,1,0:T(8,128)S(1)}, f32[4,16,128]{2,1,0:T(8,128)S(1)}, u32[]{:S(2)}, u32[]{:S(2)}) collective-permute-start(f32[4,16,128]{2,1,0:T(8,128)S(1)} %get-tuple-element.92), channel_id=1, source_target_pairs={{0,2},{2,0},{4,6},{6,4},{8,10},{10,8},{12,14},{14,12},{1,3},{3,1},... | collective-permute-start | bytes 98312 | tf_op jit(solution)/shard_map/ppermute | solution.py:397
  162.4 16.5 %collective-permute-start.35 = (f32[4,16,16,256]{3,2,1,0:T(8,128)S(1)}, f32[4,16,16,256]{3,2,1,0:T(8,128)S(1)}, u32[]{:S(2)}, u32[]{:S(2)}) collective-permute-start(f32[4,16,16,256]{3,2,1,0:T(8,128)S(1)} %shard_map.64), channel_id=1, source_target_pairs={{0,0},{2,16},{1,1},{3,17},{16,2},{18,18},{17,3},{19,19},{4,4},{6,2... | collective-permute-start | bytes 3145736 | tf_op jit(solution)/shard_map/ppermute | solution.py:513

commit v2 on v1

--- a/solution.py
+++ b/solution.py
@@ -7,7 +7,7 @@
 from jax.experimental.pallas import tpu as pltpu
 from jax.sharding import PartitionSpec as P
 
-MOVED = True
+MOVED = False
 
 eddy_step = 0.1
 viscosity = 0.5

time: 181 us -> 145 us (0.80)
  the two profiles are of different devices: /device:TPU:9 before, /device:TPU:8 now
where the time goes in v2:
time: 145 us
  Pallas kernels  54.8 us (38%)
  starting transfers between devices  44.5 us (31%)
  waiting for transfers between devices  40.7 us (28%)
  local copies, waits for them, and re-layouts  4.54 us (3%)
    pallas_call x10, Pallas kernels, call(): pl.pallas_call(body, out_shape=shapes, in_specs=[SMEM] * smem + [VMEM] *...  54.8 us
    ppermute x8, starting transfers between devices, send(): outer = lax.ppermute(outer, 'gx', odd)  16.4 us
    ppermute x8, starting transfers between devices, send(): inner = lax.ppermute(inner, 'gx', even)  16 us
    ppermute x8, waiting for transfers between devices, send(): ymsg = lax.ppermute(ymsg, 'gy', swap)  15.1 us
    ppermute x8, starting transfers between devices, send(): ymsg = lax.ppermute(ymsg, 'gy', swap)  11.8 us
    ppermute x8, waiting for transfers between devices, send(): inner = lax.ppermute(inner, 'gx', even)  11.5 us
    ppermute x8, waiting for transfers between devices, send(): zmsg = lax.ppermute(zmsg, 'grp', swap)  7.09 us
    ppermute x8, waiting for transfers between devices, send(): outer = lax.ppermute(outer, 'gx', odd)  7.01 us
  transfers between devices with their start and end apart: 32, of which 18 were waited for; matrix products, arithmetic and copies ran while one was open for 1% of the time, Pallas kernels for 7%

profile of v2, /device:TPU:8, one launch (start us, length us, event | category | flops | bytes accessed | tf_op | source)
XLA Modules:
  0.0 145.0 jit_solution(12598176798106461269)
XLA Ops:
  0.1 1.4 copy-done
  1.5 3.1 %shard_map.56 = (f32[3,16,256]{2,1,0:T(8,128)S(1)}, f32[3,16,256]{2,1,0:T(8,128)S(1)}, f32[3,4,8,256]{3,2,1,0:T(8,128)S(1)}, f32[3,16,128]{2,1,0:T(8,128)S(1)}) custom-call(s32[3]{0:T(128)S(1)} %pad_add_fusion.info, f32[32,3,16,256]{3,2,1,0:T(8,128)S(1)} %bitcast.15), custom_call_target="tpu_custom_call" | custom-call | flops 1000000 | bytes 1794060 | tf_op jit(solution)/shard_map/pallas_call | solution.py:37
  4.6 1.6 %collective-permute-start.4 = (f32[3,16,256]{2,1,0:T(8,128)S(1)}, f32[3,16,256]{2,1,0:T(8,128)S(1)}, u32[]{:S(2)}, u32[]{:S(2)}) collective-permute-start(f32[3,16,256]{2,1,0:T(8,128)S(1)} %get-tuple-element.53), channel_id=1, source_target_pairs={{0,2},{2,0},{4,6},{6,4},{8,10},{10,8},{12,14},{14,12},{1,3},{3,1},... | collective-permute-start | bytes 147464 | tf_op jit(solution)/shard_map/ppermute | solution.py:402
  6.2 1.9 %collective-permute-start.5 = (f32[3,16,256]{2,1,0:T(8,128)S(1)}, f32[3,16,256]{2,1,0:T(8,128)S(1)}, u32[]{:S(2)}, u32[]{:S(2)}) collective-permute-start(f32[3,16,256]{2,1,0:T(8,128)S(1)} %get-tuple-element.54), channel_id=1, source_target_pairs={{2,4},{4,2},{6,8},{8,6},{10,12},{12,10},{3,5},{5,3},{7,9},{9,7},{1... | collective-permute-start | bytes 147464 | tf_op jit(solution)/shard_map/ppermute | solution.py:401
  8.1 2.0 %collective-permute-start.6 = (f32[3,4,8,256]{3,2,1,0:T(8,128)S(1)}, f32[3,4,8,256]{3,2,1,0:T(8,128)S(1)}, u32[]{:S(2)}, u32[]{:S(2)}) collective-permute-start(f32[3,4,8,256]{3,2,1,0:T(8,128)S(1)} %get-tuple-element.55), channel_id=1, source_target_pairs={{0,1},{1,0},{2,3},{3,2},{4,5},{5,4},{6,7},{7,6},{8,9},{9,8},{10,11... | collective-permute-start | bytes 294920 | tf_op jit(solution)/shard_map/ppermute | solution.py:403
  11.4 1.7 %collective-permute-done.5.outer = f32[3,16,256]{2,1,0:T(8,128)S(1)} collective-permute-done((f32[3,16,256]{2,1,0:T(8,128)S(1)}, f32[3,16,256]{2,1,0:T(8,128)S(1)}, u32[]{:S(2)}, u32[]{:S(2)}) %collective-permute-start.5) | collective-permute-done | bytes 49184 | tf_op jit(solution)/shard_map/ppermute | solution.py:401
  13.0 11.5 %shard_map.57 = (f32[32,3,16,256]{3,2,1,0:T(8,128)S(1)}, f32[4,3,64,256]{3,2,1,0:T(8,128)S(1)}, f32[15,16,256]{2,1,0:T(8,128)S(1)}, f32[15,16,256]{2,1,0:T(8,128...) custom-call(s32[3]{0:T(128)S(1)} %pad_add_fusion.info, s32[8]{0:T(128)S(1)} %copy-done.2, ...), custom_call_target="tpu_custom_call" | custom-call | flops 4000000 | bytes 5292076 | tf_op jit(solution)/shard_map/pallas_call | solution.py:37
  24.5 2.8 %collective-permute-start.8 = (f32[15,16,256]{2,1,0:T(8,128)S(1)}, f32[15,16,256]{2,1,0:T(8,128)S(1)}, u32[]{:S(2)}, u32[]{:S(2)}) collective-permute-start(f32[15,16,256]{2,1,0:T(8,128)S(1)} %get-tuple-element.58), channel_id=1, source_target_pairs={{0,2},{2,0},{4,6},{6,4},{8,10},{10,8},{12,14},{14,12},{1,3},{3,1},... | collective-permute-start | bytes 737288 | tf_op jit(solution)/shard_map/ppermute | solution.py:402
  27.3 2.0 %collective-permute-start.9 = (f32[15,16,256]{2,1,0:T(8,128)S(1)}, f32[15,16,256]{2,1,0:T(8,128)S(1)}, u32[]{:S(2)}, u32[]{:S(2)}) collective-permute-start(f32[15,16,256]{2,1,0:T(8,128)S(1)} %get-tuple-element.59), channel_id=1, source_target_pairs={{2,4},{4,2},{6,8},{8,6},{10,12},{12,10},{3,5},{5,3},{7,9},{9,7},{1... | collective-permute-start | bytes 737288 | tf_op jit(solution)/shard_map/ppermute | solution.py:401
  29.5 1.8 %shard_map.55 = (f32[12,16,256]{2,1,0:T(8,128)S(1)}, f32[12,16,256]{2,1,0:T(8,128)S(1)}, f32[1,16,8,256]{3,2,1,0:T(8,128)S(1)}, f32[2,16,128]{2,1,0:T(8,128)S(1)}) custom-call(s32[3]{0:T(128)S(1)} %pad_add_fusion.info, f32[4,16,16,256]{3,2,1,0:T(8,128)S(1)} %bitcast.12), custom_call_target="tpu_custom_call" | custom-call | flops 1000000 | bytes 1589260 | tf_op jit(solution)/shard_map/pallas_call | solution.py:37
  31.4 3.1 %collective-permute-start = (f32[12,16,256]{2,1,0:T(8,128)S(1)}, f32[12,16,256]{2,1,0:T(8,128)S(1)}, u32[]{:S(2)}, u32[]{:S(2)}) collective-permute-start(f32[12,16,256]{2,1,0:T(8,128)S(1)} %get-tuple-element.49), channel_id=1, source_target_pairs={{0,2},{2,0},{4,6},{6,4},{8,10},{10,8},{12,14},{14,12},{1,3},{3,1},... | collective-permute-start | bytes 589832 | tf_op jit(solution)/shard_map/ppermute | solution.py:402
  34.4 1.9 %collective-permute-start.1 = (f32[12,16,256]{2,1,0:T(8,128)S(1)}, f32[12,16,256]{2,1,0:T(8,128)S(1)}, u32[]{:S(2)}, u32[]{:S(2)}) collective-permute-start(f32[12,16,256]{2,1,0:T(8,128)S(1)} %get-tuple-element.50), channel_id=1, source_target_pairs={{2,4},{4,2},{6,8},{8,6},{10,12},{12,10},{3,5},{5,3},{7,9},{9,7},{1... | collective-permute-start | bytes 589832 | tf_op jit(solution)/shard_map/ppermute | solution.py:401
  37.6 1.5 %collective-permute-start.2 = (f32[1,16,8,256]{3,2,1,0:T(8,128)S(1)}, f32[1,16,8,256]{3,2,1,0:T(8,128)S(1)}, u32[]{:S(2)}, u32[]{:S(2)}) collective-permute-start(f32[1,16,8,256]{3,2,1,0:T(8,128)S(1)} %get-tuple-element.51), channel_id=1, source_target_pairs={{0,1},{1,0},{2,3},{3,2},{4,5},{5,4},{6,7},{7,6},{8,9},{9,8},{10,11... | collective-permute-start | bytes 393224 | tf_op jit(solution)/shard_map/ppermute | solution.py:403
  39.1 4.1 %collective-permute-done.2.ymsg = f32[1,16,8,256]{3,2,1,0:T(8,128)S(1)} collective-permute-done((f32[1,16,8,256]{3,2,1,0:T(8,128)S(1)}, f32[1,16,8,256]{3,2,1,0:T(8,128)S(1)}, u32[]{:S(2)}, u32[]{:S(2)}) %collective-permute-start.2) | collective-permute-done | bytes 131104 | tf_op jit(solution)/shard_map/ppermute | solution.py:403
  43.2 2.6 %collective-permute-done.inner = f32[12,16,256]{2,1,0:T(8,128)S(1)} collective-permute-done((f32[12,16,256]{2,1,0:T(8,128)S(1)}, f32[12,16,256]{2,1,0:T(8,128)S(1)}, u32[]{:S(2)}, u32[]{:S(2)}) %collective-permute-start) | collective-permute-done | bytes 196640 | tf_op jit(solution)/shard_map/ppermute | solution.py:402
  45.9 5.0 %shard_map.58 = (f32[4,16,16,256]{3,2,1,0:T(8,128)S(1)}, f32[4,3,64,256]{3,2,1,0:T(8,128)S(1)}, f32[12,16,256]{2,1,0:T(8,128)S(1)}, f32[12,16,256]{2,1,0:T(8,128...) custom-call(s32[3]{0:T(128)S(1)} %pad_add_fusion.info, f32[4,16,16,256]{3,2,1,0:T(8,128)S(1)} %bitcast.13, ...), custom_call_target="tpu_custom_call" | custom-call | flops 4000000 | bytes 5373964 | tf_op jit(solution)/shard_map/pallas_call | solution.py:37
  50.9 1.8 %collective-permute-start.10 = (f32[12,16,256]{2,1,0:T(8,128)S(1)}, f32[12,16,256]{2,1,0:T(8,128)S(1)}, u32[]{:S(2)}, u32[]{:S(2)}) collective-permute-start(f32[12,16,256]{2,1,0:T(8,128)S(1)} %get-tuple-element.61), channel_id=1, source_target_pairs={{0,2},{2,0},{4,6},{6,4},{8,10},{10,8},{12,14},{14,12},{1,3},{3,1},... | collective-permute-start | bytes 589832 | tf_op jit(solution)/shard_map/ppermute | solution.py:402
  52.7 1.9 %collective-permute-start.11 = (f32[12,16,256]{2,1,0:T(8,128)S(1)}, f32[12,16,256]{2,1,0:T(8,128)S(1)}, u32[]{:S(2)}, u32[]{:S(2)}) collective-permute-start(f32[12,16,256]{2,1,0:T(8,128)S(1)} %get-tuple-element.62), channel_id=1, source_target_pairs={{2,4},{4,2},{6,8},{8,6},{10,12},{12,10},{3,5},{5,3},{7,9},{9,7},{1... | collective-permute-start | bytes 589832 | tf_op jit(solution)/shard_map/ppermute | solution.py:401
  54.6 1.6 %collective-permute-start.12 = (f32[1,16,8,256]{3,2,1,0:T(8,128)S(1)}, f32[1,16,8,256]{3,2,1,0:T(8,128)S(1)}, u32[]{:S(2)}, u32[]{:S(2)}) collective-permute-start(f32[1,16,8,256]{3,2,1,0:T(8,128)S(1)} %get-tuple-element.63), channel_id=1, source_target_pairs={{0,1},{1,0},{2,3},{3,2},{4,5},{5,4},{6,7},{7,6},{8,9},{9,8},{10,11... | collective-permute-start | bytes 393224 | tf_op jit(solution)/shard_map/ppermute | solution.py:403
  56.7 1.2 collective-permute-done.15.zmsg
  58.1 2.7 %collective-permute-done.14.ymsg = f32[3,4,8,256]{3,2,1,0:T(8,128)S(1)} collective-permute-done((f32[3,4,8,256]{3,2,1,0:T(8,128)S(1)}, f32[3,4,8,256]{3,2,1,0:T(8,128)S(1)}, u32[]{:S(2)}, u32[]{:S(2)}) %collective-permute-start.14) | collective-permute-done | bytes 98336 | tf_op jit(solution)/shard_map/ppermute | solution.py:403
  60.8 8.5 %shard_map.59 = (f32[4,3,64,256]{3,2,1,0:T(8,128)S(1)}, f32[12,16,256]{2,1,0:T(8,128)S(1)}, f32[12,16,256]{2,1,0:T(8,128)S(1)}) custom-call(s32[3]{0:T(128)S(1)} %pad_add_fusion.info, s32[8]{0:T(128)S(1)} %copy-done.2, f32[32,3,16,256]{3,2,1,0:T(8,128)S(1)} %get-tuple-element.66.v, f32[15,16,256]{2,1,0:T(8,128)S(1)} %collective-permute-done.8.t_in.inner, ...), custom_call_target="tpu_custom_call" | custom-call | flops 4000000 | bytes 3891244 | tf_op jit(solution)/shard_map/pallas_call | solution.py:37
  69.3 5.1 %shard_map.60 = (f32[4,16,16,256]{3,2,1,0:T(8,128)S(1)}, f32[24,16,256]{2,1,0:T(8,128)S(1)}, f32[24,16,256]{2,1,0:T(8,128)S(1)}, f32[2,16,8,256]{3,2,1,0:T(8,128)S(1)}, f32[4,16,128]{2,1,0:T(8,128)S(1)}) custom-call(s32[3]{0:T(128)S(1)} %pad_add_fusion.info, f32[4,16,16,256]{3,2,1,0:T(8,128)S(1)} %get-tuple-element.60.f, ...), custom_call_target="tpu_custom_call" | custom-call | flops 4000000 | bytes 6078476 | tf_op jit(solution)/shard_map/pallas_call | solution.py:37
  74.4 3.0 %collective-permute-start.16 = (f32[24,16,256]{2,1,0:T(8,128)S(1)}, f32[24,16,256]{2,1,0:T(8,128)S(1)}, u32[]{:S(2)}, u32[]{:S(2)}) collective-permute-start(f32[24,16,256]{2,1,0:T(8,128)S(1)} %get-tuple-element.72), channel_id=1, source_target_pairs={{0,2},{2,0},{4,6},{6,4},{8,10},{10,8},{12,14},{14,12},{1,3},{3,1},... | collective-permute-start | bytes 1179656 | tf_op jit(solution)/shard_map/ppermute | solution.py:402
  77.5 1.9 %collective-permute-start.17 = (f32[24,16,256]{2,1,0:T(8,128)S(1)}, f32[24,16,256]{2,1,0:T(8,128)S(1)}, u32[]{:S(2)}, u32[]{:S(2)}) collective-permute-start(f32[24,16,256]{2,1,0:T(8,128)S(1)} %get-tuple-element.73), channel_id=1, source_target_pairs={{2,4},{4,2},{6,8},{8,6},{10,12},{12,10},{3,5},{5,3},{7,9},{9,7},{1... | collective-permute-start | bytes 1179656 | tf_op jit(solution)/shard_map/ppermute | solution.py:401
  79.4 1.5 %collective-permute-start.18 = (f32[2,16,8,256]{3,2,1,0:T(8,128)S(1)}, f32[2,16,8,256]{3,2,1,0:T(8,128)S(1)}, u32[]{:S(2)}, u32[]{:S(2)}) collective-permute-start(f32[2,16,8,256]{3,2,1,0:T(8,128)S(1)} %get-tuple-element.74), channel_id=1, source_target_pairs={{0,1},{1,0},{2,3},{3,2},{4,5},{5,4},{6,7},{7,6},{8,9},{9,8},{10,11... | collective-permute-start | bytes 786440 | tf_op jit(solution)/shard_map/ppermute | solution.py:403
  80.9 1.2 collective-permute-done.19.zmsg
  82.1 3.8 %collective-permute-done.18.ymsg = f32[2,16,8,256]{3,2,1,0:T(8,128)S(1)} collective-permute-done((f32[2,16,8,256]{3,2,1,0:T(8,128)S(1)}, f32[2,16,8,256]{3,2,1,0:T(8,128)S(1)}, u32[]{:S(2)}, u32[]{:S(2)}) %collective-permute-start.18) | collective-permute-done | bytes 262176 | tf_op jit(solution)/shard_map/ppermute | solution.py:403
  85.8 7.0 %collective-permute-done.16.inner = f32[24,16,256]{2,1,0:T(8,128)S(1)} collective-permute-done((f32[24,16,256]{2,1,0:T(8,128)S(1)}, f32[24,16,256]{2,1,0:T(8,128)S(1)}, u32[]{:S(2)}, u32[]{:S(2)}) %collective-permute-start.16) | collective-permute-done | bytes 393248 | tf_op jit(solution)/shard_map/ppermute | solution.py:402
  92.8 5.5 %shard_map.61 = (f32[4,16,16,256]{3,2,1,0:T(8,128)S(1)}, f32[12,16,256]{2,1,0:T(8,128)S(1)}, f32[12,16,256]{2,1,0:T(8,128)S(1)}, f32[1,16,8,256]{3,2,1,0:T(8,128)S(1)}, f32[2,16,128]{2,1,0:T(8,128)S(1)}) custom-call(s32[3]{0:T(128)S(1)} %pad_add_fusion.info, f32[4,16,16,256]{3,2,1,0:T(8,128)S(1)} %get-tuple-element.71.f, ...), custom_call_target="tpu_custom_call" | custom-call | flops 4000000 | bytes 3719180 | tf_op jit(solution)/shard_map/pallas_call | solution.py:37
  98.3 1.8 %collective-permute-start.20 = (f32[12,16,256]{2,1,0:T(8,128)S(1)}, f32[12,16,256]{2,1,0:T(8,128)S(1)}, u32[]{:S(2)}, u32[]{:S(2)}) collective-permute-start(f32[12,16,256]{2,1,0:T(8,128)S(1)} %get-tuple-element.77), channel_id=1, source_target_pairs={{0,2},{2,0},{4,6},{6,4},{8,10},{10,8},{12,14},{14,12},{1,3},{3,1},... | collective-permute-start | bytes 589832 | tf_op jit(solution)/shard_map/ppermute | solution.py:402
  100.1 1.9 %collective-permute-start.21 = (f32[12,16,256]{2,1,0:T(8,128)S(1)}, f32[12,16,256]{2,1,0:T(8,128)S(1)}, u32[]{:S(2)}, u32[]{:S(2)}) collective-permute-start(f32[12,16,256]{2,1,0:T(8,128)S(1)} %get-tuple-element.78), channel_id=1, source_target_pairs={{2,4},{4,2},{6,8},{8,6},{10,12},{12,10},{3,5},{5,3},{7,9},{9,7},{1... | collective-permute-start | bytes 589832 | tf_op jit(solution)/shard_map/ppermute | solution.py:401
  102.0 1.6 %collective-permute-start.22 = (f32[1,16,8,256]{3,2,1,0:T(8,128)S(1)}, f32[1,16,8,256]{3,2,1,0:T(8,128)S(1)}, u32[]{:S(2)}, u32[]{:S(2)}) collective-permute-start(f32[1,16,8,256]{3,2,1,0:T(8,128)S(1)} %get-tuple-element.79), channel_id=1, source_target_pairs={{0,1},{1,0},{2,3},{3,2},{4,5},{5,4},{6,7},{7,6},{8,9},{9,8},{10,11... | collective-permute-start | bytes 393224 | tf_op jit(solution)/shard_map/ppermute | solution.py:403
  104.8 2.3 %collective-permute-done.22.ymsg = f32[1,16,8,256]{3,2,1,0:T(8,128)S(1)} collective-permute-done((f32[1,16,8,256]{3,2,1,0:T(8,128)S(1)}, f32[1,16,8,256]{3,2,1,0:T(8,128)S(1)}, u32[]{:S(2)}, u32[]{:S(2)}) %collective-permute-start.22) | collective-permute-done | bytes 131104 | tf_op jit(solution)/shard_map/ppermute | solution.py:403
  107.1 1.5 %collective-permute-done.21.outer = f32[12,16,256]{2,1,0:T(8,128)S(1)} collective-permute-done((f32[12,16,256]{2,1,0:T(8,128)S(1)}, f32[12,16,256]{2,1,0:T(8,128)S(1)}, u32[]{:S(2)}, u32[]{:S(2)}) %collective-permute-start.21) | collective-permute-done | bytes 196640 | tf_op jit(solution)/shard_map/ppermute | solution.py:401
  108.6 5.0 %shard_map.62 = (f32[4,16,16,256]{3,2,1,0:T(8,128)S(1)}, f32[4,3,64,256]{3,2,1,0:T(8,128)S(1)}, f32[12,16,256]{2,1,0:T(8,128)S(1)}, f32[12,16,256]{2,1,0:T(8,128...) custom-call(s32[3]{0:T(128)S(1)} %pad_add_fusion.info, ...), custom_call_target="tpu_custom_call" | custom-call | flops 4000000 | bytes 5275660 | tf_op jit(solution)/shard_map/pallas_call | solution.py:37
  114.0 2.9 %collective-permute-start.25 = (f32[12,16,256]{2,1,0:T(8,128)S(1)}, f32[12,16,256]{2,1,0:T(8,128)S(1)}, u32[]{:S(2)}, u32[]{:S(2)}) collective-permute-start(f32[12,16,256]{2,1,0:T(8,128)S(1)} %get-tuple-element.84), channel_id=1, source_target_pairs={{2,4},{4,2},{6,8},{8,6},{10,12},{12,10},{3,5},{5,3},{7,9},{9,7},{1... | collective-permute-start | bytes 589832 | tf_op jit(solution)/shard_map/ppermute | solution.py:401
  116.9 1.6 %collective-permute-start.26 = (f32[1,16,8,256]{3,2,1,0:T(8,128)S(1)}, f32[1,16,8,256]{3,2,1,0:T(8,128)S(1)}, u32[]{:S(2)}, u32[]{:S(2)}) collective-permute-start(f32[1,16,8,256]{3,2,1,0:T(8,128)S(1)} %get-tuple-element.85), channel_id=1, source_target_pairs={{0,1},{1,0},{2,3},{3,2},{4,5},{5,4},{6,7},{7,6},{8,9},{9,8},{10,11... | collective-permute-start | bytes 393224 | tf_op jit(solution)/shard_map/ppermute | solution.py:403
  119.7 2.3 %collective-permute-done.26.ymsg = f32[1,16,8,256]{3,2,1,0:T(8,128)S(1)} collective-permute-done((f32[1,16,8,256]{3,2,1,0:T(8,128)S(1)}, f32[1,16,8,256]{3,2,1,0:T(8,128)S(1)}, u32[]{:S(2)}, u32[]{:S(2)}) %collective-permute-start.26) | collective-permute-done | bytes 131104 | tf_op jit(solution)/shard_map/ppermute | solution.py:403
  122.5 5.1 %shard_map.63 = (f32[4,16,16,256]{3,2,1,0:T(8,128)S(1)}, f32[12,16,256]{2,1,0:T(8,128)S(1)}, f32[12,16,256]{2,1,0:T(8,128)S(1)}, f32[2,16,8,256]{3,2,1,0:T(8,128)S(1)}, f32[4,16,128]{2,1,0:T(8,128)S(1)}) custom-call(s32[3]{0:T(128)S(1)} %pad_add_fusion.info, f32[4,16,16,256]{3,2,1,0:T(8,128)S(1)} %get-tuple-element.82.f, ...), custom_call_target="tpu_custom_call" | custom-call | flops 4000000 | bytes 5292044 | tf_op jit(solution)/shard_map/pallas_call | solution.py:37
  127.6 1.5 %collective-permute-start.30 = (f32[2,16,8,256]{3,2,1,0:T(8,128)S(1)}, f32[2,16,8,256]{3,2,1,0:T(8,128)S(1)}, u32[]{:S(2)}, u32[]{:S(2)}) collective-permute-start(f32[2,16,8,256]{3,2,1,0:T(8,128)S(1)} %get-tuple-element.91), channel_id=1, source_target_pairs={{0,1},{1,0},{2,3},{3,2},{4,5},{5,4},{6,7},{7,6},{8,9},{9,8},{10,11... | collective-permute-start | bytes 786440 | tf_op jit(solution)/shard_map/ppermute | solution.py:403
  129.1 1.6 %collective-permute-start.28 = (f32[12,16,256]{2,1,0:T(8,128)S(1)}, f32[12,16,256]{2,1,0:T(8,128)S(1)}, u32[]{:S(2)}, u32[]{:S(2)}) collective-permute-start(f32[12,16,256]{2,1,0:T(8,128)S(1)} %get-tuple-element.89), channel_id=1, source_target_pairs={{0,2},{2,0},{4,6},{6,4},{8,10},{10,8},{12,14},{14,12},{1,3},{3,1},... | collective-permute-start | bytes 589832 | tf_op jit(solution)/shard_map/ppermute | solution.py:402
  130.7 1.9 %collective-permute-start.29 = (f32[12,16,256]{2,1,0:T(8,128)S(1)}, f32[12,16,256]{2,1,0:T(8,128)S(1)}, u32[]{:S(2)}, u32[]{:S(2)}) collective-permute-start(f32[12,16,256]{2,1,0:T(8,128)S(1)} %get-tuple-element.90), channel_id=1, source_target_pairs={{2,4},{4,2},{6,8},{8,6},{10,12},{12,10},{3,5},{5,3},{7,9},{9,7},{1... | collective-permute-start | bytes 589832 | tf_op jit(solution)/shard_map/ppermute | solution.py:401
  132.7 1.2 collective-permute-done.31.zmsg
  133.9 1.9 %collective-permute-done.28.inner = f32[12,16,256]{2,1,0:T(8,128)S(1)} collective-permute-done((f32[12,16,256]{2,1,0:T(8,128)S(1)}, f32[12,16,256]{2,1,0:T(8,128)S(1)}, u32[]{:S(2)}, u32[]{:S(2)}) %collective-permute-start.28) | collective-permute-done | bytes 196640 | tf_op jit(solution)/shard_map/ppermute | solution.py:402
  135.8 3.4 %collective-permute-done.29.outer = f32[12,16,256]{2,1,0:T(8,128)S(1)} collective-permute-done((f32[12,16,256]{2,1,0:T(8,128)S(1)}, f32[12,16,256]{2,1,0:T(8,128)S(1)}, u32[]{:S(2)}, u32[]{:S(2)}) %collective-permute-start.29) | collective-permute-done | bytes 196640 | tf_op jit(solution)/shard_map/ppermute | solution.py:401
  139.1 4.2 %shard_map.64 = f32[4,16,16,256]{3,2,1,0:T(8,128)S(1)} custom-call(s32[3]{0:T(128)S(1)} %pad_add_fusion.info, f32[4,16,16,256]{3,2,1,0:T(8,128)S(1)} %get-tuple-element.88.f, f32[12,16,256]{2,1,0:T(8,128)S(1)} %collective-permute-done.28.inner, f32[12,16,256]{2,1,0:T(8,128)S(1)} %collective-permute-done.29.outer, ...), custom_call_target="tpu_custom_call" | custom-call | flops 4000000 | bytes 2785292 | tf_op jit(solution)/shard_map/pallas_call | solution.py:37
  143.4 1.7 %copy.8 = f32[16,16,4,256]{3,2,1,0:T(4,128)} copy(f32[16,16,4,256]{3,1,0,2:T(8,128)S(1)} %bitcast.17) | data formatting | bytes 2097152 | tf_op jit(solution)/shard_map/transpose | solution.py:514
  (44 shorter events, 7.0 us)
Async XLA Ops:
  0.0 13.0 %copy-start.2 = (s32[8]{0:T(128)S(1)}, s32[8]{0:T(128)}, u32[]{:S(2)}) copy-start(s32[8]{0:T(128)} %offset.3) | copy-start | bytes 100
  0.1 1.4 copy-start
  1.5 11.5 %copy-start.1 = (f32[32,16,3,256]{3,1,2,0:T(8,128)S(1)}, f32[32,16,3,256]{3,1,2,0:T(8,128)}, u32[]{:S(2)}) copy-start(f32[32,16,3,256]{3,1,2,0:T(8,128)} %param.5) | copy-start | bytes 4718596
  4.6 6.8 %collective-permute-start.7 = (f32[3,16,128]{2,1,0:T(8,128)S(1)}, f32[3,16,128]{2,1,0:T(8,128)S(1)}, u32[]{:S(2)}, u32[]{:S(2)}) collective-permute-start(f32[3,16,128]{2,1,0:T(8,128)S(1)} %get-tuple-element.56), channel_id=1, source_target_pairs={{0,16},{16,0},{1,17},{17,1},{2,18},{18,2},{3,19},{19,3},{4,20},{20... | collective-permute-start | bytes 73736 | tf_op jit(solution)/shard_map/ppermute | solution.py:404
  4.6 6.8 %collective-permute-start.4 = (f32[3,16,256]{2,1,0:T(8,128)S(1)}, f32[3,16,256]{2,1,0:T(8,128)S(1)}, u32[]{:S(2)}, u32[]{:S(2)}) collective-permute-start(f32[3,16,256]{2,1,0:T(8,128)S(1)} %get-tuple-element.53), channel_id=1, source_target_pairs={{0,2},{2,0},{4,6},{6,4},{8,10},{10,8},{12,14},{14,12},{1,3},{3,1},... | collective-permute-start | bytes 147464 | tf_op jit(solution)/shard_map/ppermute | solution.py:402
  6.2 6.9 %collective-permute-start.5 = (f32[3,16,256]{2,1,0:T(8,128)S(1)}, f32[3,16,256]{2,1,0:T(8,128)S(1)}, u32[]{:S(2)}, u32[]{:S(2)}) collective-permute-start(f32[3,16,256]{2,1,0:T(8,128)S(1)} %get-tuple-element.54), channel_id=1, source_target_pairs={{2,4},{4,2},{6,8},{8,6},{10,12},{12,10},{3,5},{5,3},{7,9},{9,7},{1... | collective-permute-start | bytes 147464 | tf_op jit(solution)/shard_map/ppermute | solution.py:401
  8.1 5.0 %collective-permute-start.6 = (f32[3,4,8,256]{3,2,1,0:T(8,128)S(1)}, f32[3,4,8,256]{3,2,1,0:T(8,128)S(1)}, u32[]{:S(2)}, u32[]{:S(2)}) collective-permute-start(f32[3,4,8,256]{3,2,1,0:T(8,128)S(1)} %get-tuple-element.55), channel_id=1, source_target_pairs={{0,1},{1,0},{2,3},{3,2},{4,5},{5,4},{6,7},{7,6},{8,9},{9,8},{10,11... | collective-permute-start | bytes 294920 | tf_op jit(solution)/shard_map/ppermute | solution.py:403
  11.2 18.1 %copy-start.3 = (f32[16,16,4,256]{3,2,1,0:T(4,128)S(1)}, f32[16,16,4,256]{3,2,1,0:T(4,128)}, u32[]{:S(2)}) copy-start(f32[16,16,4,256]{3,2,1,0:T(4,128)} %param.9) | copy-start | bytes 3145732
  24.5 21.3 %collective-permute-start.8 = (f32[15,16,256]{2,1,0:T(8,128)S(1)}, f32[15,16,256]{2,1,0:T(8,128)S(1)}, u32[]{:S(2)}, u32[]{:S(2)}) collective-permute-start(f32[15,16,256]{2,1,0:T(8,128)S(1)} %get-tuple-element.58), channel_id=1, source_target_pairs={{0,2},{2,0},{4,6},{6,4},{8,10},{10,8},{12,14},{14,12},{1,3},{3,1},... | collective-permute-start | bytes 737288 | tf_op jit(solution)/shard_map/ppermute | solution.py:402
  27.3 18.6 %copy-start.4 = (f32[16,16]{1,0:T(8,128)S(1)}, f32[16,16]{1,0:T(8,128)}, u32[]{:S(2)}) copy-start(f32[16,16]{1,0:T(8,128)} %param.6) | copy-start | bytes 3076
  27.3 18.6 %collective-permute-start.9 = (f32[15,16,256]{2,1,0:T(8,128)S(1)}, f32[15,16,256]{2,1,0:T(8,128)S(1)}, u32[]{:S(2)}, u32[]{:S(2)}) collective-permute-start(f32[15,16,256]{2,1,0:T(8,128)S(1)} %get-tuple-element.59), channel_id=1, source_target_pairs={{2,4},{4,2},{6,8},{8,6},{10,12},{12,10},{3,5},{5,3},{7,9},{9,7},{1... | collective-permute-start | bytes 737288 | tf_op jit(solution)/shard_map/ppermute | solution.py:401
  31.4 14.4 %collective-permute-start = (f32[12,16,256]{2,1,0:T(8,128)S(1)}, f32[12,16,256]{2,1,0:T(8,128)S(1)}, u32[]{:S(2)}, u32[]{:S(2)}) collective-permute-start(f32[12,16,256]{2,1,0:T(8,128)S(1)} %get-tuple-element.49), channel_id=1, source_target_pairs={{0,2},{2,0},{4,6},{6,4},{8,10},{10,8},{12,14},{14,12},{1,3},{3,1},... | collective-permute-start | bytes 589832 | tf_op jit(solution)/shard_map/ppermute | solution.py:402
  34.4 11.4 %collective-permute-start.1 = (f32[12,16,256]{2,1,0:T(8,128)S(1)}, f32[12,16,256]{2,1,0:T(8,128)S(1)}, u32[]{:S(2)}, u32[]{:S(2)}) collective-permute-start(f32[12,16,256]{2,1,0:T(8,128)S(1)} %get-tuple-element.50), channel_id=1, source_target_pairs={{2,4},{4,2},{6,8},{8,6},{10,12},{12,10},{3,5},{5,3},{7,9},{9,7},{1... | collective-permute-start | bytes 589832 | tf_op jit(solution)/shard_map/ppermute | solution.py:401
  36.3 1.2 collective-permute-start.3
  37.6 5.6 %collective-permute-start.2 = (f32[1,16,8,256]{3,2,1,0:T(8,128)S(1)}, f32[1,16,8,256]{3,2,1,0:T(8,128)S(1)}, u32[]{:S(2)}, u32[]{:S(2)}) collective-permute-start(f32[1,16,8,256]{3,2,1,0:T(8,128)S(1)} %get-tuple-element.51), channel_id=1, source_target_pairs={{0,1},{1,0},{2,3},{3,2},{4,5},{5,4},{6,7},{7,6},{8,9},{9,8},{10,11... | collective-permute-start | bytes 393224 | tf_op jit(solution)/shard_map/ppermute | solution.py:403
  50.9 18.4 %collective-permute-start.10 = (f32[12,16,256]{2,1,0:T(8,128)S(1)}, f32[12,16,256]{2,1,0:T(8,128)S(1)}, u32[]{:S(2)}, u32[]{:S(2)}) collective-permute-start(f32[12,16,256]{2,1,0:T(8,128)S(1)} %get-tuple-element.61), channel_id=1, source_target_pairs={{0,2},{2,0},{4,6},{6,4},{8,10},{10,8},{12,14},{14,12},{1,3},{3,1},... | collective-permute-start | bytes 589832 | tf_op jit(solution)/shard_map/ppermute | solution.py:402
  52.7 16.6 %collective-permute-start.11 = (f32[12,16,256]{2,1,0:T(8,128)S(1)}, f32[12,16,256]{2,1,0:T(8,128)S(1)}, u32[]{:S(2)}, u32[]{:S(2)}) collective-permute-start(f32[12,16,256]{2,1,0:T(8,128)S(1)} %get-tuple-element.62), channel_id=1, source_target_pairs={{2,4},{4,2},{6,8},{8,6},{10,12},{12,10},{3,5},{5,3},{7,9},{9,7},{1... | collective-permute-start | bytes 589832 | tf_op jit(solution)/shard_map/ppermute | solution.py:401
  54.6 14.7 %collective-permute-start.12 = (f32[1,16,8,256]{3,2,1,0:T(8,128)S(1)}, f32[1,16,8,256]{3,2,1,0:T(8,128)S(1)}, u32[]{:S(2)}, u32[]{:S(2)}) collective-permute-start(f32[1,16,8,256]{3,2,1,0:T(8,128)S(1)} %get-tuple-element.63), channel_id=1, source_target_pairs={{0,1},{1,0},{2,3},{3,2},{4,5},{5,4},{6,7},{7,6},{8,9},{9,8},{10,11... | collective-permute-start | bytes 393224 | tf_op jit(solution)/shard_map/ppermute | solution.py:403
  56.2 4.6 %collective-permute-start.14 = (f32[3,4,8,256]{3,2,1,0:T(8,128)S(1)}, f32[3,4,8,256]{3,2,1,0:T(8,128)S(1)}, u32[]{:S(2)}, u32[]{:S(2)}) collective-permute-start(f32[3,4,8,256]{3,2,1,0:T(8,128)S(1)} %get-tuple-element.67), channel_id=1, source_target_pairs={{0,1},{1,0},{2,3},{3,2},{4,5},{5,4},{6,7},{7,6},{8,9},{9,8},{10,11... | collective-permute-start | bytes 294920 | tf_op jit(solution)/shard_map/ppermute | solution.py:403
  56.7 1.2 collective-permute-start.15
  57.9 11.4 %collective-permute-start.13 = (f32[2,16,128]{2,1,0:T(8,128)S(1)}, f32[2,16,128]{2,1,0:T(8,128)S(1)}, u32[]{:S(2)}, u32[]{:S(2)}) collective-permute-start(f32[2,16,128]{2,1,0:T(8,128)S(1)} %get-tuple-element.64), channel_id=1, source_target_pairs={{0,16},{16,0},{1,17},{17,1},{2,18},{18,2},{3,19},{19,3},{4,20},{20... | collective-permute-start | bytes 49160 | tf_op jit(solution)/shard_map/ppermute | solution.py:404
  74.4 18.3 %collective-permute-start.16 = (f32[24,16,256]{2,1,0:T(8,128)S(1)}, f32[24,16,256]{2,1,0:T(8,128)S(1)}, u32[]{:S(2)}, u32[]{:S(2)}) collective-permute-start(f32[24,16,256]{2,1,0:T(8,128)S(1)} %get-tuple-element.72), channel_id=1, source_target_pairs={{0,2},{2,0},{4,6},{6,4},{8,10},{10,8},{12,14},{14,12},{1,3},{3,1},... | collective-permute-start | bytes 1179656 | tf_op jit(solution)/shard_map/ppermute | solution.py:402
  77.5 15.3 %collective-permute-start.17 = (f32[24,16,256]{2,1,0:T(8,128)S(1)}, f32[24,16,256]{2,1,0:T(8,128)S(1)}, u32[]{:S(2)}, u32[]{:S(2)}) collective-permute-start(f32[24,16,256]{2,1,0:T(8,128)S(1)} %get-tuple-element.73), channel_id=1, source_target_pairs={{2,4},{4,2},{6,8},{8,6},{10,12},{12,10},{3,5},{5,3},{7,9},{9,7},{1... | collective-permute-start | bytes 1179656 | tf_op jit(solution)/shard_map/ppermute | solution.py:401
  79.4 6.4 %collective-permute-start.18 = (f32[2,16,8,256]{3,2,1,0:T(8,128)S(1)}, f32[2,16,8,256]{3,2,1,0:T(8,128)S(1)}, u32[]{:S(2)}, u32[]{:S(2)}) collective-permute-start(f32[2,16,8,256]{3,2,1,0:T(8,128)S(1)} %get-tuple-element.74), channel_id=1, source_target_pairs={{0,1},{1,0},{2,3},{3,2},{4,5},{5,4},{6,7},{7,6},{8,9},{9,8},{10,11... | collective-permute-start | bytes 786440 | tf_op jit(solution)/shard_map/ppermute | solution.py:403
  80.9 1.2 collective-permute-start.19
  98.3 8.7 %collective-permute-start.20 = (f32[12,16,256]{2,1,0:T(8,128)S(1)}, f32[12,16,256]{2,1,0:T(8,128)S(1)}, u32[]{:S(2)}, u32[]{:S(2)}) collective-permute-start(f32[12,16,256]{2,1,0:T(8,128)S(1)} %get-tuple-element.77), channel_id=1, source_target_pairs={{0,2},{2,0},{4,6},{6,4},{8,10},{10,8},{12,14},{14,12},{1,3},{3,1},... | collective-permute-start | bytes 589832 | tf_op jit(solution)/shard_map/ppermute | solution.py:402
  100.1 8.5 %collective-permute-start.21 = (f32[12,16,256]{2,1,0:T(8,128)S(1)}, f32[12,16,256]{2,1,0:T(8,128)S(1)}, u32[]{:S(2)}, u32[]{:S(2)}) collective-permute-start(f32[12,16,256]{2,1,0:T(8,128)S(1)} %get-tuple-element.78), channel_id=1, source_target_pairs={{2,4},{4,2},{6,8},{8,6},{10,12},{12,10},{3,5},{5,3},{7,9},{9,7},{1... | collective-permute-start | bytes 589832 | tf_op jit(solution)/shard_map/ppermute | solution.py:401
  102.0 5.0 %collective-permute-start.22 = (f32[1,16,8,256]{3,2,1,0:T(8,128)S(1)}, f32[1,16,8,256]{3,2,1,0:T(8,128)S(1)}, u32[]{:S(2)}, u32[]{:S(2)}) collective-permute-start(f32[1,16,8,256]{3,2,1,0:T(8,128)S(1)} %get-tuple-element.79), channel_id=1, source_target_pairs={{0,1},{1,0},{2,3},{3,2},{4,5},{5,4},{6,7},{7,6},{8,9},{9,8},{10,11... | collective-permute-start | bytes 393224 | tf_op jit(solution)/shard_map/ppermute | solution.py:403
  103.6 1.2 collective-permute-start.23
  113.6 8.4 %collective-permute-start.24 = (f32[12,16,256]{2,1,0:T(8,128)S(1)}, f32[12,16,256]{2,1,0:T(8,128)S(1)}, u32[]{:S(2)}, u32[]{:S(2)}) collective-permute-start(f32[12,16,256]{2,1,0:T(8,128)S(1)} %get-tuple-element.83), channel_id=1, source_target_pairs={{0,2},{2,0},{4,6},{6,4},{8,10},{10,8},{12,14},{14,12},{1,3},{3,1},... | collective-permute-start | bytes 589832 | tf_op jit(solution)/shard_map/ppermute | solution.py:402
  114.0 8.5 %collective-permute-start.25 = (f32[12,16,256]{2,1,0:T(8,128)S(1)}, f32[12,16,256]{2,1,0:T(8,128)S(1)}, u32[]{:S(2)}, u32[]{:S(2)}) collective-permute-start(f32[12,16,256]{2,1,0:T(8,128)S(1)} %get-tuple-element.84), channel_id=1, source_target_pairs={{2,4},{4,2},{6,8},{8,6},{10,12},{12,10},{3,5},{5,3},{7,9},{9,7},{1... | collective-permute-start | bytes 589832 | tf_op jit(solution)/shard_map/ppermute | solution.py:401
  116.9 5.0 %collective-permute-start.26 = (f32[1,16,8,256]{3,2,1,0:T(8,128)S(1)}, f32[1,16,8,256]{3,2,1,0:T(8,128)S(1)}, u32[]{:S(2)}, u32[]{:S(2)}) collective-permute-start(f32[1,16,8,256]{3,2,1,0:T(8,128)S(1)} %get-tuple-element.85), channel_id=1, source_target_pairs={{0,1},{1,0},{2,3},{3,2},{4,5},{5,4},{6,7},{7,6},{8,9},{9,8},{10,11... | collective-permute-start | bytes 393224 | tf_op jit(solution)/shard_map/ppermute | solution.py:403
  118.5 1.2 collective-permute-start.27
  127.6 11.6 %collective-permute-start.30 = (f32[2,16,8,256]{3,2,1,0:T(8,128)S(1)}, f32[2,16,8,256]{3,2,1,0:T(8,128)S(1)}, u32[]{:S(2)}, u32[]{:S(2)}) collective-permute-start(f32[2,16,8,256]{3,2,1,0:T(8,128)S(1)} %get-tuple-element.91), channel_id=1, source_target_pairs={{0,1},{1,0},{2,3},{3,2},{4,5},{5,4},{6,7},{7,6},{8,9},{9,8},{10,11... | collective-permute-start | bytes 786440 | tf_op jit(solution)/shard_map/ppermute | solution.py:403
  129.1 6.7 %collective-permute-start.28 = (f32[12,16,256]{2,1,0:T(8,128)S(1)}, f32[12,16,256]{2,1,0:T(8,128)S(1)}, u32[]{:S(2)}, u32[]{:S(2)}) collective-permute-start(f32[12,16,256]{2,1,0:T(8,128)S(1)} %get-tuple-element.89), channel_id=1, source_target_pairs={{0,2},{2,0},{4,6},{6,4},{8,10},{10,8},{12,14},{14,12},{1,3},{3,1},... | collective-permute-start | bytes 589832 | tf_op jit(solution)/shard_map/ppermute | solution.py:402
  130.7 8.5 %collective-permute-start.29 = (f32[12,16,256]{2,1,0:T(8,128)S(1)}, f32[12,16,256]{2,1,0:T(8,128)S(1)}, u32[]{:S(2)}, u32[]{:S(2)}) collective-permute-start(f32[12,16,256]{2,1,0:T(8,128)S(1)} %get-tuple-element.90), channel_id=1, source_target_pairs={{2,4},{4,2},{6,8},{8,6},{10,12},{12,10},{3,5},{5,3},{7,9},{9,7},{1... | collective-permute-start | bytes 589832 | tf_op jit(solution)/shard_map/ppermute | solution.py:401
  132.6 1.3 collective-permute-start.31

commit v3 on v0

v3 whole, which is shorter than its diff:
```python
import functools

import jax
import jax.numpy as jnp
import numpy as np
from jax import lax
from jax.experimental import pallas as pl
from jax.experimental.pallas import tpu as pltpu
from jax.sharding import PartitionSpec as P

eddy_step = 0.1
viscosity = 0.5
wave_step = 0.2
filter_weight = 0.2
deriv = (0.770882380518, -0.166705904415, 0.02084314277)
taps = (0.28739284246, -0.226146951809, 0.10630357877, -0.023853048191)

RATE_Y, RATE_Z = (0, 2), (0, 3)
ALL = (0, 1, 2, 3)
LANES = 128
VMEM = pl.BlockSpec(memory_space=pltpu.VMEM)
SMEM = pl.BlockSpec(memory_space=pltpu.SMEM)


def call(body, outs, ins, scratch=(), smem=1, flops=1000000):
    shapes = [jax.ShapeDtypeStruct(s, jnp.float32) for s in outs]
    size = sum(o.size for o in shapes) + sum(i.size for i in ins)
    return pl.pallas_call(
        body,
        out_shape=shapes,
        in_specs=[SMEM] * smem + [VMEM] * (len(ins) - smem),
        out_specs=[VMEM] * len(shapes),
        scratch_shapes=list(scratch),
        compiler_params=pltpu.CompilerParams(vmem_limit_bytes=24 * 1024 * 1024),
        cost_estimate=pl.CostEstimate(flops=flops, bytes_accessed=4 * size, transcendentals=0),
    )(*ins)


def banded(depth, weights, sign, half):
    matrix = np.zeros((depth + LANES, depth), np.float32)
    lane = np.arange(depth)
    for j, weight in enumerate(weights, 1):
        for to, factor in ((lane + j, weight), (lane - j, sign * weight)):
            ok = (to >= 0) & (to < depth)
            matrix[to[ok], lane[ok]] = factor
            beyond = to >= depth if half == 0 else to < 0
            matrix[depth + to[beyond] % LANES, lane[beyond]] = factor
    high = matrix.astype(jnp.bfloat16)
    low = (matrix - high.astype(np.float32)).astype(jnp.bfloat16)
    return np.concatenate([high, high, low])


def z_product(f, zmsg, zmat, comps, G):
    _, T, X, Y, _ = f.shape
    for n, c in enumerate(comps):
        tiles = [f[c, t].reshape(X * Y, LANES) for t in range(T)] + [zmsg[n].reshape(X * Y, LANES)]
        high = [tile.astype(jnp.bfloat16) for tile in tiles]
        low = [(tile - top.astype(jnp.float32)).astype(jnp.bfloat16) for tile, top in zip(tiles, high)]
        out = jnp.dot(jnp.concatenate(high + low + high, axis=1), zmat[...], preferred_element_type=jnp.float32)
        for t in range(T):
            G[n, t] = out[:, t * LANES : (t + 1) * LANES].reshape(X, Y, LANES)


def shift_tiles(tiles, left, right, by, lanes):
    out = []
    row = [left] + tiles + [right]
    for at in range(1, len(tiles) + 1):
        if by > 0:
            mixed = jnp.where(lanes < by, row[at + 1], row[at])
            out.append(pltpu.roll(mixed, LANES - by, 1))
        else:
            mixed = jnp.where(lanes >= LANES + by, row[at - 1], row[at])
            out.append(pltpu.roll(mixed, -by, 1))
    return out


def side_tiles(tile, half):
    zero = jnp.zeros_like(tile)
    return jnp.where(half == 1, tile, zero), jnp.where(half == 0, tile, zero)


def known(value, has):
    return jnp.where(has == 1, value, jnp.zeros_like(value))


def lane_ids(rows):
    return lax.broadcasted_iota(jnp.int32, (rows, LANES), 1)


def pack_state(o, inner, outer, ymsg, zmsg, ycomps, zcomps, info):
    pos, row, half = info[0], info[1], info[2]
    _, T, X, Y, _ = o.shape
    si = jnp.where(pos == 0, X - 3, 0)
    so = jnp.where(pos == 0, 0, X - 3)
    for c in range(4):
        for t in range(T):
            for l in range(3):
                inner[3 * (c * T + t) + l] = o[c, t, si + l]
                outer[3 * (c * T + t) + l] = o[c, t, so + l]
    rows = lax.broadcasted_iota(jnp.int32, (8, LANES), 0)
    ys = pl.multiple_of(jnp.where(row == 0, Y - 8, 0), 8)

    def normal(c, t, i):
        tile = o[c, t, i, pl.ds(ys, 8), :]
        return jnp.where(row == 0, pltpu.roll(tile, 4, 0), tile)

    edge = jnp.where(half == 0, T - 1, 0)

    def step(i, carry):
        for n in range(len(ycomps) // 2):
            for t in range(T):
                first, second = normal(ycomps[2 * n], t, i), normal(ycomps[2 * n + 1], t, i)
                ymsg[n, t, i] = jnp.where(rows < 4, first, pltpu.roll(second, 4, 0))
        for n, c in enumerate(zcomps):
            zmsg[n, i] = o[c, edge, i]
        return carry

    lax.fori_loop(0, X, step, 0, unroll=4)


def fill(F, f, inner, outer, ymsg, ycomps, info):
    pos, row, has = info[0], info[1], info[3]
    _, T, X, Y, _ = f.shape
    hi = jnp.where(pos == 0, X + 3, 0)
    ho = jnp.where(pos == 0, 0, X + 3)
    for c in range(4):
        for t in range(T):
            for l in range(3):
                F[c, t, hi + l, 8 : 8 + Y, :] = inner[3 * (c * T + t) + l]
                F[c, t, ho + l, 8 : 8 + Y, :] = known(outer[3 * (c * T + t) + l], has)

    def step(i, carry):
        for t in range(T):
            for c in range(4):
                F[c, t, i + 3, 8 : 8 + Y, :] = f[c, t, i]
            for n, c in enumerate(ycomps):
                tile = ymsg[n // 2, t, i]
                turned = pltpu.roll(tile, 4, 0)
                if n % 2:
                    tile, turned = turned, tile
                zero = jnp.zeros_like(tile)
                F[c, t, i + 3, 0:8, :] = jnp.where(row == 1, turned, zero)
                F[c, t, i + 3, 8 + Y : 16 + Y, :] = jnp.where(row == 0, tile, zero)
        return carry

    lax.fori_loop(0, X, step, 0, unroll=4)


def dx(F, c, t, i, Y):
    y = slice(8, 8 + Y)
    return sum(deriv[j - 1] * (F[c, t, i + 3 + j, y, :] - F[c, t, i + 3 - j, y, :]) for j in (1, 2, 3))


def dy(F, c, t, i, Y):
    return sum(
        deriv[j - 1] * (F[c, t, i + 3, 8 + j : 8 + Y + j, :] - F[c, t, i + 3, 8 - j : 8 + Y - j, :]) for j in (1, 2, 3)
    )


def rate_loop(F, G, mach, S, emit):
    T, X, Y = F.shape[1], F.shape[2] - 6, F.shape[3] - 16

    def step(i, carry):
        m = mach[i]
        for t in range(T):
            gp, gu, gv, gw = (dx(F, c, t, i, Y) for c in range(4))
            emit(0, t, i, -(m * gp + gu + dy(F, 2, t, i, Y) + G[1, t, i]))
            emit(1, t, i, -(m * gu + gp) - S[0, t, i])
            emit(2, t, i, -(m * gv + dy(F, 0, t, i, Y)) - S[1, t, i])
            emit(3, t, i, -(m * gw + G[0, t, i]) - S[2, t, i])
        return carry

    lax.fori_loop(0, X, step, 0, unroll=4)


def first_body(info, f, inner, outer, ymsg, zmsg, zmat, mach, own, t_in, t_out, o, S, n_in, n_out, ny, nz, F, G, *, layers):
    _, T, X, Y, _ = f.shape
    z_product(f, zmsg, zmat, RATE_Z, G)
    fill(F, f, inner, outer, ymsg, RATE_Y, info)
    at_in = jnp.where(info[0] == 0, X - layers, 0)
    at_out = jnp.where(info[0] == 0, 0, X - layers)
    S[...] = own[...]
    for c in range(3):
        for t in range(T):
            for l in range(layers):
                n = (c * T + t) * layers + l
                S[c, t, at_in + l] = S[c, t, at_in + l] + t_in[n]
                S[c, t, at_out + l] = S[c, t, at_out + l] + known(t_out[n], info[3])

    def emit(c, t, i, value):
        o[c, t, i] = f[c, t, i] + wave_step * value

    rate_loop(F, G, mach, S, emit)
    pack_state(o, n_in, n_out, ny, nz, RATE_Y, RATE_Z, info)


def second_body(info, f, inner, outer, ymsg, zmsg, zmat, mach, S, state, o, n_in, n_out, ny, nz, F, G):
    z_product(f, zmsg, zmat, RATE_Z, G)
    fill(F, f, inner, outer, ymsg, RATE_Y, info)

    def emit(c, t, i, value):
        o[c, t, i] = 0.5 * (state[c, t, i] + f[c, t, i]) + (0.5 * wave_step) * value

    rate_loop(F, G, mach, S, emit)
    pack_state(o, n_in, n_out, ny, nz, ALL, ALL, info)


def smooth_body(info, f, inner, outer, ymsg, zmsg, zmat, o, *rest):
    F, G = rest[-2:]
    _, T, X, Y, _ = f.shape
    z_product(f, zmsg, zmat, ALL, G)
    fill(F, f, inner, outer, ymsg, ALL, info)
    y = slice(8, 8 + Y)

    def step(i, carry):
        for c in range(4):
            for t in range(T):
                total = (1.0 - 3.0 * filter_weight * taps[0]) * F[c, t, i + 3, y, :] + G[c, t, i]
                for j in (1, 2, 3):
                    beside = (F[c, t, i + 3 + j, y, :] + F[c, t, i + 3 - j, y, :]) + (
                        F[c, t, i + 3, 8 + j : 8 + Y + j, :] + F[c, t, i + 3, 8 - j : 8 + Y - j, :]
                    )
                    total = total - (filter_weight * taps[j]) * beside
                if len(rest) > 2:
                    o[c, t, i] = total
                else:
                    o[c, i, :, t * LANES : (t + 1) * LANES] = total
        return carry

    lax.fori_loop(0, X, step, 0, unroll=4)
    if len(rest) > 2:
        pack_state(o, *rest[:4], RATE_Y, RATE_Z, info)


def pack_body(info, f, o, inner, outer, ymsg, zmsg):
    _, T, X, _, _ = o.shape

    def step(i, carry):
        for c in range(4):
            for t in range(T):
                o[c, t, i] = f[c, i, :, t * LANES : (t + 1) * LANES]
        return carry

    lax.fori_loop(0, X, step, 0, unroll=4)
    pack_state(o, inner, outer, ymsg, zmsg, RATE_Y, RATE_Z, info)


def pack_les(get, shape, inner, outer, ymsg, zmsg, base, info):
    pos, row, half = info[0], info[1], info[2]
    _, T, X, Y, _ = shape
    si = jnp.where(pos == 0, X - 1, 0)
    so = jnp.where(pos == 0, 0, X - 1)
    rows = lax.broadcasted_iota(jnp.int32, (8, LANES), 0)
    ys = pl.multiple_of(jnp.where(row == 0, Y - 8, 0), 8)
    for c in range(3):
        for t in range(T):
            inner[base + c * T + t] = get(c, t, si, slice(None))
            outer[base + c * T + t] = get(c, t, so, slice(None))
            for n in range(X // 8):
                acc = jnp.zeros((8, LANES), jnp.float32)
                for r in range(8):
                    tile = get(c, t, 8 * n + r, pl.ds(ys, 8))
                    moved = jnp.where(row == 0, pltpu.roll(tile, (r + 1) % 8, 0), pltpu.roll(tile, r, 0))
                    acc = jnp.where(rows == r, moved, acc)
                ymsg[c, t, n] = acc

    def step(i, carry):
        for c in range(3):
            last, first = get(c, T - 1, i, slice(None)), get(c, 0, i, slice(None))
            zmsg[c, i] = jnp.where(half == 0, last, first)
        return carry

    lax.fori_loop(0, X, step, 0, unroll=4)


def getter(v):
    if len(v.shape) == 4:
        return lambda c, t, i, rows: v[i, c, rows, t * LANES : (t + 1) * LANES]
    return lambda c, t, i, rows: v[c, t, i, rows, :]


def pack_les_body(info, v, inner, outer, ymsg, zmsg):
    X, _, Y, Z = v.shape
    pack_les(getter(v), (3, Z // LANES, X, Y, LANES), inner, outer, ymsg, zmsg, 0, info)


def les_body(info, offset, v, inner, outer, ymsg, zmsg, tiles, *rest, base, advance):
    if advance:
        v1, own, n_in, n_out, ny, nz, V, LB, ACC = rest
    else:
        own, n_in, n_out, V, LB, ACC = rest
    pos, row, half = info[0], info[1], info[2]
    _, T, X, Y, _ = V.shape
    X, Y = X - 2, Y - 16
    get = getter(v)
    blocks = 2 * LB.shape[0]
    wide = X // blocks
    plane = wide * Y
    hi = jnp.where(pos == 0, X + 1, 0)
    ho = jnp.where(pos == 0, 0, X + 1)
    for c in range(3):
        for t in range(T):
            V[c, t, hi, 8 : 8 + Y, :] = inner[base + c * T + t]
            V[c, t, ho, 8 : 8 + Y, :] = known(outer[base + c * T + t], info[3])
            for n in range(X // 8):
                tile = ymsg[c, t, n]
                zero = jnp.zeros_like(tile)
                for r in range(8):
                    low = pltpu.roll(tile, 7 - r, 0) if r < 7 else tile
                    high = pltpu.roll(tile, 8 - r, 0) if r else tile
                    V[c, t, 8 * n + r + 1, 0:8, :] = jnp.where(row == 1, low, zero)
                    V[c, t, 8 * n + r + 1, 8 + Y : 16 + Y, :] = jnp.where(row == 0, high, zero)

    def copy(i, carry):
        for c in range(3):
            for t in range(T):
                V[c, t, i + 1, 8 : 8 + Y, :] = get(c, t, i, slice(None))
        return carry

    lax.fori_loop(0, X, copy, 0, unroll=4)
    ACC[...] = jnp.zeros_like(ACC)
    lanes = lane_ids(Y)
    y = slice(8, 8 + Y)

    def step(i, carry):
        center = [[V[c, t, i + 1, y, :] for t in range(T)] for c in range(3)]
        ahead, behind = [], []
        for c in range(3 if advance else 2):
            left, right = side_tiles(zmsg[c, i], half)
            ahead.append(shift_tiles(center[c], left, right, 1, lanes))
            behind.append(shift_tiles(center[c], left, right, -1, lanes))
        at = lax.rem(i, 2 * wide) * Y
        at = at + jnp.where(at >= plane, plane, 0)
        b = i // (2 * wide)
        for t in range(T):
            xa = [V[c, t, i + 2, y, :] for c in range(3)]
            xb = [V[c, t, i, y, :] for c in range(3)]
            ya = [V[c, t, i + 1, 9 : 9 + Y, :] for c in range(3)]
            yb = [V[c, t, i + 1, 7 : 7 + Y, :] for c in range(3)]
            u, w, q = center[0][t], center[1][t], center[2][t]
            vx = 0.5 * ((ya[2] - yb[2]) - (ahead[1][t] - behind[1][t]))
            vy = 0.5 * ((ahead[0][t] - behind[0][t]) - (xa[2] - xb[2]))
            vz = 0.5 * ((xa[1] - xb[1]) - (ya[0] - yb[0]))
            lamb = [vy * q - vz * w, vz * u - vx * q, vx * w - vy * u]
            for c in range(3):
                high = lamb[c].astype(jnp.bfloat16)
                low = (lamb[c] - high.astype(jnp.float32)).astype(jnp.bfloat16)
                lane = slice((c * T + t) * LANES, (c * T + t + 1) * LANES)
                LB[b, pl.ds(pl.multiple_of(at, 16), Y), lane] = high
                LB[b, pl.ds(pl.multiple_of(plane + at, 16), Y), lane] = low
                if advance:
                    laplace = -6.0 * center[c][t] + ((xa[c] + xb[c]) + (ya[c] + yb[c]) + (ahead[c][t] + behind[c][t]))
                    v1[c, t, i] = center[c][t] + eddy_step * (viscosity * laplace - lamb[c])
        return carry

    lax.fori_loop(0, X, step, 0, unroll=4)

    for m in range(blocks // 2):
        out = jnp.dot(tiles[m].astype(jnp.bfloat16), LB[m], preferred_element_type=jnp.float32)
        at = (m + 1) * wide
        places = [(at, 0), (at + offset[2 * m] * wide, plane), (at + offset[2 * m + 1] * wide, 2 * plane)]
        for c in range(3):
            for t in range(T):
                lane = slice((c * T + t) * LANES, (c * T + t + 1) * LANES)
                for to, row0 in places:
                    for l in range(wide):
                        ACC[c, t, to + l] = ACC[c, t, to + l] + out[row0 + l * Y : row0 + (l + 1) * Y, lane]

    depth = own.shape[2]
    own[...] = ACC[:, :, wide : wide + depth]
    ti = jnp.where(pos == 0, depth + wide, 0)
    to = jnp.where(pos == 0, 0, depth + wide)
    for c in range(3):
        for t in range(T):
            for l in range(wide):
                n_in[(c * T + t) * wide + l] = ACC[c, t, ti + l]
                n_out[(c * T + t) * wide + l] = ACC[c, t, to + l]
    if advance:
        pack_les(getter(v1), v1.shape, n_in, n_out, ny, nz, 3 * T * wide, info)


def solution(mesh):
    gx = mesh.shape["gx"]
    swap = [(0, 1), (1, 0)]
    even = [pair for k in range(gx // 2) for pair in ((2 * k, 2 * k + 1), (2 * k + 1, 2 * k))]
    odd = [pair for k in range(gx // 2 - 1) for pair in ((2 * k + 1, 2 * k + 2), (2 * k + 2, 2 * k + 1))]

    def flat(**at):
        index = 0
        for axis in mesh.axis_names:
            index = index * mesh.shape[axis] + at[axis]
        return index

    ends = [(0, 1), (1, 0)]
    hops = [
        (flat(gx=a, gy=y, grp=c), flat(gx=b, gy=y, grp=c)) for a, b in odd for y in range(mesh.shape["gy"]) for c in (0, 1)
    ] + [
        (flat(gx=g, gy=y, grp=a), flat(gx=g, gy=y, grp=b))
        for g in (0, gx - 1)
        for y in range(mesh.shape["gy"])
        for a, b in ends
    ]

    def send_x(inner, outer):
        return lax.ppermute(inner, "gx", even), lax.ppermute(outer, mesh.axis_names, hops)

    def send(inner, outer, ymsg, zmsg):
        return *send_x(inner, outer), lax.ppermute(ymsg, "gy", swap), lax.ppermute(zmsg, "grp", swap)

    def body(les_velocity, mean_mach, transfer_tiles, intersection_offset, acoustic_state):
        X2, Y, _, Z = les_velocity.shape
        X = acoustic_state.shape[0]
        T = Z // LANES
        blocks, plane = transfer_tiles.shape[0], transfer_tiles.shape[-1]
        wide = plane // Y
        column = lax.axis_index("gx")
        half = lax.axis_index("grp")
        has = (column > 0) & (column < gx - 1)
        info = jnp.stack([column % 2, lax.axis_index("gy"), half, has.astype(jnp.int32)]).astype(jnp.int32)
        v = les_velocity.transpose(0, 2, 1, 3)
        state = acoustic_state.transpose(2, 0, 1, 3)
        rate_z = jnp.where(half == 0, *(banded(Z, deriv, -1, h) for h in (0, 1)))
        smooth_z = jnp.where(half == 0, *(banded(Z, [-filter_weight * w for w in taps[1:]], 1, h) for h in (0, 1)))
        pair = transfer_tiles[:, 0].swapaxes(2, 3).reshape(blocks // 2, 2, 2, plane, plane)
        none = jnp.zeros((blocks // 2, plane, 2 * plane), pair.dtype)
        twice = [[jnp.concatenate([pair[:, n, k]] * 2, axis=2) for k in (0, 1)] for n in (0, 1)]
        tiles = jnp.concatenate(
            [
                jnp.concatenate([twice[0][0], twice[1][0]], axis=2),
                jnp.concatenate([twice[0][1], none], axis=2),
                jnp.concatenate([none, twice[1][1]], axis=2),
            ],
            axis=1,
        )
        mach = jnp.broadcast_to(mean_mach[:, :, None], (X, Y, LANES))

        grid = (4, T, X, Y, LANES)
        source = (3, T, X, Y, LANES)
        edge_x, term = (12 * T, Y, LANES), (3 * T * wide, Y, LANES)
        edge_y, edge_yy = (1, T, X, 8, LANES), (2, T, X, 8, LANES)
        edge_z, edge_zz = (2, X, Y, LANES), (4, X, Y, LANES)
        les_y, les_z = (3, T, X2 // 8, 8, LANES), (3, X2, Y, LANES)
        F = pltpu.VMEM((4, T, X + 6, Y + 16, LANES), jnp.float32)
        G2 = pltpu.VMEM((2, T, X, Y, LANES), jnp.float32)
        G4 = pltpu.VMEM((4, T, X, Y, LANES), jnp.float32)
        les_scratch = [
            pltpu.VMEM((3, T, X2 + 2, Y + 16, LANES), jnp.float32),
            pltpu.VMEM((blocks // 2, 4 * plane, 3 * Z), jnp.bfloat16),
            pltpu.VMEM((3, T, X + 2 * wide, Y, LANES), jnp.float32),
        ]
        les_edges = send(*call(pack_les_body, [(3 * T, Y, LANES), (3 * T, Y, LANES), les_y, les_z], [info, v]))
        state, *state_edges = call(pack_body, [grid, edge_x, edge_x, edge_y, edge_z], [info, state])
        info, *state_edges = lax.optimization_barrier((info, *state_edges))
        state_edges = send(*state_edges)
        with_terms = (term[0] + 3 * T, Y, LANES)
        v1, own, *edges = call(
            functools.partial(les_body, base=0, advance=True),
            [(3, T, X2, Y, LANES), source, with_terms, with_terms, les_y, les_z],
            [info, intersection_offset, v, *les_edges, tiles],
            les_scratch,
            smem=2,
            flops=4000000,
        )
        edges = send(*edges)
        first = functools.partial(first_body, layers=wide)
        outs = [grid, source, edge_x, edge_x, edge_y, edge_z]
        middle, S, *middle_edges = call(
            first, outs, [info, state, *state_edges, rate_z, mach, own, edges[0], edges[1]], [F, G2], flops=4000000
        )
        middle_edges = send(*middle_edges)
        own2, *terms = call(
            functools.partial(les_body, base=term[0], advance=False),
            [source, term, term],
            [info, intersection_offset, v1, *edges, tiles],
            les_scratch,
            smem=2,
            flops=4000000,
        )
        outs = [grid, edge_x, edge_x, edge_yy, edge_zz]
        updated, *up_edges = call(
            second_body, outs, [info, middle, *middle_edges, rate_z, mach, S, state], [F, G2], flops=4000000
        )
        up_edges = send(*up_edges)
        terms = send_x(*terms)
        outs = [grid, edge_x, edge_x, edge_y, edge_z]
        state, *state_edges = call(
            smooth_body, outs, [info, updated, *up_edges, smooth_z], [F, G4], flops=4000000
        )
        state_edges = send(*state_edges)
        outs = [grid, source, edge_x, edge_x, edge_y, edge_z]
        middle, S, *middle_edges = call(
            first, outs, [info, state, *state_edges, rate_z, mach, own2, *terms], [F, G2], flops=4000000
        )
        middle_edges = send(*middle_edges)
        outs = [grid, edge_x, edge_x, edge_yy, edge_zz]
        updated, *up_edges = call(
            second_body, outs, [info, middle, *middle_edges, rate_z, mach, S, state], [F, G2], flops=4000000
        )
        up_edges = send(*up_edges)
        (state,) = call(smooth_body, [(4, X, Y, Z)], [info, updated, *up_edges, smooth_z], [F, G4], flops=4000000)
        return state.transpose(1, 2, 0, 3)

    placed = (
        P("gx", "gy", None, "grp"),
        P("gx", "gy"),
        P("gx", "gy", None, None, None),
        P("gx"),
        P("gx", "gy", None, "grp"),
    )
    return jax.shard_map(body, mesh=mesh, in_specs=placed, out_specs=P("gx", "gy", None, "grp"), check_vma=False)
```

time: 454 us -> 123 us (0.27)
  the two profiles are of different devices: /device:TPU:6 before, /device:TPU:8 now
where the time goes in v3:
time: 123 us; the launch traced here: 122 us
  waiting for transfers between devices  56.2 us (46%)
  starting transfers between devices  30.4 us (25%)
  Pallas kernels  23.9 us (19%)
  local copies, waits for them, and re-layouts  10.2 us (8%)
  other arithmetic  1.47 us (1%)
    ppermute x9, waiting for transfers between devices, send_x(): lax.ppermute(inner, 'gx', even)  42.1 us
    pallas_call x10, Pallas kernels, call(): pl.pallas_call(body, out_shape=shapes, in_specs=[SMEM] * smem + [VMEM] *...  23.9 us
    ppermute x9, starting transfers between devices, send_x(): lax.ppermute(inner, 'gx', even)  15.1 us
    ppermute x8, starting transfers between devices, send(): lax.ppermute(ymsg, 'gy', swap)  10.3 us
    unnamed x31, local copies, waits for them, and re-layouts  7.74 us
    ppermute x9, waiting for transfers between devices, send_x(): lax.ppermute(outer, mesh.axis_names, hops)  7.36 us
    ppermute x8, waiting for transfers between devices, send(): lax.ppermute(ymsg, 'gy', swap)  6.71 us
    ppermute x9, starting transfers between devices, send_x(): lax.ppermute(outer, mesh.axis_names, hops)  4.38 us
  transfers between devices with their start and end apart: 34, of which 11 were waited for; matrix products, arithmetic and copies ran while one was open for 6% of the time, Pallas kernels for 13%

profile of v3, /device:TPU:8, one launch (start us, length us, event | category | flops | bytes accessed | tf_op | source)
XLA Modules:
  0.0 122.4 jit_solution(14337341887145456811)
XLA Ops:
  0.1 1.4 %copy-done = f32[32,16,3,256]{3,1,2,0:T(8,128)S(1)} copy-done((f32[32,16,3,256]{3,1,2,0:T(8,128)S(1)}, f32[32,16,3,256]{3,1,2,0:T(8,128)}, u32[]{:S(2)}) %copy-start) | copy-done | bytes 1572888
  1.5 1.7 %shard_map.92 = (f32[6,16,128]{2,1,0:T(8,128)S(1)}, f32[6,16,128]{2,1,0:T(8,128)S(1)}, f32[3,2,4,8,128]{4,3,2,1,0:T(8,128)}, f32[3,32,16,128]{3,2,1,0:T(8,128)}) custom-call(s32[4]{0:T(128)S(1)} %pad_add_fusion.info, f32[32,3,16,256]{3,2,1,0:T(8,128)S(1)} %bitcast.17), custom_call_target="tpu_custom_call" | custom-call | flops 1000000 | bytes 2555920 | tf_op jit(solution)/shard_map/pallas_call | solution.py:28
  3.2 1.5 %collective-permute-start.6 = (f32[3,2,4,8,128]{4,3,2,1,0:T(8,128)}, f32[3,2,4,8,128]{4,3,2,1,0:T(8,128)S(1)}, u32[]{:S(2)}, u32[]{:S(2)}) collective-permute-start(f32[3,2,4,8,128]{4,3,2,1,0:T(8,128)} %get-tuple-element.67), channel_id=1, source_target_pairs={{0,1},{1,0},{2,3},{3,2},{4,5},{5,4},{6,7},{7,6},{8,9},{9,8},{10,11... | collective-permute-start | bytes 294920 | tf_op jit(solution)/shard_map/ppermute | solution.py:408
  4.7 1.5 %collective-permute-start.4 = (f32[6,16,128]{2,1,0:T(8,128)S(1)}, f32[6,16,128]{2,1,0:T(8,128)S(1)}, u32[]{:S(2)}, u32[]{:S(2)}) collective-permute-start(f32[6,16,128]{2,1,0:T(8,128)S(1)} %get-tuple-element.65), channel_id=1, source_target_pairs={{0,2},{2,0},{4,6},{6,4},{8,10},{10,8},{12,14},{14,12},{1,3},{3,1},... | collective-permute-start | bytes 147464 | tf_op jit(solution)/shard_map/ppermute | solution.py:405
  6.4 1.4 %shard_map.91 = (f32[4,2,16,16,128]{4,3,2,1,0:T(8,128)S(1)}, f32[24,16,128]{2,1,0:T(8,128)}, f32[24,16,128]{2,1,0:T(8,128)S(1)}, f32[1,2,16,8,128]{4,3,2,1,0:T(8,128)}, f32[2,16,16,128]{3,2,1,0:T(8,128)S(1)}) custom-call(s32[4]{0:T(128)S(1)} %pad_add_fusion.info, f32[4,16,16,256]{3,2,1,0:T(8,128)S(1)} %bitcast.19), custom_call_target="tpu_custom_call" | custom-call | flops 1000000 | bytes 2883600 | tf_op jit(solution)/shard_map/pallas_call | solution.py:28
  7.8 0.7 copy-done.4
  9.6 0.7 fusion
  10.3 1.5 %copy.20 = bf16[4,1,1,64,64]{4,3,0,2,1:T(8,128)(2,1)} copy(bf16[4,1,1,64,64]{3,4,2,1,0:T(8,128)(2,1)} %get-tuple-element.105) | data formatting | bytes 65536
  11.8 1.5 %copy.21 = bf16[4,1,1,64,64]{4,3,0,2,1:T(8,128)(2,1)} copy(bf16[4,1,1,64,64]{3,4,2,1,0:T(8,128)(2,1)} %get-tuple-element.107) | data formatting | bytes 65536
  13.4 1.6 %copy.22 = bf16[4,1,1,64,64]{4,3,0,2,1:T(8,128)(2,1)} copy(bf16[4,1,1,64,64]{3,4,2,1,0:T(8,128)(2,1)} %get-tuple-element.106) | data formatting | bytes 65536
  14.9 0.7 copy.23
  15.7 1.4 %collective-permute-start.5 = (f32[6,16,128]{2,1,0:T(8,128)}, f32[6,16,128]{2,1,0:T(8,128)S(1)}, u32[]{:S(2)}, u32[]{:S(2)}) collective-permute-start(f32[6,16,128]{2,1,0:T(8,128)} %copy-done.5), channel_id=1, source_target_pairs={{2,4},{18,20},{3,5},{19,21},{4,2},{20,18},{5,3},{21,19},{6,8},{22,... | collective-permute-start | bytes 147464 | tf_op jit(solution)/shard_map/ppermute | solution.py:405
  17.0 1.3 %maximum_maximum_fusion.tiles = bf16[4,192,256]{2,1,0:T(8,128)(2,1)S(1)} fusion(bf16[4,64,64]{2,1,0:T(8,128)(2,1)} %bitcast.25, bf16[4,64,128]{2,1,0:T(8,128)(2,1)S(1)} %broadcast_in_dim.10, bf16[4,64,64]{2,1,0:T(8,128)(2,1)} %bitcast.24, bf16[4,64,64]{2,1,0:T(8,128)(2,1)} %bitcast.23, bf16[4,64,64]{2,1,0:T(8,128)(2,1)} %bitcast.22), kind=kLoop, calls=%fused_computation.3 | loop fusion | flops 3932160 | bytes 589824 | tf_op jit(solution)/shard_map/concatenate | solution.py:427
  18.3 2.5 %collective-permute-done.5.outer = f32[6,16,128]{2,1,0:T(8,128)S(1)} collective-permute-done((f32[6,16,128]{2,1,0:T(8,128)}, f32[6,16,128]{2,1,0:T(8,128)S(1)}, u32[]{:S(2)}, u32[]{:S(2)}) %collective-permute-start.5) | collective-permute-done | bytes 49184 | tf_op jit(solution)/shard_map/ppermute | solution.py:405
  20.9 1.4 %collective-permute-start.1 = (f32[24,16,128]{2,1,0:T(8,128)}, f32[24,16,128]{2,1,0:T(8,128)S(1)}, u32[]{:S(2)}, u32[]{:S(2)}) collective-permute-start(f32[24,16,128]{2,1,0:T(8,128)} %copy-done.4), channel_id=1, source_target_pairs={{2,4},{18,20},{3,5},{19,21},{4,2},{20,18},{5,3},{21,19},{6,8},{22,... | collective-permute-start | bytes 589832 | tf_op jit(solution)/shard_map/ppermute | solution.py:405
  22.2 4.2 %shard_map.93 = (f32[3,2,32,16,128]{4,3,2,1,0:T(8,128)S(1)}, f32[3,2,16,16,128]{4,3,2,1,0:T(8,128)S(1)}, f32[30,16,128]{2,1,0:T(8,128)S(1)}, f32[30,16,128]{2,1,...) custom-call(s32[4]{0:T(128)S(1)} %pad_add_fusion.info, s32[8]{0:T(128)S(1)} %copy-done.2, ...), custom_call_target="tpu_custom_call" | custom-call | flops 4000000 | bytes 7077936 | tf_op jit(solution)/shard_map/pallas_call | solution.py:28
  26.8 1.7 %collective-permute-start.8 = (f32[30,16,128]{2,1,0:T(8,128)S(1)}, f32[30,16,128]{2,1,0:T(8,128)S(1)}, u32[]{:S(2)}, u32[]{:S(2)}) collective-permute-start(f32[30,16,128]{2,1,0:T(8,128)S(1)} %get-tuple-element.70), channel_id=1, source_target_pairs={{0,2},{2,0},{4,6},{6,4},{8,10},{10,8},{12,14},{14,12},{1,3},{3,1},... | collective-permute-start | bytes 737288 | tf_op jit(solution)/shard_map/ppermute | solution.py:405
  28.6 0.7 collective-permute-done.1.outer
  29.3 10.9 %collective-permute-done.8.t_in.inner = f32[30,16,128]{2,1,0:T(8,128)S(1)} collective-permute-done((f32[30,16,128]{2,1,0:T(8,128)S(1)}, f32[30,16,128]{2,1,0:T(8,128)S(1)}, u32[]{:S(2)}, u32[]{:S(2)}) %collective-permute-start.8) | collective-permute-done | bytes 245792 | tf_op jit(solution)/shard_map/ppermute | solution.py:405
  40.3 2.2 %shard_map.94 = (f32[4,2,16,16,128]{4,3,2,1,0:T(8,128)S(1)}, f32[3,2,16,16,128]{4,3,2,1,0:T(8,128)S(1)}, f32[24,16,128]{2,1,0:T(8,128)S(1)}, f32[24,16,128]{2,1,...) custom-call(s32[4]{0:T(128)S(1)} %pad_add_fusion.info, ...), custom_call_target="tpu_custom_call" | custom-call | flops 4000000 | bytes 7045136 | tf_op jit(solution)/shard_map/pallas_call | solution.py:28
  42.6 1.6 %collective-permute-start.12 = (f32[1,2,16,8,128]{4,3,2,1,0:T(8,128)S(1)}, f32[1,2,16,8,128]{4,3,2,1,0:T(8,128)S(1)}, u32[]{:S(2)}, u32[]{:S(2)}) collective-permute-start(f32[1,2,16,8,128]{4,3,2,1,0:T(8,128)S(1)} %get-tuple-element.75), channel_id=1, source_target_pairs={{0,1},{1,0},{2,3},{3,2},{4,5},{5,4},{6,7},{7,6},{8,9},{9,8},{10,11... | collective-permute-start | bytes 393224 | tf_op jit(solution)/shard_map/ppermute | solution.py:408
  44.2 1.7 %collective-permute-start.10 = (f32[24,16,128]{2,1,0:T(8,128)S(1)}, f32[24,16,128]{2,1,0:T(8,128)S(1)}, u32[]{:S(2)}, u32[]{:S(2)}) collective-permute-start(f32[24,16,128]{2,1,0:T(8,128)S(1)} %get-tuple-element.73), channel_id=1, source_target_pairs={{0,2},{2,0},{4,6},{6,4},{8,10},{10,8},{12,14},{14,12},{1,3},{3,1},... | collective-permute-start | bytes 589832 | tf_op jit(solution)/shard_map/ppermute | solution.py:405
  45.9 2.6 %collective-permute-done.12.ymsg = f32[1,2,16,8,128]{4,3,2,1,0:T(8,128)S(1)} collective-permute-done((f32[1,2,16,8,128]{4,3,2,1,0:T(8,128)S(1)}, f32[1,2,16,8,128]{4,3,2,1,0:T(8,128)S(1)}, u32[]{:S(2)}, u32[]{:S(2)}) %collective-permute-start.12) | collective-permute-done | bytes 131104 | tf_op jit(solution)/shard_map/ppermute | solution.py:408
  48.5 1.5 %collective-permute-start.22 = (f32[3,2,4,8,128]{4,3,2,1,0:T(8,128)S(1)}, f32[3,2,4,8,128]{4,3,2,1,0:T(8,128)S(1)}, u32[]{:S(2)}, u32[]{:S(2)}) collective-permute-start(f32[3,2,4,8,128]{4,3,2,1,0:T(8,128)S(1)} %get-tuple-element.89), channel_id=1, source_target_pairs={{0,1},{1,0},{2,3},{3,2},{4,5},{5,4},{6,7},{7,6},{8,9},{9,8},{10,11... | collective-permute-start | bytes 294920 | tf_op jit(solution)/shard_map/ppermute | solution.py:408
  50.0 5.3 %collective-permute-done.10.inner = f32[24,16,128]{2,1,0:T(8,128)S(1)} collective-permute-done((f32[24,16,128]{2,1,0:T(8,128)S(1)}, f32[24,16,128]{2,1,0:T(8,128)S(1)}, u32[]{:S(2)}, u32[]{:S(2)}) %collective-permute-start.10) | collective-permute-done | bytes 196640 | tf_op jit(solution)/shard_map/ppermute | solution.py:405
  55.4 2.2 %shard_map.95 = (f32[4,2,16,16,128]{4,3,2,1,0:T(8,128)S(1)}, f32[24,16,128]{2,1,0:T(8,128)S(1)}, f32[24,16,128]{2,1,0:T(8,128)S(1)}, f32[2,2,16,8,128]{4,3,2,1,0:T(8,128)S(1)}, f32[4,16,16,128]{3,2,1,0:T(8,128)S(1)}) custom-call(s32[4]{0:T(128)S(1)} %pad_add_fusion.info, f32[4,2,16,16,128]{4,3,2,1,0:T(8,128)S(1)} %get-tuple-element.72.f, ...), custom_call_target="tpu_custom_call" | custom-call | flops 4000000 | bytes 7208976 | tf_op jit(solution)/shard_map/pallas_call | solution.py:28
  57.7 0.6 collective-permute-start.16
  58.3 1.7 %collective-permute-start.14 = (f32[24,16,128]{2,1,0:T(8,128)S(1)}, f32[24,16,128]{2,1,0:T(8,128)S(1)}, u32[]{:S(2)}, u32[]{:S(2)}) collective-permute-start(f32[24,16,128]{2,1,0:T(8,128)S(1)} %get-tuple-element.79), channel_id=1, source_target_pairs={{0,2},{2,0},{4,6},{6,4},{8,10},{10,8},{12,14},{14,12},{1,3},{3,1},... | collective-permute-start | bytes 589832 | tf_op jit(solution)/shard_map/ppermute | solution.py:405
  60.0 2.8 %shard_map.97 = (f32[3,2,16,16,128]{4,3,2,1,0:T(8,128)S(1)}, f32[24,16,128]{2,1,0:T(8,128)S(1)}, f32[24,16,128]{2,1,0:T(8,128)S(1)}) custom-call(s32[4]{0:T(128)S(1)} %pad_add_fusion.info, s32[8]{0:T(128)S(1)} %copy-done.2, f32[3,2,32,16,128]{4,3,2,1,0:T(8,128)S(1)} %get-tuple-element.88.v, f32[30,16,128]{2,1,0:T(8,128)S(1)} %collective-permute-done.8.t_in.inner, ...), custom_call_target="tpu_custom_call" | custom-call | flops 4000000 | bytes 4915248 | tf_op jit(solution)/shard_map/pallas_call | solution.py:28
  62.8 3.1 %collective-permute-start.24 = (f32[24,16,128]{2,1,0:T(8,128)S(1)}, f32[24,16,128]{2,1,0:T(8,128)S(1)}, u32[]{:S(2)}, u32[]{:S(2)}) collective-permute-start(f32[24,16,128]{2,1,0:T(8,128)S(1)} %get-tuple-element.92), channel_id=1, source_target_pairs={{0,2},{2,0},{4,6},{6,4},{8,10},{10,8},{12,14},{14,12},{1,3},{3,1},... | collective-permute-start | bytes 589832 | tf_op jit(solution)/shard_map/ppermute | solution.py:405
  66.0 4.3 %collective-permute-done.14.inner = f32[24,16,128]{2,1,0:T(8,128)S(1)} collective-permute-done((f32[24,16,128]{2,1,0:T(8,128)S(1)}, f32[24,16,128]{2,1,0:T(8,128)S(1)}, u32[]{:S(2)}, u32[]{:S(2)}) %collective-permute-start.14) | collective-permute-done | bytes 196640 | tf_op jit(solution)/shard_map/ppermute | solution.py:405
  70.3 2.6 %shard_map.96 = (f32[4,2,16,16,128]{4,3,2,1,0:T(8,128)S(1)}, f32[24,16,128]{2,1,0:T(8,128)S(1)}, f32[24,16,128]{2,1,0:T(8,128)S(1)}, f32[1,2,16,8,128]{4,3,2,1,0:T(8,128)S(1)}, f32[2,16,16,128]{3,2,1,0:T(8,128)S(1)}) custom-call(s32[4]{0:T(128)S(1)} %pad_add_fusion.info, f32[4,2,16,16,128]{4,3,2,1,0:T(8,128)S(1)} %get-tuple-element.78.f, ...), custom_call_target="tpu_custom_call" | custom-call | flops 4000000 | bytes 5242896 | tf_op jit(solution)/shard_map/pallas_call | solution.py:28
  72.9 1.6 %collective-permute-start.25 = (f32[24,16,128]{2,1,0:T(8,128)S(1)}, f32[24,16,128]{2,1,0:T(8,128)S(1)}, u32[]{:S(2)}, u32[]{:S(2)}) collective-permute-start(f32[24,16,128]{2,1,0:T(8,128)S(1)} %get-tuple-element.93), channel_id=1, source_target_pairs={{2,4},{18,20},{3,5},{19,21},{4,2},{20,18},{5,3},{21,19},{6,8},{22,... | collective-permute-start | bytes 589832 | tf_op jit(solution)/shard_map/ppermute | solution.py:405
  74.5 1.5 %collective-permute-start.18 = (f32[24,16,128]{2,1,0:T(8,128)S(1)}, f32[24,16,128]{2,1,0:T(8,128)S(1)}, u32[]{:S(2)}, u32[]{:S(2)}) collective-permute-start(f32[24,16,128]{2,1,0:T(8,128)S(1)} %get-tuple-element.84), channel_id=1, source_target_pairs={{0,2},{2,0},{4,6},{6,4},{8,10},{10,8},{12,14},{14,12},{1,3},{3,1},... | collective-permute-start | bytes 589832 | tf_op jit(solution)/shard_map/ppermute | solution.py:405
  76.0 1.5 %collective-permute-start.20 = (f32[1,2,16,8,128]{4,3,2,1,0:T(8,128)S(1)}, f32[1,2,16,8,128]{4,3,2,1,0:T(8,128)S(1)}, u32[]{:S(2)}, u32[]{:S(2)}) collective-permute-start(f32[1,2,16,8,128]{4,3,2,1,0:T(8,128)S(1)} %get-tuple-element.86), channel_id=1, source_target_pairs={{0,1},{1,0},{2,3},{3,2},{4,5},{5,4},{6,7},{7,6},{8,9},{9,8},{10,11... | collective-permute-start | bytes 393224 | tf_op jit(solution)/shard_map/ppermute | solution.py:408
  77.5 4.1 %collective-permute-done.25.t_out = f32[24,16,128]{2,1,0:T(8,128)S(1)} collective-permute-done((f32[24,16,128]{2,1,0:T(8,128)S(1)}, f32[24,16,128]{2,1,0:T(8,128)S(1)}, u32[]{:S(2)}, u32[]{:S(2)}) %collective-permute-start.25) | collective-permute-done | bytes 196640 | tf_op jit(solution)/shard_map/ppermute | solution.py:405
  81.7 7.9 %collective-permute-done.18.inner = f32[24,16,128]{2,1,0:T(8,128)S(1)} collective-permute-done((f32[24,16,128]{2,1,0:T(8,128)S(1)}, f32[24,16,128]{2,1,0:T(8,128)S(1)}, u32[]{:S(2)}, u32[]{:S(2)}) %collective-permute-start.18) | collective-permute-done | bytes 196640 | tf_op jit(solution)/shard_map/ppermute | solution.py:405
  89.5 2.1 %shard_map.98 = (f32[4,2,16,16,128]{4,3,2,1,0:T(8,128)S(1)}, f32[3,2,16,16,128]{4,3,2,1,0:T(8,128)S(1)}, f32[24,16,128]{2,1,0:T(8,128)S(1)}, f32[24,16,128]{2,1,...) custom-call(s32[4]{0:T(128)S(1)} %pad_add_fusion.info, ...), custom_call_target="tpu_custom_call" | custom-call | flops 4000000 | bytes 6946832 | tf_op jit(solution)/shard_map/pallas_call | solution.py:28
  91.8 1.7 %collective-permute-start.26 = (f32[24,16,128]{2,1,0:T(8,128)S(1)}, f32[24,16,128]{2,1,0:T(8,128)S(1)}, u32[]{:S(2)}, u32[]{:S(2)}) collective-permute-start(f32[24,16,128]{2,1,0:T(8,128)S(1)} %get-tuple-element.95), channel_id=1, source_target_pairs={{0,2},{2,0},{4,6},{6,4},{8,10},{10,8},{12,14},{14,12},{1,3},{3,1},... | collective-permute-start | bytes 589832 | tf_op jit(solution)/shard_map/ppermute | solution.py:405
  93.5 1.5 %collective-permute-start.28 = (f32[1,2,16,8,128]{4,3,2,1,0:T(8,128)S(1)}, f32[1,2,16,8,128]{4,3,2,1,0:T(8,128)S(1)}, u32[]{:S(2)}, u32[]{:S(2)}) collective-permute-start(f32[1,2,16,8,128]{4,3,2,1,0:T(8,128)S(1)} %get-tuple-element.97), channel_id=1, source_target_pairs={{0,1},{1,0},{2,3},{3,2},{4,5},{5,4},{6,7},{7,6},{8,9},{9,8},{10,11... | collective-permute-start | bytes 393224 | tf_op jit(solution)/shard_map/ppermute | solution.py:408
  95.0 4.1 %collective-permute-done.28.ymsg = f32[1,2,16,8,128]{4,3,2,1,0:T(8,128)S(1)} collective-permute-done((f32[1,2,16,8,128]{4,3,2,1,0:T(8,128)S(1)}, f32[1,2,16,8,128]{4,3,2,1,0:T(8,128)S(1)}, u32[]{:S(2)}, u32[]{:S(2)}) %collective-permute-start.28) | collective-permute-done | bytes 131104 | tf_op jit(solution)/shard_map/ppermute | solution.py:408
  99.1 4.2 %collective-permute-done.26.inner = f32[24,16,128]{2,1,0:T(8,128)S(1)} collective-permute-done((f32[24,16,128]{2,1,0:T(8,128)S(1)}, f32[24,16,128]{2,1,0:T(8,128)S(1)}, u32[]{:S(2)}, u32[]{:S(2)}) %collective-permute-start.26) | collective-permute-done | bytes 196640 | tf_op jit(solution)/shard_map/ppermute | solution.py:405
  103.3 2.2 %shard_map.99 = (f32[4,2,16,16,128]{4,3,2,1,0:T(8,128)S(1)}, f32[24,16,128]{2,1,0:T(8,128)S(1)}, f32[24,16,128]{2,1,0:T(8,128)S(1)}, f32[2,2,16,8,128]{4,3,2,1,0:T(8,128)S(1)}, f32[4,16,16,128]{3,2,1,0:T(8,128)S(1)}) custom-call(s32[4]{0:T(128)S(1)} %pad_add_fusion.info, f32[4,2,16,16,128]{4,3,2,1,0:T(8,128)S(1)} %get-tuple-element.94.f, ...), custom_call_target="tpu_custom_call" | custom-call | flops 4000000 | bytes 7208976 | tf_op jit(solution)/shard_map/pallas_call | solution.py:28
  105.6 1.6 %collective-permute-start.32 = (f32[2,2,16,8,128]{4,3,2,1,0:T(8,128)S(1)}, f32[2,2,16,8,128]{4,3,2,1,0:T(8,128)S(1)}, u32[]{:S(2)}, u32[]{:S(2)}) collective-permute-start(f32[2,2,16,8,128]{4,3,2,1,0:T(8,128)S(1)} %get-tuple-element.103), channel_id=1, source_target_pairs={{0,1},{1,0},{2,3},{3,2},{4,5},{5,4},{6,7},{7,6},{8,9},{9,8},{10,11... | collective-permute-start | bytes 786440 | tf_op jit(solution)/shard_map/ppermute | solution.py:408
  107.1 1.7 %collective-permute-start.30 = (f32[24,16,128]{2,1,0:T(8,128)S(1)}, f32[24,16,128]{2,1,0:T(8,128)S(1)}, u32[]{:S(2)}, u32[]{:S(2)}) collective-permute-start(f32[24,16,128]{2,1,0:T(8,128)S(1)} %get-tuple-element.101), channel_id=1, source_target_pairs={{0,2},{2,0},{4,6},{6,4},{8,10},{10,8},{12,14},{14,12},{1,3},{3,1},... | collective-permute-start | bytes 589832 | tf_op jit(solution)/shard_map/ppermute | solution.py:405
  108.8 9.5 %collective-permute-done.30.inner = f32[24,16,128]{2,1,0:T(8,128)S(1)} collective-permute-done((f32[24,16,128]{2,1,0:T(8,128)S(1)}, f32[24,16,128]{2,1,0:T(8,128)S(1)}, u32[]{:S(2)}, u32[]{:S(2)}) %collective-permute-start.30) | collective-permute-done | bytes 196640 | tf_op jit(solution)/shard_map/ppermute | solution.py:405
  118.3 2.4 %shard_map.100 = f32[4,16,16,256]{3,2,1,0:T(8,128)S(1)} custom-call(s32[4]{0:T(128)S(1)} %pad_add_fusion.info, f32[4,2,16,16,128]{4,3,2,1,0:T(8,128)S(1)} %get-tuple-element.100.f, f32[24,16,128]{2,1,0:T(8,128)S(1)} %collective-permute-done.30.inner, f32[24,16,128]{2,1,0:T(8,128)S(1)} %collective-permute-done.31.outer, ...), custom_call_target="tpu_custom_call" | custom-call | flops 4000000 | bytes 4456464 | tf_op jit(solution)/shard_map/pallas_call | solution.py:28
  120.8 1.7 %copy.18 = f32[16,16,4,256]{3,2,1,0:T(4,128)} copy(f32[16,16,4,256]{3,1,0,2:T(8,128)S(1)} %bitcast.20) | data formatting | bytes 2097152 | tf_op jit(solution)/shard_map/transpose | solution.py:501
  (69 shorter events, 2.4 us)
Async XLA Ops:
  0.1 1.4 %copy-start = (f32[32,16,3,256]{3,1,2,0:T(8,128)S(1)}, f32[32,16,3,256]{3,1,2,0:T(8,128)}, u32[]{:S(2)}) copy-start(f32[32,16,3,256]{3,1,2,0:T(8,128)} %param.9) | copy-start | bytes 4718596
  1.5 4.7 %copy-start.6 = (f32[16,16,4,256]{3,2,1,0:T(4,128)S(1)}, f32[16,16,4,256]{3,2,1,0:T(4,128)}, u32[]{:S(2)}) copy-start(f32[16,16,4,256]{3,2,1,0:T(4,128)} %param.13) | copy-start | bytes 3145732
  3.2 4.7 %copy-start.5 = (f32[6,16,128]{2,1,0:T(8,128)}, f32[6,16,128]{2,1,0:T(8,128)S(1)}, u32[]{:S(2)}) copy-start(f32[6,16,128]{2,1,0:T(8,128)S(1)} %get-tuple-element.66) | copy-start | bytes 147460
  3.2 19.1 %collective-permute-start.7 = (f32[3,32,16,128]{3,2,1,0:T(8,128)}, f32[3,32,16,128]{3,2,1,0:T(8,128)}, u32[]{:S(2)}, u32[]{:S(2)}) collective-permute-start(f32[3,32,16,128]{3,2,1,0:T(8,128)} %get-tuple-element.68), channel_id=1, source_target_pairs={{0,16},{16,0},{1,17},{17,1},{2,18},{18,2},{3,19},{19,3},{4,20},{20... | collective-permute-start | bytes 2359304 | tf_op jit(solution)/shard_map/ppermute | solution.py:408
  3.2 17.7 %collective-permute-start.6 = (f32[3,2,4,8,128]{4,3,2,1,0:T(8,128)}, f32[3,2,4,8,128]{4,3,2,1,0:T(8,128)S(1)}, u32[]{:S(2)}, u32[]{:S(2)}) collective-permute-start(f32[3,2,4,8,128]{4,3,2,1,0:T(8,128)} %get-tuple-element.67), channel_id=1, source_target_pairs={{0,1},{1,0},{2,3},{3,2},{4,5},{5,4},{6,7},{7,6},{8,9},{9,8},{10,11... | collective-permute-start | bytes 294920 | tf_op jit(solution)/shard_map/ppermute | solution.py:408
  4.7 4.9 %copy-start.11 = (bf16[8,1,2,64,64]{4,3,2,1,0:T(8,128)(2,1)S(1)}, bf16[8,1,2,64,64]{4,3,2,1,0:T(8,128)(2,1)}, u32[]{:S(2)}) copy-start(bf16[8,1,2,64,64]{4,3,2,1,0:T(8,128)(2,1)} %param.11) | copy-start | bytes 393220
  4.7 11.0 %collective-permute-start.4 = (f32[6,16,128]{2,1,0:T(8,128)S(1)}, f32[6,16,128]{2,1,0:T(8,128)S(1)}, u32[]{:S(2)}, u32[]{:S(2)}) collective-permute-start(f32[6,16,128]{2,1,0:T(8,128)S(1)} %get-tuple-element.65), channel_id=1, source_target_pairs={{0,2},{2,0},{4,6},{6,4},{8,10},{10,8},{12,14},{14,12},{1,3},{3,1},... | collective-permute-start | bytes 147464 | tf_op jit(solution)/shard_map/ppermute | solution.py:405
  6.4 15.9 %copy-start.1 = (f32[32,16,3,256]{3,1,2,0:T(8,128)S(1)}, f32[32,16,3,256]{3,1,2,0:T(8,128)}, u32[]{:S(2)}) copy-start(f32[32,16,3,256]{3,1,2,0:T(8,128)} %param.9) | copy-start | bytes 4718596
  6.4 15.8 %copy-start.2 = (s32[8]{0:T(128)S(1)}, s32[8]{0:T(128)}, u32[]{:S(2)}) copy-start(s32[8]{0:T(128)} %offset.3) | copy-start | bytes 100
  7.8 0.7 copy-start.4
  8.5 8.5 %copy-start.3 = (f32[2,16,16,128]{3,2,1,0:T(8,128)}, f32[2,16,16,128]{3,2,1,0:T(8,128)S(1)}, u32[]{:S(2)}) copy-start(f32[2,16,16,128]{3,2,1,0:T(8,128)S(1)} %get-tuple-element.64) | copy-start | bytes 786436
  8.5 20.0 %collective-permute-start = (f32[24,16,128]{2,1,0:T(8,128)}, f32[24,16,128]{2,1,0:T(8,128)S(1)}, u32[]{:S(2)}, u32[]{:S(2)}) collective-permute-start(f32[24,16,128]{2,1,0:T(8,128)} %get-tuple-element.61), channel_id=1, source_target_pairs={{0,2},{2,0},{4,6},{6,4},{8,10},{10,8},{12,14},{14,12},{1,3},{3,1},... | collective-permute-start | bytes 589832 | tf_op jit(solution)/shard_map/ppermute | solution.py:405
  9.1 17.7 %collective-permute-start.2 = (f32[1,2,16,8,128]{4,3,2,1,0:T(8,128)}, f32[1,2,16,8,128]{4,3,2,1,0:T(8,128)S(1)}, u32[]{:S(2)}, u32[]{:S(2)}) collective-permute-start(f32[1,2,16,8,128]{4,3,2,1,0:T(8,128)} %get-tuple-element.63), channel_id=1, source_target_pairs={{0,1},{1,0},{2,3},{3,2},{4,5},{5,4},{6,7},{7,6},{8,9},{9,8},{10,11... | collective-permute-start | bytes 393224 | tf_op jit(solution)/shard_map/ppermute | solution.py:408
  15.7 5.2 %collective-permute-start.5 = (f32[6,16,128]{2,1,0:T(8,128)}, f32[6,16,128]{2,1,0:T(8,128)S(1)}, u32[]{:S(2)}, u32[]{:S(2)}) collective-permute-start(f32[6,16,128]{2,1,0:T(8,128)} %copy-done.5), channel_id=1, source_target_pairs={{2,4},{18,20},{3,5},{19,21},{4,2},{20,18},{5,3},{21,19},{6,8},{22,... | collective-permute-start | bytes 147464 | tf_op jit(solution)/shard_map/ppermute | solution.py:405
  18.3 10.2 %copy-start.9 = (bf16[1152,256]{1,0:T(8,128)(2,1)S(1)}, bf16[1152,256]{1,0:T(8,128)(2,1)}, u32[]{:S(2)}) copy-start(bf16[1152,256]{1,0:T(8,128)(2,1)} %constant.38.clone) | copy-start | bytes 1769476
  18.3 10.2 %copy-start.10 = (bf16[1152,256]{1,0:T(8,128)(2,1)S(1)}, bf16[1152,256]{1,0:T(8,128)(2,1)}, u32[]{:S(2)}) copy-start(bf16[1152,256]{1,0:T(8,128)(2,1)} %constant.39.clone) | copy-start | bytes 1769476
  20.9 8.4 %collective-permute-start.3 = (f32[2,16,16,128]{3,2,1,0:T(8,128)}, f32[2,16,16,128]{3,2,1,0:T(8,128)S(1)}, u32[]{:S(2)}, u32[]{:S(2)}) collective-permute-start(f32[2,16,16,128]{3,2,1,0:T(8,128)} %copy-done.3), channel_id=1, source_target_pairs={{0,16},{16,0},{1,17},{17,1},{2,18},{18,2},{3,19},{19,3},{4,20},{20... | collective-permute-start | bytes 786440 | tf_op jit(solution)/shard_map/ppermute | solution.py:408
  20.9 8.4 %collective-permute-start.1 = (f32[24,16,128]{2,1,0:T(8,128)}, f32[24,16,128]{2,1,0:T(8,128)S(1)}, u32[]{:S(2)}, u32[]{:S(2)}) collective-permute-start(f32[24,16,128]{2,1,0:T(8,128)} %copy-done.4), channel_id=1, source_target_pairs={{2,4},{18,20},{3,5},{19,21},{4,2},{20,18},{5,3},{21,19},{6,8},{22,... | collective-permute-start | bytes 589832 | tf_op jit(solution)/shard_map/ppermute | solution.py:405
  26.5 13.7 %copy-start.12 = (f32[16,16]{1,0:T(8,128)S(1)}, f32[16,16]{1,0:T(8,128)}, u32[]{:S(2)}) copy-start(f32[16,16]{1,0:T(8,128)} %param.10) | copy-start | bytes 3076
  26.5 33.5 %collective-permute-start.23 = (f32[3,32,16,128]{3,2,1,0:T(8,128)S(1)}, f32[3,32,16,128]{3,2,1,0:T(8,128)S(1)}, u32[]{:S(2)}, u32[]{:S(2)}) collective-permute-start(f32[3,32,16,128]{3,2,1,0:T(8,128)S(1)} %get-tuple-element.90), channel_id=1, source_target_pairs={{0,16},{16,0},{1,17},{17,1},{2,18},{18,2},{3,19},{19,3},{4,20},{20... | collective-permute-start | bytes 2359304 | tf_op jit(solution)/shard_map/ppermute | solution.py:408
  26.8 13.4 %collective-permute-start.8 = (f32[30,16,128]{2,1,0:T(8,128)S(1)}, f32[30,16,128]{2,1,0:T(8,128)S(1)}, u32[]{:S(2)}, u32[]{:S(2)}) collective-permute-start(f32[30,16,128]{2,1,0:T(8,128)S(1)} %get-tuple-element.70), channel_id=1, source_target_pairs={{0,2},{2,0},{4,6},{6,4},{8,10},{10,8},{12,14},{14,12},{1,3},{3,1},... | collective-permute-start | bytes 737288 | tf_op jit(solution)/shard_map/ppermute | solution.py:405
  28.5 11.7 %collective-permute-start.9 = (f32[30,16,128]{2,1,0:T(8,128)S(1)}, f32[30,16,128]{2,1,0:T(8,128)S(1)}, u32[]{:S(2)}, u32[]{:S(2)}) collective-permute-start(f32[30,16,128]{2,1,0:T(8,128)S(1)} %get-tuple-element.71), channel_id=1, source_target_pairs={{2,4},{18,20},{3,5},{19,21},{4,2},{20,18},{5,3},{21,19},{6,8},{22,... | collective-permute-start | bytes 737288 | tf_op jit(solution)/shard_map/ppermute | solution.py:405
  42.5 12.9 %collective-permute-start.13 = (f32[2,16,16,128]{3,2,1,0:T(8,128)S(1)}, f32[2,16,16,128]{3,2,1,0:T(8,128)S(1)}, u32[]{:S(2)}, u32[]{:S(2)}) collective-permute-start(f32[2,16,16,128]{3,2,1,0:T(8,128)S(1)} %get-tuple-element.76), channel_id=1, source_target_pairs={{0,16},{16,0},{1,17},{17,1},{2,18},{18,2},{3,19},{19,3},{4,20},{20... | collective-permute-start | bytes 786440 | tf_op jit(solution)/shard_map/ppermute | solution.py:408
  42.6 5.9 %collective-permute-start.12 = (f32[1,2,16,8,128]{4,3,2,1,0:T(8,128)S(1)}, f32[1,2,16,8,128]{4,3,2,1,0:T(8,128)S(1)}, u32[]{:S(2)}, u32[]{:S(2)}) collective-permute-start(f32[1,2,16,8,128]{4,3,2,1,0:T(8,128)S(1)} %get-tuple-element.75), channel_id=1, source_target_pairs={{0,1},{1,0},{2,3},{3,2},{4,5},{5,4},{6,7},{7,6},{8,9},{9,8},{10,11... | collective-permute-start | bytes 393224 | tf_op jit(solution)/shard_map/ppermute | solution.py:408
  44.2 11.2 %collective-permute-start.10 = (f32[24,16,128]{2,1,0:T(8,128)S(1)}, f32[24,16,128]{2,1,0:T(8,128)S(1)}, u32[]{:S(2)}, u32[]{:S(2)}) collective-permute-start(f32[24,16,128]{2,1,0:T(8,128)S(1)} %get-tuple-element.73), channel_id=1, source_target_pairs={{0,2},{2,0},{4,6},{6,4},{8,10},{10,8},{12,14},{14,12},{1,3},{3,1},... | collective-permute-start | bytes 589832 | tf_op jit(solution)/shard_map/ppermute | solution.py:405
  45.9 9.5 %collective-permute-start.11 = (f32[24,16,128]{2,1,0:T(8,128)S(1)}, f32[24,16,128]{2,1,0:T(8,128)S(1)}, u32[]{:S(2)}, u32[]{:S(2)}) collective-permute-start(f32[24,16,128]{2,1,0:T(8,128)S(1)} %get-tuple-element.74), channel_id=1, source_target_pairs={{2,4},{18,20},{3,5},{19,21},{4,2},{20,18},{5,3},{21,19},{6,8},{22,... | collective-permute-start | bytes 589832 | tf_op jit(solution)/shard_map/ppermute | solution.py:405
  48.5 11.4 %collective-permute-start.22 = (f32[3,2,4,8,128]{4,3,2,1,0:T(8,128)S(1)}, f32[3,2,4,8,128]{4,3,2,1,0:T(8,128)S(1)}, u32[]{:S(2)}, u32[]{:S(2)}) collective-permute-start(f32[3,2,4,8,128]{4,3,2,1,0:T(8,128)S(1)} %get-tuple-element.89), channel_id=1, source_target_pairs={{0,1},{1,0},{2,3},{3,2},{4,5},{5,4},{6,7},{7,6},{8,9},{9,8},{10,11... | collective-permute-start | bytes 294920 | tf_op jit(solution)/shard_map/ppermute | solution.py:408
  57.6 12.6 %collective-permute-start.17 = (f32[4,16,16,128]{3,2,1,0:T(8,128)S(1)}, f32[4,16,16,128]{3,2,1,0:T(8,128)S(1)}, u32[]{:S(2)}, u32[]{:S(2)}) collective-permute-start(f32[4,16,16,128]{3,2,1,0:T(8,128)S(1)} %get-tuple-element.82), channel_id=1, source_target_pairs={{0,16},{16,0},{1,17},{17,1},{2,18},{18,2},{3,19},{19,3},{4,20},{20... | collective-permute-start | bytes 1572872 | tf_op jit(solution)/shard_map/ppermute | solution.py:408
  57.7 12.5 %collective-permute-start.16 = (f32[2,2,16,8,128]{4,3,2,1,0:T(8,128)S(1)}, f32[2,2,16,8,128]{4,3,2,1,0:T(8,128)S(1)}, u32[]{:S(2)}, u32[]{:S(2)}) collective-permute-start(f32[2,2,16,8,128]{4,3,2,1,0:T(8,128)S(1)} %get-tuple-element.81), channel_id=1, source_target_pairs={{0,1},{1,0},{2,3},{3,2},{4,5},{5,4},{6,7},{7,6},{8,9},{9,8},{10,11... | collective-permute-start | bytes 786440 | tf_op jit(solution)/shard_map/ppermute | solution.py:408
  58.3 12.0 %collective-permute-start.14 = (f32[24,16,128]{2,1,0:T(8,128)S(1)}, f32[24,16,128]{2,1,0:T(8,128)S(1)}, u32[]{:S(2)}, u32[]{:S(2)}) collective-permute-start(f32[24,16,128]{2,1,0:T(8,128)S(1)} %get-tuple-element.79), channel_id=1, source_target_pairs={{0,2},{2,0},{4,6},{6,4},{8,10},{10,8},{12,14},{14,12},{1,3},{3,1},... | collective-permute-start | bytes 589832 | tf_op jit(solution)/shard_map/ppermute | solution.py:405
  60.0 10.3 %collective-permute-start.15 = (f32[24,16,128]{2,1,0:T(8,128)S(1)}, f32[24,16,128]{2,1,0:T(8,128)S(1)}, u32[]{:S(2)}, u32[]{:S(2)}) collective-permute-start(f32[24,16,128]{2,1,0:T(8,128)S(1)} %get-tuple-element.80), channel_id=1, source_target_pairs={{2,4},{18,20},{3,5},{19,21},{4,2},{20,18},{5,3},{21,19},{6,8},{22,... | collective-permute-start | bytes 589832 | tf_op jit(solution)/shard_map/ppermute | solution.py:405
  60.0 5.9 %copy-start.7 = (bf16[1152,256]{1,0:T(8,128)(2,1)S(1)}, bf16[1152,256]{1,0:T(8,128)(2,1)}, u32[]{:S(2)}) copy-start(bf16[1152,256]{1,0:T(8,128)(2,1)} %constant.40.clone) | copy-start | bytes 1769476
  60.0 5.9 %copy-start.8 = (bf16[1152,256]{1,0:T(8,128)(2,1)S(1)}, bf16[1152,256]{1,0:T(8,128)(2,1)}, u32[]{:S(2)}) copy-start(bf16[1152,256]{1,0:T(8,128)(2,1)} %constant.41.clone) | copy-start | bytes 1769476
  62.8 13.2 %collective-permute-start.24 = (f32[24,16,128]{2,1,0:T(8,128)S(1)}, f32[24,16,128]{2,1,0:T(8,128)S(1)}, u32[]{:S(2)}, u32[]{:S(2)}) collective-permute-start(f32[24,16,128]{2,1,0:T(8,128)S(1)} %get-tuple-element.92), channel_id=1, source_target_pairs={{0,2},{2,0},{4,6},{6,4},{8,10},{10,8},{12,14},{14,12},{1,3},{3,1},... | collective-permute-start | bytes 589832 | tf_op jit(solution)/shard_map/ppermute | solution.py:405
  72.8 16.7 %collective-permute-start.21 = (f32[2,16,16,128]{3,2,1,0:T(8,128)S(1)}, f32[2,16,16,128]{3,2,1,0:T(8,128)S(1)}, u32[]{:S(2)}, u32[]{:S(2)}) collective-permute-start(f32[2,16,16,128]{3,2,1,0:T(8,128)S(1)} %get-tuple-element.87), channel_id=1, source_target_pairs={{0,16},{16,0},{1,17},{17,1},{2,18},{18,2},{3,19},{19,3},{4,20},{20... | collective-permute-start | bytes 786440 | tf_op jit(solution)/shard_map/ppermute | solution.py:408
  72.9 8.8 %collective-permute-start.25 = (f32[24,16,128]{2,1,0:T(8,128)S(1)}, f32[24,16,128]{2,1,0:T(8,128)S(1)}, u32[]{:S(2)}, u32[]{:S(2)}) collective-permute-start(f32[24,16,128]{2,1,0:T(8,128)S(1)} %get-tuple-element.93), channel_id=1, source_target_pairs={{2,4},{18,20},{3,5},{19,21},{4,2},{20,18},{5,3},{21,19},{6,8},{22,... | collective-permute-start | bytes 589832 | tf_op jit(solution)/shard_map/ppermute | solution.py:405
  74.5 15.0 %collective-permute-start.18 = (f32[24,16,128]{2,1,0:T(8,128)S(1)}, f32[24,16,128]{2,1,0:T(8,128)S(1)}, u32[]{:S(2)}, u32[]{:S(2)}) collective-permute-start(f32[24,16,128]{2,1,0:T(8,128)S(1)} %get-tuple-element.84), channel_id=1, source_target_pairs={{0,2},{2,0},{4,6},{6,4},{8,10},{10,8},{12,14},{14,12},{1,3},{3,1},... | collective-permute-start | bytes 589832 | tf_op jit(solution)/shard_map/ppermute | solution.py:405
  76.0 13.5 %collective-permute-start.19 = (f32[24,16,128]{2,1,0:T(8,128)S(1)}, f32[24,16,128]{2,1,0:T(8,128)S(1)}, u32[]{:S(2)}, u32[]{:S(2)}) collective-permute-start(f32[24,16,128]{2,1,0:T(8,128)S(1)} %get-tuple-element.85), channel_id=1, source_target_pairs={{2,4},{18,20},{3,5},{19,21},{4,2},{20,18},{5,3},{21,19},{6,8},{22,... | collective-permute-start | bytes 589832 | tf_op jit(solution)/shard_map/ppermute | solution.py:405
  76.0 5.7 %collective-permute-start.20 = (f32[1,2,16,8,128]{4,3,2,1,0:T(8,128)S(1)}, f32[1,2,16,8,128]{4,3,2,1,0:T(8,128)S(1)}, u32[]{:S(2)}, u32[]{:S(2)}) collective-permute-start(f32[1,2,16,8,128]{4,3,2,1,0:T(8,128)S(1)} %get-tuple-element.86), channel_id=1, source_target_pairs={{0,1},{1,0},{2,3},{3,2},{4,5},{5,4},{6,7},{7,6},{8,9},{9,8},{10,11... | collective-permute-start | bytes 393224 | tf_op jit(solution)/shard_map/ppermute | solution.py:408
  91.7 11.6 %collective-permute-start.29 = (f32[2,16,16,128]{3,2,1,0:T(8,128)S(1)}, f32[2,16,16,128]{3,2,1,0:T(8,128)S(1)}, u32[]{:S(2)}, u32[]{:S(2)}) collective-permute-start(f32[2,16,16,128]{3,2,1,0:T(8,128)S(1)} %get-tuple-element.98), channel_id=1, source_target_pairs={{0,16},{16,0},{1,17},{17,1},{2,18},{18,2},{3,19},{19,3},{4,20},{20... | collective-permute-start | bytes 786440 | tf_op jit(solution)/shard_map/ppermute | solution.py:408
  91.8 11.5 %collective-permute-start.26 = (f32[24,16,128]{2,1,0:T(8,128)S(1)}, f32[24,16,128]{2,1,0:T(8,128)S(1)}, u32[]{:S(2)}, u32[]{:S(2)}) collective-permute-start(f32[24,16,128]{2,1,0:T(8,128)S(1)} %get-tuple-element.95), channel_id=1, source_target_pairs={{0,2},{2,0},{4,6},{6,4},{8,10},{10,8},{12,14},{14,12},{1,3},{3,1},... | collective-permute-start | bytes 589832 | tf_op jit(solution)/shard_map/ppermute | solution.py:405
  93.5 9.8 %collective-permute-start.27 = (f32[24,16,128]{2,1,0:T(8,128)S(1)}, f32[24,16,128]{2,1,0:T(8,128)S(1)}, u32[]{:S(2)}, u32[]{:S(2)}) collective-permute-start(f32[24,16,128]{2,1,0:T(8,128)S(1)} %get-tuple-element.96), channel_id=1, source_target_pairs={{2,4},{18,20},{3,5},{19,21},{4,2},{20,18},{5,3},{21,19},{6,8},{22,... | collective-permute-start | bytes 589832 | tf_op jit(solution)/shard_map/ppermute | solution.py:405
  93.5 5.6 %collective-permute-start.28 = (f32[1,2,16,8,128]{4,3,2,1,0:T(8,128)S(1)}, f32[1,2,16,8,128]{4,3,2,1,0:T(8,128)S(1)}, u32[]{:S(2)}, u32[]{:S(2)}) collective-permute-start(f32[1,2,16,8,128]{4,3,2,1,0:T(8,128)S(1)} %get-tuple-element.97), channel_id=1, source_target_pairs={{0,1},{1,0},{2,3},{3,2},{4,5},{5,4},{6,7},{7,6},{8,9},{9,8},{10,11... | collective-permute-start | bytes 393224 | tf_op jit(solution)/shard_map/ppermute | solution.py:408
  105.5 12.8 %collective-permute-start.33 = (f32[4,16,16,128]{3,2,1,0:T(8,128)S(1)}, f32[4,16,16,128]{3,2,1,0:T(8,128)S(1)}, u32[]{:S(2)}, u32[]{:S(2)}) collective-permute-start(f32[4,16,16,128]{3,2,1,0:T(8,128)S(1)} %get-tuple-element.104), channel_id=1, source_target_pairs={{0,16},{16,0},{1,17},{17,1},{2,18},{18,2},{3,19},{19,3},{4,20},{20... | collective-permute-start | bytes 1572872 | tf_op jit(solution)/shard_map/ppermute | solution.py:408
  105.6 12.8 %collective-permute-start.32 = (f32[2,2,16,8,128]{4,3,2,1,0:T(8,128)S(1)}, f32[2,2,16,8,128]{4,3,2,1,0:T(8,128)S(1)}, u32[]{:S(2)}, u32[]{:S(2)}) collective-permute-start(f32[2,2,16,8,128]{4,3,2,1,0:T(8,128)S(1)} %get-tuple-element.103), channel_id=1, source_target_pairs={{0,1},{1,0},{2,3},{3,2},{4,5},{5,4},{6,7},{7,6},{8,9},{9,8},{10,11... | collective-permute-start | bytes 786440 | tf_op jit(solution)/shard_map/ppermute | solution.py:408
  107.1 11.2 %collective-permute-start.30 = (f32[24,16,128]{2,1,0:T(8,128)S(1)}, f32[24,16,128]{2,1,0:T(8,128)S(1)}, u32[]{:S(2)}, u32[]{:S(2)}) collective-permute-start(f32[24,16,128]{2,1,0:T(8,128)S(1)} %get-tuple-element.101), channel_id=1, source_target_pairs={{0,2},{2,0},{4,6},{6,4},{8,10},{10,8},{12,14},{14,12},{1,3},{3,1},... | collective-permute-start | bytes 589832 | tf_op jit(solution)/shard_map/ppermute | solution.py:405
  108.8 9.5 %collective-permute-start.31 = (f32[24,16,128]{2,1,0:T(8,128)S(1)}, f32[24,16,128]{2,1,0:T(8,128)S(1)}, u32[]{:S(2)}, u32[]{:S(2)}) collective-permute-start(f32[24,16,128]{2,1,0:T(8,128)S(1)} %get-tuple-element.102), channel_id=1, source_target_pairs={{2,4},{18,20},{3,5},{19,21},{4,2},{20,18},{5,3},{21,19},{6,8},{22,... | collective-permute-start | bytes 589832 | tf_op jit(solution)/shard_map/ppermute | solution.py:405

commit v4 on v3

--- a/solution.py
+++ b/solution.py
@@ -8,6 +8,7 @@
 from jax.experimental.pallas import tpu as pltpu
 from jax.sharding import PartitionSpec as P
 
+STEPS = 2
 eddy_step = 0.1
 viscosity = 0.5
 wave_step = 0.2
@@ -31,7 +32,7 @@
         in_specs=[SMEM] * smem + [VMEM] * (len(ins) - smem),
         out_specs=[VMEM] * len(shapes),
         scratch_shapes=list(scratch),
-        compiler_params=pltpu.CompilerParams(vmem_limit_bytes=24 * 1024 * 1024),
+        compiler_params=pltpu.CompilerParams(vmem_limit_bytes=12 * 1024 * 1024),
         cost_estimate=pl.CostEstimate(flops=flops, bytes_accessed=4 * size, transcendentals=0),
     )(*ins)
 
@@ -50,10 +51,12 @@
     return np.concatenate([high, high, low])
 
 
-def z_product(f, zmsg, zmat, comps, G):
-    _, T, X, Y, _ = f.shape
+def z_product(F, zmsg, zmat, comps, G):
+    _, T, X, Y, _ = F.shape
+    X, Y = X - 6, Y - 16
     for n, c in enumerate(comps):
-        tiles = [f[c, t].reshape(X * Y, LANES) for t in range(T)] + [zmsg[n].reshape(X * Y, LANES)]
+        tiles = [F[c, t, 3 : 3 + X, 8 : 8 + Y, :].reshape(X * Y, LANES) for t in range(T)]
+        tiles.append(zmsg[n].reshape(X * Y, LANES))
         high = [tile.astype(jnp.bfloat16) for tile in tiles]
         low = [(tile - top.astype(jnp.float32)).astype(jnp.bfloat16) for tile, top in zip(tiles, high)]
         out = jnp.dot(jnp.concatenate(high + low + high, axis=1), zmat[...], preferred_element_type=jnp.float32)
@@ -87,52 +90,44 @@
     return lax.broadcasted_iota(jnp.int32, (rows, LANES), 1)
 
 
-def pack_state(o, inner, outer, ymsg, zmsg, ycomps, zcomps, info):
-    pos, row, half = info[0], info[1], info[2]
-    _, T, X, Y, _ = o.shape
-    si = jnp.where(pos == 0, X - 3, 0)
-    so = jnp.where(pos == 0, 0, X - 3)
-    for c in range(4):
-        for t in range(T):
-            for l in range(3):
-                inner[3 * (c * T + t) + l] = o[c, t, si + l]
-                outer[3 * (c * T + t) + l] = o[c, t, so + l]
+def ends(info, inner, X, deep):
+    high = (info[0] == 0) if inner else (info[0] == 1)
+    has = jnp.int32(1) if inner else info[3]
+    return high, has, lambda d: jnp.where(high, X - 1 - d, d), lambda d: jnp.where(high, 2 - d, d)
+
+
+def pack_sides(info, get, ymsg, zmsg, ycomps, zcomps, X, Y, T, layers):
+    row, half = info[1], info[2]
     rows = lax.broadcasted_iota(jnp.int32, (8, LANES), 0)
     ys = pl.multiple_of(jnp.where(row == 0, Y - 8, 0), 8)
-
-    def normal(c, t, i):
-        tile = o[c, t, i, pl.ds(ys, 8), :]
-        return jnp.where(row == 0, pltpu.roll(tile, 4, 0), tile)
-
+    turn = jnp.where(row == 0, 4, 0)
     edge = jnp.where(half == 0, T - 1, 0)
 
+    def one(i):
+        for n in range(len(ycomps) // 2):
+            for t in range(T):
+                first = pltpu.roll(get(ycomps[2 * n], t, i, pl.ds(ys, 8)), turn, 0)
+                second = pltpu.roll(get(ycomps[2 * n + 1], t, i, pl.ds(ys, 8)), 4 - turn, 0)
+                ymsg[n, t, i] = jnp.where(rows < 4, first, second)
+        for n, c in enumerate(zcomps):
+            zmsg[n, i] = get(c, edge, i, slice(None))
+
+    if layers is None:
+        lax.fori_loop(0, X, lambda i, carry: (one(i), carry)[1], 0, unroll=4)
+    else:
+        for i in layers:
+            one(i)
+
+
+def fill(F, f, nears, fars, ymsg, ycomps, info, halos=None):
+    row = info[1]
+    _, T, X, Y, _ = f.shape
+    y = slice(8, 8 + Y)
+
     def step(i, carry):
-        for n in range(len(ycomps) // 2):
-            for t in range(T):
-                first, second = normal(ycomps[2 * n], t, i), normal(ycomps[2 * n + 1], t, i)
-                ymsg[n, t, i] = jnp.where(rows < 4, first, pltpu.roll(second, 4, 0))
-        for n, c in enumerate(zcomps):
-            zmsg[n, i] = o[c, edge, i]
-        return carry
-
-    lax.fori_loop(0, X, step, 0, unroll=4)
-
-
-def fill(F, f, inner, outer, ymsg, ycomps, info):
-    pos, row, has = info[0], info[1], info[3]
-    _, T, X, Y, _ = f.shape
-    hi = jnp.where(pos == 0, X + 3, 0)
-    ho = jnp.where(pos == 0, 0, X + 3)
-    for c in range(4):
-        for t in range(T):
-            for l in range(3):
-                F[c, t, hi + l, 8 : 8 + Y, :] = inner[3 * (c * T + t) + l]
-                F[c, t, ho + l, 8 : 8 + Y, :] = known(outer[3 * (c * T + t) + l], has)
-
-    def step(i, carry):
         for t in range(T):
             for c in range(4):
-                F[c, t, i + 3, 8 : 8 + Y, :] = f[c, t, i]
+                F[c, t, i + 3, y, :] = f[c, t, i]
             for n, c in enumerate(ycomps):
                 tile = ymsg[n // 2, t, i]
                 turned = pltpu.roll(tile, 4, 0)
@@ -144,6 +139,22 @@
         return carry
 
     lax.fori_loop(0, X, step, 0, unroll=4)
+    zero = jnp.zeros((Y, LANES), jnp.float32)
+    for side, near in enumerate(nears):
+        high, has, layer, place = ends(info, side == 0, X, 3)
+        for c in range(4):
+            for t in range(T):
+                for d in range(3):
+                    F[c, t, 3 + layer(d), y, :] = near[3 * (c * T + t) + place(d)]
+                    beyond = zero
+                    if halos is not None:
+                        beyond = known(halos[side][3 * (c * T + t) + place(2 - d)], has)
+                    F[c, t, jnp.where(high, X + 3 + d, 2 - d), y, :] = beyond
+                if fars:
+                    far = fars[side]
+                    count = far.shape[0] // (4 * T)
+                    for d in range(count):
+                        F[c, t, 3 + layer(3 + d), y, :] = far[count * (c * T + t) + d]
 
 
 def dx(F, c, t, i, Y):
@@ -173,43 +184,35 @@
     lax.fori_loop(0, X, step, 0, unroll=4)
 
 
-def first_body(info, f, inner, outer, ymsg, zmsg, zmat, mach, own, t_in, t_out, o, S, n_in, n_out, ny, nz, F, G, *, layers):
+def first_main(info, f, near_in, near_out, ymsg, zmsg, zmat, mach, S, o, base, F, G):
+    Y = f.shape[3]
+    fill(F, f, (near_in, near_out), (), ymsg, RATE_Y, info)
+    z_product(F, zmsg, zmat, RATE_Z, G)
+
+    def emit(c, t, i, value):
+        center = F[c, t, i + 3, 8 : 8 + Y, :]
+        base[c, t, i] = center
+        o[c, t, i] = center + wave_step * value
+
+    rate_loop(F, G, mach, S, emit)
+
+
+def second_main(info, f, near_in, near_out, far_in, far_out, ymsg, zmsg, zmat, mach, S, base, o, F, G):
+    Y = f.shape[3]
+    fill(F, f, (near_in, near_out), (far_in, far_out), ymsg, RATE_Y, info)
+    z_product(F, zmsg, zmat, RATE_Z, G)
+
+    def emit(c, t, i, value):
+        o[c, t, i] = 0.5 * (base[c, t, i] + F[c, t, i + 3, 8 : 8 + Y, :]) + (0.5 * wave_step) * value
+
+    rate_loop(F, G, mach, S, emit)
+
+
+def smooth_main(info, f, near_in, near_out, far_in, far_out, ymsg, zmsg, zmat, *rest, last):
+    *halos, o, F, G = rest
     _, T, X, Y, _ = f.shape
-    z_product(f, zmsg, zmat, RATE_Z, G)
-    fill(F, f, inner, outer, ymsg, RATE_Y, info)
-    at_in = jnp.where(info[0] == 0, X - layers, 0)
-    at_out = jnp.where(info[0] == 0, 0, X - layers)
-    S[...] = own[...]
-    for c in range(3):
-        for t in range(T):
-            for l in range(layers):
-                n = (c * T + t) * layers + l
-                S[c, t, at_in + l] = S[c, t, at_in + l] + t_in[n]
-                S[c, t, at_out + l] = S[c, t, at_out + l] + known(t_out[n], info[3])
-
-    def emit(c, t, i, value):
-        o[c, t, i] = f[c, t, i] + wave_step * value
-
-    rate_loop(F, G, mach, S, emit)
-    pack_state(o, n_in, n_out, ny, nz, RATE_Y, RATE_Z, info)
-
-
-def second_body(info, f, inner, outer, ymsg, zmsg, zmat, mach, S, state, o, n_in, n_out, ny, nz, F, G):
-    z_product(f, zmsg, zmat, RATE_Z, G)
-    fill(F, f, inner, outer, ymsg, RATE_Y, info)
-
-    def emit(c, t, i, value):
-        o[c, t, i] = 0.5 * (state[c, t, i] + f[c, t, i]) + (0.5 * wave_step) * value
-
-    rate_loop(F, G, mach, S, emit)
-    pack_state(o, n_in, n_out, ny, nz, ALL, ALL, info)
-
-
-def smooth_body(info, f, inner, outer, ymsg, zmsg, zmat, o, *rest):
-    F, G = rest[-2:]
-    _, T, X, Y, _ = f.shape
-    z_product(f, zmsg, zmat, ALL, G)
-    fill(F, f, inner, outer, ymsg, ALL, info)
+    fill(F, f, (near_in, near_out), (far_in, far_out), ymsg, ALL, info, halos if last else None)
+    z_product(F, zmsg, zmat, ALL, G)
     y = slice(8, 8 + Y)
 
     def step(i, carry):
@@ -221,19 +224,66 @@
                         F[c, t, i + 3, 8 + j : 8 + Y + j, :] + F[c, t, i + 3, 8 - j : 8 + Y - j, :]
                     )
                     total = total - (filter_weight * taps[j]) * beside
-                if len(rest) > 2:
+                if last:
+                    o[c, i, :, t * LANES : (t + 1) * LANES] = total
+                else:
                     o[c, t, i] = total
-                else:
-                    o[c, i, :, t * LANES : (t + 1) * LANES] = total
         return carry
 
     lax.fori_loop(0, X, step, 0, unroll=4)
-    if len(rest) > 2:
-        pack_state(o, *rest[:4], RATE_Y, RATE_Z, info)
-
-
-def pack_body(info, f, o, inner, outer, ymsg, zmsg):
-    _, T, X, _, _ = o.shape
+
+
+def edge_body(info, f, halo_in, halo_out, *rest, smooth, scale, ycomps, zcomps):
+    rest = list(rest)
+    mach, *terms = (None, None, None) if smooth else [rest.pop(0) for _ in range(3)]
+    *done, ymsg, zmsg = rest
+    sides = [done[:1], done[1:]] if smooth else [done[:2], done[2:]]
+    _, T, X, Y, _ = f.shape
+    deep = 3 if smooth else 3 + sides[0][1].shape[0] // (4 * T)
+    for side, halo in enumerate((halo_in, halo_out)):
+        near = sides[side][0]
+        high, has, layer, place = ends(info, side == 0, X, deep)
+        sign = (jnp.where(high, scale, -scale) * has).astype(jnp.float32)
+        weight = has.astype(jnp.float32)
+        for t in range(T):
+            for d in range(deep):
+                at = layer(d)
+                values = [f[c, t, at] for c in range(4)]
+                if d < 3:
+                    beyond = [[halo[3 * (c * T + t) + place(2 - e)] for e in range(3 - d)] for c in range(4)]
+                    coefs = taps[1:] if smooth else deriv
+                    parts = [sum(coefs[d + e] * value for e, value in enumerate(column)) for column in beyond]
+                    if smooth:
+                        values = [value - (filter_weight * weight) * part for value, part in zip(values, parts)]
+                    else:
+                        m, (gp, gu, gv, gw) = mach[at], parts
+                        change = (m * gp + gu, m * gu + gp, m * gv, m * gw)
+                        values = [value - sign * part for value, part in zip(values, change)]
+                if not smooth:
+                    index = jnp.where(high, deep - 1 - d, d)
+                    for c in range(3):
+                        term = terms[side][(c * T + t) * deep + index]
+                        values[1 + c] = values[1 + c] - (scale * weight) * term
+                for c in range(4):
+                    if d < 3:
+                        near[3 * (c * T + t) + place(d)] = values[c]
+                    else:
+                        sides[side][1][(deep - 3) * (c * T + t) + d - 3] = values[c]
+    pack_sides(info, lambda c, t, i, rows: f[c, t, i, rows, :], ymsg, zmsg, ycomps, zcomps, X, Y, T, None)
+    for side, (near, *far) in enumerate(sides):
+        _, _, layer, place = ends(info, side == 0, X, deep)
+        for d in range(deep):
+
+            def get(c, t, i, rows):
+                if d < 3:
+                    return near[3 * (c * T + t) + place(d), rows, :]
+                return far[0][(deep - 3) * (c * T + t) + d - 3, rows, :]
+
+            pack_sides(info, get, ymsg, zmsg, ycomps, zcomps, X, Y, T, [layer(d)])
+
+
+def pack_whole(info, f, o, near_in, near_out, start, ymsg, zmsg):
+    _, T, X, Y, _ = o.shape
 
     def step(i, carry):
         for c in range(4):
@@ -242,16 +292,23 @@
         return carry
 
     lax.fori_loop(0, X, step, 0, unroll=4)
-    pack_state(o, inner, outer, ymsg, zmsg, RATE_Y, RATE_Z, info)
-
-
-def pack_les(get, shape, inner, outer, ymsg, zmsg, base, info):
+    for side, near in enumerate((near_in, near_out)):
+        _, _, layer, place = ends(info, side == 0, X, 3)
+        for c in range(4):
+            for t in range(T):
+                for d in range(3):
+                    near[start + 3 * (c * T + t) + place(d)] = o[c, t, layer(d)]
+    pack_sides(info, lambda c, t, i, rows: o[c, t, i, rows, :], ymsg, zmsg, RATE_Y, RATE_Z, X, Y, T, None)
+
+
+def pack_les(get, shape, inner, outer, ymsg, zmsg, info, base=0):
     pos, row, half = info[0], info[1], info[2]
     _, T, X, Y, _ = shape
     si = jnp.where(pos == 0, X - 1, 0)
     so = jnp.where(pos == 0, 0, X - 1)
     rows = lax.broadcasted_iota(jnp.int32, (8, LANES), 0)
     ys = pl.multiple_of(jnp.where(row == 0, Y - 8, 0), 8)
+    turn = [jnp.where(row == 0, (r + 1) % 8, r) for r in range(8)]
     for c in range(3):
         for t in range(T):
             inner[base + c * T + t] = get(c, t, si, slice(None))
@@ -260,8 +317,7 @@
                 acc = jnp.zeros((8, LANES), jnp.float32)
                 for r in range(8):
                     tile = get(c, t, 8 * n + r, pl.ds(ys, 8))
-                    moved = jnp.where(row == 0, pltpu.roll(tile, (r + 1) % 8, 0), pltpu.roll(tile, r, 0))
-                    acc = jnp.where(rows == r, moved, acc)
+                    acc = jnp.where(rows == r, pltpu.roll(tile, turn[r], 0), acc)
                 ymsg[c, t, n] = acc
 
     def step(i, carry):
@@ -281,12 +337,12 @@
 
 def pack_les_body(info, v, inner, outer, ymsg, zmsg):
     X, _, Y, Z = v.shape
-    pack_les(getter(v), (3, Z // LANES, X, Y, LANES), inner, outer, ymsg, zmsg, 0, info)
+    pack_les(getter(v), (3, Z // LANES, X, Y, LANES), inner, outer, ymsg, zmsg, info)
 
 
 def les_body(info, offset, v, inner, outer, ymsg, zmsg, tiles, *rest, base, advance):
     if advance:
-        v1, own, n_in, n_out, ny, nz, V, LB, ACC = rest
+        state, v1, own, n_in, n_out, ny, nz, f, fy, fz, V, LB, ACC = rest
     else:
         own, n_in, n_out, V, LB, ACC = rest
     pos, row, half = info[0], info[1], info[2]
@@ -356,7 +412,11 @@
     lax.fori_loop(0, X, step, 0, unroll=4)
 
     for m in range(blocks // 2):
-        out = jnp.dot(tiles[m].astype(jnp.bfloat16), LB[m], preferred_element_type=jnp.float32)
+        a, b = tiles[2 * m], tiles[2 * m + 1]
+        none = jnp.zeros((plane, 2 * plane), jnp.bfloat16)
+        rows = [(a[:plane], b[:plane]), (a[plane:], none), (none, b[plane:])]
+        weights = jnp.concatenate([jnp.concatenate(pair, axis=1) for pair in rows], axis=0)
+        out = jnp.dot(weights, LB[m], preferred_element_type=jnp.float32)
         at = (m + 1) * wide
         places = [(at, 0), (at + offset[2 * m] * wide, plane), (at + offset[2 * m + 1] * wide, 2 * plane)]
         for c in range(3):
@@ -376,7 +436,8 @@
                 n_in[(c * T + t) * wide + l] = ACC[c, t, ti + l]
                 n_out[(c * T + t) * wide + l] = ACC[c, t, to + l]
     if advance:
-        pack_les(getter(v1), v1.shape, n_in, n_out, ny, nz, 3 * T * wide, info)
+        pack_les(getter(v1), v1.shape, n_in, n_out, ny, nz, info, 3 * T * wide)
+        pack_whole(info, state, f, n_in, n_out, 3 * T * (wide + 1), fy, fz)
 
 
 def solution(mesh):
@@ -401,11 +462,14 @@
         for a, b in ends
     ]
 
-    def send_x(inner, outer):
-        return lax.ppermute(inner, "gx", even), lax.ppermute(outer, mesh.axis_names, hops)
-
-    def send(inner, outer, ymsg, zmsg):
-        return *send_x(inner, outer), lax.ppermute(ymsg, "gy", swap), lax.ppermute(zmsg, "grp", swap)
+    def send_in(message):
+        return lax.ppermute(message, "gx", even)
+
+    def send_out(message):
+        return lax.ppermute(message, mesh.axis_names, hops)
+
+    def send_sides(ymsg, zmsg):
+        return lax.ppermute(ymsg, "gy", swap), lax.ppermute(zmsg, "grp", swap)
 
     def body(les_velocity, mean_mach, transfer_tiles, intersection_offset, acoustic_state):
         X2, Y, _, Z = les_velocity.shape
@@ -421,25 +485,15 @@
         state = acoustic_state.transpose(2, 0, 1, 3)
         rate_z = jnp.where(half == 0, *(banded(Z, deriv, -1, h) for h in (0, 1)))
         smooth_z = jnp.where(half == 0, *(banded(Z, [-filter_weight * w for w in taps[1:]], 1, h) for h in (0, 1)))
-        pair = transfer_tiles[:, 0].swapaxes(2, 3).reshape(blocks // 2, 2, 2, plane, plane)
-        none = jnp.zeros((blocks // 2, plane, 2 * plane), pair.dtype)
-        twice = [[jnp.concatenate([pair[:, n, k]] * 2, axis=2) for k in (0, 1)] for n in (0, 1)]
-        tiles = jnp.concatenate(
-            [
-                jnp.concatenate([twice[0][0], twice[1][0]], axis=2),
-                jnp.concatenate([twice[0][1], none], axis=2),
-                jnp.concatenate([none, twice[1][1]], axis=2),
-            ],
-            axis=1,
-        )
         mach = jnp.broadcast_to(mean_mach[:, :, None], (X, Y, LANES))
 
         grid = (4, T, X, Y, LANES)
         source = (3, T, X, Y, LANES)
-        edge_x, term = (12 * T, Y, LANES), (3 * T * wide, Y, LANES)
+        near, far = (12 * T, Y, LANES), (4 * T * (wide - 3), Y, LANES)
+        term = (3 * T * wide, Y, LANES)
         edge_y, edge_yy = (1, T, X, 8, LANES), (2, T, X, 8, LANES)
         edge_z, edge_zz = (2, X, Y, LANES), (4, X, Y, LANES)
-        les_y, les_z = (3, T, X2 // 8, 8, LANES), (3, X2, Y, LANES)
+        les_x, les_y, les_z = (3 * T, Y, LANES), (3, T, X2 // 8, 8, LANES), (3, X2, Y, LANES)
         F = pltpu.VMEM((4, T, X + 6, Y + 16, LANES), jnp.float32)
         G2 = pltpu.VMEM((2, T, X, Y, LANES), jnp.float32)
         G4 = pltpu.VMEM((4, T, X, Y, LANES), jnp.float32)
@@ -448,56 +502,78 @@
             pltpu.VMEM((blocks // 2, 4 * plane, 3 * Z), jnp.bfloat16),
             pltpu.VMEM((3, T, X + 2 * wide, Y, LANES), jnp.float32),
         ]
-        les_edges = send(*call(pack_les_body, [(3 * T, Y, LANES), (3 * T, Y, LANES), les_y, les_z], [info, v]))
-        state, *state_edges = call(pack_body, [grid, edge_x, edge_x, edge_y, edge_z], [info, state])
-        info, *state_edges = lax.optimization_barrier((info, *state_edges))
-        state_edges = send(*state_edges)
-        with_terms = (term[0] + 3 * T, Y, LANES)
-        v1, own, *edges = call(
+        def complete(part, halos, shared, scale, next_y, next_z):
+            smooth = not shared
+            shapes = [near, near] if smooth else [near, far, near, far]
+            sides = [edge_y, edge_z] if next_y == RATE_Y else [edge_yy, edge_zz]
+            *done, ymsg, zmsg = call(
+                functools.partial(edge_body, smooth=smooth, scale=scale, ycomps=next_y, zcomps=next_z),
+                [*shapes, *sides],
+                [info, part, *halos, *([shared[0], *shared[1]] if shared else [])],
+            )
+            nears, fars = (done, []) if smooth else (done[::2], done[1::2])
+            return [part, *nears], fars, send_sides(ymsg, zmsg), (send_in(nears[0]), send_out(nears[1]))
+
+        v_in, v_out, *sides = call(pack_les_body, [les_x, les_x, les_y, les_z], [info, v])
+        les_edges = [send_in(v_in), send_out(v_out), *send_sides(*sides)]
+        les_edges[3], tiles = lax.optimization_barrier((les_edges[3], transfer_tiles))
+        tiles = tiles[:, 0].swapaxes(2, 3).reshape(blocks, 2 * plane, plane)
+        tiles = jnp.concatenate([tiles, tiles], axis=2)
+        at = term[0] + 3 * T
+        joint = (at + near[0], Y, LANES)
+        v1, S, *own, les_ym, les_zm, state, ym, zm = call(
             functools.partial(les_body, base=0, advance=True),
-            [(3, T, X2, Y, LANES), source, with_terms, with_terms, les_y, les_z],
-            [info, intersection_offset, v, *les_edges, tiles],
+            [(3, T, X2, Y, LANES), source, joint, joint, les_y, les_z, grid, edge_y, edge_z],
+            [info, intersection_offset, v, *les_edges, tiles, state],
             les_scratch,
             smem=2,
             flops=4000000,
         )
-        edges = send(*edges)
-        first = functools.partial(first_body, layers=wide)
-        outs = [grid, source, edge_x, edge_x, edge_y, edge_z]
-        middle, S, *middle_edges = call(
-            first, outs, [info, state, *state_edges, rate_z, mach, own, edges[0], edges[1]], [F, G2], flops=4000000
-        )
-        middle_edges = send(*middle_edges)
-        own2, *terms = call(
-            functools.partial(les_body, base=term[0], advance=False),
-            [source, term, term],
-            [info, intersection_offset, v1, *edges, tiles],
-            les_scratch,
-            smem=2,
+        terms = (send_in(own[0]), send_out(own[1]))
+        sides = send_sides(ym, zm)
+        les_edges = [*terms, *send_sides(les_ym, les_zm)]
+        near_in, near_out = (message[at:] for message in own)
+        halos = [message[at:] for message in terms]
+        whole = [state, near_in, near_out]
+        for step in range(STEPS):
+            if step:
+                whole[1], terms = lax.optimization_barrier((whole[1], terms))
+            part, base = call(
+                first_main, [grid, grid], [info, *whole, *sides, rate_z, mach, S], [F, G2], flops=4000000
+            )
+            whole, fars, sides, halos = complete(part, halos, (mach, terms), wave_step, RATE_Y, RATE_Z)
+            if step + 1 < STEPS:
+                S2, *terms2 = call(
+                    functools.partial(les_body, base=term[0], advance=False),
+                    [source, term, term],
+                    [info, intersection_offset, v1, *les_edges, tiles],
+                    les_scratch,
+                    smem=2,
+                    flops=4000000,
+                )
+                info, S2, *terms2 = lax.optimization_barrier((info, S2, *terms2))
+                terms2 = (send_in(terms2[0]), send_out(terms2[1]))
+            (part,) = call(
+                second_main, [grid], [info, *whole, *fars, *sides, rate_z, mach, S, base], [F, G2], flops=4000000
+            )
+            whole, fars, sides, halos = complete(part, halos, (mach, terms), 0.5 * wave_step, ALL, ALL)
+            if step + 1 < STEPS:
+                terms, S = terms2, S2
+                (part,) = call(
+                    functools.partial(smooth_main, last=False),
+                    [grid],
+                    [info, *whole, *fars, *sides, smooth_z],
+                    [F, G4],
+                    flops=4000000,
+                )
+                whole, _, sides, halos = complete(part, halos, None, 0.0, RATE_Y, RATE_Z)
+        (state,) = call(
+            functools.partial(smooth_main, last=True),
+            [(4, X, Y, Z)],
+            [info, *whole, *fars, *sides, smooth_z, *halos],
+            [F, G4],
             flops=4000000,
         )
-        outs = [grid, edge_x, edge_x, edge_yy, edge_zz]
-        updated, *up_edges = call(
-            second_body, outs, [info, middle, *middle_edges, rate_z, mach, S, state], [F, G2], flops=4000000
-        )
-        up_edges = send(*up_edges)
-        terms = send_x(*terms)
-        outs = [grid, edge_x, edge_x, edge_y, edge_z]
-        state, *state_edges = call(
-            smooth_body, outs, [info, updated, *up_edges, smooth_z], [F, G4], flops=4000000
-        )
-        state_edges = send(*state_edges)
-        outs = [grid, source, edge_x, edge_x, edge_y, edge_z]
-        middle, S, *middle_edges = call(
-            first, outs, [info, state, *state_edges, rate_z, mach, own2, *terms], [F, G2], flops=4000000
-        )
-        middle_edges = send(*middle_edges)
-        outs = [grid, edge_x, edge_x, edge_yy, edge_zz]
-        updated, *up_edges = call(
-            second_body, outs, [info, middle, *middle_edges, rate_z, mach, S, state], [F, G2], flops=4000000
-        )
-        up_edges = send(*up_edges)
-        (state,) = call(smooth_body, [(4, X, Y, Z)], [info, updated, *up_edges, smooth_z], [F, G4], flops=4000000)
         return state.transpose(1, 2, 0, 3)
 
     placed = (

time: 123 us -> 113 us (0.919)
  starting transfers between devices: 30.4 us -> 25.8 us
  waiting for transfers between devices: 56.2 us -> 52.2 us
  local copies, waits for them, and re-layouts: 10.2 us -> 6.61 us
  Pallas kernels: 23.9 us -> 25.2 us
    unnamed x31 -> x17, local copies, waits for them, and re-layouts: 7.74 us -> 3 us
    ppermute x34 -> x32, starting transfers between devices: 30.4 us -> 25.8 us  [the longest x8 15.6 us: send_in(): return lax.ppermute(message, 'gx', even)]
    ppermute x34 -> x32, waiting for transfers between devices: 56.2 us -> 52.2 us  [the longest x8 32.3 us: send_in(): return lax.ppermute(message, 'gx', even)]
    transpose x0 -> x1, local copies, waits for them, and re-layouts: none -> 1.79 us  [body(): tiles = tiles[:, 0].swapaxes(2, 3).reshape(blocks, 2 * plane, plane)]
    pallas_call x10 -> x14, Pallas kernels: 23.9 us -> 25.2 us  [call(): pl.pallas_call(body, out_shape=shapes, in_specs=[SMEM] * smem + [VMEM] *...]
  transfers between devices with their start and end apart: 34 -> 32, of which waited for: 11 -> 11; matrix products, arithmetic and copies ran while one was open for 6% -> 4% of each run, Pallas kernels for 13% -> 13%
where the time goes in v4:
time: 113 us; the launch traced here: 112 us
  waiting for transfers between devices  52.2 us (46%)
  starting transfers between devices  25.8 us (23%)
  Pallas kernels  25.2 us (22%)
  local copies, waits for them, and re-layouts  6.61 us (6%)
  other arithmetic  1.38 us (1%)
    ppermute x8, waiting for transfers between devices, send_in(): return lax.ppermute(message, 'gx', even)  32.3 us
    pallas_call x14, Pallas kernels, call(): pl.pallas_call(body, out_shape=shapes, in_specs=[SMEM] * smem + [VMEM] *...  25.2 us
    ppermute x8, starting transfers between devices, send_in(): return lax.ppermute(message, 'gx', even)  15.6 us
    ppermute x16, waiting for transfers between devices, send_sides(): return (lax.ppermute(ymsg, 'gy', swap), lax.ppermute(zmsg, 'grp', swap))  15.4 us
    ppermute x16, starting transfers between devices, send_sides(): return (lax.ppermute(ymsg, 'gy', swap), lax.ppermute(zmsg, 'grp', swap))  8.46 us
    ppermute x8, waiting for transfers between devices, send_out(): return lax.ppermute(message, mesh.axis_names, hops)  4.53 us
    unnamed x17, local copies, waits for them, and re-layouts  3 us
  transfers between devices with their start and end apart: 32, of which 11 were waited for; matrix products, arithmetic and copies ran while one was open for 4% of the time, Pallas kernels for 13%

profile of v4, /device:TPU:8, one launch (start us, length us, event | category | flops | bytes accessed | tf_op | source)
XLA Modules:
  0.0 111.6 jit_solution(15213109363670097604)
XLA Ops:
  0.1 1.4 %copy-done = f32[32,16,3,256]{3,1,2,0:T(8,128)S(1)} copy-done((f32[32,16,3,256]{3,1,2,0:T(8,128)S(1)}, f32[32,16,3,256]{3,1,2,0:T(8,128)}, u32[]{:S(2)}) %copy-start) | copy-done | bytes 1572888
  1.5 1.7 %shard_map.91 = (f32[6,16,128]{2,1,0:T(8,128)}, f32[6,16,128]{2,1,0:T(8,128)}, f32[3,2,4,8,128]{4,3,2,1,0:T(8,128)}, f32[3,32,16,128]{3,2,1,0:T(8,128)}) custom-call(s32[4]{0:T(128)S(1)} %pad_add_fusion.info, f32[32,3,16,256]{3,2,1,0:T(8,128)S(1)} %bitcast.13), custom_call_target="tpu_custom_call" | custom-call | flops 1000000 | bytes 2555920 | tf_op jit(solution)/shard_map/pallas_call | solution.py:29
  3.2 1.5 %collective-permute-start = (f32[6,16,128]{2,1,0:T(8,128)}, f32[6,16,128]{2,1,0:T(8,128)}, u32[]{:S(2)}, u32[]{:S(2)}) collective-permute-start(f32[6,16,128]{2,1,0:T(8,128)} %get-tuple-element.62), channel_id=1, source_target_pairs={{0,2},{2,0},{4,6},{6,4},{8,10},{10,8},{12,14},{14,12},{1,3},{3,1},... | collective-permute-start | bytes 147464 | tf_op jit(solution)/shard_map/ppermute | solution.py:466
  4.7 1.9 %collective-permute-start.2 = (f32[3,2,4,8,128]{4,3,2,1,0:T(8,128)}, f32[3,2,4,8,128]{4,3,2,1,0:T(8,128)S(1)}, u32[]{:S(2)}, u32[]{:S(2)}) collective-permute-start(f32[3,2,4,8,128]{4,3,2,1,0:T(8,128)} %get-tuple-element.64), channel_id=1, source_target_pairs={{0,1},{1,0},{2,3},{3,2},{4,5},{5,4},{6,7},{7,6},{8,9},{9,8},{10,11... | collective-permute-start | bytes 294920 | tf_op jit(solution)/shard_map/ppermute | solution.py:472
  6.6 1.5 %copy.14 = f32[16,16,4,256]{3,1,0,2:T(8,128)S(1)} copy(f32[16,16,4,256]{3,2,1,0:T(4,128)} %param.13) | data formatting | bytes 2097152 | tf_op args[4]
  8.2 1.8 %copy.10 = bf16[8,2,64,64]{3,2,1,0:T(8,128)(2,1)} copy(bf16[8,2,64,64]{2,3,1,0:T(8,128)(2,1)} %bitcast.18) | data formatting | bytes 262144 | tf_op jit(solution)/shard_map/transpose | solution.py:520
  9.9 1.2 %pad_maximum_fusion.tiles = bf16[8,128,128]{2,1,0:T(8,128)(2,1)S(1)} fusion(bf16[8,128,64]{2,1,0:T(8,128)(2,1)} %bitcast.17), kind=kLoop, calls=%fused_computation.3 | loop fusion | flops 524288 | bytes 393216 | tf_op jit(solution)/shard_map/concatenate | solution.py:521
  11.2 4.1 %shard_map.92 = (f32[3,2,32,16,128]{4,3,2,1,0:T(8,128)S(1)}, f32[3,2,16,16,128]{4,3,2,1,0:T(8,128)S(1)}, f32[54,16,128]{2,1,0:T(8,128)S(1)}, f32[54,16,128]{2,1,...) custom-call(s32[4]{0:T(128)S(1)} %pad_add_fusion.info, ...), custom_call_target="tpu_custom_call" | custom-call | flops 4000000 | bytes 9699376 | tf_op jit(solution)/shard_map/pallas_call | solution.py:29
  15.3 2.7 %collective-permute-start.4 = (f32[54,16,128]{2,1,0:T(8,128)S(1)}, f32[54,16,128]{2,1,0:T(8,128)S(1)}, u32[]{:S(2)}, u32[]{:S(2)}) collective-permute-start(f32[54,16,128]{2,1,0:T(8,128)S(1)} %get-tuple-element.69), channel_id=1, source_target_pairs={{0,2},{2,0},{4,6},{6,4},{8,10},{10,8},{12,14},{14,12},{1,3},{3,1},... | collective-permute-start | bytes 1327112 | tf_op jit(solution)/shard_map/ppermute | solution.py:466
  18.0 0.5 collective-permute-start.8
  18.5 0.2 collective-permute-start.9
  18.8 5.1 %collective-permute-done.8.ymsg = f32[1,2,16,8,128]{4,3,2,1,0:T(8,128)S(1)} collective-permute-done((f32[1,2,16,8,128]{4,3,2,1,0:T(8,128)S(1)}, f32[1,2,16,8,128]{4,3,2,1,0:T(8,128)S(1)}, u32[]{:S(2)}, u32[]{:S(2)}) %collective-permute-start.8) | collective-permute-done | bytes 131104 | tf_op jit(solution)/shard_map/ppermute | solution.py:472
  24.0 2.0 %shard_map.94 = (f32[4,2,16,16,128]{4,3,2,1,0:T(8,128)S(1)}, f32[4,2,16,16,128]{4,3,2,1,0:T(8,128)S(1)}) custom-call(s32[4]{0:T(128)S(1)} %pad_add_fusion.info, f32[4,2,16,16,128]{4,3,2,1,0:T(8,128)S(1)} %get-tuple-element.77.f, f32[24,16,128]{2,1,0:T(8,128)S(1)} %slice.12.near_in, f32[24,16,128]{2,1,0:T(8,128)S(1)} %slice.13.near_out, ...), custom_call_target="tpu_custom_call" | custom-call | flops 4000000 | bytes 6029328 | tf_op jit(solution)/shard_map/pallas_call | solution.py:29
  26.0 11.5 %collective-permute-done.4.inner.rest_1_ = f32[54,16,128]{2,1,0:T(8,128)S(1)} collective-permute-done((f32[54,16,128]{2,1,0:T(8,128)S(1)}, f32[54,16,128]{2,1,0:T(8,128)S(1)}, u32[]{:S(2)}, u32[]{:S(2)}) %collective-permute-start.4) | collective-permute-done | bytes 442400 | tf_op jit(solution)/shard_map/ppermute | solution.py:466
  37.5 0.8 shard_map.95
  38.3 0.6 collective-permute-start.6
  38.9 1.7 %collective-permute-start.12 = (f32[24,16,128]{2,1,0:T(8,128)S(1)}, f32[24,16,128]{2,1,0:T(8,128)S(1)}, u32[]{:S(2)}, u32[]{:S(2)}) collective-permute-start(f32[24,16,128]{2,1,0:T(8,128)S(1)} %get-tuple-element.82.near_in), channel_id=1, source_target_pairs={{0,2},{2,0},{4,6},{6,4},{8,10},{10,8},{12,14},{14,12},{1,3},{3,1},... | collective-permute-start | bytes 589832 | tf_op jit(solution)/shard_map/ppermute | solution.py:466
  40.6 2.9 %collective-permute-done.6.ymsg = f32[3,2,4,8,128]{4,3,2,1,0:T(8,128)S(1)} collective-permute-done((f32[3,2,4,8,128]{4,3,2,1,0:T(8,128)S(1)}, f32[3,2,4,8,128]{4,3,2,1,0:T(8,128)S(1)}, u32[]{:S(2)}, u32[]{:S(2)}) %collective-permute-start.6) | collective-permute-done | bytes 98336 | tf_op jit(solution)/shard_map/ppermute | solution.py:472
  43.5 0.5 collective-permute-start.10
  44.1 2.8 %shard_map.93 = (f32[3,2,16,16,128]{4,3,2,1,0:T(8,128)S(1)}, f32[24,16,128]{2,1,0:T(8,128)S(1)}, f32[24,16,128]{2,1,0:T(8,128)S(1)}) custom-call(s32[4]{0:T(128)S(1)} %pad_add_fusion.info, s32[8]{0:T(128)S(1)} %copy-done.2, f32[3,2,32,16,128]{4,3,2,1,0:T(8,128)S(1)} %get-tuple-element.68.v, f32[54,16,128]{2,1,0:T(8,128)S(1)} %collective-permute-done.4.inner.rest_1_, ...), custom_call_target="tpu_custom_call" | custom-call | flops 4000000 | bytes 5046320 | tf_op jit(solution)/shard_map/pallas_call | solution.py:29
  46.9 1.7 %collective-permute-done.10.ymsg = f32[1,2,16,8,128]{4,3,2,1,0:T(8,128)S(1)} collective-permute-done((f32[1,2,16,8,128]{4,3,2,1,0:T(8,128)S(1)}, f32[1,2,16,8,128]{4,3,2,1,0:T(8,128)S(1)}, u32[]{:S(2)}, u32[]{:S(2)}) %collective-permute-start.10) | collective-permute-done | bytes 131104 | tf_op jit(solution)/shard_map/ppermute | solution.py:472
  48.6 2.0 %shard_map.96.f = f32[4,2,16,16,128]{4,3,2,1,0:T(8,128)S(1)} custom-call(s32[4]{0:T(128)S(1)} %pad_add_fusion.info, f32[4,2,16,16,128]{4,3,2,1,0:T(8,128)S(1)} %get-tuple-element.81.f, f32[24,16,128]{2,1,0:T(8,128)S(1)} %get-tuple-element.82.near_in, f32[24,16,128]{2,1,0:T(8,128)S(1)} %get-tuple-element.83.near_out, ...), custom_call_target="tpu_custom_call" | custom-call | flops 4000000 | bytes 6160400 | tf_op jit(solution)/shard_map/pallas_call | solution.py:29
  50.7 0.8 shard_map.97
  51.5 1.0 collective-permute-start.14
  52.5 1.7 %collective-permute-start.16 = (f32[24,16,128]{2,1,0:T(8,128)S(1)}, f32[24,16,128]{2,1,0:T(8,128)S(1)}, u32[]{:S(2)}, u32[]{:S(2)}) collective-permute-start(f32[24,16,128]{2,1,0:T(8,128)S(1)} %get-tuple-element.89.near_in), channel_id=1, source_target_pairs={{0,2},{2,0},{4,6},{6,4},{8,10},{10,8},{12,14},{14,12},{1,3},{3,1},... | collective-permute-start | bytes 589832 | tf_op jit(solution)/shard_map/ppermute | solution.py:466
  54.2 3.0 %collective-permute-start.18 = (f32[24,16,128]{2,1,0:T(8,128)S(1)}, f32[24,16,128]{2,1,0:T(8,128)S(1)}, u32[]{:S(2)}, u32[]{:S(2)}) collective-permute-start(f32[24,16,128]{2,1,0:T(8,128)S(1)} %get-tuple-element.96), channel_id=1, source_target_pairs={{0,2},{2,0},{4,6},{6,4},{8,10},{10,8},{12,14},{14,12},{1,3},{3,1},... | collective-permute-start | bytes 589832 | tf_op jit(solution)/shard_map/ppermute | solution.py:466
  57.3 1.2 %collective-permute-done.14.ymsg = f32[2,2,16,8,128]{4,3,2,1,0:T(8,128)S(1)} collective-permute-done((f32[2,2,16,8,128]{4,3,2,1,0:T(8,128)S(1)}, f32[2,2,16,8,128]{4,3,2,1,0:T(8,128)S(1)}, u32[]{:S(2)}, u32[]{:S(2)}) %collective-permute-start.14) | collective-permute-done | bytes 262176 | tf_op jit(solution)/shard_map/ppermute | solution.py:472
  58.6 2.4 %shard_map.98.f = f32[4,2,16,16,128]{4,3,2,1,0:T(8,128)S(1)} custom-call(s32[4]{0:T(128)S(1)} %pad_add_fusion.info, f32[4,2,16,16,128]{4,3,2,1,0:T(8,128)S(1)} %shard_map.96.f, f32[24,16,128]{2,1,0:T(8,128)S(1)} %get-tuple-element.89.near_in, f32[24,16,128]{2,1,0:T(8,128)S(1)} %get-tuple-element.90.near_out, f32[8,16,128]{2,1,0:T(8,128)S(1)} %get-tuple-element.91.far_in, ...), custom_call_target="tpu_custom_call" | custom-call | flops 4000000 | bytes 4587536 | tf_op jit(solution)/shard_map/pallas_call | solution.py:29
  61.0 3.4 %collective-permute-done.16.halo_in = f32[24,16,128]{2,1,0:T(8,128)S(1)} collective-permute-done((f32[24,16,128]{2,1,0:T(8,128)S(1)}, f32[24,16,128]{2,1,0:T(8,128)S(1)}, u32[]{:S(2)}, u32[]{:S(2)}) %collective-permute-start.16) | collective-permute-done | bytes 196640 | tf_op jit(solution)/shard_map/ppermute | solution.py:466
  64.4 0.7 shard_map.99
  65.2 1.7 %collective-permute-start.19 = (f32[24,16,128]{2,1,0:T(8,128)S(1)}, f32[24,16,128]{2,1,0:T(8,128)S(1)}, u32[]{:S(2)}, u32[]{:S(2)}) collective-permute-start(f32[24,16,128]{2,1,0:T(8,128)S(1)} %get-tuple-element.97), channel_id=1, source_target_pairs={{2,4},{18,20},{3,5},{19,21},{4,2},{20,18},{5,3},{21,19},{6,8},{22,... | collective-permute-start | bytes 589832 | tf_op jit(solution)/shard_map/ppermute | solution.py:469
  66.9 1.4 %collective-permute-start.22 = (f32[24,16,128]{2,1,0:T(8,128)S(1)}, f32[24,16,128]{2,1,0:T(8,128)S(1)}, u32[]{:S(2)}, u32[]{:S(2)}) collective-permute-start(f32[24,16,128]{2,1,0:T(8,128)S(1)} %get-tuple-element.98.near_in), channel_id=1, source_target_pairs={{0,2},{2,0},{4,6},{6,4},{8,10},{10,8},{12,14},{14,12},{1,3},{3,1},... | collective-permute-start | bytes 589832 | tf_op jit(solution)/shard_map/ppermute | solution.py:466
  68.3 1.1 %collective-permute-start.20 = (f32[1,2,16,8,128]{4,3,2,1,0:T(8,128)S(1)}, f32[1,2,16,8,128]{4,3,2,1,0:T(8,128)S(1)}, u32[]{:S(2)}, u32[]{:S(2)}) collective-permute-start(f32[1,2,16,8,128]{4,3,2,1,0:T(8,128)S(1)} %get-tuple-element.100), channel_id=1, source_target_pairs={{0,1},{1,0},{2,3},{3,2},{4,5},{5,4},{6,7},{7,6},{8,9},{9,8},{10,11... | collective-permute-start | bytes 393224 | tf_op jit(solution)/shard_map/ppermute | solution.py:472
  69.4 4.5 %collective-permute-done.19.rest_2_ = f32[24,16,128]{2,1,0:T(8,128)S(1)} collective-permute-done((f32[24,16,128]{2,1,0:T(8,128)S(1)}, f32[24,16,128]{2,1,0:T(8,128)S(1)}, u32[]{:S(2)}, u32[]{:S(2)}) %collective-permute-start.19) | collective-permute-done | bytes 196640 | tf_op jit(solution)/shard_map/ppermute | solution.py:469
  73.9 2.0 %shard_map.100 = (f32[4,2,16,16,128]{4,3,2,1,0:T(8,128)S(1)}, f32[4,2,16,16,128]{4,3,2,1,0:T(8,128)S(1)}) custom-call(s32[4]{0:T(128)S(1)} %pad_add_fusion.info, f32[4,2,16,16,128]{4,3,2,1,0:T(8,128)S(1)} %shard_map.98.f, f32[24,16,128]{2,1,0:T(8,128)S(1)} %get-tuple-element.98.near_in, f32[24,16,128]{2,1,0:T(8,128)S(1)} %get-tuple-element.99.near_out, ...), custom_call_target="tpu_custom_call" | custom-call | flops 4000000 | bytes 6029328 | tf_op jit(solution)/shard_map/pallas_call | solution.py:29
  75.9 5.9 %collective-permute-done.22.halo_in = f32[24,16,128]{2,1,0:T(8,128)S(1)} collective-permute-done((f32[24,16,128]{2,1,0:T(8,128)S(1)}, f32[24,16,128]{2,1,0:T(8,128)S(1)}, u32[]{:S(2)}, u32[]{:S(2)}) %collective-permute-start.22) | collective-permute-done | bytes 196640 | tf_op jit(solution)/shard_map/ppermute | solution.py:466
  81.8 0.7 shard_map.101
  82.7 1.8 %collective-permute-start.26 = (f32[24,16,128]{2,1,0:T(8,128)S(1)}, f32[24,16,128]{2,1,0:T(8,128)S(1)}, u32[]{:S(2)}, u32[]{:S(2)}) collective-permute-start(f32[24,16,128]{2,1,0:T(8,128)S(1)} %get-tuple-element.106.near_in), channel_id=1, source_target_pairs={{0,2},{2,0},{4,6},{6,4},{8,10},{10,8},{12,14},{14,12},{1,3},{3,1},... | collective-permute-start | bytes 589832 | tf_op jit(solution)/shard_map/ppermute | solution.py:466
  84.5 1.1 %collective-permute-start.24 = (f32[1,2,16,8,128]{4,3,2,1,0:T(8,128)S(1)}, f32[1,2,16,8,128]{4,3,2,1,0:T(8,128)S(1)}, u32[]{:S(2)}, u32[]{:S(2)}) collective-permute-start(f32[1,2,16,8,128]{4,3,2,1,0:T(8,128)S(1)} %get-tuple-element.110), channel_id=1, source_target_pairs={{0,1},{1,0},{2,3},{3,2},{4,5},{5,4},{6,7},{7,6},{8,9},{9,8},{10,11... | collective-permute-start | bytes 393224 | tf_op jit(solution)/shard_map/ppermute | solution.py:472
  85.6 4.4 %collective-permute-done.24.ymsg = f32[1,2,16,8,128]{4,3,2,1,0:T(8,128)S(1)} collective-permute-done((f32[1,2,16,8,128]{4,3,2,1,0:T(8,128)S(1)}, f32[1,2,16,8,128]{4,3,2,1,0:T(8,128)S(1)}, u32[]{:S(2)}, u32[]{:S(2)}) %collective-permute-start.24) | collective-permute-done | bytes 131104 | tf_op jit(solution)/shard_map/ppermute | solution.py:472
  90.0 2.0 %shard_map.102.f = f32[4,2,16,16,128]{4,3,2,1,0:T(8,128)S(1)} custom-call(s32[4]{0:T(128)S(1)} %pad_add_fusion.info, f32[4,2,16,16,128]{4,3,2,1,0:T(8,128)S(1)} %get-tuple-element.103.f, f32[24,16,128]{2,1,0:T(8,128)S(1)} %get-tuple-element.106.near_in, f32[24,16,128]{2,1,0:T(8,128)S(1)} %get-tuple-element.107.near_out, ...), custom_call_target="tpu_custom_call" | custom-call | flops 4000000 | bytes 6160400 | tf_op jit(solution)/shard_map/pallas_call | solution.py:29
  92.1 2.1 %collective-permute-done.26.halo_in = f32[24,16,128]{2,1,0:T(8,128)S(1)} collective-permute-done((f32[24,16,128]{2,1,0:T(8,128)S(1)}, f32[24,16,128]{2,1,0:T(8,128)S(1)}, u32[]{:S(2)}, u32[]{:S(2)}) %collective-permute-start.26) | collective-permute-done | bytes 196640 | tf_op jit(solution)/shard_map/ppermute | solution.py:466
  94.2 0.8 shard_map.103
  95.1 1.2 %collective-permute-start.28 = (f32[2,2,16,8,128]{4,3,2,1,0:T(8,128)S(1)}, f32[2,2,16,8,128]{4,3,2,1,0:T(8,128)S(1)}, u32[]{:S(2)}, u32[]{:S(2)}) collective-permute-start(f32[2,2,16,8,128]{4,3,2,1,0:T(8,128)S(1)} %get-tuple-element.117), channel_id=1, source_target_pairs={{0,1},{1,0},{2,3},{3,2},{4,5},{5,4},{6,7},{7,6},{8,9},{9,8},{10,11... | collective-permute-start | bytes 786440 | tf_op jit(solution)/shard_map/ppermute | solution.py:472
  96.2 1.8 %collective-permute-start.30 = (f32[24,16,128]{2,1,0:T(8,128)S(1)}, f32[24,16,128]{2,1,0:T(8,128)S(1)}, u32[]{:S(2)}, u32[]{:S(2)}) collective-permute-start(f32[24,16,128]{2,1,0:T(8,128)S(1)} %get-tuple-element.113.near_in), channel_id=1, source_target_pairs={{0,2},{2,0},{4,6},{6,4},{8,10},{10,8},{12,14},{14,12},{1,3},{3,1},... | collective-permute-start | bytes 589832 | tf_op jit(solution)/shard_map/ppermute | solution.py:466
  98.0 9.4 %collective-permute-done.30.rest_0_ = f32[24,16,128]{2,1,0:T(8,128)S(1)} collective-permute-done((f32[24,16,128]{2,1,0:T(8,128)S(1)}, f32[24,16,128]{2,1,0:T(8,128)S(1)}, u32[]{:S(2)}, u32[]{:S(2)}) %collective-permute-start.30) | collective-permute-done | bytes 196640 | tf_op jit(solution)/shard_map/ppermute | solution.py:466
  107.5 2.5 %shard_map.104 = f32[4,16,16,256]{3,2,1,0:T(8,128)S(1)} custom-call(s32[4]{0:T(128)S(1)} %pad_add_fusion.info, f32[4,2,16,16,128]{4,3,2,1,0:T(8,128)S(1)} %shard_map.102.f, f32[24,16,128]{2,1,0:T(8,128)S(1)} %get-tuple-element.113.near_in, f32[24,16,128]{2,1,0:T(8,128)S(1)} %get-tuple-element.114.near_out, f32[8,16,128]{2,1,0:T(8,128)S(1)} %get-tuple-element.115.far_in, ...), custom_call_target="tpu_custom_call" | custom-call | flops 4000000 | bytes 4980752 | tf_op jit(solution)/shard_map/pallas_call | solution.py:29
  109.9 1.7 %copy.12 = f32[16,16,4,256]{3,2,1,0:T(4,128)} copy(f32[16,16,4,256]{3,1,0,2:T(8,128)S(1)} %bitcast.15) | data formatting | bytes 2097152 | tf_op jit(solution)/shard_map/transpose | solution.py:577
  (58 shorter events, 0.8 us)
Async XLA Ops:
  0.1 1.4 %copy-start = (f32[32,16,3,256]{3,1,2,0:T(8,128)S(1)}, f32[32,16,3,256]{3,1,2,0:T(8,128)}, u32[]{:S(2)}) copy-start(f32[32,16,3,256]{3,1,2,0:T(8,128)} %param.9) | copy-start | bytes 4718596
  3.2 5.0 %collective-permute-start.3 = (f32[3,32,16,128]{3,2,1,0:T(8,128)}, f32[3,32,16,128]{3,2,1,0:T(8,128)S(1)}, u32[]{:S(2)}, u32[]{:S(2)}) collective-permute-start(f32[3,32,16,128]{3,2,1,0:T(8,128)} %get-tuple-element.65), channel_id=1, source_target_pairs={{0,16},{16,0},{1,17},{17,1},{2,18},{18,2},{3,19},{19,3},{4,20},{20... | collective-permute-start | bytes 2359304 | tf_op jit(solution)/shard_map/ppermute | solution.py:472
  3.2 8.0 %collective-permute-start = (f32[6,16,128]{2,1,0:T(8,128)}, f32[6,16,128]{2,1,0:T(8,128)}, u32[]{:S(2)}, u32[]{:S(2)}) collective-permute-start(f32[6,16,128]{2,1,0:T(8,128)} %get-tuple-element.62), channel_id=1, source_target_pairs={{0,2},{2,0},{4,6},{6,4},{8,10},{10,8},{12,14},{14,12},{1,3},{3,1},... | collective-permute-start | bytes 147464 | tf_op jit(solution)/shard_map/ppermute | solution.py:466
  4.6 6.5 %collective-permute-start.1 = (f32[6,16,128]{2,1,0:T(8,128)}, f32[6,16,128]{2,1,0:T(8,128)}, u32[]{:S(2)}, u32[]{:S(2)}) collective-permute-start(f32[6,16,128]{2,1,0:T(8,128)} %get-tuple-element.63), channel_id=1, source_target_pairs={{2,4},{18,20},{3,5},{19,21},{4,2},{20,18},{5,3},{21,19},{6,8},{22,... | collective-permute-start | bytes 147464 | tf_op jit(solution)/shard_map/ppermute | solution.py:469
  4.7 6.5 %collective-permute-start.2 = (f32[3,2,4,8,128]{4,3,2,1,0:T(8,128)}, f32[3,2,4,8,128]{4,3,2,1,0:T(8,128)S(1)}, u32[]{:S(2)}, u32[]{:S(2)}) collective-permute-start(f32[3,2,4,8,128]{4,3,2,1,0:T(8,128)} %get-tuple-element.64), channel_id=1, source_target_pairs={{0,1},{1,0},{2,3},{3,2},{4,5},{5,4},{6,7},{7,6},{8,9},{9,8},{10,11... | collective-permute-start | bytes 294920 | tf_op jit(solution)/shard_map/ppermute | solution.py:472
  6.6 4.6 %copy-start.1 = (f32[32,16,3,256]{3,1,2,0:T(8,128)S(1)}, f32[32,16,3,256]{3,1,2,0:T(8,128)}, u32[]{:S(2)}) copy-start(f32[32,16,3,256]{3,1,2,0:T(8,128)} %param.9) | copy-start | bytes 4718596
  6.6 4.6 %copy-start.2 = (s32[8]{0:T(128)S(1)}, s32[8]{0:T(128)}, u32[]{:S(2)}) copy-start(s32[8]{0:T(128)} %offset.3) | copy-start | bytes 100
  11.2 7.5 %copy-start.5 = (bf16[1152,256]{1,0:T(8,128)(2,1)S(1)}, bf16[1152,256]{1,0:T(8,128)(2,1)}, u32[]{:S(2)}) copy-start(bf16[1152,256]{1,0:T(8,128)(2,1)} %constant.36.clone) | copy-start | bytes 1769476
  11.2 7.5 %copy-start.6 = (bf16[1152,256]{1,0:T(8,128)(2,1)S(1)}, bf16[1152,256]{1,0:T(8,128)(2,1)}, u32[]{:S(2)}) copy-start(bf16[1152,256]{1,0:T(8,128)(2,1)} %constant.37.clone) | copy-start | bytes 1769476
  15.3 8.6 %copy-start.7 = (f32[16,16]{1,0:T(8,128)S(1)}, f32[16,16]{1,0:T(8,128)}, u32[]{:S(2)}) copy-start(f32[16,16]{1,0:T(8,128)} %param.10) | copy-start | bytes 3076
  15.3 22.1 %collective-permute-start.4 = (f32[54,16,128]{2,1,0:T(8,128)S(1)}, f32[54,16,128]{2,1,0:T(8,128)S(1)}, u32[]{:S(2)}, u32[]{:S(2)}) collective-permute-start(f32[54,16,128]{2,1,0:T(8,128)S(1)} %get-tuple-element.69), channel_id=1, source_target_pairs={{0,2},{2,0},{4,6},{6,4},{8,10},{10,8},{12,14},{14,12},{1,3},{3,1},... | collective-permute-start | bytes 1327112 | tf_op jit(solution)/shard_map/ppermute | solution.py:466
  18.0 19.5 %collective-permute-start.5 = (f32[54,16,128]{2,1,0:T(8,128)S(1)}, f32[54,16,128]{2,1,0:T(8,128)S(1)}, u32[]{:S(2)}, u32[]{:S(2)}) collective-permute-start(f32[54,16,128]{2,1,0:T(8,128)S(1)} %get-tuple-element.70), channel_id=1, source_target_pairs={{2,4},{18,20},{3,5},{19,21},{4,2},{20,18},{5,3},{21,19},{6,8},{22,... | collective-permute-start | bytes 1327112 | tf_op jit(solution)/shard_map/ppermute | solution.py:469
  18.0 26.1 %collective-permute-start.7 = (f32[3,32,16,128]{3,2,1,0:T(8,128)S(1)}, f32[3,32,16,128]{3,2,1,0:T(8,128)S(1)}, u32[]{:S(2)}, u32[]{:S(2)}) collective-permute-start(f32[3,32,16,128]{3,2,1,0:T(8,128)S(1)} %get-tuple-element.72), channel_id=1, source_target_pairs={{0,16},{16,0},{1,17},{17,1},{2,18},{18,2},{3,19},{19,3},{4,20},{20... | collective-permute-start | bytes 2359304 | tf_op jit(solution)/shard_map/ppermute | solution.py:472
  18.0 5.9 %collective-permute-start.8 = (f32[1,2,16,8,128]{4,3,2,1,0:T(8,128)S(1)}, f32[1,2,16,8,128]{4,3,2,1,0:T(8,128)S(1)}, u32[]{:S(2)}, u32[]{:S(2)}) collective-permute-start(f32[1,2,16,8,128]{4,3,2,1,0:T(8,128)S(1)} %get-tuple-element.78), channel_id=1, source_target_pairs={{0,1},{1,0},{2,3},{3,2},{4,5},{5,4},{6,7},{7,6},{8,9},{9,8},{10,11... | collective-permute-start | bytes 393224 | tf_op jit(solution)/shard_map/ppermute | solution.py:472
  18.5 5.4 %collective-permute-start.9 = (f32[2,16,16,128]{3,2,1,0:T(8,128)S(1)}, f32[2,16,16,128]{3,2,1,0:T(8,128)S(1)}, u32[]{:S(2)}, u32[]{:S(2)}) collective-permute-start(f32[2,16,16,128]{3,2,1,0:T(8,128)S(1)} %get-tuple-element.79), channel_id=1, source_target_pairs={{0,16},{16,0},{1,17},{17,1},{2,18},{18,2},{3,19},{19,3},{4,20},{20... | collective-permute-start | bytes 786440 | tf_op jit(solution)/shard_map/ppermute | solution.py:472
  38.3 10.4 %collective-permute-start.11 = (f32[2,16,16,128]{3,2,1,0:T(8,128)S(1)}, f32[2,16,16,128]{3,2,1,0:T(8,128)S(1)}, u32[]{:S(2)}, u32[]{:S(2)}) collective-permute-start(f32[2,16,16,128]{3,2,1,0:T(8,128)S(1)} %get-tuple-element.87), channel_id=1, source_target_pairs={{0,16},{16,0},{1,17},{17,1},{2,18},{18,2},{3,19},{19,3},{4,20},{20... | collective-permute-start | bytes 786440 | tf_op jit(solution)/shard_map/ppermute | solution.py:472
  38.3 5.2 %collective-permute-start.6 = (f32[3,2,4,8,128]{4,3,2,1,0:T(8,128)S(1)}, f32[3,2,4,8,128]{4,3,2,1,0:T(8,128)S(1)}, u32[]{:S(2)}, u32[]{:S(2)}) collective-permute-start(f32[3,2,4,8,128]{4,3,2,1,0:T(8,128)S(1)} %get-tuple-element.71), channel_id=1, source_target_pairs={{0,1},{1,0},{2,3},{3,2},{4,5},{5,4},{6,7},{7,6},{8,9},{9,8},{10,11... | collective-permute-start | bytes 294920 | tf_op jit(solution)/shard_map/ppermute | solution.py:472
  38.9 11.8 %collective-permute-start.12 = (f32[24,16,128]{2,1,0:T(8,128)S(1)}, f32[24,16,128]{2,1,0:T(8,128)S(1)}, u32[]{:S(2)}, u32[]{:S(2)}) collective-permute-start(f32[24,16,128]{2,1,0:T(8,128)S(1)} %get-tuple-element.82.near_in), channel_id=1, source_target_pairs={{0,2},{2,0},{4,6},{6,4},{8,10},{10,8},{12,14},{14,12},{1,3},{3,1},... | collective-permute-start | bytes 589832 | tf_op jit(solution)/shard_map/ppermute | solution.py:466
  40.6 10.0 %collective-permute-start.13 = (f32[24,16,128]{2,1,0:T(8,128)S(1)}, f32[24,16,128]{2,1,0:T(8,128)S(1)}, u32[]{:S(2)}, u32[]{:S(2)}) collective-permute-start(f32[24,16,128]{2,1,0:T(8,128)S(1)} %get-tuple-element.83.near_out), channel_id=1, source_target_pairs={{2,4},{18,20},{3,5},{19,21},{4,2},{20,18},{5,3},{21,19},{6,8},{22,... | collective-permute-start | bytes 589832 | tf_op jit(solution)/shard_map/ppermute | solution.py:469
  43.5 5.1 %collective-permute-start.10 = (f32[1,2,16,8,128]{4,3,2,1,0:T(8,128)S(1)}, f32[1,2,16,8,128]{4,3,2,1,0:T(8,128)S(1)}, u32[]{:S(2)}, u32[]{:S(2)}) collective-permute-start(f32[1,2,16,8,128]{4,3,2,1,0:T(8,128)S(1)} %get-tuple-element.86), channel_id=1, source_target_pairs={{0,1},{1,0},{2,3},{3,2},{4,5},{5,4},{6,7},{7,6},{8,9},{9,8},{10,11... | collective-permute-start | bytes 393224 | tf_op jit(solution)/shard_map/ppermute | solution.py:472
  50.7 6.6 %copy-start.3 = (bf16[1152,256]{1,0:T(8,128)(2,1)S(1)}, bf16[1152,256]{1,0:T(8,128)(2,1)}, u32[]{:S(2)}) copy-start(bf16[1152,256]{1,0:T(8,128)(2,1)} %constant.38.clone) | copy-start | bytes 1769476
  50.7 6.6 %copy-start.4 = (bf16[1152,256]{1,0:T(8,128)(2,1)S(1)}, bf16[1152,256]{1,0:T(8,128)(2,1)}, u32[]{:S(2)}) copy-start(bf16[1152,256]{1,0:T(8,128)(2,1)} %constant.39.clone) | copy-start | bytes 1769476
  51.5 7.0 %collective-permute-start.14 = (f32[2,2,16,8,128]{4,3,2,1,0:T(8,128)S(1)}, f32[2,2,16,8,128]{4,3,2,1,0:T(8,128)S(1)}, u32[]{:S(2)}, u32[]{:S(2)}) collective-permute-start(f32[2,2,16,8,128]{4,3,2,1,0:T(8,128)S(1)} %get-tuple-element.93), channel_id=1, source_target_pairs={{0,1},{1,0},{2,3},{3,2},{4,5},{5,4},{6,7},{7,6},{8,9},{9,8},{10,11... | collective-permute-start | bytes 786440 | tf_op jit(solution)/shard_map/ppermute | solution.py:472
  52.5 6.1 %collective-permute-start.15 = (f32[4,16,16,128]{3,2,1,0:T(8,128)S(1)}, f32[4,16,16,128]{3,2,1,0:T(8,128)S(1)}, u32[]{:S(2)}, u32[]{:S(2)}) collective-permute-start(f32[4,16,16,128]{3,2,1,0:T(8,128)S(1)} %get-tuple-element.94), channel_id=1, source_target_pairs={{0,16},{16,0},{1,17},{17,1},{2,18},{18,2},{3,19},{19,3},{4,20},{20... | collective-permute-start | bytes 1572872 | tf_op jit(solution)/shard_map/ppermute | solution.py:472
  52.5 11.9 %collective-permute-start.16 = (f32[24,16,128]{2,1,0:T(8,128)S(1)}, f32[24,16,128]{2,1,0:T(8,128)S(1)}, u32[]{:S(2)}, u32[]{:S(2)}) collective-permute-start(f32[24,16,128]{2,1,0:T(8,128)S(1)} %get-tuple-element.89.near_in), channel_id=1, source_target_pairs={{0,2},{2,0},{4,6},{6,4},{8,10},{10,8},{12,14},{14,12},{1,3},{3,1},... | collective-permute-start | bytes 589832 | tf_op jit(solution)/shard_map/ppermute | solution.py:466
  54.2 10.2 %collective-permute-start.17 = (f32[24,16,128]{2,1,0:T(8,128)S(1)}, f32[24,16,128]{2,1,0:T(8,128)S(1)}, u32[]{:S(2)}, u32[]{:S(2)}) collective-permute-start(f32[24,16,128]{2,1,0:T(8,128)S(1)} %get-tuple-element.90.near_out), channel_id=1, source_target_pairs={{2,4},{18,20},{3,5},{19,21},{4,2},{20,18},{5,3},{21,19},{6,8},{22,... | collective-permute-start | bytes 589832 | tf_op jit(solution)/shard_map/ppermute | solution.py:469
  54.2 14.1 %collective-permute-start.18 = (f32[24,16,128]{2,1,0:T(8,128)S(1)}, f32[24,16,128]{2,1,0:T(8,128)S(1)}, u32[]{:S(2)}, u32[]{:S(2)}) collective-permute-start(f32[24,16,128]{2,1,0:T(8,128)S(1)} %get-tuple-element.96), channel_id=1, source_target_pairs={{0,2},{2,0},{4,6},{6,4},{8,10},{10,8},{12,14},{14,12},{1,3},{3,1},... | collective-permute-start | bytes 589832 | tf_op jit(solution)/shard_map/ppermute | solution.py:466
  65.1 8.9 %collective-permute-start.21 = (f32[2,16,16,128]{3,2,1,0:T(8,128)S(1)}, f32[2,16,16,128]{3,2,1,0:T(8,128)S(1)}, u32[]{:S(2)}, u32[]{:S(2)}) collective-permute-start(f32[2,16,16,128]{3,2,1,0:T(8,128)S(1)} %get-tuple-element.101), channel_id=1, source_target_pairs={{0,16},{16,0},{1,17},{17,1},{2,18},{18,2},{3,19},{19,3},{4,20},{20... | collective-permute-start | bytes 786440 | tf_op jit(solution)/shard_map/ppermute | solution.py:472
  65.2 8.8 %collective-permute-start.19 = (f32[24,16,128]{2,1,0:T(8,128)S(1)}, f32[24,16,128]{2,1,0:T(8,128)S(1)}, u32[]{:S(2)}, u32[]{:S(2)}) collective-permute-start(f32[24,16,128]{2,1,0:T(8,128)S(1)} %get-tuple-element.97), channel_id=1, source_target_pairs={{2,4},{18,20},{3,5},{19,21},{4,2},{20,18},{5,3},{21,19},{6,8},{22,... | collective-permute-start | bytes 589832 | tf_op jit(solution)/shard_map/ppermute | solution.py:469
  66.9 14.9 %collective-permute-start.22 = (f32[24,16,128]{2,1,0:T(8,128)S(1)}, f32[24,16,128]{2,1,0:T(8,128)S(1)}, u32[]{:S(2)}, u32[]{:S(2)}) collective-permute-start(f32[24,16,128]{2,1,0:T(8,128)S(1)} %get-tuple-element.98.near_in), channel_id=1, source_target_pairs={{0,2},{2,0},{4,6},{6,4},{8,10},{10,8},{12,14},{14,12},{1,3},{3,1},... | collective-permute-start | bytes 589832 | tf_op jit(solution)/shard_map/ppermute | solution.py:466
  68.3 13.5 %collective-permute-start.23 = (f32[24,16,128]{2,1,0:T(8,128)S(1)}, f32[24,16,128]{2,1,0:T(8,128)S(1)}, u32[]{:S(2)}, u32[]{:S(2)}) collective-permute-start(f32[24,16,128]{2,1,0:T(8,128)S(1)} %get-tuple-element.99.near_out), channel_id=1, source_target_pairs={{2,4},{18,20},{3,5},{19,21},{4,2},{20,18},{5,3},{21,19},{6,8},{22,... | collective-permute-start | bytes 589832 | tf_op jit(solution)/shard_map/ppermute | solution.py:469
  68.3 5.7 %collective-permute-start.20 = (f32[1,2,16,8,128]{4,3,2,1,0:T(8,128)S(1)}, f32[1,2,16,8,128]{4,3,2,1,0:T(8,128)S(1)}, u32[]{:S(2)}, u32[]{:S(2)}) collective-permute-start(f32[1,2,16,8,128]{4,3,2,1,0:T(8,128)S(1)} %get-tuple-element.100), channel_id=1, source_target_pairs={{0,1},{1,0},{2,3},{3,2},{4,5},{5,4},{6,7},{7,6},{8,9},{9,8},{10,11... | collective-permute-start | bytes 393224 | tf_op jit(solution)/shard_map/ppermute | solution.py:472
  82.6 7.5 %collective-permute-start.25 = (f32[2,16,16,128]{3,2,1,0:T(8,128)S(1)}, f32[2,16,16,128]{3,2,1,0:T(8,128)S(1)}, u32[]{:S(2)}, u32[]{:S(2)}) collective-permute-start(f32[2,16,16,128]{3,2,1,0:T(8,128)S(1)} %get-tuple-element.111), channel_id=1, source_target_pairs={{0,16},{16,0},{1,17},{17,1},{2,18},{18,2},{3,19},{19,3},{4,20},{20... | collective-permute-start | bytes 786440 | tf_op jit(solution)/shard_map/ppermute | solution.py:472
  82.7 11.5 %collective-permute-start.26 = (f32[24,16,128]{2,1,0:T(8,128)S(1)}, f32[24,16,128]{2,1,0:T(8,128)S(1)}, u32[]{:S(2)}, u32[]{:S(2)}) collective-permute-start(f32[24,16,128]{2,1,0:T(8,128)S(1)} %get-tuple-element.106.near_in), channel_id=1, source_target_pairs={{0,2},{2,0},{4,6},{6,4},{8,10},{10,8},{12,14},{14,12},{1,3},{3,1},... | collective-permute-start | bytes 589832 | tf_op jit(solution)/shard_map/ppermute | solution.py:466
  84.5 9.7 %collective-permute-start.27 = (f32[24,16,128]{2,1,0:T(8,128)S(1)}, f32[24,16,128]{2,1,0:T(8,128)S(1)}, u32[]{:S(2)}, u32[]{:S(2)}) collective-permute-start(f32[24,16,128]{2,1,0:T(8,128)S(1)} %get-tuple-element.107.near_out), channel_id=1, source_target_pairs={{2,4},{18,20},{3,5},{19,21},{4,2},{20,18},{5,3},{21,19},{6,8},{22,... | collective-permute-start | bytes 589832 | tf_op jit(solution)/shard_map/ppermute | solution.py:469
  84.5 5.6 %collective-permute-start.24 = (f32[1,2,16,8,128]{4,3,2,1,0:T(8,128)S(1)}, f32[1,2,16,8,128]{4,3,2,1,0:T(8,128)S(1)}, u32[]{:S(2)}, u32[]{:S(2)}) collective-permute-start(f32[1,2,16,8,128]{4,3,2,1,0:T(8,128)S(1)} %get-tuple-element.110), channel_id=1, source_target_pairs={{0,1},{1,0},{2,3},{3,2},{4,5},{5,4},{6,7},{7,6},{8,9},{9,8},{10,11... | collective-permute-start | bytes 393224 | tf_op jit(solution)/shard_map/ppermute | solution.py:472
  95.0 12.5 %collective-permute-start.29 = (f32[4,16,16,128]{3,2,1,0:T(8,128)S(1)}, f32[4,16,16,128]{3,2,1,0:T(8,128)S(1)}, u32[]{:S(2)}, u32[]{:S(2)}) collective-permute-start(f32[4,16,16,128]{3,2,1,0:T(8,128)S(1)} %get-tuple-element.118), channel_id=1, source_target_pairs={{0,16},{16,0},{1,17},{17,1},{2,18},{18,2},{3,19},{19,3},{4,20},{20... | collective-permute-start | bytes 1572872 | tf_op jit(solution)/shard_map/ppermute | solution.py:472
  95.1 12.4 %collective-permute-start.28 = (f32[2,2,16,8,128]{4,3,2,1,0:T(8,128)S(1)}, f32[2,2,16,8,128]{4,3,2,1,0:T(8,128)S(1)}, u32[]{:S(2)}, u32[]{:S(2)}) collective-permute-start(f32[2,2,16,8,128]{4,3,2,1,0:T(8,128)S(1)} %get-tuple-element.117), channel_id=1, source_target_pairs={{0,1},{1,0},{2,3},{3,2},{4,5},{5,4},{6,7},{7,6},{8,9},{9,8},{10,11... | collective-permute-start | bytes 786440 | tf_op jit(solution)/shard_map/ppermute | solution.py:472
  96.2 11.2 %collective-permute-start.30 = (f32[24,16,128]{2,1,0:T(8,128)S(1)}, f32[24,16,128]{2,1,0:T(8,128)S(1)}, u32[]{:S(2)}, u32[]{:S(2)}) collective-permute-start(f32[24,16,128]{2,1,0:T(8,128)S(1)} %get-tuple-element.113.near_in), channel_id=1, source_target_pairs={{0,2},{2,0},{4,6},{6,4},{8,10},{10,8},{12,14},{14,12},{1,3},{3,1},... | collective-permute-start | bytes 589832 | tf_op jit(solution)/shard_map/ppermute | solution.py:466
  98.0 9.4 %collective-permute-start.31 = (f32[24,16,128]{2,1,0:T(8,128)S(1)}, f32[24,16,128]{2,1,0:T(8,128)S(1)}, u32[]{:S(2)}, u32[]{:S(2)}) collective-permute-start(f32[24,16,128]{2,1,0:T(8,128)S(1)} %get-tuple-element.114.near_out), channel_id=1, source_target_pairs={{2,4},{18,20},{3,5},{19,21},{4,2},{20,18},{5,3},{21,19},{6,8},{22,... | collective-permute-start | bytes 589832 | tf_op jit(solution)/shard_map/ppermute | solution.py:469

commit v5 on v4

--- a/solution.py
+++ b/solution.py
@@ -23,7 +23,7 @@
 SMEM = pl.BlockSpec(memory_space=pltpu.SMEM)
 
 
-def call(body, outs, ins, scratch=(), smem=1, flops=1000000):
+def call(body, outs, ins, scratch=(), smem=1, flops=1000000, alias=None):
     shapes = [jax.ShapeDtypeStruct(s, jnp.float32) for s in outs]
     size = sum(o.size for o in shapes) + sum(i.size for i in ins)
     return pl.pallas_call(
@@ -32,6 +32,7 @@
         in_specs=[SMEM] * smem + [VMEM] * (len(ins) - smem),
         out_specs=[VMEM] * len(shapes),
         scratch_shapes=list(scratch),
+        input_output_aliases=alias or {},
         compiler_params=pltpu.CompilerParams(vmem_limit_bytes=12 * 1024 * 1024),
         cost_estimate=pl.CostEstimate(flops=flops, bytes_accessed=4 * size, transcendentals=0),
     )(*ins)
@@ -119,7 +120,7 @@
             one(i)
 
 
-def fill(F, f, nears, fars, ymsg, ycomps, info, halos=None):
+def fill(F, f, nears, fars, ymsg, ycomps, info):
     row = info[1]
     _, T, X, Y, _ = f.shape
     y = slice(8, 8 + Y)
@@ -141,15 +142,12 @@
     lax.fori_loop(0, X, step, 0, unroll=4)
     zero = jnp.zeros((Y, LANES), jnp.float32)
     for side, near in enumerate(nears):
-        high, has, layer, place = ends(info, side == 0, X, 3)
+        high, _, layer, place = ends(info, side == 0, X, 3)
         for c in range(4):
             for t in range(T):
                 for d in range(3):
                     F[c, t, 3 + layer(d), y, :] = near[3 * (c * T + t) + place(d)]
-                    beyond = zero
-                    if halos is not None:
-                        beyond = known(halos[side][3 * (c * T + t) + place(2 - d)], has)
-                    F[c, t, jnp.where(high, X + 3 + d, 2 - d), y, :] = beyond
+                    F[c, t, jnp.where(high, X + 3 + d, 2 - d), y, :] = zero
                 if fars:
                     far = fars[side]
                     count = far.shape[0] // (4 * T)
@@ -208,10 +206,9 @@
     rate_loop(F, G, mach, S, emit)
 
 
-def smooth_main(info, f, near_in, near_out, far_in, far_out, ymsg, zmsg, zmat, *rest, last):
-    *halos, o, F, G = rest
+def smooth_main(info, f, near_in, near_out, far_in, far_out, ymsg, zmsg, zmat, o, F, G, *, last):
     _, T, X, Y, _ = f.shape
-    fill(F, f, (near_in, near_out), (far_in, far_out), ymsg, ALL, info, halos if last else None)
+    fill(F, f, (near_in, near_out), (far_in, far_out), ymsg, ALL, info)
     z_product(F, zmsg, zmat, ALL, G)
     y = slice(8, 8 + Y)
 
@@ -231,6 +228,21 @@
         return carry
 
     lax.fori_loop(0, X, step, 0, unroll=4)
+
+
+def last_body(info, f, halo_in, halo_out, o):
+    _, X, Y, Z = f.shape
+    T = Z // LANES
+    for side, halo in enumerate((halo_in, halo_out)):
+        _, has, layer, place = ends(info, side == 0, X, 3)
+        weight = filter_weight * has.astype(jnp.float32)
+        for c in range(4):
+            for t in range(T):
+                lane = slice(t * LANES, (t + 1) * LANES)
+                beyond = [halo[3 * (c * T + t) + place(2 - e)] for e in range(3)]
+                for d in range(3):
+                    part = sum(taps[1 + d + e] * beyond[e] for e in range(3 - d))
+                    o[c, layer(d), :, lane] = f[c, layer(d), :, lane] - weight * part
 
 
 def edge_body(info, f, halo_in, halo_out, *rest, smooth, scale, ycomps, zcomps):
@@ -412,19 +424,23 @@
     lax.fori_loop(0, X, step, 0, unroll=4)
 
     for m in range(blocks // 2):
-        a, b = tiles[2 * m], tiles[2 * m + 1]
-        none = jnp.zeros((plane, 2 * plane), jnp.bfloat16)
-        rows = [(a[:plane], b[:plane]), (a[plane:], none), (none, b[plane:])]
-        weights = jnp.concatenate([jnp.concatenate(pair, axis=1) for pair in rows], axis=0)
-        out = jnp.dot(weights, LB[m], preferred_element_type=jnp.float32)
+        a, b = [[tiles[2 * m + n, k] for k in (0, 1)] for n in (0, 1)]
+        parts = [
+            (jnp.concatenate([a[0], a[0], b[0], b[0]]), LB[m]),
+            (jnp.concatenate([a[1], a[1]]), LB[m, : 2 * plane]),
+            (jnp.concatenate([b[1], b[1]]), LB[m, 2 * plane :]),
+        ]
+        out = [
+            lax.dot_general(w, x, (((0,), (0,)), ((), ())), preferred_element_type=jnp.float32) for w, x in parts
+        ]
         at = (m + 1) * wide
-        places = [(at, 0), (at + offset[2 * m] * wide, plane), (at + offset[2 * m + 1] * wide, 2 * plane)]
+        places = [at, at + offset[2 * m] * wide, at + offset[2 * m + 1] * wide]
         for c in range(3):
             for t in range(T):
                 lane = slice((c * T + t) * LANES, (c * T + t + 1) * LANES)
-                for to, row0 in places:
+                for to, value in zip(places, out):
                     for l in range(wide):
-                        ACC[c, t, to + l] = ACC[c, t, to + l] + out[row0 + l * Y : row0 + (l + 1) * Y, lane]
+                        ACC[c, t, to + l] = ACC[c, t, to + l] + value[l * Y : (l + 1) * Y, lane]
 
     depth = own.shape[2]
     own[...] = ACC[:, :, wide : wide + depth]
@@ -516,9 +532,7 @@
 
         v_in, v_out, *sides = call(pack_les_body, [les_x, les_x, les_y, les_z], [info, v])
         les_edges = [send_in(v_in), send_out(v_out), *send_sides(*sides)]
-        les_edges[3], tiles = lax.optimization_barrier((les_edges[3], transfer_tiles))
-        tiles = tiles[:, 0].swapaxes(2, 3).reshape(blocks, 2 * plane, plane)
-        tiles = jnp.concatenate([tiles, tiles], axis=2)
+        tiles = transfer_tiles[:, 0]
         at = term[0] + 3 * T
         joint = (at + near[0], Y, LANES)
         v1, S, *own, les_ym, les_zm, state, ym, zm = call(
@@ -567,13 +581,14 @@
                     flops=4000000,
                 )
                 whole, _, sides, halos = complete(part, halos, None, 0.0, RATE_Y, RATE_Z)
-        (state,) = call(
+        (part,) = call(
             functools.partial(smooth_main, last=True),
             [(4, X, Y, Z)],
-            [info, *whole, *fars, *sides, smooth_z, *halos],
+            [info, *whole, *fars, *sides, smooth_z],
             [F, G4],
             flops=4000000,
         )
+        (state,) = call(last_body, [(4, X, Y, Z)], [info, part, *halos], alias={1: 0})
         return state.transpose(1, 2, 0, 3)
 
     placed = (

time: 113 us -> 108 us (0.956)
  starting transfers between devices: 25.8 us -> 19.3 us
  waiting for transfers between devices: 52.2 us -> 57.7 us
  local copies, waits for them, and re-layouts: 6.61 us -> 4.7 us
  other arithmetic: 1.38 us -> 0.2 us
    ppermute x16, waiting for transfers between devices: 15.4 us -> 24.4 us  [send_sides(): return (lax.ppermute(ymsg, 'gy', swap), lax.ppermute(zmsg, 'grp', swap))]
    ppermute x8, waiting for transfers between devices: 32.3 us -> 26.3 us  [send_in(): return lax.ppermute(message, 'gx', even)]
    ppermute x8, starting transfers between devices: 15.6 us -> 10.2 us  [send_in(): return lax.ppermute(message, 'gx', even)]
    ppermute x8, waiting for transfers between devices: 4.53 us -> 6.92 us  [send_out(): return lax.ppermute(message, mesh.axis_names, hops)]
    transpose x1 -> x0, local copies, waits for them, and re-layouts: 1.79 us -> none  [body(): tiles = tiles[:, 0].swapaxes(2, 3).reshape(blocks, 2 * plane, plane)]
    concatenate x1 -> x0, other arithmetic: 1.18 us -> none  [body(): tiles = jnp.concatenate([tiles, tiles], axis=2)]
    pallas_call x14 -> x15, Pallas kernels: 25.2 us -> 25.6 us  [call(): pl.pallas_call(body, out_shape=shapes, in_specs=[SMEM] * smem + [VMEM] *...]
    unnamed x17 -> x19, local copies, waits for them, and re-layouts: 3 us -> 2.88 us
  transfers between devices with their start and end apart: 32 -> 32, of which waited for: 11 -> 14; matrix products, arithmetic and copies ran while one was open for 4% -> 2% of each run, Pallas kernels for 13% -> 16%
where the time goes in v5:
time: 108 us
  waiting for transfers between devices  57.7 us (53%)
  Pallas kernels  25.6 us (24%)
  starting transfers between devices  19.3 us (18%)
  local copies, waits for them, and re-layouts  4.7 us (4%)
    ppermute x8, waiting for transfers between devices, send_in(): return lax.ppermute(message, 'gx', even)  26.3 us
    pallas_call x15, Pallas kernels, call(): pl.pallas_call(body, out_shape=shapes, in_specs=[SMEM] * smem + [VMEM] *...  25.6 us
    ppermute x16, waiting for transfers between devices, send_sides(): return (lax.ppermute(ymsg, 'gy', swap), lax.ppermute(zmsg, 'grp', swap))  24.4 us
    ppermute x8, starting transfers between devices, send_in(): return lax.ppermute(message, 'gx', even)  10.2 us
    ppermute x16, starting transfers between devices, send_sides(): return (lax.ppermute(ymsg, 'gy', swap), lax.ppermute(zmsg, 'grp', swap))  8.08 us
    ppermute x8, waiting for transfers between devices, send_out(): return lax.ppermute(message, mesh.axis_names, hops)  6.92 us
    unnamed x19, local copies, waits for them, and re-layouts  2.88 us
  transfers between devices with their start and end apart: 32, of which 14 were waited for; matrix products, arithmetic and copies ran while one was open for 2% of the time, Pallas kernels for 16%

profile of v5, /device:TPU:8, one launch (start us, length us, event | category | flops | bytes accessed | tf_op | source)
XLA Modules:
  0.0 107.7 jit_solution(3829017933947395889)
XLA Ops:
  0.1 1.4 %copy-done = f32[32,16,3,256]{3,1,2,0:T(8,128)S(1)} copy-done((f32[32,16,3,256]{3,1,2,0:T(8,128)S(1)}, f32[32,16,3,256]{3,1,2,0:T(8,128)}, u32[]{:S(2)}) %copy-start) | copy-done | bytes 1572888
  1.5 1.6 %shard_map.91 = (f32[6,16,128]{2,1,0:T(8,128)S(1)}, f32[6,16,128]{2,1,0:T(8,128)S(1)}, f32[3,2,4,8,128]{4,3,2,1,0:T(8,128)S(1)}, f32[3,32,16,128]{3,2,1,0:T(8,128)}) custom-call(s32[4]{0:T(128)S(1)} %pad_add_fusion.info, f32[32,3,16,256]{3,2,1,0:T(8,128)S(1)} %bitcast.11), custom_call_target="tpu_custom_call" | custom-call | flops 1000000 | bytes 2555920 | tf_op jit(solution)/shard_map/pallas_call | solution.py:29
  3.1 1.5 %collective-permute-start.2 = (f32[3,2,4,8,128]{4,3,2,1,0:T(8,128)S(1)}, f32[3,2,4,8,128]{4,3,2,1,0:T(8,128)S(1)}, u32[]{:S(2)}, u32[]{:S(2)}) collective-permute-start(f32[3,2,4,8,128]{4,3,2,1,0:T(8,128)S(1)} %get-tuple-element.62), channel_id=1, source_target_pairs={{0,1},{1,0},{2,3},{3,2},{4,5},{5,4},{6,7},{7,6},{8,9},{9,8},{10,11... | collective-permute-start | bytes 294920 | tf_op jit(solution)/shard_map/ppermute | solution.py:488
  4.6 1.5 %collective-permute-start = (f32[6,16,128]{2,1,0:T(8,128)S(1)}, f32[6,16,128]{2,1,0:T(8,128)S(1)}, u32[]{:S(2)}, u32[]{:S(2)}) collective-permute-start(f32[6,16,128]{2,1,0:T(8,128)S(1)} %get-tuple-element.60), channel_id=1, source_target_pairs={{0,2},{2,0},{4,6},{6,4},{8,10},{10,8},{12,14},{14,12},{1,3},{3,1},... | collective-permute-start | bytes 147464 | tf_op jit(solution)/shard_map/ppermute | solution.py:482
  6.5 1.4 %copy.14 = f32[16,16,4,256]{3,1,0,2:T(8,128)S(1)} copy(f32[16,16,4,256]{3,2,1,0:T(4,128)} %param.13) | data formatting | bytes 2097152 | tf_op args[4]
  8.0 0.7 collective-permute-done.inner
  8.7 2.4 %collective-permute-done.1.outer = f32[6,16,128]{2,1,0:T(8,128)S(1)} collective-permute-done((f32[6,16,128]{2,1,0:T(8,128)S(1)}, f32[6,16,128]{2,1,0:T(8,128)S(1)}, u32[]{:S(2)}, u32[]{:S(2)}) %collective-permute-start.1) | collective-permute-done | bytes 49184 | tf_op jit(solution)/shard_map/ppermute | solution.py:485
  11.2 3.8 %shard_map.92 = (f32[3,2,32,16,128]{4,3,2,1,0:T(8,128)S(1)}, f32[3,2,16,16,128]{4,3,2,1,0:T(8,128)S(1)}, f32[54,16,128]{2,1,0:T(8,128)S(1)}, f32[54,16,128]{2,1,...) custom-call(s32[4]{0:T(128)S(1)} %pad_add_fusion.info, ...), custom_call_target="tpu_custom_call" | custom-call | flops 4000000 | bytes 9437232 | tf_op jit(solution)/shard_map/pallas_call | solution.py:29
  15.0 0.6 collective-permute-start.4
  15.6 0.5 collective-permute-start.8
  16.4 5.1 %collective-permute-done.8.ymsg = f32[1,2,16,8,128]{4,3,2,1,0:T(8,128)S(1)} collective-permute-done((f32[1,2,16,8,128]{4,3,2,1,0:T(8,128)S(1)}, f32[1,2,16,8,128]{4,3,2,1,0:T(8,128)S(1)}, u32[]{:S(2)}, u32[]{:S(2)}) %collective-permute-start.8) | collective-permute-done | bytes 131104 | tf_op jit(solution)/shard_map/ppermute | solution.py:488
  21.6 2.0 %shard_map.94 = (f32[4,2,16,16,128]{4,3,2,1,0:T(8,128)S(1)}, f32[4,2,16,16,128]{4,3,2,1,0:T(8,128)S(1)}) custom-call(s32[4]{0:T(128)S(1)} %pad_add_fusion.info, f32[4,2,16,16,128]{4,3,2,1,0:T(8,128)S(1)} %get-tuple-element.73.f, f32[24,16,128]{2,1,0:T(8,128)S(1)} %slice.12.near_in, f32[24,16,128]{2,1,0:T(8,128)S(1)} %slice.13.near_out, ...), custom_call_target="tpu_custom_call" | custom-call | flops 4000000 | bytes 6029328 | tf_op jit(solution)/shard_map/pallas_call | solution.py:29
  23.6 11.8 %collective-permute-done.4.inner.rest_1_ = f32[54,16,128]{2,1,0:T(8,128)S(1)} collective-permute-done((f32[54,16,128]{2,1,0:T(8,128)S(1)}, f32[54,16,128]{2,1,0:T(8,128)S(1)}, u32[]{:S(2)}, u32[]{:S(2)}) %collective-permute-start.4) | collective-permute-done | bytes 442400 | tf_op jit(solution)/shard_map/ppermute | solution.py:482
  35.5 0.8 shard_map.95
  36.3 0.6 collective-permute-start.6
  36.9 0.6 collective-permute-start.12
  37.5 4.0 %collective-permute-done.6.ymsg = f32[3,2,4,8,128]{4,3,2,1,0:T(8,128)S(1)} collective-permute-done((f32[3,2,4,8,128]{4,3,2,1,0:T(8,128)S(1)}, f32[3,2,4,8,128]{4,3,2,1,0:T(8,128)S(1)}, u32[]{:S(2)}, u32[]{:S(2)}) %collective-permute-start.6) | collective-permute-done | bytes 98336 | tf_op jit(solution)/shard_map/ppermute | solution.py:488
  42.0 2.9 %shard_map.93 = (f32[3,2,16,16,128]{4,3,2,1,0:T(8,128)S(1)}, f32[24,16,128]{2,1,0:T(8,128)S(1)}, f32[24,16,128]{2,1,0:T(8,128)S(1)}) custom-call(s32[4]{0:T(128)S(1)} %pad_add_fusion.info, s32[8]{0:T(128)S(1)} %copy-done.3, f32[3,2,32,16,128]{4,3,2,1,0:T(8,128)S(1)} %get-tuple-element.64.v, f32[54,16,128]{2,1,0:T(8,128)S(1)} %collective-permute-done.4.inner.rest_1_, ...), custom_call_target="tpu_custom_call" | custom-call | flops 4000000 | bytes 4784176 | tf_op jit(solution)/shard_map/pallas_call | solution.py:29
  44.9 1.6 %collective-permute-done.10.ymsg = f32[1,2,16,8,128]{4,3,2,1,0:T(8,128)S(1)} collective-permute-done((f32[1,2,16,8,128]{4,3,2,1,0:T(8,128)S(1)}, f32[1,2,16,8,128]{4,3,2,1,0:T(8,128)S(1)}, u32[]{:S(2)}, u32[]{:S(2)}) %collective-permute-start.10) | collective-permute-done | bytes 131104 | tf_op jit(solution)/shard_map/ppermute | solution.py:488
  46.6 2.0 %shard_map.96.f = f32[4,2,16,16,128]{4,3,2,1,0:T(8,128)S(1)} custom-call(s32[4]{0:T(128)S(1)} %pad_add_fusion.info, f32[4,2,16,16,128]{4,3,2,1,0:T(8,128)S(1)} %get-tuple-element.77.f, f32[24,16,128]{2,1,0:T(8,128)S(1)} %get-tuple-element.78.near_in, f32[24,16,128]{2,1,0:T(8,128)S(1)} %get-tuple-element.79.near_out, ...), custom_call_target="tpu_custom_call" | custom-call | flops 4000000 | bytes 6160400 | tf_op jit(solution)/shard_map/pallas_call | solution.py:29
  48.7 0.8 shard_map.97
  49.5 1.0 collective-permute-start.14
  50.4 0.6 collective-permute-start.16
  51.1 3.0 %collective-permute-start.18 = (f32[24,16,128]{2,1,0:T(8,128)S(1)}, f32[24,16,128]{2,1,0:T(8,128)S(1)}, u32[]{:S(2)}, u32[]{:S(2)}) collective-permute-start(f32[24,16,128]{2,1,0:T(8,128)S(1)} %get-tuple-element.92), channel_id=1, source_target_pairs={{0,2},{2,0},{4,6},{6,4},{8,10},{10,8},{12,14},{14,12},{1,3},{3,1},... | collective-permute-start | bytes 589832 | tf_op jit(solution)/shard_map/ppermute | solution.py:482
  54.2 2.3 %collective-permute-done.14.ymsg = f32[2,2,16,8,128]{4,3,2,1,0:T(8,128)S(1)} collective-permute-done((f32[2,2,16,8,128]{4,3,2,1,0:T(8,128)S(1)}, f32[2,2,16,8,128]{4,3,2,1,0:T(8,128)S(1)}, u32[]{:S(2)}, u32[]{:S(2)}) %collective-permute-start.14) | collective-permute-done | bytes 262176 | tf_op jit(solution)/shard_map/ppermute | solution.py:488
  56.5 2.4 %shard_map.98.f = f32[4,2,16,16,128]{4,3,2,1,0:T(8,128)S(1)} custom-call(s32[4]{0:T(128)S(1)} %pad_add_fusion.info, f32[4,2,16,16,128]{4,3,2,1,0:T(8,128)S(1)} %shard_map.96.f, f32[24,16,128]{2,1,0:T(8,128)S(1)} %get-tuple-element.85.near_in, f32[24,16,128]{2,1,0:T(8,128)S(1)} %get-tuple-element.86.near_out, f32[8,16,128]{2,1,0:T(8,128)S(1)} %get-tuple-element.87.far_in, ...), custom_call_target="tpu_custom_call" | custom-call | flops 4000000 | bytes 4587536 | tf_op jit(solution)/shard_map/pallas_call | solution.py:29
  58.9 3.4 %collective-permute-done.16.halo_in = f32[24,16,128]{2,1,0:T(8,128)S(1)} collective-permute-done((f32[24,16,128]{2,1,0:T(8,128)S(1)}, f32[24,16,128]{2,1,0:T(8,128)S(1)}, u32[]{:S(2)}, u32[]{:S(2)}) %collective-permute-start.16) | collective-permute-done | bytes 196640 | tf_op jit(solution)/shard_map/ppermute | solution.py:482
  62.3 0.7 shard_map.99
  63.1 0.6 collective-permute-start.19
  63.7 2.5 %collective-permute-start.22 = (f32[24,16,128]{2,1,0:T(8,128)S(1)}, f32[24,16,128]{2,1,0:T(8,128)S(1)}, u32[]{:S(2)}, u32[]{:S(2)}) collective-permute-start(f32[24,16,128]{2,1,0:T(8,128)S(1)} %get-tuple-element.94.near_in), channel_id=1, source_target_pairs={{0,2},{2,0},{4,6},{6,4},{8,10},{10,8},{12,14},{14,12},{1,3},{3,1},... | collective-permute-start | bytes 589832 | tf_op jit(solution)/shard_map/ppermute | solution.py:482
  66.2 1.1 %collective-permute-start.20 = (f32[1,2,16,8,128]{4,3,2,1,0:T(8,128)S(1)}, f32[1,2,16,8,128]{4,3,2,1,0:T(8,128)S(1)}, u32[]{:S(2)}, u32[]{:S(2)}) collective-permute-start(f32[1,2,16,8,128]{4,3,2,1,0:T(8,128)S(1)} %get-tuple-element.96), channel_id=1, source_target_pairs={{0,1},{1,0},{2,3},{3,2},{4,5},{5,4},{6,7},{7,6},{8,9},{9,8},{10,11... | collective-permute-start | bytes 393224 | tf_op jit(solution)/shard_map/ppermute | solution.py:488
  67.4 4.5 %collective-permute-done.19.rest_2_ = f32[24,16,128]{2,1,0:T(8,128)S(1)} collective-permute-done((f32[24,16,128]{2,1,0:T(8,128)S(1)}, f32[24,16,128]{2,1,0:T(8,128)S(1)}, u32[]{:S(2)}, u32[]{:S(2)}) %collective-permute-start.19) | collective-permute-done | bytes 196640 | tf_op jit(solution)/shard_map/ppermute | solution.py:485
  71.9 2.0 %shard_map.100 = (f32[4,2,16,16,128]{4,3,2,1,0:T(8,128)S(1)}, f32[4,2,16,16,128]{4,3,2,1,0:T(8,128)S(1)}) custom-call(s32[4]{0:T(128)S(1)} %pad_add_fusion.info, f32[4,2,16,16,128]{4,3,2,1,0:T(8,128)S(1)} %shard_map.98.f, f32[24,16,128]{2,1,0:T(8,128)S(1)} %get-tuple-element.94.near_in, f32[24,16,128]{2,1,0:T(8,128)S(1)} %get-tuple-element.95.near_out, ...), custom_call_target="tpu_custom_call" | custom-call | flops 4000000 | bytes 6029328 | tf_op jit(solution)/shard_map/pallas_call | solution.py:29
  73.9 5.9 %collective-permute-done.22.halo_in = f32[24,16,128]{2,1,0:T(8,128)S(1)} collective-permute-done((f32[24,16,128]{2,1,0:T(8,128)S(1)}, f32[24,16,128]{2,1,0:T(8,128)S(1)}, u32[]{:S(2)}, u32[]{:S(2)}) %collective-permute-start.22) | collective-permute-done | bytes 196640 | tf_op jit(solution)/shard_map/ppermute | solution.py:482
  79.8 0.7 shard_map.101
  80.7 0.6 collective-permute-start.26
  81.3 1.1 %collective-permute-start.24 = (f32[1,2,16,8,128]{4,3,2,1,0:T(8,128)S(1)}, f32[1,2,16,8,128]{4,3,2,1,0:T(8,128)S(1)}, u32[]{:S(2)}, u32[]{:S(2)}) collective-permute-start(f32[1,2,16,8,128]{4,3,2,1,0:T(8,128)S(1)} %get-tuple-element.106), channel_id=1, source_target_pairs={{0,1},{1,0},{2,3},{3,2},{4,5},{5,4},{6,7},{7,6},{8,9},{9,8},{10,11... | collective-permute-start | bytes 393224 | tf_op jit(solution)/shard_map/ppermute | solution.py:488
  82.4 4.4 %collective-permute-done.24.ymsg = f32[1,2,16,8,128]{4,3,2,1,0:T(8,128)S(1)} collective-permute-done((f32[1,2,16,8,128]{4,3,2,1,0:T(8,128)S(1)}, f32[1,2,16,8,128]{4,3,2,1,0:T(8,128)S(1)}, u32[]{:S(2)}, u32[]{:S(2)}) %collective-permute-start.24) | collective-permute-done | bytes 131104 | tf_op jit(solution)/shard_map/ppermute | solution.py:488
  86.9 2.0 %shard_map.102.f = f32[4,2,16,16,128]{4,3,2,1,0:T(8,128)S(1)} custom-call(s32[4]{0:T(128)S(1)} %pad_add_fusion.info, f32[4,2,16,16,128]{4,3,2,1,0:T(8,128)S(1)} %get-tuple-element.99.f, f32[24,16,128]{2,1,0:T(8,128)S(1)} %get-tuple-element.102.near_in, f32[24,16,128]{2,1,0:T(8,128)S(1)} %get-tuple-element.103.near_out, ...), custom_call_target="tpu_custom_call" | custom-call | flops 4000000 | bytes 6160400 | tf_op jit(solution)/shard_map/pallas_call | solution.py:29
  88.9 3.2 %collective-permute-done.26.halo_in = f32[24,16,128]{2,1,0:T(8,128)S(1)} collective-permute-done((f32[24,16,128]{2,1,0:T(8,128)S(1)}, f32[24,16,128]{2,1,0:T(8,128)S(1)}, u32[]{:S(2)}, u32[]{:S(2)}) %collective-permute-start.26) | collective-permute-done | bytes 196640 | tf_op jit(solution)/shard_map/ppermute | solution.py:482
  92.1 0.8 shard_map.103
  93.0 1.2 %collective-permute-start.28 = (f32[2,2,16,8,128]{4,3,2,1,0:T(8,128)S(1)}, f32[2,2,16,8,128]{4,3,2,1,0:T(8,128)S(1)}, u32[]{:S(2)}, u32[]{:S(2)}) collective-permute-start(f32[2,2,16,8,128]{4,3,2,1,0:T(8,128)S(1)} %get-tuple-element.113), channel_id=1, source_target_pairs={{0,1},{1,0},{2,3},{3,2},{4,5},{5,4},{6,7},{7,6},{8,9},{9,8},{10,11... | collective-permute-start | bytes 786440 | tf_op jit(solution)/shard_map/ppermute | solution.py:488
  94.2 0.6 collective-permute-start.30
  94.8 6.9 %collective-permute-done.28.ymsg = f32[2,2,16,8,128]{4,3,2,1,0:T(8,128)S(1)} collective-permute-done((f32[2,2,16,8,128]{4,3,2,1,0:T(8,128)S(1)}, f32[2,2,16,8,128]{4,3,2,1,0:T(8,128)S(1)}, u32[]{:S(2)}, u32[]{:S(2)}) %collective-permute-start.28) | collective-permute-done | bytes 262176 | tf_op jit(solution)/shard_map/ppermute | solution.py:488
  101.8 2.4 %shard_map.104.f = f32[4,16,16,256]{3,2,1,0:T(8,128)S(1)} custom-call(s32[4]{0:T(128)S(1)} %pad_add_fusion.info, f32[4,2,16,16,128]{4,3,2,1,0:T(8,128)S(1)} %shard_map.102.f, f32[24,16,128]{2,1,0:T(8,128)S(1)} %get-tuple-element.109.near_in, f32[24,16,128]{2,1,0:T(8,128)S(1)} %get-tuple-element.110.near_out, f32[8,16,128]{2,1,0:T(8,128)S(1)} %get-tuple-element.111.far_in, ...), custom_call_target="tpu_custom_call" | custom-call | flops 4000000 | bytes 4587536 | tf_op jit(solution)/shard_map/pallas_call | solution.py:29
  104.2 1.2 %collective-permute-done.30.halo_in = f32[24,16,128]{2,1,0:T(8,128)S(1)} collective-permute-done((f32[24,16,128]{2,1,0:T(8,128)S(1)}, f32[24,16,128]{2,1,0:T(8,128)S(1)}, u32[]{:S(2)}, u32[]{:S(2)}) %collective-permute-start.30) | collective-permute-done | bytes 196640 | tf_op jit(solution)/shard_map/ppermute | solution.py:482
  105.4 0.7 shard_map.105
  106.1 1.7 %copy.12 = f32[16,16,4,256]{3,2,1,0:T(4,128)} copy(f32[16,16,4,256]{3,1,0,2:T(8,128)S(1)} %bitcast.10) | data formatting | bytes 2097152 | tf_op jit(solution)/shard_map/transpose | solution.py:592
  (59 shorter events, 2.0 us)
Async XLA Ops:
  0.1 1.4 %copy-start = (f32[32,16,3,256]{3,1,2,0:T(8,128)S(1)}, f32[32,16,3,256]{3,1,2,0:T(8,128)}, u32[]{:S(2)}) copy-start(f32[32,16,3,256]{3,1,2,0:T(8,128)} %param.9) | copy-start | bytes 4718596
  1.5 9.6 %copy-start.1 = (f32[32,16,3,256]{3,1,2,0:T(8,128)S(1)}, f32[32,16,3,256]{3,1,2,0:T(8,128)}, u32[]{:S(2)}) copy-start(f32[32,16,3,256]{3,1,2,0:T(8,128)} %param.9) | copy-start | bytes 4718596
  1.5 9.6 %copy-start.2 = (bf16[8,1,2,64,64]{4,3,2,1,0:T(8,128)(2,1)S(1)}, bf16[8,1,2,64,64]{4,3,2,1,0:T(8,128)(2,1)}, u32[]{:S(2)}) copy-start(bf16[8,1,2,64,64]{4,3,2,1,0:T(8,128)(2,1)} %param.11) | copy-start | bytes 393220
  1.5 9.6 %copy-start.3 = (s32[8]{0:T(128)S(1)}, s32[8]{0:T(128)}, u32[]{:S(2)}) copy-start(s32[8]{0:T(128)} %offset.3) | copy-start | bytes 100
  3.1 8.0 %collective-permute-start.3 = (f32[3,32,16,128]{3,2,1,0:T(8,128)}, f32[3,32,16,128]{3,2,1,0:T(8,128)S(1)}, u32[]{:S(2)}, u32[]{:S(2)}) collective-permute-start(f32[3,32,16,128]{3,2,1,0:T(8,128)} %get-tuple-element.63), channel_id=1, source_target_pairs={{0,16},{16,0},{1,17},{17,1},{2,18},{18,2},{3,19},{19,3},{4,20},{20... | collective-permute-start | bytes 2359304 | tf_op jit(solution)/shard_map/ppermute | solution.py:488
  3.1 8.0 %collective-permute-start.2 = (f32[3,2,4,8,128]{4,3,2,1,0:T(8,128)S(1)}, f32[3,2,4,8,128]{4,3,2,1,0:T(8,128)S(1)}, u32[]{:S(2)}, u32[]{:S(2)}) collective-permute-start(f32[3,2,4,8,128]{4,3,2,1,0:T(8,128)S(1)} %get-tuple-element.62), channel_id=1, source_target_pairs={{0,1},{1,0},{2,3},{3,2},{4,5},{5,4},{6,7},{7,6},{8,9},{9,8},{10,11... | collective-permute-start | bytes 294920 | tf_op jit(solution)/shard_map/ppermute | solution.py:488
  4.6 4.1 %collective-permute-start = (f32[6,16,128]{2,1,0:T(8,128)S(1)}, f32[6,16,128]{2,1,0:T(8,128)S(1)}, u32[]{:S(2)}, u32[]{:S(2)}) collective-permute-start(f32[6,16,128]{2,1,0:T(8,128)S(1)} %get-tuple-element.60), channel_id=1, source_target_pairs={{0,2},{2,0},{4,6},{6,4},{8,10},{10,8},{12,14},{14,12},{1,3},{3,1},... | collective-permute-start | bytes 147464 | tf_op jit(solution)/shard_map/ppermute | solution.py:482
  6.1 5.0 %collective-permute-start.1 = (f32[6,16,128]{2,1,0:T(8,128)S(1)}, f32[6,16,128]{2,1,0:T(8,128)S(1)}, u32[]{:S(2)}, u32[]{:S(2)}) collective-permute-start(f32[6,16,128]{2,1,0:T(8,128)S(1)} %get-tuple-element.61), channel_id=1, source_target_pairs={{2,4},{18,20},{3,5},{19,21},{4,2},{20,18},{5,3},{21,19},{6,8},{22,... | collective-permute-start | bytes 147464 | tf_op jit(solution)/shard_map/ppermute | solution.py:485
  11.1 5.2 %copy-start.6 = (bf16[1152,256]{1,0:T(8,128)(2,1)S(1)}, bf16[1152,256]{1,0:T(8,128)(2,1)}, u32[]{:S(2)}) copy-start(bf16[1152,256]{1,0:T(8,128)(2,1)} %constant.36.clone) | copy-start | bytes 1769476
  11.1 5.2 %copy-start.7 = (bf16[1152,256]{1,0:T(8,128)(2,1)S(1)}, bf16[1152,256]{1,0:T(8,128)(2,1)}, u32[]{:S(2)}) copy-start(bf16[1152,256]{1,0:T(8,128)(2,1)} %constant.37.clone) | copy-start | bytes 1769476
  15.0 6.5 %copy-start.8 = (f32[16,16]{1,0:T(8,128)S(1)}, f32[16,16]{1,0:T(8,128)}, u32[]{:S(2)}) copy-start(f32[16,16]{1,0:T(8,128)} %param.10) | copy-start | bytes 3076
  15.0 20.4 %collective-permute-start.4 = (f32[54,16,128]{2,1,0:T(8,128)S(1)}, f32[54,16,128]{2,1,0:T(8,128)S(1)}, u32[]{:S(2)}, u32[]{:S(2)}) collective-permute-start(f32[54,16,128]{2,1,0:T(8,128)S(1)} %get-tuple-element.65), channel_id=1, source_target_pairs={{0,2},{2,0},{4,6},{6,4},{8,10},{10,8},{12,14},{14,12},{1,3},{3,1},... | collective-permute-start | bytes 1327112 | tf_op jit(solution)/shard_map/ppermute | solution.py:482
  15.6 19.9 %collective-permute-start.5 = (f32[54,16,128]{2,1,0:T(8,128)S(1)}, f32[54,16,128]{2,1,0:T(8,128)S(1)}, u32[]{:S(2)}, u32[]{:S(2)}) collective-permute-start(f32[54,16,128]{2,1,0:T(8,128)S(1)} %get-tuple-element.66), channel_id=1, source_target_pairs={{2,4},{18,20},{3,5},{19,21},{4,2},{20,18},{5,3},{21,19},{6,8},{22,... | collective-permute-start | bytes 1327112 | tf_op jit(solution)/shard_map/ppermute | solution.py:485
  15.6 26.4 %collective-permute-start.7 = (f32[3,32,16,128]{3,2,1,0:T(8,128)S(1)}, f32[3,32,16,128]{3,2,1,0:T(8,128)S(1)}, u32[]{:S(2)}, u32[]{:S(2)}) collective-permute-start(f32[3,32,16,128]{3,2,1,0:T(8,128)S(1)} %get-tuple-element.68), channel_id=1, source_target_pairs={{0,16},{16,0},{1,17},{17,1},{2,18},{18,2},{3,19},{19,3},{4,20},{20... | collective-permute-start | bytes 2359304 | tf_op jit(solution)/shard_map/ppermute | solution.py:488
  15.6 5.9 %collective-permute-start.8 = (f32[1,2,16,8,128]{4,3,2,1,0:T(8,128)S(1)}, f32[1,2,16,8,128]{4,3,2,1,0:T(8,128)S(1)}, u32[]{:S(2)}, u32[]{:S(2)}) collective-permute-start(f32[1,2,16,8,128]{4,3,2,1,0:T(8,128)S(1)} %get-tuple-element.74), channel_id=1, source_target_pairs={{0,1},{1,0},{2,3},{3,2},{4,5},{5,4},{6,7},{7,6},{8,9},{9,8},{10,11... | collective-permute-start | bytes 393224 | tf_op jit(solution)/shard_map/ppermute | solution.py:488
  16.1 5.4 %collective-permute-start.9 = (f32[2,16,16,128]{3,2,1,0:T(8,128)S(1)}, f32[2,16,16,128]{3,2,1,0:T(8,128)S(1)}, u32[]{:S(2)}, u32[]{:S(2)}) collective-permute-start(f32[2,16,16,128]{3,2,1,0:T(8,128)S(1)} %get-tuple-element.75), channel_id=1, source_target_pairs={{0,16},{16,0},{1,17},{17,1},{2,18},{18,2},{3,19},{19,3},{4,20},{20... | collective-permute-start | bytes 786440 | tf_op jit(solution)/shard_map/ppermute | solution.py:488
  36.2 10.4 %collective-permute-start.11 = (f32[2,16,16,128]{3,2,1,0:T(8,128)S(1)}, f32[2,16,16,128]{3,2,1,0:T(8,128)S(1)}, u32[]{:S(2)}, u32[]{:S(2)}) collective-permute-start(f32[2,16,16,128]{3,2,1,0:T(8,128)S(1)} %get-tuple-element.83), channel_id=1, source_target_pairs={{0,16},{16,0},{1,17},{17,1},{2,18},{18,2},{3,19},{19,3},{4,20},{20... | collective-permute-start | bytes 786440 | tf_op jit(solution)/shard_map/ppermute | solution.py:488
  36.3 5.2 %collective-permute-start.6 = (f32[3,2,4,8,128]{4,3,2,1,0:T(8,128)S(1)}, f32[3,2,4,8,128]{4,3,2,1,0:T(8,128)S(1)}, u32[]{:S(2)}, u32[]{:S(2)}) collective-permute-start(f32[3,2,4,8,128]{4,3,2,1,0:T(8,128)S(1)} %get-tuple-element.67), channel_id=1, source_target_pairs={{0,1},{1,0},{2,3},{3,2},{4,5},{5,4},{6,7},{7,6},{8,9},{9,8},{10,11... | collective-permute-start | bytes 294920 | tf_op jit(solution)/shard_map/ppermute | solution.py:488
  36.9 11.8 %collective-permute-start.12 = (f32[24,16,128]{2,1,0:T(8,128)S(1)}, f32[24,16,128]{2,1,0:T(8,128)S(1)}, u32[]{:S(2)}, u32[]{:S(2)}) collective-permute-start(f32[24,16,128]{2,1,0:T(8,128)S(1)} %get-tuple-element.78.near_in), channel_id=1, source_target_pairs={{0,2},{2,0},{4,6},{6,4},{8,10},{10,8},{12,14},{14,12},{1,3},{3,1},... | collective-permute-start | bytes 589832 | tf_op jit(solution)/shard_map/ppermute | solution.py:482
  37.5 11.2 %collective-permute-start.13 = (f32[24,16,128]{2,1,0:T(8,128)S(1)}, f32[24,16,128]{2,1,0:T(8,128)S(1)}, u32[]{:S(2)}, u32[]{:S(2)}) collective-permute-start(f32[24,16,128]{2,1,0:T(8,128)S(1)} %get-tuple-element.79.near_out), channel_id=1, source_target_pairs={{2,4},{18,20},{3,5},{19,21},{4,2},{20,18},{5,3},{21,19},{6,8},{22,... | collective-permute-start | bytes 589832 | tf_op jit(solution)/shard_map/ppermute | solution.py:485
  41.5 5.1 %collective-permute-start.10 = (f32[1,2,16,8,128]{4,3,2,1,0:T(8,128)S(1)}, f32[1,2,16,8,128]{4,3,2,1,0:T(8,128)S(1)}, u32[]{:S(2)}, u32[]{:S(2)}) collective-permute-start(f32[1,2,16,8,128]{4,3,2,1,0:T(8,128)S(1)} %get-tuple-element.82), channel_id=1, source_target_pairs={{0,1},{1,0},{2,3},{3,2},{4,5},{5,4},{6,7},{7,6},{8,9},{9,8},{10,11... | collective-permute-start | bytes 393224 | tf_op jit(solution)/shard_map/ppermute | solution.py:488
  48.6 5.5 %copy-start.4 = (bf16[1152,256]{1,0:T(8,128)(2,1)S(1)}, bf16[1152,256]{1,0:T(8,128)(2,1)}, u32[]{:S(2)}) copy-start(bf16[1152,256]{1,0:T(8,128)(2,1)} %constant.38.clone) | copy-start | bytes 1769476
  48.6 5.5 %copy-start.5 = (bf16[1152,256]{1,0:T(8,128)(2,1)S(1)}, bf16[1152,256]{1,0:T(8,128)(2,1)}, u32[]{:S(2)}) copy-start(bf16[1152,256]{1,0:T(8,128)(2,1)} %constant.39.clone) | copy-start | bytes 1769476
  49.5 7.0 %collective-permute-start.14 = (f32[2,2,16,8,128]{4,3,2,1,0:T(8,128)S(1)}, f32[2,2,16,8,128]{4,3,2,1,0:T(8,128)S(1)}, u32[]{:S(2)}, u32[]{:S(2)}) collective-permute-start(f32[2,2,16,8,128]{4,3,2,1,0:T(8,128)S(1)} %get-tuple-element.89), channel_id=1, source_target_pairs={{0,1},{1,0},{2,3},{3,2},{4,5},{5,4},{6,7},{7,6},{8,9},{9,8},{10,11... | collective-permute-start | bytes 786440 | tf_op jit(solution)/shard_map/ppermute | solution.py:488
  50.4 6.1 %collective-permute-start.15 = (f32[4,16,16,128]{3,2,1,0:T(8,128)S(1)}, f32[4,16,16,128]{3,2,1,0:T(8,128)S(1)}, u32[]{:S(2)}, u32[]{:S(2)}) collective-permute-start(f32[4,16,16,128]{3,2,1,0:T(8,128)S(1)} %get-tuple-element.90), channel_id=1, source_target_pairs={{0,16},{16,0},{1,17},{17,1},{2,18},{18,2},{3,19},{19,3},{4,20},{20... | collective-permute-start | bytes 1572872 | tf_op jit(solution)/shard_map/ppermute | solution.py:488
  50.4 11.9 %collective-permute-start.16 = (f32[24,16,128]{2,1,0:T(8,128)S(1)}, f32[24,16,128]{2,1,0:T(8,128)S(1)}, u32[]{:S(2)}, u32[]{:S(2)}) collective-permute-start(f32[24,16,128]{2,1,0:T(8,128)S(1)} %get-tuple-element.85.near_in), channel_id=1, source_target_pairs={{0,2},{2,0},{4,6},{6,4},{8,10},{10,8},{12,14},{14,12},{1,3},{3,1},... | collective-permute-start | bytes 589832 | tf_op jit(solution)/shard_map/ppermute | solution.py:482
  51.1 11.3 %collective-permute-start.17 = (f32[24,16,128]{2,1,0:T(8,128)S(1)}, f32[24,16,128]{2,1,0:T(8,128)S(1)}, u32[]{:S(2)}, u32[]{:S(2)}) collective-permute-start(f32[24,16,128]{2,1,0:T(8,128)S(1)} %get-tuple-element.86.near_out), channel_id=1, source_target_pairs={{2,4},{18,20},{3,5},{19,21},{4,2},{20,18},{5,3},{21,19},{6,8},{22,... | collective-permute-start | bytes 589832 | tf_op jit(solution)/shard_map/ppermute | solution.py:485
  51.1 15.2 %collective-permute-start.18 = (f32[24,16,128]{2,1,0:T(8,128)S(1)}, f32[24,16,128]{2,1,0:T(8,128)S(1)}, u32[]{:S(2)}, u32[]{:S(2)}) collective-permute-start(f32[24,16,128]{2,1,0:T(8,128)S(1)} %get-tuple-element.92), channel_id=1, source_target_pairs={{0,2},{2,0},{4,6},{6,4},{8,10},{10,8},{12,14},{14,12},{1,3},{3,1},... | collective-permute-start | bytes 589832 | tf_op jit(solution)/shard_map/ppermute | solution.py:482
  63.1 8.9 %collective-permute-start.21 = (f32[2,16,16,128]{3,2,1,0:T(8,128)S(1)}, f32[2,16,16,128]{3,2,1,0:T(8,128)S(1)}, u32[]{:S(2)}, u32[]{:S(2)}) collective-permute-start(f32[2,16,16,128]{3,2,1,0:T(8,128)S(1)} %get-tuple-element.97), channel_id=1, source_target_pairs={{0,16},{16,0},{1,17},{17,1},{2,18},{18,2},{3,19},{19,3},{4,20},{20... | collective-permute-start | bytes 786440 | tf_op jit(solution)/shard_map/ppermute | solution.py:488
  63.1 8.8 %collective-permute-start.19 = (f32[24,16,128]{2,1,0:T(8,128)S(1)}, f32[24,16,128]{2,1,0:T(8,128)S(1)}, u32[]{:S(2)}, u32[]{:S(2)}) collective-permute-start(f32[24,16,128]{2,1,0:T(8,128)S(1)} %get-tuple-element.93), channel_id=1, source_target_pairs={{2,4},{18,20},{3,5},{19,21},{4,2},{20,18},{5,3},{21,19},{6,8},{22,... | collective-permute-start | bytes 589832 | tf_op jit(solution)/shard_map/ppermute | solution.py:485
  63.7 16.1 %collective-permute-start.22 = (f32[24,16,128]{2,1,0:T(8,128)S(1)}, f32[24,16,128]{2,1,0:T(8,128)S(1)}, u32[]{:S(2)}, u32[]{:S(2)}) collective-permute-start(f32[24,16,128]{2,1,0:T(8,128)S(1)} %get-tuple-element.94.near_in), channel_id=1, source_target_pairs={{0,2},{2,0},{4,6},{6,4},{8,10},{10,8},{12,14},{14,12},{1,3},{3,1},... | collective-permute-start | bytes 589832 | tf_op jit(solution)/shard_map/ppermute | solution.py:482
  66.2 13.5 %collective-permute-start.23 = (f32[24,16,128]{2,1,0:T(8,128)S(1)}, f32[24,16,128]{2,1,0:T(8,128)S(1)}, u32[]{:S(2)}, u32[]{:S(2)}) collective-permute-start(f32[24,16,128]{2,1,0:T(8,128)S(1)} %get-tuple-element.95.near_out), channel_id=1, source_target_pairs={{2,4},{18,20},{3,5},{19,21},{4,2},{20,18},{5,3},{21,19},{6,8},{22,... | collective-permute-start | bytes 589832 | tf_op jit(solution)/shard_map/ppermute | solution.py:485
  66.2 5.7 %collective-permute-start.20 = (f32[1,2,16,8,128]{4,3,2,1,0:T(8,128)S(1)}, f32[1,2,16,8,128]{4,3,2,1,0:T(8,128)S(1)}, u32[]{:S(2)}, u32[]{:S(2)}) collective-permute-start(f32[1,2,16,8,128]{4,3,2,1,0:T(8,128)S(1)} %get-tuple-element.96), channel_id=1, source_target_pairs={{0,1},{1,0},{2,3},{3,2},{4,5},{5,4},{6,7},{7,6},{8,9},{9,8},{10,11... | collective-permute-start | bytes 393224 | tf_op jit(solution)/shard_map/ppermute | solution.py:488
  80.5 6.3 %collective-permute-start.25 = (f32[2,16,16,128]{3,2,1,0:T(8,128)S(1)}, f32[2,16,16,128]{3,2,1,0:T(8,128)S(1)}, u32[]{:S(2)}, u32[]{:S(2)}) collective-permute-start(f32[2,16,16,128]{3,2,1,0:T(8,128)S(1)} %get-tuple-element.107), channel_id=1, source_target_pairs={{0,16},{16,0},{1,17},{17,1},{2,18},{18,2},{3,19},{19,3},{4,20},{20... | collective-permute-start | bytes 786440 | tf_op jit(solution)/shard_map/ppermute | solution.py:488
  80.7 11.5 %collective-permute-start.26 = (f32[24,16,128]{2,1,0:T(8,128)S(1)}, f32[24,16,128]{2,1,0:T(8,128)S(1)}, u32[]{:S(2)}, u32[]{:S(2)}) collective-permute-start(f32[24,16,128]{2,1,0:T(8,128)S(1)} %get-tuple-element.102.near_in), channel_id=1, source_target_pairs={{0,2},{2,0},{4,6},{6,4},{8,10},{10,8},{12,14},{14,12},{1,3},{3,1},... | collective-permute-start | bytes 589832 | tf_op jit(solution)/shard_map/ppermute | solution.py:482
  81.3 10.8 %collective-permute-start.27 = (f32[24,16,128]{2,1,0:T(8,128)S(1)}, f32[24,16,128]{2,1,0:T(8,128)S(1)}, u32[]{:S(2)}, u32[]{:S(2)}) collective-permute-start(f32[24,16,128]{2,1,0:T(8,128)S(1)} %get-tuple-element.103.near_out), channel_id=1, source_target_pairs={{2,4},{18,20},{3,5},{19,21},{4,2},{20,18},{5,3},{21,19},{6,8},{22,... | collective-permute-start | bytes 589832 | tf_op jit(solution)/shard_map/ppermute | solution.py:485
  81.3 5.6 %collective-permute-start.24 = (f32[1,2,16,8,128]{4,3,2,1,0:T(8,128)S(1)}, f32[1,2,16,8,128]{4,3,2,1,0:T(8,128)S(1)}, u32[]{:S(2)}, u32[]{:S(2)}) collective-permute-start(f32[1,2,16,8,128]{4,3,2,1,0:T(8,128)S(1)} %get-tuple-element.106), channel_id=1, source_target_pairs={{0,1},{1,0},{2,3},{3,2},{4,5},{5,4},{6,7},{7,6},{8,9},{9,8},{10,11... | collective-permute-start | bytes 393224 | tf_op jit(solution)/shard_map/ppermute | solution.py:488
  93.0 8.8 %collective-permute-start.29 = (f32[4,16,16,128]{3,2,1,0:T(8,128)S(1)}, f32[4,16,16,128]{3,2,1,0:T(8,128)S(1)}, u32[]{:S(2)}, u32[]{:S(2)}) collective-permute-start(f32[4,16,16,128]{3,2,1,0:T(8,128)S(1)} %get-tuple-element.114), channel_id=1, source_target_pairs={{0,16},{16,0},{1,17},{17,1},{2,18},{18,2},{3,19},{19,3},{4,20},{20... | collective-permute-start | bytes 1572872 | tf_op jit(solution)/shard_map/ppermute | solution.py:488
  93.0 8.7 %collective-permute-start.28 = (f32[2,2,16,8,128]{4,3,2,1,0:T(8,128)S(1)}, f32[2,2,16,8,128]{4,3,2,1,0:T(8,128)S(1)}, u32[]{:S(2)}, u32[]{:S(2)}) collective-permute-start(f32[2,2,16,8,128]{4,3,2,1,0:T(8,128)S(1)} %get-tuple-element.113), channel_id=1, source_target_pairs={{0,1},{1,0},{2,3},{3,2},{4,5},{5,4},{6,7},{7,6},{8,9},{9,8},{10,11... | collective-permute-start | bytes 786440 | tf_op jit(solution)/shard_map/ppermute | solution.py:488
  94.2 11.2 %collective-permute-start.30 = (f32[24,16,128]{2,1,0:T(8,128)S(1)}, f32[24,16,128]{2,1,0:T(8,128)S(1)}, u32[]{:S(2)}, u32[]{:S(2)}) collective-permute-start(f32[24,16,128]{2,1,0:T(8,128)S(1)} %get-tuple-element.109.near_in), channel_id=1, source_target_pairs={{0,2},{2,0},{4,6},{6,4},{8,10},{10,8},{12,14},{14,12},{1,3},{3,1},... | collective-permute-start | bytes 589832 | tf_op jit(solution)/shard_map/ppermute | solution.py:482
  94.8 10.6 %collective-permute-start.31 = (f32[24,16,128]{2,1,0:T(8,128)S(1)}, f32[24,16,128]{2,1,0:T(8,128)S(1)}, u32[]{:S(2)}, u32[]{:S(2)}) collective-permute-start(f32[24,16,128]{2,1,0:T(8,128)S(1)} %get-tuple-element.110.near_out), channel_id=1, source_target_pairs={{2,4},{18,20},{3,5},{19,21},{4,2},{20,18},{5,3},{21,19},{6,8},{22,... | collective-permute-start | bytes 589832 | tf_op jit(solution)/shard_map/ppermute | solution.py:485

commit v6 on v5

--- a/solution.py
+++ b/solution.py
@@ -20,16 +20,22 @@
 ALL = (0, 1, 2, 3)
 LANES = 128
 VMEM = pl.BlockSpec(memory_space=pltpu.VMEM)
-SMEM = pl.BlockSpec(memory_space=pltpu.SMEM)
-
-
-def call(body, outs, ins, scratch=(), smem=1, flops=1000000, alias=None):
+ANY = pl.BlockSpec(memory_space=pl.ANY)
+
+
+def place():
+    column = lax.axis_index("gx")
+    inside = (column > 0) & (column < lax.axis_size("gx") - 1)
+    return lax.rem(column, 2), lax.axis_index("gy"), lax.axis_index("grp"), inside.astype(jnp.int32)
+
+
+def call(body, outs, ins, scratch=(), away=0, flops=1000000, alias=None):
     shapes = [jax.ShapeDtypeStruct(s, jnp.float32) for s in outs]
     size = sum(o.size for o in shapes) + sum(i.size for i in ins)
     return pl.pallas_call(
-        body,
+        lambda *refs: body(place(), *refs),
         out_shape=shapes,
-        in_specs=[SMEM] * smem + [VMEM] * (len(ins) - smem),
+        in_specs=[ANY] * away + [VMEM] * (len(ins) - away),
         out_specs=[VMEM] * len(shapes),
         scratch_shapes=list(scratch),
         input_output_aliases=alias or {},
@@ -52,15 +58,15 @@
     return np.concatenate([high, high, low])
 
 
-def z_product(F, zmsg, zmat, comps, G):
+def z_product(F, zmsg, zmat, comps, G, half):
     _, T, X, Y, _ = F.shape
     X, Y = X - 6, Y - 16
     for n, c in enumerate(comps):
         tiles = [F[c, t, 3 : 3 + X, 8 : 8 + Y, :].reshape(X * Y, LANES) for t in range(T)]
-        tiles.append(zmsg[n].reshape(X * Y, LANES))
+        tiles.append(zmsg[n * X : (n + 1) * X].reshape(X * Y, LANES))
         high = [tile.astype(jnp.bfloat16) for tile in tiles]
         low = [(tile - top.astype(jnp.float32)).astype(jnp.bfloat16) for tile, top in zip(tiles, high)]
-        out = jnp.dot(jnp.concatenate(high + low + high, axis=1), zmat[...], preferred_element_type=jnp.float32)
+        out = jnp.dot(jnp.concatenate(high + low + high, axis=1), zmat[half], preferred_element_type=jnp.float32)
         for t in range(T):
             G[n, t] = out[:, t * LANES : (t + 1) * LANES].reshape(X, Y, LANES)
 
@@ -109,9 +115,9 @@
             for t in range(T):
                 first = pltpu.roll(get(ycomps[2 * n], t, i, pl.ds(ys, 8)), turn, 0)
                 second = pltpu.roll(get(ycomps[2 * n + 1], t, i, pl.ds(ys, 8)), 4 - turn, 0)
-                ymsg[n, t, i] = jnp.where(rows < 4, first, second)
+                ymsg[(n * T + t) * X + i] = jnp.where(rows < 4, first, second)
         for n, c in enumerate(zcomps):
-            zmsg[n, i] = get(c, edge, i, slice(None))
+            zmsg[n * X + i] = get(c, edge, i, slice(None))
 
     if layers is None:
         lax.fori_loop(0, X, lambda i, carry: (one(i), carry)[1], 0, unroll=4)
@@ -130,7 +136,7 @@
             for c in range(4):
                 F[c, t, i + 3, y, :] = f[c, t, i]
             for n, c in enumerate(ycomps):
-                tile = ymsg[n // 2, t, i]
+                tile = ymsg[(n // 2 * T + t) * X + i]
                 turned = pltpu.roll(tile, 4, 0)
                 if n % 2:
                     tile, turned = turned, tile
@@ -182,10 +188,10 @@
     lax.fori_loop(0, X, step, 0, unroll=4)
 
 
-def first_main(info, f, near_in, near_out, ymsg, zmsg, zmat, mach, S, o, base, F, G):
+def first_main(info, f, near_in, near_out, ymsg, zmsg, zmat, mach, S, o, base, F, G, *, near_base):
     Y = f.shape[3]
-    fill(F, f, (near_in, near_out), (), ymsg, RATE_Y, info)
-    z_product(F, zmsg, zmat, RATE_Z, G)
+    fill(F, f, (near_in.at[near_base:], near_out.at[near_base:]), (), ymsg, RATE_Y, info)
+    z_product(F, zmsg, zmat, RATE_Z, G, info[2])
 
     def emit(c, t, i, value):
         center = F[c, t, i + 3, 8 : 8 + Y, :]
@@ -198,7 +204,7 @@
 def second_main(info, f, near_in, near_out, far_in, far_out, ymsg, zmsg, zmat, mach, S, base, o, F, G):
     Y = f.shape[3]
     fill(F, f, (near_in, near_out), (far_in, far_out), ymsg, RATE_Y, info)
-    z_product(F, zmsg, zmat, RATE_Z, G)
+    z_product(F, zmsg, zmat, RATE_Z, G, info[2])
 
     def emit(c, t, i, value):
         o[c, t, i] = 0.5 * (base[c, t, i] + F[c, t, i + 3, 8 : 8 + Y, :]) + (0.5 * wave_step) * value
@@ -209,7 +215,7 @@
 def smooth_main(info, f, near_in, near_out, far_in, far_out, ymsg, zmsg, zmat, o, F, G, *, last):
     _, T, X, Y, _ = f.shape
     fill(F, f, (near_in, near_out), (far_in, far_out), ymsg, ALL, info)
-    z_product(F, zmsg, zmat, ALL, G)
+    z_product(F, zmsg, zmat, ALL, G, info[2])
     y = slice(8, 8 + Y)
 
     def step(i, carry):
@@ -245,14 +251,14 @@
                     o[c, layer(d), :, lane] = f[c, layer(d), :, lane] - weight * part
 
 
-def edge_body(info, f, halo_in, halo_out, *rest, smooth, scale, ycomps, zcomps):
+def edge_body(info, f, halo_in, halo_out, *rest, smooth, scale, ycomps, zcomps, halo_base):
     rest = list(rest)
     mach, *terms = (None, None, None) if smooth else [rest.pop(0) for _ in range(3)]
     *done, ymsg, zmsg = rest
     sides = [done[:1], done[1:]] if smooth else [done[:2], done[2:]]
     _, T, X, Y, _ = f.shape
     deep = 3 if smooth else 3 + sides[0][1].shape[0] // (4 * T)
-    for side, halo in enumerate((halo_in, halo_out)):
+    for side, halo in enumerate((halo_in.at[halo_base:], halo_out.at[halo_base:])):
         near = sides[side][0]
         high, has, layer, place = ends(info, side == 0, X, deep)
         sign = (jnp.where(high, scale, -scale) * has).astype(jnp.float32)
@@ -313,7 +319,7 @@
     pack_sides(info, lambda c, t, i, rows: o[c, t, i, rows, :], ymsg, zmsg, RATE_Y, RATE_Z, X, Y, T, None)
 
 
-def pack_les(get, shape, inner, outer, ymsg, zmsg, info, base=0):
+def pack_les(get, shape, inner, outer, ymsg, zmsg, info, base=0, ybase=0, zbase=0):
     pos, row, half = info[0], info[1], info[2]
     _, T, X, Y, _ = shape
     si = jnp.where(pos == 0, X - 1, 0)
@@ -330,12 +336,12 @@
                 for r in range(8):
                     tile = get(c, t, 8 * n + r, pl.ds(ys, 8))
                     acc = jnp.where(rows == r, pltpu.roll(tile, turn[r], 0), acc)
-                ymsg[c, t, n] = acc
+                ymsg[ybase + (c * T + t) * (X // 8) + n] = acc
 
     def step(i, carry):
         for c in range(3):
             last, first = get(c, T - 1, i, slice(None)), get(c, 0, i, slice(None))
-            zmsg[c, i] = jnp.where(half == 0, last, first)
+            zmsg[zbase + c * X + i] = jnp.where(half == 0, last, first)
         return carry
 
     lax.fori_loop(0, X, step, 0, unroll=4)
@@ -352,11 +358,13 @@
     pack_les(getter(v), (3, Z // LANES, X, Y, LANES), inner, outer, ymsg, zmsg, info)
 
 
-def les_body(info, offset, v, inner, outer, ymsg, zmsg, tiles, *rest, base, advance):
+def les_body(info, offsets, v, inner, outer, ymsg, zmsg, tiles, *rest, base, ybase, zbase, advance):
     if advance:
-        state, v1, own, n_in, n_out, ny, nz, f, fy, fz, V, LB, ACC = rest
+        state, v1, own, n_in, n_out, f, ny, nz, V, LB, ACC, offset, sem = rest
     else:
-        own, n_in, n_out, V, LB, ACC = rest
+        own, n_in, n_out, V, LB, ACC, offset, sem = rest
+    copy_in = pltpu.make_async_copy(offsets, offset, sem)
+    copy_in.start()
     pos, row, half = info[0], info[1], info[2]
     _, T, X, Y, _ = V.shape
     X, Y = X - 2, Y - 16
@@ -371,7 +379,7 @@
             V[c, t, hi, 8 : 8 + Y, :] = inner[base + c * T + t]
             V[c, t, ho, 8 : 8 + Y, :] = known(outer[base + c * T + t], info[3])
             for n in range(X // 8):
-                tile = ymsg[c, t, n]
+                tile = ymsg[ybase + (c * T + t) * (X // 8) + n]
                 zero = jnp.zeros_like(tile)
                 for r in range(8):
                     low = pltpu.roll(tile, 7 - r, 0) if r < 7 else tile
@@ -394,7 +402,7 @@
         center = [[V[c, t, i + 1, y, :] for t in range(T)] for c in range(3)]
         ahead, behind = [], []
         for c in range(3 if advance else 2):
-            left, right = side_tiles(zmsg[c, i], half)
+            left, right = side_tiles(zmsg[zbase + c * X + i], half)
             ahead.append(shift_tiles(center[c], left, right, 1, lanes))
             behind.append(shift_tiles(center[c], left, right, -1, lanes))
         at = lax.rem(i, 2 * wide) * Y
@@ -423,6 +431,7 @@
 
     lax.fori_loop(0, X, step, 0, unroll=4)
 
+    copy_in.wait()
     for m in range(blocks // 2):
         a, b = [[tiles[2 * m + n, k] for k in (0, 1)] for n in (0, 1)]
         parts = [
@@ -452,8 +461,8 @@
                 n_in[(c * T + t) * wide + l] = ACC[c, t, ti + l]
                 n_out[(c * T + t) * wide + l] = ACC[c, t, to + l]
     if advance:
-        pack_les(getter(v1), v1.shape, n_in, n_out, ny, nz, info, 3 * T * wide)
-        pack_whole(info, state, f, n_in, n_out, 3 * T * (wide + 1), fy, fz)
+        pack_whole(info, state, f, n_in, n_out, 3 * T * (wide + 1), ny, nz)
+        pack_les(getter(v1), v1.shape, n_in, n_out, ny, nz, info, 3 * T * wide, T * f.shape[2], 2 * f.shape[2])
 
 
 def solution(mesh):
@@ -493,23 +502,22 @@
         T = Z // LANES
         blocks, plane = transfer_tiles.shape[0], transfer_tiles.shape[-1]
         wide = plane // Y
-        column = lax.axis_index("gx")
-        half = lax.axis_index("grp")
-        has = (column > 0) & (column < gx - 1)
-        info = jnp.stack([column % 2, lax.axis_index("gy"), half, has.astype(jnp.int32)]).astype(jnp.int32)
         v = les_velocity.transpose(0, 2, 1, 3)
         state = acoustic_state.transpose(2, 0, 1, 3)
-        rate_z = jnp.where(half == 0, *(banded(Z, deriv, -1, h) for h in (0, 1)))
-        smooth_z = jnp.where(half == 0, *(banded(Z, [-filter_weight * w for w in taps[1:]], 1, h) for h in (0, 1)))
+        rate_z, smooth_z = (
+            jnp.asarray(np.stack([banded(Z, weights, sign, h) for h in (0, 1)]))
+            for weights, sign in ((deriv, -1), ([-filter_weight * w for w in taps[1:]], 1))
+        )
         mach = jnp.broadcast_to(mean_mach[:, :, None], (X, Y, LANES))
 
         grid = (4, T, X, Y, LANES)
         source = (3, T, X, Y, LANES)
         near, far = (12 * T, Y, LANES), (4 * T * (wide - 3), Y, LANES)
         term = (3 * T * wide, Y, LANES)
-        edge_y, edge_yy = (1, T, X, 8, LANES), (2, T, X, 8, LANES)
-        edge_z, edge_zz = (2, X, Y, LANES), (4, X, Y, LANES)
-        les_x, les_y, les_z = (3 * T, Y, LANES), (3, T, X2 // 8, 8, LANES), (3, X2, Y, LANES)
+        edge_y, edge_yy = (T * X, 8, LANES), (2 * T * X, 8, LANES)
+        edge_z, edge_zz = (2 * X, Y, LANES), (4 * X, Y, LANES)
+        les_x, les_y, les_z = (3 * T, Y, LANES), (3 * T * X2 // 8, 8, LANES), (3 * X2, Y, LANES)
+        both_y, both_z = [(a[0] + b[0], *a[1:]) for a, b in ((edge_y, les_y), (edge_z, les_z))]
         F = pltpu.VMEM((4, T, X + 6, Y + 16, LANES), jnp.float32)
         G2 = pltpu.VMEM((2, T, X, Y, LANES), jnp.float32)
         G4 = pltpu.VMEM((4, T, X, Y, LANES), jnp.float32)
@@ -517,58 +525,64 @@
             pltpu.VMEM((3, T, X2 + 2, Y + 16, LANES), jnp.float32),
             pltpu.VMEM((blocks // 2, 4 * plane, 3 * Z), jnp.bfloat16),
             pltpu.VMEM((3, T, X + 2 * wide, Y, LANES), jnp.float32),
+            pltpu.SMEM((blocks,), jnp.int32),
+            pltpu.SemaphoreType.DMA(()),
         ]
-        def complete(part, halos, shared, scale, next_y, next_z):
+        def complete(part, halos, shared, scale, next_y, next_z, halo_base=0):
             smooth = not shared
             shapes = [near, near] if smooth else [near, far, near, far]
             sides = [edge_y, edge_z] if next_y == RATE_Y else [edge_yy, edge_zz]
             *done, ymsg, zmsg = call(
-                functools.partial(edge_body, smooth=smooth, scale=scale, ycomps=next_y, zcomps=next_z),
+                functools.partial(
+                    edge_body, smooth=smooth, scale=scale, ycomps=next_y, zcomps=next_z, halo_base=halo_base
+                ),
                 [*shapes, *sides],
-                [info, part, *halos, *([shared[0], *shared[1]] if shared else [])],
+                [part, *halos, *([shared[0], *shared[1]] if shared else [])],
             )
             nears, fars = (done, []) if smooth else (done[::2], done[1::2])
             return [part, *nears], fars, send_sides(ymsg, zmsg), (send_in(nears[0]), send_out(nears[1]))
 
-        v_in, v_out, *sides = call(pack_les_body, [les_x, les_x, les_y, les_z], [info, v])
+        v_in, v_out, *sides = call(pack_les_body, [les_x, les_x, les_y, les_z], [v])
         les_edges = [send_in(v_in), send_out(v_out), *send_sides(*sides)]
         tiles = transfer_tiles[:, 0]
         at = term[0] + 3 * T
         joint = (at + near[0], Y, LANES)
-        v1, S, *own, les_ym, les_zm, state, ym, zm = call(
-            functools.partial(les_body, base=0, advance=True),
-            [(3, T, X2, Y, LANES), source, joint, joint, les_y, les_z, grid, edge_y, edge_z],
-            [info, intersection_offset, v, *les_edges, tiles, state],
+        v1, S, *own, state, ym, zm = call(
+            functools.partial(les_body, base=0, ybase=0, zbase=0, advance=True),
+            [(3, T, X2, Y, LANES), source, joint, joint, grid, both_y, both_z],
+            [intersection_offset, v, *les_edges, tiles, state],
             les_scratch,
-            smem=2,
+            away=1,
             flops=4000000,
         )
         terms = (send_in(own[0]), send_out(own[1]))
         sides = send_sides(ym, zm)
-        les_edges = [*terms, *send_sides(les_ym, les_zm)]
-        near_in, near_out = (message[at:] for message in own)
-        halos = [message[at:] for message in terms]
+        les_edges = [*terms, *sides]
+        near_in, near_out = own
+        halos = terms
         whole = [state, near_in, near_out]
         for step in range(STEPS):
             if step:
                 whole[1], terms = lax.optimization_barrier((whole[1], terms))
             part, base = call(
-                first_main, [grid, grid], [info, *whole, *sides, rate_z, mach, S], [F, G2], flops=4000000
+                functools.partial(first_main, near_base=at if step == 0 else 0), [grid, grid], [*whole, *sides, rate_z, mach, S], [F, G2], flops=4000000
             )
-            whole, fars, sides, halos = complete(part, halos, (mach, terms), wave_step, RATE_Y, RATE_Z)
+            whole, fars, sides, halos = complete(
+                part, halos, (mach, terms), wave_step, RATE_Y, RATE_Z, at if step == 0 else 0
+            )
             if step + 1 < STEPS:
                 S2, *terms2 = call(
-                    functools.partial(les_body, base=term[0], advance=False),
+                    functools.partial(les_body, base=term[0], ybase=edge_y[0], zbase=edge_z[0], advance=False),
                     [source, term, term],
-                    [info, intersection_offset, v1, *les_edges, tiles],
+                    [intersection_offset, v1, *les_edges, tiles],
                     les_scratch,
-                    smem=2,
+                    away=1,
                     flops=4000000,
                 )
-                info, S2, *terms2 = lax.optimization_barrier((info, S2, *terms2))
+                whole[1], S2, *terms2 = lax.optimization_barrier((whole[1], S2, *terms2))
                 terms2 = (send_in(terms2[0]), send_out(terms2[1]))
             (part,) = call(
-                second_main, [grid], [info, *whole, *fars, *sides, rate_z, mach, S, base], [F, G2], flops=4000000
+                second_main, [grid], [*whole, *fars, *sides, rate_z, mach, S, base], [F, G2], flops=4000000
             )
             whole, fars, sides, halos = complete(part, halos, (mach, terms), 0.5 * wave_step, ALL, ALL)
             if step + 1 < STEPS:
@@ -576,7 +590,7 @@
                 (part,) = call(
                     functools.partial(smooth_main, last=False),
                     [grid],
-                    [info, *whole, *fars, *sides, smooth_z],
+                    [*whole, *fars, *sides, smooth_z],
                     [F, G4],
                     flops=4000000,
                 )
@@ -584,11 +598,11 @@
         (part,) = call(
             functools.partial(smooth_main, last=True),
             [(4, X, Y, Z)],
-            [info, *whole, *fars, *sides, smooth_z],
+            [*whole, *fars, *sides, smooth_z],
             [F, G4],
             flops=4000000,
         )
-        (state,) = call(last_body, [(4, X, Y, Z)], [info, part, *halos], alias={1: 0})
+        (state,) = call(last_body, [(4, X, Y, Z)], [part, *halos], alias={0: 0})
         return state.transpose(1, 2, 0, 3)
 
     placed = (

time: 108 us -> 104 us (0.963)
  Pallas kernels: 25.6 us -> 17.2 us
  waiting for transfers between devices: 57.7 us -> 62.5 us
    pallas_call x15, Pallas kernels: 25.6 us -> 17.2 us  [call(): pl.pallas_call(lambda *refs: body(place(), *refs), out_shape=shapes, in_s...]
    ppermute x8, waiting for transfers between devices: 26.3 us -> 30.9 us  [send_in(): return lax.ppermute(message, 'gx', even)]
    ppermute x16 -> x14, waiting for transfers between devices: 24.4 us -> 25.1 us  [send_sides(): return (lax.ppermute(ymsg, 'gy', swap), lax.ppermute(zmsg, 'grp', swap))]
    ppermute x16 -> x14, starting transfers between devices: 8.08 us -> 8.37 us  [send_sides(): return (lax.ppermute(ymsg, 'gy', swap), lax.ppermute(zmsg, 'grp', swap))]
    unnamed x19 -> x15, local copies, waits for them, and re-layouts: 2.88 us -> 2.87 us
  transfers between devices with their start and end apart: 32 -> 30, of which waited for: 14 -> 15; matrix products, arithmetic and copies ran while one was open for 2% -> 1% of each run, Pallas kernels for 16% -> 12%
where the time goes in v6:
time: 104 us
  waiting for transfers between devices  62.5 us (60%)
  starting transfers between devices  19.1 us (18%)
  Pallas kernels  17.2 us (17%)
  local copies, waits for them, and re-layouts  4.63 us (4%)
    ppermute x8, waiting for transfers between devices, send_in(): return lax.ppermute(message, 'gx', even)  30.9 us
    ppermute x14, waiting for transfers between devices, send_sides(): return (lax.ppermute(ymsg, 'gy', swap), lax.ppermute(zmsg, 'grp', swap))  25.1 us
    pallas_call x15, Pallas kernels, call(): pl.pallas_call(lambda *refs: body(place(), *refs), out_shape=shapes, in_s...  17.2 us
    ppermute x8, starting transfers between devices, send_in(): return lax.ppermute(message, 'gx', even)  10.3 us
    ppermute x14, starting transfers between devices, send_sides(): return (lax.ppermute(ymsg, 'gy', swap), lax.ppermute(zmsg, 'grp', swap))  8.37 us
    ppermute x8, waiting for transfers between devices, send_out(): return lax.ppermute(message, mesh.axis_names, hops)  6.44 us
    unnamed x15, local copies, waits for them, and re-layouts  2.87 us
  transfers between devices with their start and end apart: 30, of which 15 were waited for; matrix products, arithmetic and copies ran while one was open for 1% of the time, Pallas kernels for 12%

profile of v6, /device:TPU:8, one launch (start us, length us, event | category | flops | bytes accessed | tf_op | source)
XLA Modules:
  0.0 103.6 jit_solution(18356840179962152442)
XLA Ops:
  0.0 1.4 %copy-done.1 = f32[32,16,3,256]{3,1,2,0:T(8,128)S(1)} copy-done((f32[32,16,3,256]{3,1,2,0:T(8,128)S(1)}, f32[32,16,3,256]{3,1,2,0:T(8,128)}, u32[]{:S(2)}) %copy-start.1) | copy-done | bytes 1572888
  1.4 0.2 shard_map.73
  1.7 1.6 %collective-permute-start.2 = (f32[24,8,128]{2,1,0:T(8,128)S(1)}, f32[24,8,128]{2,1,0:T(8,128)S(1)}, u32[]{:S(2)}, u32[]{:S(2)}) collective-permute-start(f32[24,8,128]{2,1,0:T(8,128)S(1)} %get-tuple-element.60), channel_id=1, source_target_pairs={{0,1},{1,0},{2,3},{3,2},{4,5},{5,4},{6,7},{7,6},{8,9},{9,8},{10,11... | collective-permute-start | bytes 294920 | tf_op jit(solution)/shard_map/ppermute | solution.py:497
  3.3 1.5 %collective-permute-start = (f32[6,16,128]{2,1,0:T(8,128)S(1)}, f32[6,16,128]{2,1,0:T(8,128)S(1)}, u32[]{:S(2)}, u32[]{:S(2)}) collective-permute-start(f32[6,16,128]{2,1,0:T(8,128)S(1)} %get-tuple-element.58), channel_id=1, source_target_pairs={{0,2},{2,0},{4,6},{6,4},{8,10},{10,8},{12,14},{14,12},{1,3},{3,1},... | collective-permute-start | bytes 147464 | tf_op jit(solution)/shard_map/ppermute | solution.py:491
  4.8 0.4 collective-permute-start.1
  5.2 1.4 %copy.12 = f32[16,16,4,256]{3,1,0,2:T(8,128)S(1)} copy(f32[16,16,4,256]{3,2,1,0:T(4,128)} %param.11) | data formatting | bytes 2097152 | tf_op args[4]
  6.6 0.7 collective-permute-done.refs_2_
  7.4 2.4 %collective-permute-done.1.refs_3_ = f32[6,16,128]{2,1,0:T(8,128)S(1)} collective-permute-done((f32[6,16,128]{2,1,0:T(8,128)S(1)}, f32[6,16,128]{2,1,0:T(8,128)S(1)}, u32[]{:S(2)}, u32[]{:S(2)}) %collective-permute-start.1) | collective-permute-done | bytes 49184 | tf_op jit(solution)/shard_map/ppermute | solution.py:494
  9.8 3.3 %shard_map.74 = (f32[3,2,32,16,128]{4,3,2,1,0:T(8,128)S(1)}, f32[3,2,16,16,128]{4,3,2,1,0:T(8,128)S(1)}, f32[54,16,128]{2,1,0:T(8,128)S(1)}, f32[54,16,128]{2,1,...) custom-call(s32[8]{0:T(128)S(1)} %copy-done.5, ...), custom_call_target="tpu_custom_call" | custom-call | flops 4000000 | bytes 9437216 | tf_op jit(solution)/shard_map/pallas_call | solution.py:35
  13.2 0.6 collective-permute-start.6
  13.8 0.5 collective-permute-start.4
  14.3 7.2 %collective-permute-done.4.refs_3_.refs_4_ = f32[56,8,128]{2,1,0:T(8,128)S(1)} collective-permute-done((f32[56,8,128]{2,1,0:T(8,128)S(1)}, f32[56,8,128]{2,1,0:T(8,128)S(1)}, u32[]{:S(2)}, u32[]{:S(2)}) %collective-permute-start.4) | collective-permute-done | bytes 229408 | tf_op jit(solution)/shard_map/ppermute | solution.py:497
  21.6 1.5 %shard_map.75 = (f32[4,2,16,16,128]{4,3,2,1,0:T(8,128)S(1)}, f32[4,2,16,16,128]{4,3,2,1,0:T(8,128)S(1)}) custom-call(f32[4,2,16,16,128]{4,3,2,1,0:T(8,128)S(1)} %get-tuple-element.62.refs_0_, f32[54,16,128]{2,1,0:T(8,128)S(1)} %get-tuple-element.63.refs_1_, f32[54,16,128]{2,1,0:T(8,128)S(1)} %get-tuple-element.64.refs_2_, ...), custom_call_target="tpu_custom_call" | custom-call | flops 4000000 | bytes 8585216 | tf_op jit(solution)/shard_map/pallas_call | solution.py:35
  23.1 12.2 %collective-permute-done.6.refs_1_.refs_4_.refs_2_ = f32[54,16,128]{2,1,0:T(8,128)S(1)} collective-permute-done((f32[54,16,128]{2,1,0:T(8,128)S(1)}, f32[54,16,128]{2,1,0:T(8,128)S(1)}, u32[]{:S(2)}, u32[]{:S(2)}) %collective-permute-start.6) | collective-permute-done | bytes 442400 | tf_op jit(solution)/shard_map/ppermute | solution.py:491
  35.3 0.2 shard_map.76
  35.6 0.6 collective-permute-start.10
  36.1 0.5 collective-permute-start.8
  36.6 2.4 %shard_map.77 = (f32[3,2,16,16,128]{4,3,2,1,0:T(8,128)S(1)}, f32[24,16,128]{2,1,0:T(8,128)S(1)}, f32[24,16,128]{2,1,0:T(8,128)S(1)}) custom-call(s32[8]{0:T(128)S(1)} %copy-done.5, f32[3,2,32,16,128]{4,3,2,1,0:T(8,128)S(1)} %get-tuple-element.70.refs_1_, f32[54,16,128]{2,1,0:T(8,128)S(1)} %collective-permute-done.6.refs_1_.refs_4_.refs_2_, ...), custom_call_target="tpu_custom_call" | custom-call | flops 4000000 | bytes 5177376 | tf_op jit(solution)/shard_map/pallas_call | solution.py:35
  39.1 2.7 %collective-permute-done.8.refs_5_ = f32[32,8,128]{2,1,0:T(8,128)S(1)} collective-permute-done((f32[32,8,128]{2,1,0:T(8,128)S(1)}, f32[32,8,128]{2,1,0:T(8,128)S(1)}, u32[]{:S(2)}, u32[]{:S(2)}) %collective-permute-start.8) | collective-permute-done | bytes 131104 | tf_op jit(solution)/shard_map/ppermute | solution.py:497
  41.7 1.6 %shard_map.78.refs_0_ = f32[4,2,16,16,128]{4,3,2,1,0:T(8,128)S(1)} custom-call(f32[4,2,16,16,128]{4,3,2,1,0:T(8,128)S(1)} %get-tuple-element.68.refs_0_, f32[24,16,128]{2,1,0:T(8,128)S(1)} %get-tuple-element.74.refs_1_, f32[24,16,128]{2,1,0:T(8,128)S(1)} %get-tuple-element.75.refs_2_, f32[8,16,128]{2,1,0:T(8,128)S(1)} %get-tuple-element.76.refs_3_, ...), custom_call_target="tpu_custom_call" | custom-call | flops 4000000 | bytes 7340032 | tf_op jit(solution)/shard_map/pallas_call | solution.py:35
  43.3 3.8 %collective-permute-done.10.refs_1_ = f32[24,16,128]{2,1,0:T(8,128)S(1)} collective-permute-done((f32[24,16,128]{2,1,0:T(8,128)S(1)}, f32[24,16,128]{2,1,0:T(8,128)S(1)}, u32[]{:S(2)}, u32[]{:S(2)}) %collective-permute-start.10) | collective-permute-done | bytes 196640 | tf_op jit(solution)/shard_map/ppermute | solution.py:491
  47.1 0.3 shard_map.79
  47.5 0.5 collective-permute-start.12
  48.0 0.5 collective-permute-start.14
  48.5 3.1 %collective-permute-start.16 = (f32[24,16,128]{2,1,0:T(8,128)S(1)}, f32[24,16,128]{2,1,0:T(8,128)S(1)}, u32[]{:S(2)}, u32[]{:S(2)}) collective-permute-start(f32[24,16,128]{2,1,0:T(8,128)S(1)} %get-tuple-element.88), channel_id=1, source_target_pairs={{0,2},{2,0},{4,6},{6,4},{8,10},{10,8},{12,14},{14,12},{1,3},{3,1},... | collective-permute-start | bytes 589832 | tf_op jit(solution)/shard_map/ppermute | solution.py:491
  51.6 4.6 %collective-permute-done.12.refs_5_ = f32[64,8,128]{2,1,0:T(8,128)S(1)} collective-permute-done((f32[64,8,128]{2,1,0:T(8,128)S(1)}, f32[64,8,128]{2,1,0:T(8,128)S(1)}, u32[]{:S(2)}, u32[]{:S(2)}) %collective-permute-start.12) | collective-permute-done | bytes 262176 | tf_op jit(solution)/shard_map/ppermute | solution.py:497
  56.2 1.9 %shard_map.80.refs_0_ = f32[4,2,16,16,128]{4,3,2,1,0:T(8,128)S(1)} custom-call(f32[4,2,16,16,128]{4,3,2,1,0:T(8,128)S(1)} %shard_map.78.refs_0_, f32[24,16,128]{2,1,0:T(8,128)S(1)} %get-tuple-element.81.refs_1_, f32[24,16,128]{2,1,0:T(8,128)S(1)} %get-tuple-element.82.refs_2_, f32[8,16,128]{2,1,0:T(8,128)S(1)} %get-tuple-element.83.refs_3_, ...), custom_call_target="tpu_custom_call" | custom-call | flops 4000000 | bytes 5767168 | tf_op jit(solution)/shard_map/pallas_call | solution.py:35
  58.1 1.9 %collective-permute-done.14.refs_1_ = f32[24,16,128]{2,1,0:T(8,128)S(1)} collective-permute-done((f32[24,16,128]{2,1,0:T(8,128)S(1)}, f32[24,16,128]{2,1,0:T(8,128)S(1)}, u32[]{:S(2)}, u32[]{:S(2)}) %collective-permute-start.14) | collective-permute-done | bytes 196640 | tf_op jit(solution)/shard_map/ppermute | solution.py:491
  60.0 0.2 shard_map.81
  60.3 3.0 %collective-permute-start.20 = (f32[24,16,128]{2,1,0:T(8,128)S(1)}, f32[24,16,128]{2,1,0:T(8,128)S(1)}, u32[]{:S(2)}, u32[]{:S(2)}) collective-permute-start(f32[24,16,128]{2,1,0:T(8,128)S(1)} %get-tuple-element.90.refs_1_), channel_id=1, source_target_pairs={{0,2},{2,0},{4,6},{6,4},{8,10},{10,8},{12,14},{14,12},{1,3},{3,1},... | collective-permute-start | bytes 589832 | tf_op jit(solution)/shard_map/ppermute | solution.py:491
  63.4 1.5 %collective-permute-start.18 = (f32[32,8,128]{2,1,0:T(8,128)S(1)}, f32[32,8,128]{2,1,0:T(8,128)S(1)}, u32[]{:S(2)}, u32[]{:S(2)}) collective-permute-start(f32[32,8,128]{2,1,0:T(8,128)S(1)} %get-tuple-element.92), channel_id=1, source_target_pairs={{0,1},{1,0},{2,3},{3,2},{4,5},{5,4},{6,7},{7,6},{8,9},{9,8},{10,11... | collective-permute-start | bytes 393224 | tf_op jit(solution)/shard_map/ppermute | solution.py:497
  65.0 4.0 %collective-permute-done.17.refs_5_ = f32[24,16,128]{2,1,0:T(8,128)S(1)} collective-permute-done((f32[24,16,128]{2,1,0:T(8,128)S(1)}, f32[24,16,128]{2,1,0:T(8,128)S(1)}, u32[]{:S(2)}, u32[]{:S(2)}) %collective-permute-start.17) | collective-permute-done | bytes 196640 | tf_op jit(solution)/shard_map/ppermute | solution.py:494
  69.0 1.5 %shard_map.82 = (f32[4,2,16,16,128]{4,3,2,1,0:T(8,128)S(1)}, f32[4,2,16,16,128]{4,3,2,1,0:T(8,128)S(1)}) custom-call(f32[4,2,16,16,128]{4,3,2,1,0:T(8,128)S(1)} %shard_map.80.refs_0_, f32[24,16,128]{2,1,0:T(8,128)S(1)} %get-tuple-element.90.refs_1_, f32[24,16,128]{2,1,0:T(8,128)S(1)} %get-tuple-element.91.refs_2_, ...), custom_call_target="tpu_custom_call" | custom-call | flops 4000000 | bytes 7208960 | tf_op jit(solution)/shard_map/pallas_call | solution.py:35
  70.5 6.4 %collective-permute-done.20.refs_1_ = f32[24,16,128]{2,1,0:T(8,128)S(1)} collective-permute-done((f32[24,16,128]{2,1,0:T(8,128)S(1)}, f32[24,16,128]{2,1,0:T(8,128)S(1)}, u32[]{:S(2)}, u32[]{:S(2)}) %collective-permute-start.20) | collective-permute-done | bytes 196640 | tf_op jit(solution)/shard_map/ppermute | solution.py:491
  76.9 0.2 shard_map.83
  77.1 0.1 collective-permute-start.23
  77.2 0.5 collective-permute-start.24
  77.8 1.5 %collective-permute-start.22 = (f32[32,8,128]{2,1,0:T(8,128)S(1)}, f32[32,8,128]{2,1,0:T(8,128)S(1)}, u32[]{:S(2)}, u32[]{:S(2)}) collective-permute-start(f32[32,8,128]{2,1,0:T(8,128)S(1)} %get-tuple-element.102), channel_id=1, source_target_pairs={{0,1},{1,0},{2,3},{3,2},{4,5},{5,4},{6,7},{7,6},{8,9},{9,8},{10,11... | collective-permute-start | bytes 393224 | tf_op jit(solution)/shard_map/ppermute | solution.py:497
  79.3 4.0 %collective-permute-done.22.refs_5_ = f32[32,8,128]{2,1,0:T(8,128)S(1)} collective-permute-done((f32[32,8,128]{2,1,0:T(8,128)S(1)}, f32[32,8,128]{2,1,0:T(8,128)S(1)}, u32[]{:S(2)}, u32[]{:S(2)}) %collective-permute-start.22) | collective-permute-done | bytes 131104 | tf_op jit(solution)/shard_map/ppermute | solution.py:497
  83.3 1.6 %shard_map.84.refs_0_ = f32[4,2,16,16,128]{4,3,2,1,0:T(8,128)S(1)} custom-call(f32[4,2,16,16,128]{4,3,2,1,0:T(8,128)S(1)} %get-tuple-element.95.refs_0_, f32[24,16,128]{2,1,0:T(8,128)S(1)} %get-tuple-element.98.refs_1_, f32[24,16,128]{2,1,0:T(8,128)S(1)} %get-tuple-element.99.refs_2_, f32[8,16,128]{2,1,0:T(8,128)S(1)} %get-tuple-element.100.refs_3_, ...), custom_call_target="tpu_custom_call" | custom-call | flops 4000000 | bytes 7340032 | tf_op jit(solution)/shard_map/pallas_call | solution.py:35
  84.9 3.8 %collective-permute-done.24.refs_1_ = f32[24,16,128]{2,1,0:T(8,128)S(1)} collective-permute-done((f32[24,16,128]{2,1,0:T(8,128)S(1)}, f32[24,16,128]{2,1,0:T(8,128)S(1)}, u32[]{:S(2)}, u32[]{:S(2)}) %collective-permute-start.24) | collective-permute-done | bytes 196640 | tf_op jit(solution)/shard_map/ppermute | solution.py:491
  88.7 0.3 shard_map.85
  89.1 1.6 %collective-permute-start.26 = (f32[64,8,128]{2,1,0:T(8,128)S(1)}, f32[64,8,128]{2,1,0:T(8,128)S(1)}, u32[]{:S(2)}, u32[]{:S(2)}) collective-permute-start(f32[64,8,128]{2,1,0:T(8,128)S(1)} %get-tuple-element.109), channel_id=1, source_target_pairs={{0,1},{1,0},{2,3},{3,2},{4,5},{5,4},{6,7},{7,6},{8,9},{9,8},{10,11... | collective-permute-start | bytes 786440 | tf_op jit(solution)/shard_map/ppermute | solution.py:497
  90.6 0.5 collective-permute-start.28
  91.2 6.6 %collective-permute-done.26.refs_5_ = f32[64,8,128]{2,1,0:T(8,128)S(1)} collective-permute-done((f32[64,8,128]{2,1,0:T(8,128)S(1)}, f32[64,8,128]{2,1,0:T(8,128)S(1)}, u32[]{:S(2)}, u32[]{:S(2)}) %collective-permute-start.26) | collective-permute-done | bytes 262176 | tf_op jit(solution)/shard_map/ppermute | solution.py:497
  97.8 1.9 %shard_map.86.refs_0_ = f32[4,16,16,256]{3,2,1,0:T(8,128)S(1)} custom-call(f32[4,2,16,16,128]{4,3,2,1,0:T(8,128)S(1)} %shard_map.84.refs_0_, f32[24,16,128]{2,1,0:T(8,128)S(1)} %get-tuple-element.105.refs_1_, f32[24,16,128]{2,1,0:T(8,128)S(1)} %get-tuple-element.106.refs_2_, f32[8,16,128]{2,1,0:T(8,128)S(1)} %get-tuple-element.107.refs_3_, ...), custom_call_target="tpu_custom_call" | custom-call | flops 4000000 | bytes 5767168 | tf_op jit(solution)/shard_map/pallas_call | solution.py:35
  99.7 2.2 %collective-permute-done.28.refs_1_ = f32[24,16,128]{2,1,0:T(8,128)S(1)} collective-permute-done((f32[24,16,128]{2,1,0:T(8,128)S(1)}, f32[24,16,128]{2,1,0:T(8,128)S(1)}, u32[]{:S(2)}, u32[]{:S(2)}) %collective-permute-start.28) | collective-permute-done | bytes 196640 | tf_op jit(solution)/shard_map/ppermute | solution.py:491
  102.0 1.7 %copy.10 = f32[16,16,4,256]{3,2,1,0:T(4,128)} copy(f32[16,16,4,256]{3,1,0,2:T(8,128)S(1)} %bitcast.6) | data formatting | bytes 2097152 | tf_op jit(solution)/shard_map/transpose | solution.py:606
  (44 shorter events, 0.9 us)
Async XLA Ops:
  0.0 1.4 %copy-start.1 = (f32[32,16,3,256]{3,1,2,0:T(8,128)S(1)}, f32[32,16,3,256]{3,1,2,0:T(8,128)}, u32[]{:S(2)}) copy-start(f32[32,16,3,256]{3,1,2,0:T(8,128)} %param.7) | copy-start | bytes 4718596
  1.4 8.3 %copy-start.2 = (f32[32,16,3,256]{3,1,2,0:T(8,128)S(1)}, f32[32,16,3,256]{3,1,2,0:T(8,128)}, u32[]{:S(2)}) copy-start(f32[32,16,3,256]{3,1,2,0:T(8,128)} %param.7) | copy-start | bytes 4718596
  1.4 8.4 %copy-start.4 = (bf16[8,1,2,64,64]{4,3,2,1,0:T(8,128)(2,1)S(1)}, bf16[8,1,2,64,64]{4,3,2,1,0:T(8,128)(2,1)}, u32[]{:S(2)}) copy-start(bf16[8,1,2,64,64]{4,3,2,1,0:T(8,128)(2,1)} %param.9) | copy-start | bytes 393220
  1.4 8.4 %copy-start.5 = (s32[8]{0:T(128)S(1)}, s32[8]{0:T(128)}, u32[]{:S(2)}) copy-start(s32[8]{0:T(128)} %refs_0_.3) | copy-start | bytes 100
  1.6 8.2 %collective-permute-start.3 = (f32[96,16,128]{2,1,0:T(8,128)S(1)}, f32[96,16,128]{2,1,0:T(8,128)S(1)}, u32[]{:S(2)}, u32[]{:S(2)}) collective-permute-start(f32[96,16,128]{2,1,0:T(8,128)S(1)} %get-tuple-element.61), channel_id=1, source_target_pairs={{0,16},{16,0},{1,17},{17,1},{2,18},{18,2},{3,19},{19,3},{4,20},{20... | collective-permute-start | bytes 2359304 | tf_op jit(solution)/shard_map/ppermute | solution.py:497
  1.7 8.1 %collective-permute-start.2 = (f32[24,8,128]{2,1,0:T(8,128)S(1)}, f32[24,8,128]{2,1,0:T(8,128)S(1)}, u32[]{:S(2)}, u32[]{:S(2)}) collective-permute-start(f32[24,8,128]{2,1,0:T(8,128)S(1)} %get-tuple-element.60), channel_id=1, source_target_pairs={{0,1},{1,0},{2,3},{3,2},{4,5},{5,4},{6,7},{7,6},{8,9},{9,8},{10,11... | collective-permute-start | bytes 294920 | tf_op jit(solution)/shard_map/ppermute | solution.py:497
  3.3 4.1 %collective-permute-start = (f32[6,16,128]{2,1,0:T(8,128)S(1)}, f32[6,16,128]{2,1,0:T(8,128)S(1)}, u32[]{:S(2)}, u32[]{:S(2)}) collective-permute-start(f32[6,16,128]{2,1,0:T(8,128)S(1)} %get-tuple-element.58), channel_id=1, source_target_pairs={{0,2},{2,0},{4,6},{6,4},{8,10},{10,8},{12,14},{14,12},{1,3},{3,1},... | collective-permute-start | bytes 147464 | tf_op jit(solution)/shard_map/ppermute | solution.py:491
  4.8 5.0 %collective-permute-start.1 = (f32[6,16,128]{2,1,0:T(8,128)S(1)}, f32[6,16,128]{2,1,0:T(8,128)S(1)}, u32[]{:S(2)}, u32[]{:S(2)}) collective-permute-start(f32[6,16,128]{2,1,0:T(8,128)S(1)} %get-tuple-element.59), channel_id=1, source_target_pairs={{2,4},{18,20},{3,5},{19,21},{4,2},{20,18},{5,3},{21,19},{6,8},{22,... | collective-permute-start | bytes 147464 | tf_op jit(solution)/shard_map/ppermute | solution.py:494
  9.8 11.7 %copy-start.6 = (f32[16,16]{1,0:T(8,128)S(1)}, f32[16,16]{1,0:T(8,128)}, u32[]{:S(2)}) copy-start(f32[16,16]{1,0:T(8,128)} %param.8) | copy-start | bytes 3076
  9.8 11.8 %copy-start = (bf16[2,1152,256]{2,1,0:T(8,128)(2,1)S(1)}, bf16[2,1152,256]{2,1,0:T(8,128)(2,1)}, u32[]{:S(2)}) copy-start(bf16[2,1152,256]{2,1,0:T(8,128)(2,1)} %constant.4.clone.refs_5_.refs_7_) | copy-start | bytes 3538948
  13.1 8.3 %collective-permute-start.5 = (f32[128,16,128]{2,1,0:T(8,128)S(1)}, f32[128,16,128]{2,1,0:T(8,128)S(1)}, u32[]{:S(2)}, u32[]{:S(2)}) collective-permute-start(f32[128,16,128]{2,1,0:T(8,128)S(1)} %get-tuple-element.66), channel_id=1, source_target_pairs={{0,16},{16,0},{1,17},{17,1},{2,18},{18,2},{3,19},{19,3},{4,20},{20... | collective-permute-start | bytes 3145736 | tf_op jit(solution)/shard_map/ppermute | solution.py:497
  13.2 22.1 %collective-permute-start.6 = (f32[54,16,128]{2,1,0:T(8,128)S(1)}, f32[54,16,128]{2,1,0:T(8,128)S(1)}, u32[]{:S(2)}, u32[]{:S(2)}) collective-permute-start(f32[54,16,128]{2,1,0:T(8,128)S(1)} %get-tuple-element.63.refs_1_), channel_id=1, source_target_pairs={{0,2},{2,0},{4,6},{6,4},{8,10},{10,8},{12,14},{14,12},{1,3},{3,1},... | collective-permute-start | bytes 1327112 | tf_op jit(solution)/shard_map/ppermute | solution.py:491
  13.8 21.5 %collective-permute-start.7 = (f32[54,16,128]{2,1,0:T(8,128)S(1)}, f32[54,16,128]{2,1,0:T(8,128)S(1)}, u32[]{:S(2)}, u32[]{:S(2)}) collective-permute-start(f32[54,16,128]{2,1,0:T(8,128)S(1)} %get-tuple-element.64.refs_2_), channel_id=1, source_target_pairs={{2,4},{18,20},{3,5},{19,21},{4,2},{20,18},{5,3},{21,19},{6,8},{22,... | collective-permute-start | bytes 1327112 | tf_op jit(solution)/shard_map/ppermute | solution.py:494
  13.8 7.7 %collective-permute-start.4 = (f32[56,8,128]{2,1,0:T(8,128)S(1)}, f32[56,8,128]{2,1,0:T(8,128)S(1)}, u32[]{:S(2)}, u32[]{:S(2)}) collective-permute-start(f32[56,8,128]{2,1,0:T(8,128)S(1)} %get-tuple-element.65), channel_id=1, source_target_pairs={{0,1},{1,0},{2,3},{3,2},{4,5},{5,4},{6,7},{7,6},{8,9},{9,8},{10,11... | collective-permute-start | bytes 688136 | tf_op jit(solution)/shard_map/ppermute | solution.py:497
  35.5 6.2 %collective-permute-start.9 = (f32[32,16,128]{2,1,0:T(8,128)S(1)}, f32[32,16,128]{2,1,0:T(8,128)S(1)}, u32[]{:S(2)}, u32[]{:S(2)}) collective-permute-start(f32[32,16,128]{2,1,0:T(8,128)S(1)} %get-tuple-element.79), channel_id=1, source_target_pairs={{0,16},{16,0},{1,17},{17,1},{2,18},{18,2},{3,19},{19,3},{4,20},{20... | collective-permute-start | bytes 786440 | tf_op jit(solution)/shard_map/ppermute | solution.py:497
  35.6 11.5 %collective-permute-start.10 = (f32[24,16,128]{2,1,0:T(8,128)S(1)}, f32[24,16,128]{2,1,0:T(8,128)S(1)}, u32[]{:S(2)}, u32[]{:S(2)}) collective-permute-start(f32[24,16,128]{2,1,0:T(8,128)S(1)} %get-tuple-element.74.refs_1_), channel_id=1, source_target_pairs={{0,2},{2,0},{4,6},{6,4},{8,10},{10,8},{12,14},{14,12},{1,3},{3,1},... | collective-permute-start | bytes 589832 | tf_op jit(solution)/shard_map/ppermute | solution.py:491
  36.1 11.0 %collective-permute-start.11 = (f32[24,16,128]{2,1,0:T(8,128)S(1)}, f32[24,16,128]{2,1,0:T(8,128)S(1)}, u32[]{:S(2)}, u32[]{:S(2)}) collective-permute-start(f32[24,16,128]{2,1,0:T(8,128)S(1)} %get-tuple-element.75.refs_2_), channel_id=1, source_target_pairs={{2,4},{18,20},{3,5},{19,21},{4,2},{20,18},{5,3},{21,19},{6,8},{22,... | collective-permute-start | bytes 589832 | tf_op jit(solution)/shard_map/ppermute | solution.py:494
  36.1 5.6 %collective-permute-start.8 = (f32[32,8,128]{2,1,0:T(8,128)S(1)}, f32[32,8,128]{2,1,0:T(8,128)S(1)}, u32[]{:S(2)}, u32[]{:S(2)}) collective-permute-start(f32[32,8,128]{2,1,0:T(8,128)S(1)} %get-tuple-element.78), channel_id=1, source_target_pairs={{0,1},{1,0},{2,3},{3,2},{4,5},{5,4},{6,7},{7,6},{8,9},{9,8},{10,11... | collective-permute-start | bytes 393224 | tf_op jit(solution)/shard_map/ppermute | solution.py:497
  43.3 12.9 %copy-start.3 = (bf16[2,1152,256]{2,1,0:T(8,128)(2,1)S(1)}, bf16[2,1152,256]{2,1,0:T(8,128)(2,1)}, u32[]{:S(2)}) copy-start(bf16[2,1152,256]{2,1,0:T(8,128)(2,1)} %constant.5.clone.refs_7_) | copy-start | bytes 3538948
  47.4 8.8 %collective-permute-start.13 = (f32[64,16,128]{2,1,0:T(8,128)S(1)}, f32[64,16,128]{2,1,0:T(8,128)S(1)}, u32[]{:S(2)}, u32[]{:S(2)}) collective-permute-start(f32[64,16,128]{2,1,0:T(8,128)S(1)} %get-tuple-element.86), channel_id=1, source_target_pairs={{0,16},{16,0},{1,17},{17,1},{2,18},{18,2},{3,19},{19,3},{4,20},{20... | collective-permute-start | bytes 1572872 | tf_op jit(solution)/shard_map/ppermute | solution.py:497
  47.5 8.7 %collective-permute-start.12 = (f32[64,8,128]{2,1,0:T(8,128)S(1)}, f32[64,8,128]{2,1,0:T(8,128)S(1)}, u32[]{:S(2)}, u32[]{:S(2)}) collective-permute-start(f32[64,8,128]{2,1,0:T(8,128)S(1)} %get-tuple-element.85), channel_id=1, source_target_pairs={{0,1},{1,0},{2,3},{3,2},{4,5},{5,4},{6,7},{7,6},{8,9},{9,8},{10,11... | collective-permute-start | bytes 786440 | tf_op jit(solution)/shard_map/ppermute | solution.py:497
  48.0 12.0 %collective-permute-start.14 = (f32[24,16,128]{2,1,0:T(8,128)S(1)}, f32[24,16,128]{2,1,0:T(8,128)S(1)}, u32[]{:S(2)}, u32[]{:S(2)}) collective-permute-start(f32[24,16,128]{2,1,0:T(8,128)S(1)} %get-tuple-element.81.refs_1_), channel_id=1, source_target_pairs={{0,2},{2,0},{4,6},{6,4},{8,10},{10,8},{12,14},{14,12},{1,3},{3,1},... | collective-permute-start | bytes 589832 | tf_op jit(solution)/shard_map/ppermute | solution.py:491
  48.5 11.5 %collective-permute-start.15 = (f32[24,16,128]{2,1,0:T(8,128)S(1)}, f32[24,16,128]{2,1,0:T(8,128)S(1)}, u32[]{:S(2)}, u32[]{:S(2)}) collective-permute-start(f32[24,16,128]{2,1,0:T(8,128)S(1)} %get-tuple-element.82.refs_2_), channel_id=1, source_target_pairs={{2,4},{18,20},{3,5},{19,21},{4,2},{20,18},{5,3},{21,19},{6,8},{22,... | collective-permute-start | bytes 589832 | tf_op jit(solution)/shard_map/ppermute | solution.py:494
  48.5 14.9 %collective-permute-start.16 = (f32[24,16,128]{2,1,0:T(8,128)S(1)}, f32[24,16,128]{2,1,0:T(8,128)S(1)}, u32[]{:S(2)}, u32[]{:S(2)}) collective-permute-start(f32[24,16,128]{2,1,0:T(8,128)S(1)} %get-tuple-element.88), channel_id=1, source_target_pairs={{0,2},{2,0},{4,6},{6,4},{8,10},{10,8},{12,14},{14,12},{1,3},{3,1},... | collective-permute-start | bytes 589832 | tf_op jit(solution)/shard_map/ppermute | solution.py:491
  60.1 8.9 %collective-permute-start.19 = (f32[32,16,128]{2,1,0:T(8,128)S(1)}, f32[32,16,128]{2,1,0:T(8,128)S(1)}, u32[]{:S(2)}, u32[]{:S(2)}) collective-permute-start(f32[32,16,128]{2,1,0:T(8,128)S(1)} %get-tuple-element.93), channel_id=1, source_target_pairs={{0,16},{16,0},{1,17},{17,1},{2,18},{18,2},{3,19},{19,3},{4,20},{20... | collective-permute-start | bytes 786440 | tf_op jit(solution)/shard_map/ppermute | solution.py:497
  60.2 8.8 %collective-permute-start.17 = (f32[24,16,128]{2,1,0:T(8,128)S(1)}, f32[24,16,128]{2,1,0:T(8,128)S(1)}, u32[]{:S(2)}, u32[]{:S(2)}) collective-permute-start(f32[24,16,128]{2,1,0:T(8,128)S(1)} %get-tuple-element.89), channel_id=1, source_target_pairs={{2,4},{18,20},{3,5},{19,21},{4,2},{20,18},{5,3},{21,19},{6,8},{22,... | collective-permute-start | bytes 589832 | tf_op jit(solution)/shard_map/ppermute | solution.py:494
  60.3 16.6 %collective-permute-start.20 = (f32[24,16,128]{2,1,0:T(8,128)S(1)}, f32[24,16,128]{2,1,0:T(8,128)S(1)}, u32[]{:S(2)}, u32[]{:S(2)}) collective-permute-start(f32[24,16,128]{2,1,0:T(8,128)S(1)} %get-tuple-element.90.refs_1_), channel_id=1, source_target_pairs={{0,2},{2,0},{4,6},{6,4},{8,10},{10,8},{12,14},{14,12},{1,3},{3,1},... | collective-permute-start | bytes 589832 | tf_op jit(solution)/shard_map/ppermute | solution.py:491
  63.3 13.5 %collective-permute-start.21 = (f32[24,16,128]{2,1,0:T(8,128)S(1)}, f32[24,16,128]{2,1,0:T(8,128)S(1)}, u32[]{:S(2)}, u32[]{:S(2)}) collective-permute-start(f32[24,16,128]{2,1,0:T(8,128)S(1)} %get-tuple-element.91.refs_2_), channel_id=1, source_target_pairs={{2,4},{18,20},{3,5},{19,21},{4,2},{20,18},{5,3},{21,19},{6,8},{22,... | collective-permute-start | bytes 589832 | tf_op jit(solution)/shard_map/ppermute | solution.py:494
  63.4 5.6 %collective-permute-start.18 = (f32[32,8,128]{2,1,0:T(8,128)S(1)}, f32[32,8,128]{2,1,0:T(8,128)S(1)}, u32[]{:S(2)}, u32[]{:S(2)}) collective-permute-start(f32[32,8,128]{2,1,0:T(8,128)S(1)} %get-tuple-element.92), channel_id=1, source_target_pairs={{0,1},{1,0},{2,3},{3,2},{4,5},{5,4},{6,7},{7,6},{8,9},{9,8},{10,11... | collective-permute-start | bytes 393224 | tf_op jit(solution)/shard_map/ppermute | solution.py:497
  77.1 6.2 %collective-permute-start.23 = (f32[32,16,128]{2,1,0:T(8,128)S(1)}, f32[32,16,128]{2,1,0:T(8,128)S(1)}, u32[]{:S(2)}, u32[]{:S(2)}) collective-permute-start(f32[32,16,128]{2,1,0:T(8,128)S(1)} %get-tuple-element.103), channel_id=1, source_target_pairs={{0,16},{16,0},{1,17},{17,1},{2,18},{18,2},{3,19},{19,3},{4,20},{20... | collective-permute-start | bytes 786440 | tf_op jit(solution)/shard_map/ppermute | solution.py:497
  77.2 11.5 %collective-permute-start.24 = (f32[24,16,128]{2,1,0:T(8,128)S(1)}, f32[24,16,128]{2,1,0:T(8,128)S(1)}, u32[]{:S(2)}, u32[]{:S(2)}) collective-permute-start(f32[24,16,128]{2,1,0:T(8,128)S(1)} %get-tuple-element.98.refs_1_), channel_id=1, source_target_pairs={{0,2},{2,0},{4,6},{6,4},{8,10},{10,8},{12,14},{14,12},{1,3},{3,1},... | collective-permute-start | bytes 589832 | tf_op jit(solution)/shard_map/ppermute | solution.py:491
  77.7 11.0 %collective-permute-start.25 = (f32[24,16,128]{2,1,0:T(8,128)S(1)}, f32[24,16,128]{2,1,0:T(8,128)S(1)}, u32[]{:S(2)}, u32[]{:S(2)}) collective-permute-start(f32[24,16,128]{2,1,0:T(8,128)S(1)} %get-tuple-element.99.refs_2_), channel_id=1, source_target_pairs={{2,4},{18,20},{3,5},{19,21},{4,2},{20,18},{5,3},{21,19},{6,8},{22,... | collective-permute-start | bytes 589832 | tf_op jit(solution)/shard_map/ppermute | solution.py:494
  77.8 5.6 %collective-permute-start.22 = (f32[32,8,128]{2,1,0:T(8,128)S(1)}, f32[32,8,128]{2,1,0:T(8,128)S(1)}, u32[]{:S(2)}, u32[]{:S(2)}) collective-permute-start(f32[32,8,128]{2,1,0:T(8,128)S(1)} %get-tuple-element.102), channel_id=1, source_target_pairs={{0,1},{1,0},{2,3},{3,2},{4,5},{5,4},{6,7},{7,6},{8,9},{9,8},{10,11... | collective-permute-start | bytes 393224 | tf_op jit(solution)/shard_map/ppermute | solution.py:497
  89.0 8.8 %collective-permute-start.27 = (f32[64,16,128]{2,1,0:T(8,128)S(1)}, f32[64,16,128]{2,1,0:T(8,128)S(1)}, u32[]{:S(2)}, u32[]{:S(2)}) collective-permute-start(f32[64,16,128]{2,1,0:T(8,128)S(1)} %get-tuple-element.110), channel_id=1, source_target_pairs={{0,16},{16,0},{1,17},{17,1},{2,18},{18,2},{3,19},{19,3},{4,20},{20... | collective-permute-start | bytes 1572872 | tf_op jit(solution)/shard_map/ppermute | solution.py:497
  89.1 8.7 %collective-permute-start.26 = (f32[64,8,128]{2,1,0:T(8,128)S(1)}, f32[64,8,128]{2,1,0:T(8,128)S(1)}, u32[]{:S(2)}, u32[]{:S(2)}) collective-permute-start(f32[64,8,128]{2,1,0:T(8,128)S(1)} %get-tuple-element.109), channel_id=1, source_target_pairs={{0,1},{1,0},{2,3},{3,2},{4,5},{5,4},{6,7},{7,6},{8,9},{9,8},{10,11... | collective-permute-start | bytes 786440 | tf_op jit(solution)/shard_map/ppermute | solution.py:497
  90.6 11.2 %collective-permute-start.28 = (f32[24,16,128]{2,1,0:T(8,128)S(1)}, f32[24,16,128]{2,1,0:T(8,128)S(1)}, u32[]{:S(2)}, u32[]{:S(2)}) collective-permute-start(f32[24,16,128]{2,1,0:T(8,128)S(1)} %get-tuple-element.105.refs_1_), channel_id=1, source_target_pairs={{0,2},{2,0},{4,6},{6,4},{8,10},{10,8},{12,14},{14,12},{1,3},{3,1},... | collective-permute-start | bytes 589832 | tf_op jit(solution)/shard_map/ppermute | solution.py:491
  91.2 10.7 %collective-permute-start.29 = (f32[24,16,128]{2,1,0:T(8,128)S(1)}, f32[24,16,128]{2,1,0:T(8,128)S(1)}, u32[]{:S(2)}, u32[]{:S(2)}) collective-permute-start(f32[24,16,128]{2,1,0:T(8,128)S(1)} %get-tuple-element.106.refs_2_), channel_id=1, source_target_pairs={{2,4},{18,20},{3,5},{19,21},{4,2},{20,18},{5,3},{21,19},{6,8},{22,... | collective-permute-start | bytes 589832 | tf_op jit(solution)/shard_map/ppermute | solution.py:494

commit v7 on v6

--- a/solution.py
+++ b/solution.py
@@ -29,7 +29,7 @@
     return lax.rem(column, 2), lax.axis_index("gy"), lax.axis_index("grp"), inside.astype(jnp.int32)
 
 
-def call(body, outs, ins, scratch=(), away=0, flops=1000000, alias=None):
+def call(body, outs, ins, scratch=(), away=0, flops=1000000):
     shapes = [jax.ShapeDtypeStruct(s, jnp.float32) for s in outs]
     size = sum(o.size for o in shapes) + sum(i.size for i in ins)
     return pl.pallas_call(
@@ -38,7 +38,6 @@
         in_specs=[ANY] * away + [VMEM] * (len(ins) - away),
         out_specs=[VMEM] * len(shapes),
         scratch_shapes=list(scratch),
-        input_output_aliases=alias or {},
         compiler_params=pltpu.CompilerParams(vmem_limit_bytes=12 * 1024 * 1024),
         cost_estimate=pl.CostEstimate(flops=flops, bytes_accessed=4 * size, transcendentals=0),
     )(*ins)
@@ -239,6 +238,13 @@
 def last_body(info, f, halo_in, halo_out, o):
     _, X, Y, Z = f.shape
     T = Z // LANES
+
+    def copy(i, carry):
+        for c in range(4):
+            o[c, i] = f[c, i]
+        return carry
+
+    lax.fori_loop(0, X, copy, 0, unroll=4)
     for side, halo in enumerate((halo_in, halo_out)):
         _, has, layer, place = ends(info, side == 0, X, 3)
         weight = filter_weight * has.astype(jnp.float32)
@@ -602,7 +608,7 @@
             [F, G4],
             flops=4000000,
         )
-        (state,) = call(last_body, [(4, X, Y, Z)], [part, *halos], alias={0: 0})
+        (state,) = call(last_body, [(4, X, Y, Z)], [part, *halos])
         return state.transpose(1, 2, 0, 3)
 
     placed = (

time: 104 us -> 104 us (level)
  no operation moved by 1% of the time
where the time goes in v7:
time: 104 us
  waiting for transfers between devices  62.5 us (60%)
  starting transfers between devices  19.2 us (18%)
  Pallas kernels  17.2 us (17%)
  local copies, waits for them, and re-layouts  4.63 us (4%)
    ppermute x8, waiting for transfers between devices, send_in(): return lax.ppermute(message, 'gx', even)  30.9 us
    ppermute x14, waiting for transfers between devices, send_sides(): return (lax.ppermute(ymsg, 'gy', swap), lax.ppermute(zmsg, 'grp', swap))  25.1 us
    pallas_call x15, Pallas kernels, call(): pl.pallas_call(lambda *refs: body(place(), *refs), out_shape=shapes, in_s...  17.2 us
    ppermute x8, starting transfers between devices, send_in(): return lax.ppermute(message, 'gx', even)  10.3 us
    ppermute x14, starting transfers between devices, send_sides(): return (lax.ppermute(ymsg, 'gy', swap), lax.ppermute(zmsg, 'grp', swap))  8.36 us
    ppermute x8, waiting for transfers between devices, send_out(): return lax.ppermute(message, mesh.axis_names, hops)  6.44 us
    unnamed x15, local copies, waits for them, and re-layouts  2.87 us
  transfers between devices with their start and end apart: 30, of which 15 were waited for; matrix products, arithmetic and copies ran while one was open for 1% of the time, Pallas kernels for 12%

profile of v7, /device:TPU:8, one launch (start us, length us, event | category | flops | bytes accessed | tf_op | source)
XLA Modules:
  0.0 103.7 jit_solution(15405304457260910457)
XLA Ops:
  0.0 1.4 %copy-done.1 = f32[32,16,3,256]{3,1,2,0:T(8,128)S(1)} copy-done((f32[32,16,3,256]{3,1,2,0:T(8,128)S(1)}, f32[32,16,3,256]{3,1,2,0:T(8,128)}, u32[]{:S(2)}) %copy-start.1) | copy-done | bytes 1572888
  1.4 0.2 shard_map.73
  1.7 1.6 %collective-permute-start.2 = (f32[24,8,128]{2,1,0:T(8,128)S(1)}, f32[24,8,128]{2,1,0:T(8,128)S(1)}, u32[]{:S(2)}, u32[]{:S(2)}) collective-permute-start(f32[24,8,128]{2,1,0:T(8,128)S(1)} %get-tuple-element.60), channel_id=1, source_target_pairs={{0,1},{1,0},{2,3},{3,2},{4,5},{5,4},{6,7},{7,6},{8,9},{9,8},{10,11... | collective-permute-start | bytes 294920 | tf_op jit(solution)/shard_map/ppermute | solution.py:503
  3.3 1.5 %collective-permute-start = (f32[6,16,128]{2,1,0:T(8,128)S(1)}, f32[6,16,128]{2,1,0:T(8,128)S(1)}, u32[]{:S(2)}, u32[]{:S(2)}) collective-permute-start(f32[6,16,128]{2,1,0:T(8,128)S(1)} %get-tuple-element.58), channel_id=1, source_target_pairs={{0,2},{2,0},{4,6},{6,4},{8,10},{10,8},{12,14},{14,12},{1,3},{3,1},... | collective-permute-start | bytes 147464 | tf_op jit(solution)/shard_map/ppermute | solution.py:497
  4.8 0.4 collective-permute-start.1
  5.2 1.4 %copy.11 = f32[16,16,4,256]{3,1,0,2:T(8,128)S(1)} copy(f32[16,16,4,256]{3,2,1,0:T(4,128)} %param.11) | data formatting | bytes 2097152 | tf_op args[4]
  6.6 0.7 collective-permute-done.refs_2_
  7.4 2.4 %collective-permute-done.1.refs_3_ = f32[6,16,128]{2,1,0:T(8,128)S(1)} collective-permute-done((f32[6,16,128]{2,1,0:T(8,128)S(1)}, f32[6,16,128]{2,1,0:T(8,128)S(1)}, u32[]{:S(2)}, u32[]{:S(2)}) %collective-permute-start.1) | collective-permute-done | bytes 49184 | tf_op jit(solution)/shard_map/ppermute | solution.py:500
  9.8 3.3 %shard_map.74 = (f32[3,2,32,16,128]{4,3,2,1,0:T(8,128)S(1)}, f32[3,2,16,16,128]{4,3,2,1,0:T(8,128)S(1)}, f32[54,16,128]{2,1,0:T(8,128)S(1)}, f32[54,16,128]{2,1,...) custom-call(s32[8]{0:T(128)S(1)} %copy-done.5, ...), custom_call_target="tpu_custom_call" | custom-call | flops 4000000 | bytes 9437216 | tf_op jit(solution)/shard_map/pallas_call | solution.py:35
  13.2 0.6 collective-permute-start.6
  13.8 0.5 collective-permute-start.4
  14.3 7.2 %collective-permute-done.4.refs_3_.refs_4_ = f32[56,8,128]{2,1,0:T(8,128)S(1)} collective-permute-done((f32[56,8,128]{2,1,0:T(8,128)S(1)}, f32[56,8,128]{2,1,0:T(8,128)S(1)}, u32[]{:S(2)}, u32[]{:S(2)}) %collective-permute-start.4) | collective-permute-done | bytes 229408 | tf_op jit(solution)/shard_map/ppermute | solution.py:503
  21.6 1.5 %shard_map.75 = (f32[4,2,16,16,128]{4,3,2,1,0:T(8,128)S(1)}, f32[4,2,16,16,128]{4,3,2,1,0:T(8,128)S(1)}) custom-call(f32[4,2,16,16,128]{4,3,2,1,0:T(8,128)S(1)} %get-tuple-element.62.refs_0_, f32[54,16,128]{2,1,0:T(8,128)S(1)} %get-tuple-element.63.refs_1_, f32[54,16,128]{2,1,0:T(8,128)S(1)} %get-tuple-element.64.refs_2_, ...), custom_call_target="tpu_custom_call" | custom-call | flops 4000000 | bytes 8585216 | tf_op jit(solution)/shard_map/pallas_call | solution.py:35
  23.1 12.2 %collective-permute-done.6.refs_1_.refs_4_.refs_2_ = f32[54,16,128]{2,1,0:T(8,128)S(1)} collective-permute-done((f32[54,16,128]{2,1,0:T(8,128)S(1)}, f32[54,16,128]{2,1,0:T(8,128)S(1)}, u32[]{:S(2)}, u32[]{:S(2)}) %collective-permute-start.6) | collective-permute-done | bytes 442400 | tf_op jit(solution)/shard_map/ppermute | solution.py:497
  35.3 0.2 shard_map.76
  35.6 0.6 collective-permute-start.10
  36.2 0.5 collective-permute-start.8
  36.7 2.4 %shard_map.77 = (f32[3,2,16,16,128]{4,3,2,1,0:T(8,128)S(1)}, f32[24,16,128]{2,1,0:T(8,128)S(1)}, f32[24,16,128]{2,1,0:T(8,128)S(1)}) custom-call(s32[8]{0:T(128)S(1)} %copy-done.5, f32[3,2,32,16,128]{4,3,2,1,0:T(8,128)S(1)} %get-tuple-element.70.refs_1_, f32[54,16,128]{2,1,0:T(8,128)S(1)} %collective-permute-done.6.refs_1_.refs_4_.refs_2_, ...), custom_call_target="tpu_custom_call" | custom-call | flops 4000000 | bytes 5177376 | tf_op jit(solution)/shard_map/pallas_call | solution.py:35
  39.1 2.7 %collective-permute-done.8.refs_5_ = f32[32,8,128]{2,1,0:T(8,128)S(1)} collective-permute-done((f32[32,8,128]{2,1,0:T(8,128)S(1)}, f32[32,8,128]{2,1,0:T(8,128)S(1)}, u32[]{:S(2)}, u32[]{:S(2)}) %collective-permute-start.8) | collective-permute-done | bytes 131104 | tf_op jit(solution)/shard_map/ppermute | solution.py:503
  41.7 1.6 %shard_map.78.refs_0_ = f32[4,2,16,16,128]{4,3,2,1,0:T(8,128)S(1)} custom-call(f32[4,2,16,16,128]{4,3,2,1,0:T(8,128)S(1)} %get-tuple-element.68.refs_0_, f32[24,16,128]{2,1,0:T(8,128)S(1)} %get-tuple-element.74.refs_1_, f32[24,16,128]{2,1,0:T(8,128)S(1)} %get-tuple-element.75.refs_2_, f32[8,16,128]{2,1,0:T(8,128)S(1)} %get-tuple-element.76.refs_3_, ...), custom_call_target="tpu_custom_call" | custom-call | flops 4000000 | bytes 7340032 | tf_op jit(solution)/shard_map/pallas_call | solution.py:35
  43.4 3.7 %collective-permute-done.10.refs_1_ = f32[24,16,128]{2,1,0:T(8,128)S(1)} collective-permute-done((f32[24,16,128]{2,1,0:T(8,128)S(1)}, f32[24,16,128]{2,1,0:T(8,128)S(1)}, u32[]{:S(2)}, u32[]{:S(2)}) %collective-permute-start.10) | collective-permute-done | bytes 196640 | tf_op jit(solution)/shard_map/ppermute | solution.py:497
  47.1 0.3 shard_map.79
  47.5 0.5 collective-permute-start.12
  48.0 0.5 collective-permute-start.14
  48.5 3.0 %collective-permute-start.16 = (f32[24,16,128]{2,1,0:T(8,128)S(1)}, f32[24,16,128]{2,1,0:T(8,128)S(1)}, u32[]{:S(2)}, u32[]{:S(2)}) collective-permute-start(f32[24,16,128]{2,1,0:T(8,128)S(1)} %get-tuple-element.88), channel_id=1, source_target_pairs={{0,2},{2,0},{4,6},{6,4},{8,10},{10,8},{12,14},{14,12},{1,3},{3,1},... | collective-permute-start | bytes 589832 | tf_op jit(solution)/shard_map/ppermute | solution.py:497
  51.6 4.6 %collective-permute-done.12.refs_5_ = f32[64,8,128]{2,1,0:T(8,128)S(1)} collective-permute-done((f32[64,8,128]{2,1,0:T(8,128)S(1)}, f32[64,8,128]{2,1,0:T(8,128)S(1)}, u32[]{:S(2)}, u32[]{:S(2)}) %collective-permute-start.12) | collective-permute-done | bytes 262176 | tf_op jit(solution)/shard_map/ppermute | solution.py:503
  56.2 1.9 %shard_map.80.refs_0_ = f32[4,2,16,16,128]{4,3,2,1,0:T(8,128)S(1)} custom-call(f32[4,2,16,16,128]{4,3,2,1,0:T(8,128)S(1)} %shard_map.78.refs_0_, f32[24,16,128]{2,1,0:T(8,128)S(1)} %get-tuple-element.81.refs_1_, f32[24,16,128]{2,1,0:T(8,128)S(1)} %get-tuple-element.82.refs_2_, f32[8,16,128]{2,1,0:T(8,128)S(1)} %get-tuple-element.83.refs_3_, ...), custom_call_target="tpu_custom_call" | custom-call | flops 4000000 | bytes 5767168 | tf_op jit(solution)/shard_map/pallas_call | solution.py:35
  58.1 1.9 %collective-permute-done.14.refs_1_ = f32[24,16,128]{2,1,0:T(8,128)S(1)} collective-permute-done((f32[24,16,128]{2,1,0:T(8,128)S(1)}, f32[24,16,128]{2,1,0:T(8,128)S(1)}, u32[]{:S(2)}, u32[]{:S(2)}) %collective-permute-start.14) | collective-permute-done | bytes 196640 | tf_op jit(solution)/shard_map/ppermute | solution.py:497
  60.0 0.2 shard_map.81
  60.3 3.0 %collective-permute-start.20 = (f32[24,16,128]{2,1,0:T(8,128)S(1)}, f32[24,16,128]{2,1,0:T(8,128)S(1)}, u32[]{:S(2)}, u32[]{:S(2)}) collective-permute-start(f32[24,16,128]{2,1,0:T(8,128)S(1)} %get-tuple-element.90.refs_1_), channel_id=1, source_target_pairs={{0,2},{2,0},{4,6},{6,4},{8,10},{10,8},{12,14},{14,12},{1,3},{3,1},... | collective-permute-start | bytes 589832 | tf_op jit(solution)/shard_map/ppermute | solution.py:497
  63.4 1.5 %collective-permute-start.18 = (f32[32,8,128]{2,1,0:T(8,128)S(1)}, f32[32,8,128]{2,1,0:T(8,128)S(1)}, u32[]{:S(2)}, u32[]{:S(2)}) collective-permute-start(f32[32,8,128]{2,1,0:T(8,128)S(1)} %get-tuple-element.92), channel_id=1, source_target_pairs={{0,1},{1,0},{2,3},{3,2},{4,5},{5,4},{6,7},{7,6},{8,9},{9,8},{10,11... | collective-permute-start | bytes 393224 | tf_op jit(solution)/shard_map/ppermute | solution.py:503
  65.0 4.0 %collective-permute-done.17.refs_5_ = f32[24,16,128]{2,1,0:T(8,128)S(1)} collective-permute-done((f32[24,16,128]{2,1,0:T(8,128)S(1)}, f32[24,16,128]{2,1,0:T(8,128)S(1)}, u32[]{:S(2)}, u32[]{:S(2)}) %collective-permute-start.17) | collective-permute-done | bytes 196640 | tf_op jit(solution)/shard_map/ppermute | solution.py:500
  69.0 1.5 %shard_map.82 = (f32[4,2,16,16,128]{4,3,2,1,0:T(8,128)S(1)}, f32[4,2,16,16,128]{4,3,2,1,0:T(8,128)S(1)}) custom-call(f32[4,2,16,16,128]{4,3,2,1,0:T(8,128)S(1)} %shard_map.80.refs_0_, f32[24,16,128]{2,1,0:T(8,128)S(1)} %get-tuple-element.90.refs_1_, f32[24,16,128]{2,1,0:T(8,128)S(1)} %get-tuple-element.91.refs_2_, ...), custom_call_target="tpu_custom_call" | custom-call | flops 4000000 | bytes 7208960 | tf_op jit(solution)/shard_map/pallas_call | solution.py:35
  70.5 6.4 %collective-permute-done.20.refs_1_ = f32[24,16,128]{2,1,0:T(8,128)S(1)} collective-permute-done((f32[24,16,128]{2,1,0:T(8,128)S(1)}, f32[24,16,128]{2,1,0:T(8,128)S(1)}, u32[]{:S(2)}, u32[]{:S(2)}) %collective-permute-start.20) | collective-permute-done | bytes 196640 | tf_op jit(solution)/shard_map/ppermute | solution.py:497
  76.9 0.2 shard_map.83
  77.2 0.5 collective-permute-start.24
  77.8 1.5 %collective-permute-start.22 = (f32[32,8,128]{2,1,0:T(8,128)S(1)}, f32[32,8,128]{2,1,0:T(8,128)S(1)}, u32[]{:S(2)}, u32[]{:S(2)}) collective-permute-start(f32[32,8,128]{2,1,0:T(8,128)S(1)} %get-tuple-element.102), channel_id=1, source_target_pairs={{0,1},{1,0},{2,3},{3,2},{4,5},{5,4},{6,7},{7,6},{8,9},{9,8},{10,11... | collective-permute-start | bytes 393224 | tf_op jit(solution)/shard_map/ppermute | solution.py:503
  79.3 4.0 %collective-permute-done.22.refs_5_ = f32[32,8,128]{2,1,0:T(8,128)S(1)} collective-permute-done((f32[32,8,128]{2,1,0:T(8,128)S(1)}, f32[32,8,128]{2,1,0:T(8,128)S(1)}, u32[]{:S(2)}, u32[]{:S(2)}) %collective-permute-start.22) | collective-permute-done | bytes 131104 | tf_op jit(solution)/shard_map/ppermute | solution.py:503
  83.3 1.6 %shard_map.84.refs_0_ = f32[4,2,16,16,128]{4,3,2,1,0:T(8,128)S(1)} custom-call(f32[4,2,16,16,128]{4,3,2,1,0:T(8,128)S(1)} %get-tuple-element.95.refs_0_, f32[24,16,128]{2,1,0:T(8,128)S(1)} %get-tuple-element.98.refs_1_, f32[24,16,128]{2,1,0:T(8,128)S(1)} %get-tuple-element.99.refs_2_, f32[8,16,128]{2,1,0:T(8,128)S(1)} %get-tuple-element.100.refs_3_, ...), custom_call_target="tpu_custom_call" | custom-call | flops 4000000 | bytes 7340032 | tf_op jit(solution)/shard_map/pallas_call | solution.py:35
  85.0 3.8 %collective-permute-done.24.refs_1_ = f32[24,16,128]{2,1,0:T(8,128)S(1)} collective-permute-done((f32[24,16,128]{2,1,0:T(8,128)S(1)}, f32[24,16,128]{2,1,0:T(8,128)S(1)}, u32[]{:S(2)}, u32[]{:S(2)}) %collective-permute-start.24) | collective-permute-done | bytes 196640 | tf_op jit(solution)/shard_map/ppermute | solution.py:497
  88.7 0.3 shard_map.85
  89.1 1.6 %collective-permute-start.26 = (f32[64,8,128]{2,1,0:T(8,128)S(1)}, f32[64,8,128]{2,1,0:T(8,128)S(1)}, u32[]{:S(2)}, u32[]{:S(2)}) collective-permute-start(f32[64,8,128]{2,1,0:T(8,128)S(1)} %get-tuple-element.109), channel_id=1, source_target_pairs={{0,1},{1,0},{2,3},{3,2},{4,5},{5,4},{6,7},{7,6},{8,9},{9,8},{10,11... | collective-permute-start | bytes 786440 | tf_op jit(solution)/shard_map/ppermute | solution.py:503
  90.6 0.5 collective-permute-start.28
  91.2 6.6 %collective-permute-done.26.refs_5_ = f32[64,8,128]{2,1,0:T(8,128)S(1)} collective-permute-done((f32[64,8,128]{2,1,0:T(8,128)S(1)}, f32[64,8,128]{2,1,0:T(8,128)S(1)}, u32[]{:S(2)}, u32[]{:S(2)}) %collective-permute-start.26) | collective-permute-done | bytes 262176 | tf_op jit(solution)/shard_map/ppermute | solution.py:503
  97.8 1.9 %shard_map.86.refs_0_ = f32[4,16,16,256]{3,2,1,0:T(8,128)S(1)} custom-call(f32[4,2,16,16,128]{4,3,2,1,0:T(8,128)S(1)} %shard_map.84.refs_0_, f32[24,16,128]{2,1,0:T(8,128)S(1)} %get-tuple-element.105.refs_1_, f32[24,16,128]{2,1,0:T(8,128)S(1)} %get-tuple-element.106.refs_2_, f32[8,16,128]{2,1,0:T(8,128)S(1)} %get-tuple-element.107.refs_3_, ...), custom_call_target="tpu_custom_call" | custom-call | flops 4000000 | bytes 5767168 | tf_op jit(solution)/shard_map/pallas_call | solution.py:35
  99.7 2.2 %collective-permute-done.28.refs_1_ = f32[24,16,128]{2,1,0:T(8,128)S(1)} collective-permute-done((f32[24,16,128]{2,1,0:T(8,128)S(1)}, f32[24,16,128]{2,1,0:T(8,128)S(1)}, u32[]{:S(2)}, u32[]{:S(2)}) %collective-permute-start.28) | collective-permute-done | bytes 196640 | tf_op jit(solution)/shard_map/ppermute | solution.py:497
  101.8 0.1 shard_map.87
  102.0 1.7 %copy.9 = f32[16,16,4,256]{3,2,1,0:T(4,128)} copy(f32[16,16,4,256]{3,1,0,2:T(8,128)S(1)} %bitcast.8) | data formatting | bytes 2097152 | tf_op jit(solution)/shard_map/transpose | solution.py:612
  (44 shorter events, 0.9 us)
Async XLA Ops:
  0.0 1.4 %copy-start.1 = (f32[32,16,3,256]{3,1,2,0:T(8,128)S(1)}, f32[32,16,3,256]{3,1,2,0:T(8,128)}, u32[]{:S(2)}) copy-start(f32[32,16,3,256]{3,1,2,0:T(8,128)} %param.7) | copy-start | bytes 4718596
  1.4 8.3 %copy-start.2 = (f32[32,16,3,256]{3,1,2,0:T(8,128)S(1)}, f32[32,16,3,256]{3,1,2,0:T(8,128)}, u32[]{:S(2)}) copy-start(f32[32,16,3,256]{3,1,2,0:T(8,128)} %param.7) | copy-start | bytes 4718596
  1.4 8.4 %copy-start.4 = (bf16[8,1,2,64,64]{4,3,2,1,0:T(8,128)(2,1)S(1)}, bf16[8,1,2,64,64]{4,3,2,1,0:T(8,128)(2,1)}, u32[]{:S(2)}) copy-start(bf16[8,1,2,64,64]{4,3,2,1,0:T(8,128)(2,1)} %param.9) | copy-start | bytes 393220
  1.4 8.4 %copy-start.5 = (s32[8]{0:T(128)S(1)}, s32[8]{0:T(128)}, u32[]{:S(2)}) copy-start(s32[8]{0:T(128)} %refs_0_.3) | copy-start | bytes 100
  1.6 8.2 %collective-permute-start.3 = (f32[96,16,128]{2,1,0:T(8,128)S(1)}, f32[96,16,128]{2,1,0:T(8,128)S(1)}, u32[]{:S(2)}, u32[]{:S(2)}) collective-permute-start(f32[96,16,128]{2,1,0:T(8,128)S(1)} %get-tuple-element.61), channel_id=1, source_target_pairs={{0,16},{16,0},{1,17},{17,1},{2,18},{18,2},{3,19},{19,3},{4,20},{20... | collective-permute-start | bytes 2359304 | tf_op jit(solution)/shard_map/ppermute | solution.py:503
  1.7 8.1 %collective-permute-start.2 = (f32[24,8,128]{2,1,0:T(8,128)S(1)}, f32[24,8,128]{2,1,0:T(8,128)S(1)}, u32[]{:S(2)}, u32[]{:S(2)}) collective-permute-start(f32[24,8,128]{2,1,0:T(8,128)S(1)} %get-tuple-element.60), channel_id=1, source_target_pairs={{0,1},{1,0},{2,3},{3,2},{4,5},{5,4},{6,7},{7,6},{8,9},{9,8},{10,11... | collective-permute-start | bytes 294920 | tf_op jit(solution)/shard_map/ppermute | solution.py:503
  3.3 4.1 %collective-permute-start = (f32[6,16,128]{2,1,0:T(8,128)S(1)}, f32[6,16,128]{2,1,0:T(8,128)S(1)}, u32[]{:S(2)}, u32[]{:S(2)}) collective-permute-start(f32[6,16,128]{2,1,0:T(8,128)S(1)} %get-tuple-element.58), channel_id=1, source_target_pairs={{0,2},{2,0},{4,6},{6,4},{8,10},{10,8},{12,14},{14,12},{1,3},{3,1},... | collective-permute-start | bytes 147464 | tf_op jit(solution)/shard_map/ppermute | solution.py:497
  4.8 5.0 %collective-permute-start.1 = (f32[6,16,128]{2,1,0:T(8,128)S(1)}, f32[6,16,128]{2,1,0:T(8,128)S(1)}, u32[]{:S(2)}, u32[]{:S(2)}) collective-permute-start(f32[6,16,128]{2,1,0:T(8,128)S(1)} %get-tuple-element.59), channel_id=1, source_target_pairs={{2,4},{18,20},{3,5},{19,21},{4,2},{20,18},{5,3},{21,19},{6,8},{22,... | collective-permute-start | bytes 147464 | tf_op jit(solution)/shard_map/ppermute | solution.py:500
  9.8 11.7 %copy-start.6 = (f32[16,16]{1,0:T(8,128)S(1)}, f32[16,16]{1,0:T(8,128)}, u32[]{:S(2)}) copy-start(f32[16,16]{1,0:T(8,128)} %param.8) | copy-start | bytes 3076
  9.8 11.8 %copy-start = (bf16[2,1152,256]{2,1,0:T(8,128)(2,1)S(1)}, bf16[2,1152,256]{2,1,0:T(8,128)(2,1)}, u32[]{:S(2)}) copy-start(bf16[2,1152,256]{2,1,0:T(8,128)(2,1)} %constant.4.clone.refs_5_.refs_7_) | copy-start | bytes 3538948
  13.1 8.4 %collective-permute-start.5 = (f32[128,16,128]{2,1,0:T(8,128)S(1)}, f32[128,16,128]{2,1,0:T(8,128)S(1)}, u32[]{:S(2)}, u32[]{:S(2)}) collective-permute-start(f32[128,16,128]{2,1,0:T(8,128)S(1)} %get-tuple-element.66), channel_id=1, source_target_pairs={{0,16},{16,0},{1,17},{17,1},{2,18},{18,2},{3,19},{19,3},{4,20},{20... | collective-permute-start | bytes 3145736 | tf_op jit(solution)/shard_map/ppermute | solution.py:503
  13.2 22.1 %collective-permute-start.6 = (f32[54,16,128]{2,1,0:T(8,128)S(1)}, f32[54,16,128]{2,1,0:T(8,128)S(1)}, u32[]{:S(2)}, u32[]{:S(2)}) collective-permute-start(f32[54,16,128]{2,1,0:T(8,128)S(1)} %get-tuple-element.63.refs_1_), channel_id=1, source_target_pairs={{0,2},{2,0},{4,6},{6,4},{8,10},{10,8},{12,14},{14,12},{1,3},{3,1},... | collective-permute-start | bytes 1327112 | tf_op jit(solution)/shard_map/ppermute | solution.py:497
  13.8 21.5 %collective-permute-start.7 = (f32[54,16,128]{2,1,0:T(8,128)S(1)}, f32[54,16,128]{2,1,0:T(8,128)S(1)}, u32[]{:S(2)}, u32[]{:S(2)}) collective-permute-start(f32[54,16,128]{2,1,0:T(8,128)S(1)} %get-tuple-element.64.refs_2_), channel_id=1, source_target_pairs={{2,4},{18,20},{3,5},{19,21},{4,2},{20,18},{5,3},{21,19},{6,8},{22,... | collective-permute-start | bytes 1327112 | tf_op jit(solution)/shard_map/ppermute | solution.py:500
  13.8 7.7 %collective-permute-start.4 = (f32[56,8,128]{2,1,0:T(8,128)S(1)}, f32[56,8,128]{2,1,0:T(8,128)S(1)}, u32[]{:S(2)}, u32[]{:S(2)}) collective-permute-start(f32[56,8,128]{2,1,0:T(8,128)S(1)} %get-tuple-element.65), channel_id=1, source_target_pairs={{0,1},{1,0},{2,3},{3,2},{4,5},{5,4},{6,7},{7,6},{8,9},{9,8},{10,11... | collective-permute-start | bytes 688136 | tf_op jit(solution)/shard_map/ppermute | solution.py:503
  35.5 6.2 %collective-permute-start.9 = (f32[32,16,128]{2,1,0:T(8,128)S(1)}, f32[32,16,128]{2,1,0:T(8,128)S(1)}, u32[]{:S(2)}, u32[]{:S(2)}) collective-permute-start(f32[32,16,128]{2,1,0:T(8,128)S(1)} %get-tuple-element.79), channel_id=1, source_target_pairs={{0,16},{16,0},{1,17},{17,1},{2,18},{18,2},{3,19},{19,3},{4,20},{20... | collective-permute-start | bytes 786440 | tf_op jit(solution)/shard_map/ppermute | solution.py:503
  35.6 11.5 %collective-permute-start.10 = (f32[24,16,128]{2,1,0:T(8,128)S(1)}, f32[24,16,128]{2,1,0:T(8,128)S(1)}, u32[]{:S(2)}, u32[]{:S(2)}) collective-permute-start(f32[24,16,128]{2,1,0:T(8,128)S(1)} %get-tuple-element.74.refs_1_), channel_id=1, source_target_pairs={{0,2},{2,0},{4,6},{6,4},{8,10},{10,8},{12,14},{14,12},{1,3},{3,1},... | collective-permute-start | bytes 589832 | tf_op jit(solution)/shard_map/ppermute | solution.py:497
  36.2 10.9 %collective-permute-start.11 = (f32[24,16,128]{2,1,0:T(8,128)S(1)}, f32[24,16,128]{2,1,0:T(8,128)S(1)}, u32[]{:S(2)}, u32[]{:S(2)}) collective-permute-start(f32[24,16,128]{2,1,0:T(8,128)S(1)} %get-tuple-element.75.refs_2_), channel_id=1, source_target_pairs={{2,4},{18,20},{3,5},{19,21},{4,2},{20,18},{5,3},{21,19},{6,8},{22,... | collective-permute-start | bytes 589832 | tf_op jit(solution)/shard_map/ppermute | solution.py:500
  36.2 5.6 %collective-permute-start.8 = (f32[32,8,128]{2,1,0:T(8,128)S(1)}, f32[32,8,128]{2,1,0:T(8,128)S(1)}, u32[]{:S(2)}, u32[]{:S(2)}) collective-permute-start(f32[32,8,128]{2,1,0:T(8,128)S(1)} %get-tuple-element.78), channel_id=1, source_target_pairs={{0,1},{1,0},{2,3},{3,2},{4,5},{5,4},{6,7},{7,6},{8,9},{9,8},{10,11... | collective-permute-start | bytes 393224 | tf_op jit(solution)/shard_map/ppermute | solution.py:503
  43.4 12.8 %copy-start.3 = (bf16[2,1152,256]{2,1,0:T(8,128)(2,1)S(1)}, bf16[2,1152,256]{2,1,0:T(8,128)(2,1)}, u32[]{:S(2)}) copy-start(bf16[2,1152,256]{2,1,0:T(8,128)(2,1)} %constant.5.clone.refs_7_) | copy-start | bytes 3538948
  47.4 8.8 %collective-permute-start.13 = (f32[64,16,128]{2,1,0:T(8,128)S(1)}, f32[64,16,128]{2,1,0:T(8,128)S(1)}, u32[]{:S(2)}, u32[]{:S(2)}) collective-permute-start(f32[64,16,128]{2,1,0:T(8,128)S(1)} %get-tuple-element.86), channel_id=1, source_target_pairs={{0,16},{16,0},{1,17},{17,1},{2,18},{18,2},{3,19},{19,3},{4,20},{20... | collective-permute-start | bytes 1572872 | tf_op jit(solution)/shard_map/ppermute | solution.py:503
  47.5 8.7 %collective-permute-start.12 = (f32[64,8,128]{2,1,0:T(8,128)S(1)}, f32[64,8,128]{2,1,0:T(8,128)S(1)}, u32[]{:S(2)}, u32[]{:S(2)}) collective-permute-start(f32[64,8,128]{2,1,0:T(8,128)S(1)} %get-tuple-element.85), channel_id=1, source_target_pairs={{0,1},{1,0},{2,3},{3,2},{4,5},{5,4},{6,7},{7,6},{8,9},{9,8},{10,11... | collective-permute-start | bytes 786440 | tf_op jit(solution)/shard_map/ppermute | solution.py:503
  48.0 12.0 %collective-permute-start.14 = (f32[24,16,128]{2,1,0:T(8,128)S(1)}, f32[24,16,128]{2,1,0:T(8,128)S(1)}, u32[]{:S(2)}, u32[]{:S(2)}) collective-permute-start(f32[24,16,128]{2,1,0:T(8,128)S(1)} %get-tuple-element.81.refs_1_), channel_id=1, source_target_pairs={{0,2},{2,0},{4,6},{6,4},{8,10},{10,8},{12,14},{14,12},{1,3},{3,1},... | collective-permute-start | bytes 589832 | tf_op jit(solution)/shard_map/ppermute | solution.py:497
  48.5 11.4 %collective-permute-start.15 = (f32[24,16,128]{2,1,0:T(8,128)S(1)}, f32[24,16,128]{2,1,0:T(8,128)S(1)}, u32[]{:S(2)}, u32[]{:S(2)}) collective-permute-start(f32[24,16,128]{2,1,0:T(8,128)S(1)} %get-tuple-element.82.refs_2_), channel_id=1, source_target_pairs={{2,4},{18,20},{3,5},{19,21},{4,2},{20,18},{5,3},{21,19},{6,8},{22,... | collective-permute-start | bytes 589832 | tf_op jit(solution)/shard_map/ppermute | solution.py:500
  48.5 14.9 %collective-permute-start.16 = (f32[24,16,128]{2,1,0:T(8,128)S(1)}, f32[24,16,128]{2,1,0:T(8,128)S(1)}, u32[]{:S(2)}, u32[]{:S(2)}) collective-permute-start(f32[24,16,128]{2,1,0:T(8,128)S(1)} %get-tuple-element.88), channel_id=1, source_target_pairs={{0,2},{2,0},{4,6},{6,4},{8,10},{10,8},{12,14},{14,12},{1,3},{3,1},... | collective-permute-start | bytes 589832 | tf_op jit(solution)/shard_map/ppermute | solution.py:497
  60.1 8.9 %collective-permute-start.19 = (f32[32,16,128]{2,1,0:T(8,128)S(1)}, f32[32,16,128]{2,1,0:T(8,128)S(1)}, u32[]{:S(2)}, u32[]{:S(2)}) collective-permute-start(f32[32,16,128]{2,1,0:T(8,128)S(1)} %get-tuple-element.93), channel_id=1, source_target_pairs={{0,16},{16,0},{1,17},{17,1},{2,18},{18,2},{3,19},{19,3},{4,20},{20... | collective-permute-start | bytes 786440 | tf_op jit(solution)/shard_map/ppermute | solution.py:503
  60.2 8.8 %collective-permute-start.17 = (f32[24,16,128]{2,1,0:T(8,128)S(1)}, f32[24,16,128]{2,1,0:T(8,128)S(1)}, u32[]{:S(2)}, u32[]{:S(2)}) collective-permute-start(f32[24,16,128]{2,1,0:T(8,128)S(1)} %get-tuple-element.89), channel_id=1, source_target_pairs={{2,4},{18,20},{3,5},{19,21},{4,2},{20,18},{5,3},{21,19},{6,8},{22,... | collective-permute-start | bytes 589832 | tf_op jit(solution)/shard_map/ppermute | solution.py:500
  60.3 16.6 %collective-permute-start.20 = (f32[24,16,128]{2,1,0:T(8,128)S(1)}, f32[24,16,128]{2,1,0:T(8,128)S(1)}, u32[]{:S(2)}, u32[]{:S(2)}) collective-permute-start(f32[24,16,128]{2,1,0:T(8,128)S(1)} %get-tuple-element.90.refs_1_), channel_id=1, source_target_pairs={{0,2},{2,0},{4,6},{6,4},{8,10},{10,8},{12,14},{14,12},{1,3},{3,1},... | collective-permute-start | bytes 589832 | tf_op jit(solution)/shard_map/ppermute | solution.py:497
  63.3 13.6 %collective-permute-start.21 = (f32[24,16,128]{2,1,0:T(8,128)S(1)}, f32[24,16,128]{2,1,0:T(8,128)S(1)}, u32[]{:S(2)}, u32[]{:S(2)}) collective-permute-start(f32[24,16,128]{2,1,0:T(8,128)S(1)} %get-tuple-element.91.refs_2_), channel_id=1, source_target_pairs={{2,4},{18,20},{3,5},{19,21},{4,2},{20,18},{5,3},{21,19},{6,8},{22,... | collective-permute-start | bytes 589832 | tf_op jit(solution)/shard_map/ppermute | solution.py:500
  63.4 5.6 %collective-permute-start.18 = (f32[32,8,128]{2,1,0:T(8,128)S(1)}, f32[32,8,128]{2,1,0:T(8,128)S(1)}, u32[]{:S(2)}, u32[]{:S(2)}) collective-permute-start(f32[32,8,128]{2,1,0:T(8,128)S(1)} %get-tuple-element.92), channel_id=1, source_target_pairs={{0,1},{1,0},{2,3},{3,2},{4,5},{5,4},{6,7},{7,6},{8,9},{9,8},{10,11... | collective-permute-start | bytes 393224 | tf_op jit(solution)/shard_map/ppermute | solution.py:503
  77.1 6.2 %collective-permute-start.23 = (f32[32,16,128]{2,1,0:T(8,128)S(1)}, f32[32,16,128]{2,1,0:T(8,128)S(1)}, u32[]{:S(2)}, u32[]{:S(2)}) collective-permute-start(f32[32,16,128]{2,1,0:T(8,128)S(1)} %get-tuple-element.103), channel_id=1, source_target_pairs={{0,16},{16,0},{1,17},{17,1},{2,18},{18,2},{3,19},{19,3},{4,20},{20... | collective-permute-start | bytes 786440 | tf_op jit(solution)/shard_map/ppermute | solution.py:503
  77.2 11.5 %collective-permute-start.24 = (f32[24,16,128]{2,1,0:T(8,128)S(1)}, f32[24,16,128]{2,1,0:T(8,128)S(1)}, u32[]{:S(2)}, u32[]{:S(2)}) collective-permute-start(f32[24,16,128]{2,1,0:T(8,128)S(1)} %get-tuple-element.98.refs_1_), channel_id=1, source_target_pairs={{0,2},{2,0},{4,6},{6,4},{8,10},{10,8},{12,14},{14,12},{1,3},{3,1},... | collective-permute-start | bytes 589832 | tf_op jit(solution)/shard_map/ppermute | solution.py:497
  77.8 10.9 %collective-permute-start.25 = (f32[24,16,128]{2,1,0:T(8,128)S(1)}, f32[24,16,128]{2,1,0:T(8,128)S(1)}, u32[]{:S(2)}, u32[]{:S(2)}) collective-permute-start(f32[24,16,128]{2,1,0:T(8,128)S(1)} %get-tuple-element.99.refs_2_), channel_id=1, source_target_pairs={{2,4},{18,20},{3,5},{19,21},{4,2},{20,18},{5,3},{21,19},{6,8},{22,... | collective-permute-start | bytes 589832 | tf_op jit(solution)/shard_map/ppermute | solution.py:500
  77.8 5.6 %collective-permute-start.22 = (f32[32,8,128]{2,1,0:T(8,128)S(1)}, f32[32,8,128]{2,1,0:T(8,128)S(1)}, u32[]{:S(2)}, u32[]{:S(2)}) collective-permute-start(f32[32,8,128]{2,1,0:T(8,128)S(1)} %get-tuple-element.102), channel_id=1, source_target_pairs={{0,1},{1,0},{2,3},{3,2},{4,5},{5,4},{6,7},{7,6},{8,9},{9,8},{10,11... | collective-permute-start | bytes 393224 | tf_op jit(solution)/shard_map/ppermute | solution.py:503
  89.0 8.8 %collective-permute-start.27 = (f32[64,16,128]{2,1,0:T(8,128)S(1)}, f32[64,16,128]{2,1,0:T(8,128)S(1)}, u32[]{:S(2)}, u32[]{:S(2)}) collective-permute-start(f32[64,16,128]{2,1,0:T(8,128)S(1)} %get-tuple-element.110), channel_id=1, source_target_pairs={{0,16},{16,0},{1,17},{17,1},{2,18},{18,2},{3,19},{19,3},{4,20},{20... | collective-permute-start | bytes 1572872 | tf_op jit(solution)/shard_map/ppermute | solution.py:503
  89.1 8.7 %collective-permute-start.26 = (f32[64,8,128]{2,1,0:T(8,128)S(1)}, f32[64,8,128]{2,1,0:T(8,128)S(1)}, u32[]{:S(2)}, u32[]{:S(2)}) collective-permute-start(f32[64,8,128]{2,1,0:T(8,128)S(1)} %get-tuple-element.109), channel_id=1, source_target_pairs={{0,1},{1,0},{2,3},{3,2},{4,5},{5,4},{6,7},{7,6},{8,9},{9,8},{10,11... | collective-permute-start | bytes 786440 | tf_op jit(solution)/shard_map/ppermute | solution.py:503
  90.6 11.2 %collective-permute-start.28 = (f32[24,16,128]{2,1,0:T(8,128)S(1)}, f32[24,16,128]{2,1,0:T(8,128)S(1)}, u32[]{:S(2)}, u32[]{:S(2)}) collective-permute-start(f32[24,16,128]{2,1,0:T(8,128)S(1)} %get-tuple-element.105.refs_1_), channel_id=1, source_target_pairs={{0,2},{2,0},{4,6},{6,4},{8,10},{10,8},{12,14},{14,12},{1,3},{3,1},... | collective-permute-start | bytes 589832 | tf_op jit(solution)/shard_map/ppermute | solution.py:497
  91.2 10.7 %collective-permute-start.29 = (f32[24,16,128]{2,1,0:T(8,128)S(1)}, f32[24,16,128]{2,1,0:T(8,128)S(1)}, u32[]{:S(2)}, u32[]{:S(2)}) collective-permute-start(f32[24,16,128]{2,1,0:T(8,128)S(1)} %get-tuple-element.106.refs_2_), channel_id=1, source_target_pairs={{2,4},{18,20},{3,5},{19,21},{4,2},{20,18},{5,3},{21,19},{6,8},{22,... | collective-permute-start | bytes 589832 | tf_op jit(solution)/shard_map/ppermute | solution.py:500

commit v8 on v7

--- a/solution.py
+++ b/solution.py
@@ -119,7 +119,7 @@
             zmsg[n * X + i] = get(c, edge, i, slice(None))
 
     if layers is None:
-        lax.fori_loop(0, X, lambda i, carry: (one(i), carry)[1], 0, unroll=4)
+        lax.fori_loop(0, X, lambda i, carry: (one(i), carry)[1], 0, unroll=16)
     else:
         for i in layers:
             one(i)
@@ -144,7 +144,7 @@
                 F[c, t, i + 3, 8 + Y : 16 + Y, :] = jnp.where(row == 0, tile, zero)
         return carry
 
-    lax.fori_loop(0, X, step, 0, unroll=4)
+    lax.fori_loop(0, X, step, 0, unroll=16)
     zero = jnp.zeros((Y, LANES), jnp.float32)
     for side, near in enumerate(nears):
         high, _, layer, place = ends(info, side == 0, X, 3)
@@ -184,7 +184,7 @@
             emit(3, t, i, -(m * gw + G[0, t, i]) - S[2, t, i])
         return carry
 
-    lax.fori_loop(0, X, step, 0, unroll=4)
+    lax.fori_loop(0, X, step, 0, unroll=16)
 
 
 def first_main(info, f, near_in, near_out, ymsg, zmsg, zmat, mach, S, o, base, F, G, *, near_base):
@@ -232,7 +232,7 @@
                     o[c, t, i] = total
         return carry
 
-    lax.fori_loop(0, X, step, 0, unroll=4)
+    lax.fori_loop(0, X, step, 0, unroll=16)
 
 
 def last_body(info, f, halo_in, halo_out, o):
@@ -244,7 +244,7 @@
             o[c, i] = f[c, i]
         return carry
 
-    lax.fori_loop(0, X, copy, 0, unroll=4)
+    lax.fori_loop(0, X, copy, 0, unroll=16)
     for side, halo in enumerate((halo_in, halo_out)):
         _, has, layer, place = ends(info, side == 0, X, 3)
         weight = filter_weight * has.astype(jnp.float32)
@@ -315,7 +315,7 @@
                 o[c, t, i] = f[c, i, :, t * LANES : (t + 1) * LANES]
         return carry
 
-    lax.fori_loop(0, X, step, 0, unroll=4)
+    lax.fori_loop(0, X, step, 0, unroll=16)
     for side, near in enumerate((near_in, near_out)):
         _, _, layer, place = ends(info, side == 0, X, 3)
         for c in range(4):
@@ -350,7 +350,7 @@
             zmsg[zbase + c * X + i] = jnp.where(half == 0, last, first)
         return carry
 
-    lax.fori_loop(0, X, step, 0, unroll=4)
+    lax.fori_loop(0, X, step, 0, unroll=16)
 
 
 def getter(v):
@@ -399,7 +399,7 @@
                 V[c, t, i + 1, 8 : 8 + Y, :] = get(c, t, i, slice(None))
         return carry
 
-    lax.fori_loop(0, X, copy, 0, unroll=4)
+    lax.fori_loop(0, X, copy, 0, unroll=16)
     ACC[...] = jnp.zeros_like(ACC)
     lanes = lane_ids(Y)
     y = slice(8, 8 + Y)
@@ -435,7 +435,7 @@
                     v1[c, t, i] = center[c][t] + eddy_step * (viscosity * laplace - lamb[c])
         return carry
 
-    lax.fori_loop(0, X, step, 0, unroll=4)
+    lax.fori_loop(0, X, step, 0, unroll=16)
 
     copy_in.wait()
     for m in range(blocks // 2):

time: 104 us -> 103 us (level)
  no operation moved by 1% of the time
where the time goes in v8:
time: 103 us
  waiting for transfers between devices  62.1 us (60%)
  starting transfers between devices  19.3 us (19%)
  Pallas kernels  16.8 us (16%)
  local copies, waits for them, and re-layouts  4.63 us (4%)
    ppermute x8, waiting for transfers between devices, send_in(): return lax.ppermute(message, 'gx', even)  30.4 us
    ppermute x14, waiting for transfers between devices, send_sides(): return (lax.ppermute(ymsg, 'gy', swap), lax.ppermute(zmsg, 'grp', swap))  25.3 us
    pallas_call x15, Pallas kernels, call(): pl.pallas_call(lambda *refs: body(place(), *refs), out_shape=shapes, in_s...  16.8 us
    ppermute x8, starting transfers between devices, send_in(): return lax.ppermute(message, 'gx', even)  10.4 us
    ppermute x14, starting transfers between devices, send_sides(): return (lax.ppermute(ymsg, 'gy', swap), lax.ppermute(zmsg, 'grp', swap))  8.36 us
    ppermute x8, waiting for transfers between devices, send_out(): return lax.ppermute(message, mesh.axis_names, hops)  6.41 us
    unnamed x15, local copies, waits for them, and re-layouts  2.87 us
  transfers between devices with their start and end apart: 30, of which 15 were waited for; matrix products, arithmetic and copies ran while one was open for 1% of the time, Pallas kernels for 12%

profile of v8, /device:TPU:8, one launch (start us, length us, event | category | flops | bytes accessed | tf_op | source)
XLA Modules:
  0.0 103.1 jit_solution(8142023900579851779)
XLA Ops:
  0.0 1.4 %copy-done.1 = f32[32,16,3,256]{3,1,2,0:T(8,128)S(1)} copy-done((f32[32,16,3,256]{3,1,2,0:T(8,128)S(1)}, f32[32,16,3,256]{3,1,2,0:T(8,128)}, u32[]{:S(2)}) %copy-start.1) | copy-done | bytes 1572888
  1.4 0.2 shard_map.73
  1.7 1.6 %collective-permute-start.2 = (f32[24,8,128]{2,1,0:T(8,128)S(1)}, f32[24,8,128]{2,1,0:T(8,128)S(1)}, u32[]{:S(2)}, u32[]{:S(2)}) collective-permute-start(f32[24,8,128]{2,1,0:T(8,128)S(1)} %get-tuple-element.60), channel_id=1, source_target_pairs={{0,1},{1,0},{2,3},{3,2},{4,5},{5,4},{6,7},{7,6},{8,9},{9,8},{10,11... | collective-permute-start | bytes 294920 | tf_op jit(solution)/shard_map/ppermute | solution.py:503
  3.2 1.5 %collective-permute-start = (f32[6,16,128]{2,1,0:T(8,128)S(1)}, f32[6,16,128]{2,1,0:T(8,128)S(1)}, u32[]{:S(2)}, u32[]{:S(2)}) collective-permute-start(f32[6,16,128]{2,1,0:T(8,128)S(1)} %get-tuple-element.58), channel_id=1, source_target_pairs={{0,2},{2,0},{4,6},{6,4},{8,10},{10,8},{12,14},{14,12},{1,3},{3,1},... | collective-permute-start | bytes 147464 | tf_op jit(solution)/shard_map/ppermute | solution.py:497
  4.7 0.4 collective-permute-start.1
  5.2 1.4 %copy.11 = f32[16,16,4,256]{3,1,0,2:T(8,128)S(1)} copy(f32[16,16,4,256]{3,2,1,0:T(4,128)} %param.11) | data formatting | bytes 2097152 | tf_op args[4]
  6.6 0.7 collective-permute-done.refs_2_
  7.3 2.4 %collective-permute-done.1.refs_3_ = f32[6,16,128]{2,1,0:T(8,128)S(1)} collective-permute-done((f32[6,16,128]{2,1,0:T(8,128)S(1)}, f32[6,16,128]{2,1,0:T(8,128)S(1)}, u32[]{:S(2)}, u32[]{:S(2)}) %collective-permute-start.1) | collective-permute-done | bytes 49184 | tf_op jit(solution)/shard_map/ppermute | solution.py:500
  9.8 2.9 %shard_map.74 = (f32[3,2,32,16,128]{4,3,2,1,0:T(8,128)S(1)}, f32[3,2,16,16,128]{4,3,2,1,0:T(8,128)S(1)}, f32[54,16,128]{2,1,0:T(8,128)S(1)}, f32[54,16,128]{2,1,...) custom-call(s32[8]{0:T(128)S(1)} %copy-done.5, ...), custom_call_target="tpu_custom_call" | custom-call | flops 4000000 | bytes 9437216 | tf_op jit(solution)/shard_map/pallas_call | solution.py:35
  12.8 0.6 collective-permute-start.6
  13.4 0.5 collective-permute-start.4
  13.9 7.2 %collective-permute-done.4.refs_3_.refs_4_ = f32[56,8,128]{2,1,0:T(8,128)S(1)} collective-permute-done((f32[56,8,128]{2,1,0:T(8,128)S(1)}, f32[56,8,128]{2,1,0:T(8,128)S(1)}, u32[]{:S(2)}, u32[]{:S(2)}) %collective-permute-start.4) | collective-permute-done | bytes 229408 | tf_op jit(solution)/shard_map/ppermute | solution.py:503
  21.2 1.6 %shard_map.75 = (f32[4,2,16,16,128]{4,3,2,1,0:T(8,128)S(1)}, f32[4,2,16,16,128]{4,3,2,1,0:T(8,128)S(1)}) custom-call(f32[4,2,16,16,128]{4,3,2,1,0:T(8,128)S(1)} %get-tuple-element.62.refs_0_, f32[54,16,128]{2,1,0:T(8,128)S(1)} %get-tuple-element.63.refs_1_, f32[54,16,128]{2,1,0:T(8,128)S(1)} %get-tuple-element.64.refs_2_, ...), custom_call_target="tpu_custom_call" | custom-call | flops 4000000 | bytes 8585216 | tf_op jit(solution)/shard_map/pallas_call | solution.py:35
  22.8 12.0 %collective-permute-done.6.refs_1_.refs_4_.refs_2_ = f32[54,16,128]{2,1,0:T(8,128)S(1)} collective-permute-done((f32[54,16,128]{2,1,0:T(8,128)S(1)}, f32[54,16,128]{2,1,0:T(8,128)S(1)}, u32[]{:S(2)}, u32[]{:S(2)}) %collective-permute-start.6) | collective-permute-done | bytes 442400 | tf_op jit(solution)/shard_map/ppermute | solution.py:497
  34.8 0.2 shard_map.76
  35.1 0.6 collective-permute-start.10
  35.7 0.5 collective-permute-start.8
  36.2 2.2 %shard_map.77 = (f32[3,2,16,16,128]{4,3,2,1,0:T(8,128)S(1)}, f32[24,16,128]{2,1,0:T(8,128)S(1)}, f32[24,16,128]{2,1,0:T(8,128)S(1)}) custom-call(s32[8]{0:T(128)S(1)} %copy-done.5, f32[3,2,32,16,128]{4,3,2,1,0:T(8,128)S(1)} %get-tuple-element.70.refs_1_, f32[54,16,128]{2,1,0:T(8,128)S(1)} %collective-permute-done.6.refs_1_.refs_4_.refs_2_, ...), custom_call_target="tpu_custom_call" | custom-call | flops 4000000 | bytes 5177376 | tf_op jit(solution)/shard_map/pallas_call | solution.py:35
  38.4 2.9 %collective-permute-done.8.refs_5_ = f32[32,8,128]{2,1,0:T(8,128)S(1)} collective-permute-done((f32[32,8,128]{2,1,0:T(8,128)S(1)}, f32[32,8,128]{2,1,0:T(8,128)S(1)}, u32[]{:S(2)}, u32[]{:S(2)}) %collective-permute-start.8) | collective-permute-done | bytes 131104 | tf_op jit(solution)/shard_map/ppermute | solution.py:503
  41.3 1.8 %shard_map.78.refs_0_ = f32[4,2,16,16,128]{4,3,2,1,0:T(8,128)S(1)} custom-call(f32[4,2,16,16,128]{4,3,2,1,0:T(8,128)S(1)} %get-tuple-element.68.refs_0_, f32[24,16,128]{2,1,0:T(8,128)S(1)} %get-tuple-element.74.refs_1_, f32[24,16,128]{2,1,0:T(8,128)S(1)} %get-tuple-element.75.refs_2_, f32[8,16,128]{2,1,0:T(8,128)S(1)} %get-tuple-element.76.refs_3_, ...), custom_call_target="tpu_custom_call" | custom-call | flops 4000000 | bytes 7340032 | tf_op jit(solution)/shard_map/pallas_call | solution.py:35
  43.1 3.6 %collective-permute-done.10.refs_1_ = f32[24,16,128]{2,1,0:T(8,128)S(1)} collective-permute-done((f32[24,16,128]{2,1,0:T(8,128)S(1)}, f32[24,16,128]{2,1,0:T(8,128)S(1)}, u32[]{:S(2)}, u32[]{:S(2)}) %collective-permute-start.10) | collective-permute-done | bytes 196640 | tf_op jit(solution)/shard_map/ppermute | solution.py:497
  46.6 0.2 shard_map.79
  47.0 0.6 collective-permute-start.12
  47.5 0.5 collective-permute-start.14
  48.0 3.0 %collective-permute-start.16 = (f32[24,16,128]{2,1,0:T(8,128)S(1)}, f32[24,16,128]{2,1,0:T(8,128)S(1)}, u32[]{:S(2)}, u32[]{:S(2)}) collective-permute-start(f32[24,16,128]{2,1,0:T(8,128)S(1)} %get-tuple-element.88), channel_id=1, source_target_pairs={{0,2},{2,0},{4,6},{6,4},{8,10},{10,8},{12,14},{14,12},{1,3},{3,1},... | collective-permute-start | bytes 589832 | tf_op jit(solution)/shard_map/ppermute | solution.py:497
  51.1 4.6 %collective-permute-done.12.refs_5_ = f32[64,8,128]{2,1,0:T(8,128)S(1)} collective-permute-done((f32[64,8,128]{2,1,0:T(8,128)S(1)}, f32[64,8,128]{2,1,0:T(8,128)S(1)}, u32[]{:S(2)}, u32[]{:S(2)}) %collective-permute-start.12) | collective-permute-done | bytes 262176 | tf_op jit(solution)/shard_map/ppermute | solution.py:503
  55.7 1.9 %shard_map.80.refs_0_ = f32[4,2,16,16,128]{4,3,2,1,0:T(8,128)S(1)} custom-call(f32[4,2,16,16,128]{4,3,2,1,0:T(8,128)S(1)} %shard_map.78.refs_0_, f32[24,16,128]{2,1,0:T(8,128)S(1)} %get-tuple-element.81.refs_1_, f32[24,16,128]{2,1,0:T(8,128)S(1)} %get-tuple-element.82.refs_2_, f32[8,16,128]{2,1,0:T(8,128)S(1)} %get-tuple-element.83.refs_3_, ...), custom_call_target="tpu_custom_call" | custom-call | flops 4000000 | bytes 5767168 | tf_op jit(solution)/shard_map/pallas_call | solution.py:35
  57.6 1.9 %collective-permute-done.14.refs_1_ = f32[24,16,128]{2,1,0:T(8,128)S(1)} collective-permute-done((f32[24,16,128]{2,1,0:T(8,128)S(1)}, f32[24,16,128]{2,1,0:T(8,128)S(1)}, u32[]{:S(2)}, u32[]{:S(2)}) %collective-permute-start.14) | collective-permute-done | bytes 196640 | tf_op jit(solution)/shard_map/ppermute | solution.py:497
  59.8 3.0 %collective-permute-start.20 = (f32[24,16,128]{2,1,0:T(8,128)S(1)}, f32[24,16,128]{2,1,0:T(8,128)S(1)}, u32[]{:S(2)}, u32[]{:S(2)}) collective-permute-start(f32[24,16,128]{2,1,0:T(8,128)S(1)} %get-tuple-element.90.refs_1_), channel_id=1, source_target_pairs={{0,2},{2,0},{4,6},{6,4},{8,10},{10,8},{12,14},{14,12},{1,3},{3,1},... | collective-permute-start | bytes 589832 | tf_op jit(solution)/shard_map/ppermute | solution.py:497
  62.9 1.5 %collective-permute-start.18 = (f32[32,8,128]{2,1,0:T(8,128)S(1)}, f32[32,8,128]{2,1,0:T(8,128)S(1)}, u32[]{:S(2)}, u32[]{:S(2)}) collective-permute-start(f32[32,8,128]{2,1,0:T(8,128)S(1)} %get-tuple-element.92), channel_id=1, source_target_pairs={{0,1},{1,0},{2,3},{3,2},{4,5},{5,4},{6,7},{7,6},{8,9},{9,8},{10,11... | collective-permute-start | bytes 393224 | tf_op jit(solution)/shard_map/ppermute | solution.py:503
  64.4 4.0 %collective-permute-done.17.refs_5_ = f32[24,16,128]{2,1,0:T(8,128)S(1)} collective-permute-done((f32[24,16,128]{2,1,0:T(8,128)S(1)}, f32[24,16,128]{2,1,0:T(8,128)S(1)}, u32[]{:S(2)}, u32[]{:S(2)}) %collective-permute-start.17) | collective-permute-done | bytes 196640 | tf_op jit(solution)/shard_map/ppermute | solution.py:500
  68.5 1.6 %shard_map.82 = (f32[4,2,16,16,128]{4,3,2,1,0:T(8,128)S(1)}, f32[4,2,16,16,128]{4,3,2,1,0:T(8,128)S(1)}) custom-call(f32[4,2,16,16,128]{4,3,2,1,0:T(8,128)S(1)} %shard_map.80.refs_0_, f32[24,16,128]{2,1,0:T(8,128)S(1)} %get-tuple-element.90.refs_1_, f32[24,16,128]{2,1,0:T(8,128)S(1)} %get-tuple-element.91.refs_2_, ...), custom_call_target="tpu_custom_call" | custom-call | flops 4000000 | bytes 7208960 | tf_op jit(solution)/shard_map/pallas_call | solution.py:35
  70.1 6.3 %collective-permute-done.20.refs_1_ = f32[24,16,128]{2,1,0:T(8,128)S(1)} collective-permute-done((f32[24,16,128]{2,1,0:T(8,128)S(1)}, f32[24,16,128]{2,1,0:T(8,128)S(1)}, u32[]{:S(2)}, u32[]{:S(2)}) %collective-permute-start.20) | collective-permute-done | bytes 196640 | tf_op jit(solution)/shard_map/ppermute | solution.py:497
  76.3 0.2 shard_map.83
  76.5 0.1 collective-permute-start.23
  76.7 0.5 collective-permute-start.24
  77.2 1.5 %collective-permute-start.22 = (f32[32,8,128]{2,1,0:T(8,128)S(1)}, f32[32,8,128]{2,1,0:T(8,128)S(1)}, u32[]{:S(2)}, u32[]{:S(2)}) collective-permute-start(f32[32,8,128]{2,1,0:T(8,128)S(1)} %get-tuple-element.102), channel_id=1, source_target_pairs={{0,1},{1,0},{2,3},{3,2},{4,5},{5,4},{6,7},{7,6},{8,9},{9,8},{10,11... | collective-permute-start | bytes 393224 | tf_op jit(solution)/shard_map/ppermute | solution.py:503
  78.7 4.0 %collective-permute-done.22.refs_5_ = f32[32,8,128]{2,1,0:T(8,128)S(1)} collective-permute-done((f32[32,8,128]{2,1,0:T(8,128)S(1)}, f32[32,8,128]{2,1,0:T(8,128)S(1)}, u32[]{:S(2)}, u32[]{:S(2)}) %collective-permute-start.22) | collective-permute-done | bytes 131104 | tf_op jit(solution)/shard_map/ppermute | solution.py:503
  82.8 1.8 %shard_map.84.refs_0_ = f32[4,2,16,16,128]{4,3,2,1,0:T(8,128)S(1)} custom-call(f32[4,2,16,16,128]{4,3,2,1,0:T(8,128)S(1)} %get-tuple-element.95.refs_0_, f32[24,16,128]{2,1,0:T(8,128)S(1)} %get-tuple-element.98.refs_1_, f32[24,16,128]{2,1,0:T(8,128)S(1)} %get-tuple-element.99.refs_2_, f32[8,16,128]{2,1,0:T(8,128)S(1)} %get-tuple-element.100.refs_3_, ...), custom_call_target="tpu_custom_call" | custom-call | flops 4000000 | bytes 7340032 | tf_op jit(solution)/shard_map/pallas_call | solution.py:35
  84.5 3.6 %collective-permute-done.24.refs_1_ = f32[24,16,128]{2,1,0:T(8,128)S(1)} collective-permute-done((f32[24,16,128]{2,1,0:T(8,128)S(1)}, f32[24,16,128]{2,1,0:T(8,128)S(1)}, u32[]{:S(2)}, u32[]{:S(2)}) %collective-permute-start.24) | collective-permute-done | bytes 196640 | tf_op jit(solution)/shard_map/ppermute | solution.py:497
  88.1 0.2 shard_map.85
  88.4 1.6 %collective-permute-start.26 = (f32[64,8,128]{2,1,0:T(8,128)S(1)}, f32[64,8,128]{2,1,0:T(8,128)S(1)}, u32[]{:S(2)}, u32[]{:S(2)}) collective-permute-start(f32[64,8,128]{2,1,0:T(8,128)S(1)} %get-tuple-element.109), channel_id=1, source_target_pairs={{0,1},{1,0},{2,3},{3,2},{4,5},{5,4},{6,7},{7,6},{8,9},{9,8},{10,11... | collective-permute-start | bytes 786440 | tf_op jit(solution)/shard_map/ppermute | solution.py:503
  90.0 0.5 collective-permute-start.28
  90.6 6.6 %collective-permute-done.26.refs_5_ = f32[64,8,128]{2,1,0:T(8,128)S(1)} collective-permute-done((f32[64,8,128]{2,1,0:T(8,128)S(1)}, f32[64,8,128]{2,1,0:T(8,128)S(1)}, u32[]{:S(2)}, u32[]{:S(2)}) %collective-permute-start.26) | collective-permute-done | bytes 262176 | tf_op jit(solution)/shard_map/ppermute | solution.py:503
  97.2 1.9 %shard_map.86.refs_0_ = f32[4,16,16,256]{3,2,1,0:T(8,128)S(1)} custom-call(f32[4,2,16,16,128]{4,3,2,1,0:T(8,128)S(1)} %shard_map.84.refs_0_, f32[24,16,128]{2,1,0:T(8,128)S(1)} %get-tuple-element.105.refs_1_, f32[24,16,128]{2,1,0:T(8,128)S(1)} %get-tuple-element.106.refs_2_, f32[8,16,128]{2,1,0:T(8,128)S(1)} %get-tuple-element.107.refs_3_, ...), custom_call_target="tpu_custom_call" | custom-call | flops 4000000 | bytes 5767168 | tf_op jit(solution)/shard_map/pallas_call | solution.py:35
  99.0 2.2 %collective-permute-done.28.refs_1_ = f32[24,16,128]{2,1,0:T(8,128)S(1)} collective-permute-done((f32[24,16,128]{2,1,0:T(8,128)S(1)}, f32[24,16,128]{2,1,0:T(8,128)S(1)}, u32[]{:S(2)}, u32[]{:S(2)}) %collective-permute-start.28) | collective-permute-done | bytes 196640 | tf_op jit(solution)/shard_map/ppermute | solution.py:497
  101.2 0.1 shard_map.87
  101.4 1.7 %copy.9 = f32[16,16,4,256]{3,2,1,0:T(4,128)} copy(f32[16,16,4,256]{3,1,0,2:T(8,128)S(1)} %bitcast.8) | data formatting | bytes 2097152 | tf_op jit(solution)/shard_map/transpose | solution.py:612
  (44 shorter events, 0.9 us)
Async XLA Ops:
  0.0 1.4 %copy-start.1 = (f32[32,16,3,256]{3,1,2,0:T(8,128)S(1)}, f32[32,16,3,256]{3,1,2,0:T(8,128)}, u32[]{:S(2)}) copy-start(f32[32,16,3,256]{3,1,2,0:T(8,128)} %param.7) | copy-start | bytes 4718596
  1.4 8.3 %copy-start.2 = (f32[32,16,3,256]{3,1,2,0:T(8,128)S(1)}, f32[32,16,3,256]{3,1,2,0:T(8,128)}, u32[]{:S(2)}) copy-start(f32[32,16,3,256]{3,1,2,0:T(8,128)} %param.7) | copy-start | bytes 4718596
  1.4 8.3 %copy-start.4 = (bf16[8,1,2,64,64]{4,3,2,1,0:T(8,128)(2,1)S(1)}, bf16[8,1,2,64,64]{4,3,2,1,0:T(8,128)(2,1)}, u32[]{:S(2)}) copy-start(bf16[8,1,2,64,64]{4,3,2,1,0:T(8,128)(2,1)} %param.9) | copy-start | bytes 393220
  1.4 8.3 %copy-start.5 = (s32[8]{0:T(128)S(1)}, s32[8]{0:T(128)}, u32[]{:S(2)}) copy-start(s32[8]{0:T(128)} %refs_0_.3) | copy-start | bytes 100
  1.6 8.2 %collective-permute-start.3 = (f32[96,16,128]{2,1,0:T(8,128)S(1)}, f32[96,16,128]{2,1,0:T(8,128)S(1)}, u32[]{:S(2)}, u32[]{:S(2)}) collective-permute-start(f32[96,16,128]{2,1,0:T(8,128)S(1)} %get-tuple-element.61), channel_id=1, source_target_pairs={{0,16},{16,0},{1,17},{17,1},{2,18},{18,2},{3,19},{19,3},{4,20},{20... | collective-permute-start | bytes 2359304 | tf_op jit(solution)/shard_map/ppermute | solution.py:503
  1.7 8.1 %collective-permute-start.2 = (f32[24,8,128]{2,1,0:T(8,128)S(1)}, f32[24,8,128]{2,1,0:T(8,128)S(1)}, u32[]{:S(2)}, u32[]{:S(2)}) collective-permute-start(f32[24,8,128]{2,1,0:T(8,128)S(1)} %get-tuple-element.60), channel_id=1, source_target_pairs={{0,1},{1,0},{2,3},{3,2},{4,5},{5,4},{6,7},{7,6},{8,9},{9,8},{10,11... | collective-permute-start | bytes 294920 | tf_op jit(solution)/shard_map/ppermute | solution.py:503
  3.2 4.1 %collective-permute-start = (f32[6,16,128]{2,1,0:T(8,128)S(1)}, f32[6,16,128]{2,1,0:T(8,128)S(1)}, u32[]{:S(2)}, u32[]{:S(2)}) collective-permute-start(f32[6,16,128]{2,1,0:T(8,128)S(1)} %get-tuple-element.58), channel_id=1, source_target_pairs={{0,2},{2,0},{4,6},{6,4},{8,10},{10,8},{12,14},{14,12},{1,3},{3,1},... | collective-permute-start | bytes 147464 | tf_op jit(solution)/shard_map/ppermute | solution.py:497
  4.7 5.0 %collective-permute-start.1 = (f32[6,16,128]{2,1,0:T(8,128)S(1)}, f32[6,16,128]{2,1,0:T(8,128)S(1)}, u32[]{:S(2)}, u32[]{:S(2)}) collective-permute-start(f32[6,16,128]{2,1,0:T(8,128)S(1)} %get-tuple-element.59), channel_id=1, source_target_pairs={{2,4},{18,20},{3,5},{19,21},{4,2},{20,18},{5,3},{21,19},{6,8},{22,... | collective-permute-start | bytes 147464 | tf_op jit(solution)/shard_map/ppermute | solution.py:500
  9.8 11.3 %copy-start.6 = (f32[16,16]{1,0:T(8,128)S(1)}, f32[16,16]{1,0:T(8,128)}, u32[]{:S(2)}) copy-start(f32[16,16]{1,0:T(8,128)} %param.8) | copy-start | bytes 3076
  9.8 11.4 %copy-start = (bf16[2,1152,256]{2,1,0:T(8,128)(2,1)S(1)}, bf16[2,1152,256]{2,1,0:T(8,128)(2,1)}, u32[]{:S(2)}) copy-start(bf16[2,1152,256]{2,1,0:T(8,128)(2,1)} %constant.4.clone.refs_5_.refs_7_) | copy-start | bytes 3538948
  12.7 8.4 %collective-permute-start.5 = (f32[128,16,128]{2,1,0:T(8,128)S(1)}, f32[128,16,128]{2,1,0:T(8,128)S(1)}, u32[]{:S(2)}, u32[]{:S(2)}) collective-permute-start(f32[128,16,128]{2,1,0:T(8,128)S(1)} %get-tuple-element.66), channel_id=1, source_target_pairs={{0,16},{16,0},{1,17},{17,1},{2,18},{18,2},{3,19},{19,3},{4,20},{20... | collective-permute-start | bytes 3145736 | tf_op jit(solution)/shard_map/ppermute | solution.py:503
  12.8 22.1 %collective-permute-start.6 = (f32[54,16,128]{2,1,0:T(8,128)S(1)}, f32[54,16,128]{2,1,0:T(8,128)S(1)}, u32[]{:S(2)}, u32[]{:S(2)}) collective-permute-start(f32[54,16,128]{2,1,0:T(8,128)S(1)} %get-tuple-element.63.refs_1_), channel_id=1, source_target_pairs={{0,2},{2,0},{4,6},{6,4},{8,10},{10,8},{12,14},{14,12},{1,3},{3,1},... | collective-permute-start | bytes 1327112 | tf_op jit(solution)/shard_map/ppermute | solution.py:497
  13.4 21.5 %collective-permute-start.7 = (f32[54,16,128]{2,1,0:T(8,128)S(1)}, f32[54,16,128]{2,1,0:T(8,128)S(1)}, u32[]{:S(2)}, u32[]{:S(2)}) collective-permute-start(f32[54,16,128]{2,1,0:T(8,128)S(1)} %get-tuple-element.64.refs_2_), channel_id=1, source_target_pairs={{2,4},{18,20},{3,5},{19,21},{4,2},{20,18},{5,3},{21,19},{6,8},{22,... | collective-permute-start | bytes 1327112 | tf_op jit(solution)/shard_map/ppermute | solution.py:500
  13.4 7.7 %collective-permute-start.4 = (f32[56,8,128]{2,1,0:T(8,128)S(1)}, f32[56,8,128]{2,1,0:T(8,128)S(1)}, u32[]{:S(2)}, u32[]{:S(2)}) collective-permute-start(f32[56,8,128]{2,1,0:T(8,128)S(1)} %get-tuple-element.65), channel_id=1, source_target_pairs={{0,1},{1,0},{2,3},{3,2},{4,5},{5,4},{6,7},{7,6},{8,9},{9,8},{10,11... | collective-permute-start | bytes 688136 | tf_op jit(solution)/shard_map/ppermute | solution.py:503
  35.0 6.3 %collective-permute-start.9 = (f32[32,16,128]{2,1,0:T(8,128)S(1)}, f32[32,16,128]{2,1,0:T(8,128)S(1)}, u32[]{:S(2)}, u32[]{:S(2)}) collective-permute-start(f32[32,16,128]{2,1,0:T(8,128)S(1)} %get-tuple-element.79), channel_id=1, source_target_pairs={{0,16},{16,0},{1,17},{17,1},{2,18},{18,2},{3,19},{19,3},{4,20},{20... | collective-permute-start | bytes 786440 | tf_op jit(solution)/shard_map/ppermute | solution.py:503
  35.1 11.5 %collective-permute-start.10 = (f32[24,16,128]{2,1,0:T(8,128)S(1)}, f32[24,16,128]{2,1,0:T(8,128)S(1)}, u32[]{:S(2)}, u32[]{:S(2)}) collective-permute-start(f32[24,16,128]{2,1,0:T(8,128)S(1)} %get-tuple-element.74.refs_1_), channel_id=1, source_target_pairs={{0,2},{2,0},{4,6},{6,4},{8,10},{10,8},{12,14},{14,12},{1,3},{3,1},... | collective-permute-start | bytes 589832 | tf_op jit(solution)/shard_map/ppermute | solution.py:497
  35.7 10.9 %collective-permute-start.11 = (f32[24,16,128]{2,1,0:T(8,128)S(1)}, f32[24,16,128]{2,1,0:T(8,128)S(1)}, u32[]{:S(2)}, u32[]{:S(2)}) collective-permute-start(f32[24,16,128]{2,1,0:T(8,128)S(1)} %get-tuple-element.75.refs_2_), channel_id=1, source_target_pairs={{2,4},{18,20},{3,5},{19,21},{4,2},{20,18},{5,3},{21,19},{6,8},{22,... | collective-permute-start | bytes 589832 | tf_op jit(solution)/shard_map/ppermute | solution.py:500
  35.7 5.6 %collective-permute-start.8 = (f32[32,8,128]{2,1,0:T(8,128)S(1)}, f32[32,8,128]{2,1,0:T(8,128)S(1)}, u32[]{:S(2)}, u32[]{:S(2)}) collective-permute-start(f32[32,8,128]{2,1,0:T(8,128)S(1)} %get-tuple-element.78), channel_id=1, source_target_pairs={{0,1},{1,0},{2,3},{3,2},{4,5},{5,4},{6,7},{7,6},{8,9},{9,8},{10,11... | collective-permute-start | bytes 393224 | tf_op jit(solution)/shard_map/ppermute | solution.py:503
  43.0 12.6 %copy-start.3 = (bf16[2,1152,256]{2,1,0:T(8,128)(2,1)S(1)}, bf16[2,1152,256]{2,1,0:T(8,128)(2,1)}, u32[]{:S(2)}) copy-start(bf16[2,1152,256]{2,1,0:T(8,128)(2,1)} %constant.5.clone.refs_7_) | copy-start | bytes 3538948
  46.9 8.8 %collective-permute-start.13 = (f32[64,16,128]{2,1,0:T(8,128)S(1)}, f32[64,16,128]{2,1,0:T(8,128)S(1)}, u32[]{:S(2)}, u32[]{:S(2)}) collective-permute-start(f32[64,16,128]{2,1,0:T(8,128)S(1)} %get-tuple-element.86), channel_id=1, source_target_pairs={{0,16},{16,0},{1,17},{17,1},{2,18},{18,2},{3,19},{19,3},{4,20},{20... | collective-permute-start | bytes 1572872 | tf_op jit(solution)/shard_map/ppermute | solution.py:503
  47.0 8.7 %collective-permute-start.12 = (f32[64,8,128]{2,1,0:T(8,128)S(1)}, f32[64,8,128]{2,1,0:T(8,128)S(1)}, u32[]{:S(2)}, u32[]{:S(2)}) collective-permute-start(f32[64,8,128]{2,1,0:T(8,128)S(1)} %get-tuple-element.85), channel_id=1, source_target_pairs={{0,1},{1,0},{2,3},{3,2},{4,5},{5,4},{6,7},{7,6},{8,9},{9,8},{10,11... | collective-permute-start | bytes 786440 | tf_op jit(solution)/shard_map/ppermute | solution.py:503
  47.5 12.0 %collective-permute-start.14 = (f32[24,16,128]{2,1,0:T(8,128)S(1)}, f32[24,16,128]{2,1,0:T(8,128)S(1)}, u32[]{:S(2)}, u32[]{:S(2)}) collective-permute-start(f32[24,16,128]{2,1,0:T(8,128)S(1)} %get-tuple-element.81.refs_1_), channel_id=1, source_target_pairs={{0,2},{2,0},{4,6},{6,4},{8,10},{10,8},{12,14},{14,12},{1,3},{3,1},... | collective-permute-start | bytes 589832 | tf_op jit(solution)/shard_map/ppermute | solution.py:497
  48.0 11.4 %collective-permute-start.15 = (f32[24,16,128]{2,1,0:T(8,128)S(1)}, f32[24,16,128]{2,1,0:T(8,128)S(1)}, u32[]{:S(2)}, u32[]{:S(2)}) collective-permute-start(f32[24,16,128]{2,1,0:T(8,128)S(1)} %get-tuple-element.82.refs_2_), channel_id=1, source_target_pairs={{2,4},{18,20},{3,5},{19,21},{4,2},{20,18},{5,3},{21,19},{6,8},{22,... | collective-permute-start | bytes 589832 | tf_op jit(solution)/shard_map/ppermute | solution.py:500
  48.0 14.9 %collective-permute-start.16 = (f32[24,16,128]{2,1,0:T(8,128)S(1)}, f32[24,16,128]{2,1,0:T(8,128)S(1)}, u32[]{:S(2)}, u32[]{:S(2)}) collective-permute-start(f32[24,16,128]{2,1,0:T(8,128)S(1)} %get-tuple-element.88), channel_id=1, source_target_pairs={{0,2},{2,0},{4,6},{6,4},{8,10},{10,8},{12,14},{14,12},{1,3},{3,1},... | collective-permute-start | bytes 589832 | tf_op jit(solution)/shard_map/ppermute | solution.py:497
  59.6 8.9 %collective-permute-start.19 = (f32[32,16,128]{2,1,0:T(8,128)S(1)}, f32[32,16,128]{2,1,0:T(8,128)S(1)}, u32[]{:S(2)}, u32[]{:S(2)}) collective-permute-start(f32[32,16,128]{2,1,0:T(8,128)S(1)} %get-tuple-element.93), channel_id=1, source_target_pairs={{0,16},{16,0},{1,17},{17,1},{2,18},{18,2},{3,19},{19,3},{4,20},{20... | collective-permute-start | bytes 786440 | tf_op jit(solution)/shard_map/ppermute | solution.py:503
  59.7 8.8 %collective-permute-start.17 = (f32[24,16,128]{2,1,0:T(8,128)S(1)}, f32[24,16,128]{2,1,0:T(8,128)S(1)}, u32[]{:S(2)}, u32[]{:S(2)}) collective-permute-start(f32[24,16,128]{2,1,0:T(8,128)S(1)} %get-tuple-element.89), channel_id=1, source_target_pairs={{2,4},{18,20},{3,5},{19,21},{4,2},{20,18},{5,3},{21,19},{6,8},{22,... | collective-permute-start | bytes 589832 | tf_op jit(solution)/shard_map/ppermute | solution.py:500
  59.8 16.6 %collective-permute-start.20 = (f32[24,16,128]{2,1,0:T(8,128)S(1)}, f32[24,16,128]{2,1,0:T(8,128)S(1)}, u32[]{:S(2)}, u32[]{:S(2)}) collective-permute-start(f32[24,16,128]{2,1,0:T(8,128)S(1)} %get-tuple-element.90.refs_1_), channel_id=1, source_target_pairs={{0,2},{2,0},{4,6},{6,4},{8,10},{10,8},{12,14},{14,12},{1,3},{3,1},... | collective-permute-start | bytes 589832 | tf_op jit(solution)/shard_map/ppermute | solution.py:497
  62.8 13.5 %collective-permute-start.21 = (f32[24,16,128]{2,1,0:T(8,128)S(1)}, f32[24,16,128]{2,1,0:T(8,128)S(1)}, u32[]{:S(2)}, u32[]{:S(2)}) collective-permute-start(f32[24,16,128]{2,1,0:T(8,128)S(1)} %get-tuple-element.91.refs_2_), channel_id=1, source_target_pairs={{2,4},{18,20},{3,5},{19,21},{4,2},{20,18},{5,3},{21,19},{6,8},{22,... | collective-permute-start | bytes 589832 | tf_op jit(solution)/shard_map/ppermute | solution.py:500
  62.9 5.5 %collective-permute-start.18 = (f32[32,8,128]{2,1,0:T(8,128)S(1)}, f32[32,8,128]{2,1,0:T(8,128)S(1)}, u32[]{:S(2)}, u32[]{:S(2)}) collective-permute-start(f32[32,8,128]{2,1,0:T(8,128)S(1)} %get-tuple-element.92), channel_id=1, source_target_pairs={{0,1},{1,0},{2,3},{3,2},{4,5},{5,4},{6,7},{7,6},{8,9},{9,8},{10,11... | collective-permute-start | bytes 393224 | tf_op jit(solution)/shard_map/ppermute | solution.py:503
  76.5 6.3 %collective-permute-start.23 = (f32[32,16,128]{2,1,0:T(8,128)S(1)}, f32[32,16,128]{2,1,0:T(8,128)S(1)}, u32[]{:S(2)}, u32[]{:S(2)}) collective-permute-start(f32[32,16,128]{2,1,0:T(8,128)S(1)} %get-tuple-element.103), channel_id=1, source_target_pairs={{0,16},{16,0},{1,17},{17,1},{2,18},{18,2},{3,19},{19,3},{4,20},{20... | collective-permute-start | bytes 786440 | tf_op jit(solution)/shard_map/ppermute | solution.py:503
  76.7 11.5 %collective-permute-start.24 = (f32[24,16,128]{2,1,0:T(8,128)S(1)}, f32[24,16,128]{2,1,0:T(8,128)S(1)}, u32[]{:S(2)}, u32[]{:S(2)}) collective-permute-start(f32[24,16,128]{2,1,0:T(8,128)S(1)} %get-tuple-element.98.refs_1_), channel_id=1, source_target_pairs={{0,2},{2,0},{4,6},{6,4},{8,10},{10,8},{12,14},{14,12},{1,3},{3,1},... | collective-permute-start | bytes 589832 | tf_op jit(solution)/shard_map/ppermute | solution.py:497
  77.2 10.9 %collective-permute-start.25 = (f32[24,16,128]{2,1,0:T(8,128)S(1)}, f32[24,16,128]{2,1,0:T(8,128)S(1)}, u32[]{:S(2)}, u32[]{:S(2)}) collective-permute-start(f32[24,16,128]{2,1,0:T(8,128)S(1)} %get-tuple-element.99.refs_2_), channel_id=1, source_target_pairs={{2,4},{18,20},{3,5},{19,21},{4,2},{20,18},{5,3},{21,19},{6,8},{22,... | collective-permute-start | bytes 589832 | tf_op jit(solution)/shard_map/ppermute | solution.py:500
  77.2 5.6 %collective-permute-start.22 = (f32[32,8,128]{2,1,0:T(8,128)S(1)}, f32[32,8,128]{2,1,0:T(8,128)S(1)}, u32[]{:S(2)}, u32[]{:S(2)}) collective-permute-start(f32[32,8,128]{2,1,0:T(8,128)S(1)} %get-tuple-element.102), channel_id=1, source_target_pairs={{0,1},{1,0},{2,3},{3,2},{4,5},{5,4},{6,7},{7,6},{8,9},{9,8},{10,11... | collective-permute-start | bytes 393224 | tf_op jit(solution)/shard_map/ppermute | solution.py:503
  88.4 8.8 %collective-permute-start.27 = (f32[64,16,128]{2,1,0:T(8,128)S(1)}, f32[64,16,128]{2,1,0:T(8,128)S(1)}, u32[]{:S(2)}, u32[]{:S(2)}) collective-permute-start(f32[64,16,128]{2,1,0:T(8,128)S(1)} %get-tuple-element.110), channel_id=1, source_target_pairs={{0,16},{16,0},{1,17},{17,1},{2,18},{18,2},{3,19},{19,3},{4,20},{20... | collective-permute-start | bytes 1572872 | tf_op jit(solution)/shard_map/ppermute | solution.py:503
  88.4 8.7 %collective-permute-start.26 = (f32[64,8,128]{2,1,0:T(8,128)S(1)}, f32[64,8,128]{2,1,0:T(8,128)S(1)}, u32[]{:S(2)}, u32[]{:S(2)}) collective-permute-start(f32[64,8,128]{2,1,0:T(8,128)S(1)} %get-tuple-element.109), channel_id=1, source_target_pairs={{0,1},{1,0},{2,3},{3,2},{4,5},{5,4},{6,7},{7,6},{8,9},{9,8},{10,11... | collective-permute-start | bytes 786440 | tf_op jit(solution)/shard_map/ppermute | solution.py:503
  90.0 11.2 %collective-permute-start.28 = (f32[24,16,128]{2,1,0:T(8,128)S(1)}, f32[24,16,128]{2,1,0:T(8,128)S(1)}, u32[]{:S(2)}, u32[]{:S(2)}) collective-permute-start(f32[24,16,128]{2,1,0:T(8,128)S(1)} %get-tuple-element.105.refs_1_), channel_id=1, source_target_pairs={{0,2},{2,0},{4,6},{6,4},{8,10},{10,8},{12,14},{14,12},{1,3},{3,1},... | collective-permute-start | bytes 589832 | tf_op jit(solution)/shard_map/ppermute | solution.py:497
  90.6 10.6 %collective-permute-start.29 = (f32[24,16,128]{2,1,0:T(8,128)S(1)}, f32[24,16,128]{2,1,0:T(8,128)S(1)}, u32[]{:S(2)}, u32[]{:S(2)}) collective-permute-start(f32[24,16,128]{2,1,0:T(8,128)S(1)} %get-tuple-element.106.refs_2_), channel_id=1, source_target_pairs={{2,4},{18,20},{3,5},{19,21},{4,2},{20,18},{5,3},{21,19},{6,8},{22,... | collective-permute-start | bytes 589832 | tf_op jit(solution)/shard_map/ppermute | solution.py:500

commit v9 on v8

--- a/solution.py
+++ b/solution.py
@@ -569,7 +569,8 @@
         whole = [state, near_in, near_out]
         for step in range(STEPS):
             if step:
-                whole[1], terms = lax.optimization_barrier((whole[1], terms))
+                terms = list(terms)
+                whole[1], terms[0] = lax.optimization_barrier((whole[1], terms[0]))
             part, base = call(
                 functools.partial(first_main, near_base=at if step == 0 else 0), [grid, grid], [*whole, *sides, rate_z, mach, S], [F, G2], flops=4000000
             )

time: 103 us -> 103 us (level)
    ppermute x8, waiting for transfers between devices: 6.41 us -> 2.41 us  [send_out(): return lax.ppermute(message, mesh.axis_names, hops)]
    ppermute x14, waiting for transfers between devices: 25.3 us -> 28.9 us  [send_sides(): return (lax.ppermute(ymsg, 'gy', swap), lax.ppermute(zmsg, 'grp', swap))]
where the time goes in v9:
time: 103 us
  waiting for transfers between devices  62.1 us (60%)
  starting transfers between devices  19.2 us (19%)
  Pallas kernels  16.9 us (16%)
  local copies, waits for them, and re-layouts  4.63 us (4%)
    ppermute x8, waiting for transfers between devices, send_in(): return lax.ppermute(message, 'gx', even)  30.8 us
    ppermute x14, waiting for transfers between devices, send_sides(): return (lax.ppermute(ymsg, 'gy', swap), lax.ppermute(zmsg, 'grp', swap))  28.9 us
    pallas_call x15, Pallas kernels, call(): pl.pallas_call(lambda *refs: body(place(), *refs), out_shape=shapes, in_s...  16.9 us
    ppermute x8, starting transfers between devices, send_in(): return lax.ppermute(message, 'gx', even)  10.4 us
    ppermute x14, starting transfers between devices, send_sides(): return (lax.ppermute(ymsg, 'gy', swap), lax.ppermute(zmsg, 'grp', swap))  8.36 us
    unnamed x15, local copies, waits for them, and re-layouts  2.87 us
    ppermute x8, waiting for transfers between devices, send_out(): return lax.ppermute(message, mesh.axis_names, hops)  2.41 us
  transfers between devices with their start and end apart: 30, of which 15 were waited for; matrix products, arithmetic and copies ran while one was open for 1% of the time, Pallas kernels for 12%

profile of v9, /device:TPU:8, one launch (start us, length us, event | category | flops | bytes accessed | tf_op | source)
XLA Modules:
  0.0 103.1 jit_solution(17942596811619460433)
XLA Ops:
  0.0 1.4 %copy-done.1 = f32[32,16,3,256]{3,1,2,0:T(8,128)S(1)} copy-done((f32[32,16,3,256]{3,1,2,0:T(8,128)S(1)}, f32[32,16,3,256]{3,1,2,0:T(8,128)}, u32[]{:S(2)}) %copy-start.1) | copy-done | bytes 1572888
  1.4 0.2 shard_map.73
  1.7 1.6 %collective-permute-start.2 = (f32[24,8,128]{2,1,0:T(8,128)S(1)}, f32[24,8,128]{2,1,0:T(8,128)S(1)}, u32[]{:S(2)}, u32[]{:S(2)}) collective-permute-start(f32[24,8,128]{2,1,0:T(8,128)S(1)} %get-tuple-element.59), channel_id=1, source_target_pairs={{0,1},{1,0},{2,3},{3,2},{4,5},{5,4},{6,7},{7,6},{8,9},{9,8},{10,11... | collective-permute-start | bytes 294920 | tf_op jit(solution)/shard_map/ppermute | solution.py:503
  3.2 1.5 %collective-permute-start = (f32[6,16,128]{2,1,0:T(8,128)S(1)}, f32[6,16,128]{2,1,0:T(8,128)S(1)}, u32[]{:S(2)}, u32[]{:S(2)}) collective-permute-start(f32[6,16,128]{2,1,0:T(8,128)S(1)} %get-tuple-element.57), channel_id=1, source_target_pairs={{0,2},{2,0},{4,6},{6,4},{8,10},{10,8},{12,14},{14,12},{1,3},{3,1},... | collective-permute-start | bytes 147464 | tf_op jit(solution)/shard_map/ppermute | solution.py:497
  4.7 0.4 collective-permute-start.1
  5.2 1.4 %copy.11 = f32[16,16,4,256]{3,1,0,2:T(8,128)S(1)} copy(f32[16,16,4,256]{3,2,1,0:T(4,128)} %param.11) | data formatting | bytes 2097152 | tf_op args[4]
  6.6 0.7 collective-permute-done.refs_2_
  7.3 2.4 %collective-permute-done.1.refs_3_ = f32[6,16,128]{2,1,0:T(8,128)S(1)} collective-permute-done((f32[6,16,128]{2,1,0:T(8,128)S(1)}, f32[6,16,128]{2,1,0:T(8,128)S(1)}, u32[]{:S(2)}, u32[]{:S(2)}) %collective-permute-start.1) | collective-permute-done | bytes 49184 | tf_op jit(solution)/shard_map/ppermute | solution.py:500
  9.8 2.9 %shard_map.74 = (f32[3,2,32,16,128]{4,3,2,1,0:T(8,128)S(1)}, f32[3,2,16,16,128]{4,3,2,1,0:T(8,128)S(1)}, f32[54,16,128]{2,1,0:T(8,128)S(1)}, f32[54,16,128]{2,1,...) custom-call(s32[8]{0:T(128)S(1)} %copy-done.5, ...), custom_call_target="tpu_custom_call" | custom-call | flops 4000000 | bytes 9437216 | tf_op jit(solution)/shard_map/pallas_call | solution.py:35
  12.8 0.6 collective-permute-start.6
  13.4 0.5 collective-permute-start.4
  13.9 7.2 %collective-permute-done.4.refs_3_.refs_4_ = f32[56,8,128]{2,1,0:T(8,128)S(1)} collective-permute-done((f32[56,8,128]{2,1,0:T(8,128)S(1)}, f32[56,8,128]{2,1,0:T(8,128)S(1)}, u32[]{:S(2)}, u32[]{:S(2)}) %collective-permute-start.4) | collective-permute-done | bytes 229408 | tf_op jit(solution)/shard_map/ppermute | solution.py:503
  21.2 1.6 %shard_map.75 = (f32[4,2,16,16,128]{4,3,2,1,0:T(8,128)S(1)}, f32[4,2,16,16,128]{4,3,2,1,0:T(8,128)S(1)}) custom-call(f32[4,2,16,16,128]{4,3,2,1,0:T(8,128)S(1)} %get-tuple-element.61.refs_0_, f32[54,16,128]{2,1,0:T(8,128)S(1)} %get-tuple-element.62.refs_1_, f32[54,16,128]{2,1,0:T(8,128)S(1)} %get-tuple-element.63.refs_2_, ...), custom_call_target="tpu_custom_call" | custom-call | flops 4000000 | bytes 8585216 | tf_op jit(solution)/shard_map/pallas_call | solution.py:35
  22.8 12.0 %collective-permute-done.6.refs_1_.refs_4_.refs_2_ = f32[54,16,128]{2,1,0:T(8,128)S(1)} collective-permute-done((f32[54,16,128]{2,1,0:T(8,128)S(1)}, f32[54,16,128]{2,1,0:T(8,128)S(1)}, u32[]{:S(2)}, u32[]{:S(2)}) %collective-permute-start.6) | collective-permute-done | bytes 442400 | tf_op jit(solution)/shard_map/ppermute | solution.py:497
  34.9 0.2 shard_map.76
  35.1 0.6 collective-permute-start.10
  35.7 0.5 collective-permute-start.8
  36.2 2.2 %shard_map.77 = (f32[3,2,16,16,128]{4,3,2,1,0:T(8,128)S(1)}, f32[24,16,128]{2,1,0:T(8,128)S(1)}, f32[24,16,128]{2,1,0:T(8,128)S(1)}) custom-call(s32[8]{0:T(128)S(1)} %copy-done.5, f32[3,2,32,16,128]{4,3,2,1,0:T(8,128)S(1)} %get-tuple-element.69.refs_1_, f32[54,16,128]{2,1,0:T(8,128)S(1)} %collective-permute-done.6.refs_1_.refs_4_.refs_2_, ...), custom_call_target="tpu_custom_call" | custom-call | flops 4000000 | bytes 5177376 | tf_op jit(solution)/shard_map/pallas_call | solution.py:35
  38.4 2.9 %collective-permute-done.8.refs_5_ = f32[32,8,128]{2,1,0:T(8,128)S(1)} collective-permute-done((f32[32,8,128]{2,1,0:T(8,128)S(1)}, f32[32,8,128]{2,1,0:T(8,128)S(1)}, u32[]{:S(2)}, u32[]{:S(2)}) %collective-permute-start.8) | collective-permute-done | bytes 131104 | tf_op jit(solution)/shard_map/ppermute | solution.py:503
  41.3 1.8 %shard_map.78.refs_0_ = f32[4,2,16,16,128]{4,3,2,1,0:T(8,128)S(1)} custom-call(f32[4,2,16,16,128]{4,3,2,1,0:T(8,128)S(1)} %get-tuple-element.67.refs_0_, f32[24,16,128]{2,1,0:T(8,128)S(1)} %get-tuple-element.73.refs_1_, f32[24,16,128]{2,1,0:T(8,128)S(1)} %get-tuple-element.74.refs_2_, f32[8,16,128]{2,1,0:T(8,128)S(1)} %get-tuple-element.75.refs_3_, ...), custom_call_target="tpu_custom_call" | custom-call | flops 4000000 | bytes 7340032 | tf_op jit(solution)/shard_map/pallas_call | solution.py:35
  43.1 3.6 %collective-permute-done.10.refs_1_ = f32[24,16,128]{2,1,0:T(8,128)S(1)} collective-permute-done((f32[24,16,128]{2,1,0:T(8,128)S(1)}, f32[24,16,128]{2,1,0:T(8,128)S(1)}, u32[]{:S(2)}, u32[]{:S(2)}) %collective-permute-start.10) | collective-permute-done | bytes 196640 | tf_op jit(solution)/shard_map/ppermute | solution.py:497
  46.6 0.2 shard_map.79
  47.0 0.6 collective-permute-start.12
  47.5 0.5 collective-permute-start.14
  48.1 3.0 %collective-permute-start.16 = (f32[24,16,128]{2,1,0:T(8,128)S(1)}, f32[24,16,128]{2,1,0:T(8,128)S(1)}, u32[]{:S(2)}, u32[]{:S(2)}) collective-permute-start(f32[24,16,128]{2,1,0:T(8,128)S(1)} %get-tuple-element.87), channel_id=1, source_target_pairs={{0,2},{2,0},{4,6},{6,4},{8,10},{10,8},{12,14},{14,12},{1,3},{3,1},... | collective-permute-start | bytes 589832 | tf_op jit(solution)/shard_map/ppermute | solution.py:497
  51.1 4.6 %collective-permute-done.12.refs_5_ = f32[64,8,128]{2,1,0:T(8,128)S(1)} collective-permute-done((f32[64,8,128]{2,1,0:T(8,128)S(1)}, f32[64,8,128]{2,1,0:T(8,128)S(1)}, u32[]{:S(2)}, u32[]{:S(2)}) %collective-permute-start.12) | collective-permute-done | bytes 262176 | tf_op jit(solution)/shard_map/ppermute | solution.py:503
  55.7 1.9 %shard_map.80.refs_0_ = f32[4,2,16,16,128]{4,3,2,1,0:T(8,128)S(1)} custom-call(f32[4,2,16,16,128]{4,3,2,1,0:T(8,128)S(1)} %shard_map.78.refs_0_, f32[24,16,128]{2,1,0:T(8,128)S(1)} %get-tuple-element.80.refs_1_, f32[24,16,128]{2,1,0:T(8,128)S(1)} %get-tuple-element.81.refs_2_, f32[8,16,128]{2,1,0:T(8,128)S(1)} %get-tuple-element.82.refs_3_, ...), custom_call_target="tpu_custom_call" | custom-call | flops 4000000 | bytes 5767168 | tf_op jit(solution)/shard_map/pallas_call | solution.py:35
  57.6 1.9 %collective-permute-done.14.refs_1_ = f32[24,16,128]{2,1,0:T(8,128)S(1)} collective-permute-done((f32[24,16,128]{2,1,0:T(8,128)S(1)}, f32[24,16,128]{2,1,0:T(8,128)S(1)}, u32[]{:S(2)}, u32[]{:S(2)}) %collective-permute-start.14) | collective-permute-done | bytes 196640 | tf_op jit(solution)/shard_map/ppermute | solution.py:497
  59.8 3.0 %collective-permute-start.19 = (f32[24,16,128]{2,1,0:T(8,128)S(1)}, f32[24,16,128]{2,1,0:T(8,128)S(1)}, u32[]{:S(2)}, u32[]{:S(2)}) collective-permute-start(f32[24,16,128]{2,1,0:T(8,128)S(1)} %get-tuple-element.88.refs_1_), channel_id=1, source_target_pairs={{0,2},{2,0},{4,6},{6,4},{8,10},{10,8},{12,14},{14,12},{1,3},{3,1},... | collective-permute-start | bytes 589832 | tf_op jit(solution)/shard_map/ppermute | solution.py:497
  62.9 1.5 %collective-permute-start.17 = (f32[32,8,128]{2,1,0:T(8,128)S(1)}, f32[32,8,128]{2,1,0:T(8,128)S(1)}, u32[]{:S(2)}, u32[]{:S(2)}) collective-permute-start(f32[32,8,128]{2,1,0:T(8,128)S(1)} %get-tuple-element.90), channel_id=1, source_target_pairs={{0,1},{1,0},{2,3},{3,2},{4,5},{5,4},{6,7},{7,6},{8,9},{9,8},{10,11... | collective-permute-start | bytes 393224 | tf_op jit(solution)/shard_map/ppermute | solution.py:503
  64.5 3.6 %collective-permute-done.17.refs_3_ = f32[32,8,128]{2,1,0:T(8,128)S(1)} collective-permute-done((f32[32,8,128]{2,1,0:T(8,128)S(1)}, f32[32,8,128]{2,1,0:T(8,128)S(1)}, u32[]{:S(2)}, u32[]{:S(2)}) %collective-permute-start.17) | collective-permute-done | bytes 131104 | tf_op jit(solution)/shard_map/ppermute | solution.py:503
  68.1 1.6 %shard_map.82 = (f32[4,2,16,16,128]{4,3,2,1,0:T(8,128)S(1)}, f32[4,2,16,16,128]{4,3,2,1,0:T(8,128)S(1)}) custom-call(f32[4,2,16,16,128]{4,3,2,1,0:T(8,128)S(1)} %shard_map.80.refs_0_, f32[24,16,128]{2,1,0:T(8,128)S(1)} %get-tuple-element.88.refs_1_, f32[24,16,128]{2,1,0:T(8,128)S(1)} %get-tuple-element.89.refs_2_, ...), custom_call_target="tpu_custom_call" | custom-call | flops 4000000 | bytes 7208960 | tf_op jit(solution)/shard_map/pallas_call | solution.py:35
  69.7 6.6 %collective-permute-done.19.refs_1_ = f32[24,16,128]{2,1,0:T(8,128)S(1)} collective-permute-done((f32[24,16,128]{2,1,0:T(8,128)S(1)}, f32[24,16,128]{2,1,0:T(8,128)S(1)}, u32[]{:S(2)}, u32[]{:S(2)}) %collective-permute-start.19) | collective-permute-done | bytes 196640 | tf_op jit(solution)/shard_map/ppermute | solution.py:497
  76.4 0.2 shard_map.83
  76.5 0.1 collective-permute-start.23
  76.7 0.5 collective-permute-start.24
  77.2 1.5 %collective-permute-start.22 = (f32[32,8,128]{2,1,0:T(8,128)S(1)}, f32[32,8,128]{2,1,0:T(8,128)S(1)}, u32[]{:S(2)}, u32[]{:S(2)}) collective-permute-start(f32[32,8,128]{2,1,0:T(8,128)S(1)} %get-tuple-element.100), channel_id=1, source_target_pairs={{0,1},{1,0},{2,3},{3,2},{4,5},{5,4},{6,7},{7,6},{8,9},{9,8},{10,11... | collective-permute-start | bytes 393224 | tf_op jit(solution)/shard_map/ppermute | solution.py:503
  78.8 4.0 %collective-permute-done.22.refs_5_ = f32[32,8,128]{2,1,0:T(8,128)S(1)} collective-permute-done((f32[32,8,128]{2,1,0:T(8,128)S(1)}, f32[32,8,128]{2,1,0:T(8,128)S(1)}, u32[]{:S(2)}, u32[]{:S(2)}) %collective-permute-start.22) | collective-permute-done | bytes 131104 | tf_op jit(solution)/shard_map/ppermute | solution.py:503
  82.8 1.8 %shard_map.84.refs_0_ = f32[4,2,16,16,128]{4,3,2,1,0:T(8,128)S(1)} custom-call(f32[4,2,16,16,128]{4,3,2,1,0:T(8,128)S(1)} %get-tuple-element.93.refs_0_, f32[24,16,128]{2,1,0:T(8,128)S(1)} %get-tuple-element.96.refs_1_, f32[24,16,128]{2,1,0:T(8,128)S(1)} %get-tuple-element.97.refs_2_, f32[8,16,128]{2,1,0:T(8,128)S(1)} %get-tuple-element.98.refs_3_, ...), custom_call_target="tpu_custom_call" | custom-call | flops 4000000 | bytes 7340032 | tf_op jit(solution)/shard_map/pallas_call | solution.py:35
  84.6 3.6 %collective-permute-done.24.refs_1_ = f32[24,16,128]{2,1,0:T(8,128)S(1)} collective-permute-done((f32[24,16,128]{2,1,0:T(8,128)S(1)}, f32[24,16,128]{2,1,0:T(8,128)S(1)}, u32[]{:S(2)}, u32[]{:S(2)}) %collective-permute-start.24) | collective-permute-done | bytes 196640 | tf_op jit(solution)/shard_map/ppermute | solution.py:497
  88.1 0.2 shard_map.85
  88.5 1.6 %collective-permute-start.26 = (f32[64,8,128]{2,1,0:T(8,128)S(1)}, f32[64,8,128]{2,1,0:T(8,128)S(1)}, u32[]{:S(2)}, u32[]{:S(2)}) collective-permute-start(f32[64,8,128]{2,1,0:T(8,128)S(1)} %get-tuple-element.107), channel_id=1, source_target_pairs={{0,1},{1,0},{2,3},{3,2},{4,5},{5,4},{6,7},{7,6},{8,9},{9,8},{10,11... | collective-permute-start | bytes 786440 | tf_op jit(solution)/shard_map/ppermute | solution.py:503
  90.1 0.5 collective-permute-start.28
  90.6 6.6 %collective-permute-done.26.refs_5_ = f32[64,8,128]{2,1,0:T(8,128)S(1)} collective-permute-done((f32[64,8,128]{2,1,0:T(8,128)S(1)}, f32[64,8,128]{2,1,0:T(8,128)S(1)}, u32[]{:S(2)}, u32[]{:S(2)}) %collective-permute-start.26) | collective-permute-done | bytes 262176 | tf_op jit(solution)/shard_map/ppermute | solution.py:503
  97.2 1.9 %shard_map.86.refs_0_ = f32[4,16,16,256]{3,2,1,0:T(8,128)S(1)} custom-call(f32[4,2,16,16,128]{4,3,2,1,0:T(8,128)S(1)} %shard_map.84.refs_0_, f32[24,16,128]{2,1,0:T(8,128)S(1)} %get-tuple-element.103.refs_1_, f32[24,16,128]{2,1,0:T(8,128)S(1)} %get-tuple-element.104.refs_2_, f32[8,16,128]{2,1,0:T(8,128)S(1)} %get-tuple-element.105.refs_3_, ...), custom_call_target="tpu_custom_call" | custom-call | flops 4000000 | bytes 5767168 | tf_op jit(solution)/shard_map/pallas_call | solution.py:35
  99.1 2.2 %collective-permute-done.28.refs_1_ = f32[24,16,128]{2,1,0:T(8,128)S(1)} collective-permute-done((f32[24,16,128]{2,1,0:T(8,128)S(1)}, f32[24,16,128]{2,1,0:T(8,128)S(1)}, u32[]{:S(2)}, u32[]{:S(2)}) %collective-permute-start.28) | collective-permute-done | bytes 196640 | tf_op jit(solution)/shard_map/ppermute | solution.py:497
  101.3 0.1 shard_map.87
  101.4 1.7 %copy.9 = f32[16,16,4,256]{3,2,1,0:T(4,128)} copy(f32[16,16,4,256]{3,1,0,2:T(8,128)S(1)} %bitcast.8) | data formatting | bytes 2097152 | tf_op jit(solution)/shard_map/transpose | solution.py:613
  (44 shorter events, 0.9 us)
Async XLA Ops:
  0.0 1.4 %copy-start.1 = (f32[32,16,3,256]{3,1,2,0:T(8,128)S(1)}, f32[32,16,3,256]{3,1,2,0:T(8,128)}, u32[]{:S(2)}) copy-start(f32[32,16,3,256]{3,1,2,0:T(8,128)} %param.7) | copy-start | bytes 4718596
  1.4 8.3 %copy-start.2 = (f32[32,16,3,256]{3,1,2,0:T(8,128)S(1)}, f32[32,16,3,256]{3,1,2,0:T(8,128)}, u32[]{:S(2)}) copy-start(f32[32,16,3,256]{3,1,2,0:T(8,128)} %param.7) | copy-start | bytes 4718596
  1.4 8.3 %copy-start.4 = (bf16[8,1,2,64,64]{4,3,2,1,0:T(8,128)(2,1)S(1)}, bf16[8,1,2,64,64]{4,3,2,1,0:T(8,128)(2,1)}, u32[]{:S(2)}) copy-start(bf16[8,1,2,64,64]{4,3,2,1,0:T(8,128)(2,1)} %param.9) | copy-start | bytes 393220
  1.4 8.3 %copy-start.5 = (s32[8]{0:T(128)S(1)}, s32[8]{0:T(128)}, u32[]{:S(2)}) copy-start(s32[8]{0:T(128)} %refs_0_.3) | copy-start | bytes 100
  1.6 8.2 %collective-permute-start.3 = (f32[96,16,128]{2,1,0:T(8,128)S(1)}, f32[96,16,128]{2,1,0:T(8,128)S(1)}, u32[]{:S(2)}, u32[]{:S(2)}) collective-permute-start(f32[96,16,128]{2,1,0:T(8,128)S(1)} %get-tuple-element.60), channel_id=1, source_target_pairs={{0,16},{16,0},{1,17},{17,1},{2,18},{18,2},{3,19},{19,3},{4,20},{20... | collective-permute-start | bytes 2359304 | tf_op jit(solution)/shard_map/ppermute | solution.py:503
  1.7 8.1 %collective-permute-start.2 = (f32[24,8,128]{2,1,0:T(8,128)S(1)}, f32[24,8,128]{2,1,0:T(8,128)S(1)}, u32[]{:S(2)}, u32[]{:S(2)}) collective-permute-start(f32[24,8,128]{2,1,0:T(8,128)S(1)} %get-tuple-element.59), channel_id=1, source_target_pairs={{0,1},{1,0},{2,3},{3,2},{4,5},{5,4},{6,7},{7,6},{8,9},{9,8},{10,11... | collective-permute-start | bytes 294920 | tf_op jit(solution)/shard_map/ppermute | solution.py:503
  3.2 4.1 %collective-permute-start = (f32[6,16,128]{2,1,0:T(8,128)S(1)}, f32[6,16,128]{2,1,0:T(8,128)S(1)}, u32[]{:S(2)}, u32[]{:S(2)}) collective-permute-start(f32[6,16,128]{2,1,0:T(8,128)S(1)} %get-tuple-element.57), channel_id=1, source_target_pairs={{0,2},{2,0},{4,6},{6,4},{8,10},{10,8},{12,14},{14,12},{1,3},{3,1},... | collective-permute-start | bytes 147464 | tf_op jit(solution)/shard_map/ppermute | solution.py:497
  4.7 5.0 %collective-permute-start.1 = (f32[6,16,128]{2,1,0:T(8,128)S(1)}, f32[6,16,128]{2,1,0:T(8,128)S(1)}, u32[]{:S(2)}, u32[]{:S(2)}) collective-permute-start(f32[6,16,128]{2,1,0:T(8,128)S(1)} %get-tuple-element.58), channel_id=1, source_target_pairs={{2,4},{18,20},{3,5},{19,21},{4,2},{20,18},{5,3},{21,19},{6,8},{22,... | collective-permute-start | bytes 147464 | tf_op jit(solution)/shard_map/ppermute | solution.py:500
  9.8 11.3 %copy-start.6 = (f32[16,16]{1,0:T(8,128)S(1)}, f32[16,16]{1,0:T(8,128)}, u32[]{:S(2)}) copy-start(f32[16,16]{1,0:T(8,128)} %param.8) | copy-start | bytes 3076
  9.8 11.4 %copy-start = (bf16[2,1152,256]{2,1,0:T(8,128)(2,1)S(1)}, bf16[2,1152,256]{2,1,0:T(8,128)(2,1)}, u32[]{:S(2)}) copy-start(bf16[2,1152,256]{2,1,0:T(8,128)(2,1)} %constant.4.clone.refs_5_.refs_7_) | copy-start | bytes 3538948
  12.7 8.4 %collective-permute-start.5 = (f32[128,16,128]{2,1,0:T(8,128)S(1)}, f32[128,16,128]{2,1,0:T(8,128)S(1)}, u32[]{:S(2)}, u32[]{:S(2)}) collective-permute-start(f32[128,16,128]{2,1,0:T(8,128)S(1)} %get-tuple-element.65), channel_id=1, source_target_pairs={{0,16},{16,0},{1,17},{17,1},{2,18},{18,2},{3,19},{19,3},{4,20},{20... | collective-permute-start | bytes 3145736 | tf_op jit(solution)/shard_map/ppermute | solution.py:503
  12.8 22.1 %collective-permute-start.6 = (f32[54,16,128]{2,1,0:T(8,128)S(1)}, f32[54,16,128]{2,1,0:T(8,128)S(1)}, u32[]{:S(2)}, u32[]{:S(2)}) collective-permute-start(f32[54,16,128]{2,1,0:T(8,128)S(1)} %get-tuple-element.62.refs_1_), channel_id=1, source_target_pairs={{0,2},{2,0},{4,6},{6,4},{8,10},{10,8},{12,14},{14,12},{1,3},{3,1},... | collective-permute-start | bytes 1327112 | tf_op jit(solution)/shard_map/ppermute | solution.py:497
  13.4 21.5 %collective-permute-start.7 = (f32[54,16,128]{2,1,0:T(8,128)S(1)}, f32[54,16,128]{2,1,0:T(8,128)S(1)}, u32[]{:S(2)}, u32[]{:S(2)}) collective-permute-start(f32[54,16,128]{2,1,0:T(8,128)S(1)} %get-tuple-element.63.refs_2_), channel_id=1, source_target_pairs={{2,4},{18,20},{3,5},{19,21},{4,2},{20,18},{5,3},{21,19},{6,8},{22,... | collective-permute-start | bytes 1327112 | tf_op jit(solution)/shard_map/ppermute | solution.py:500
  13.4 7.7 %collective-permute-start.4 = (f32[56,8,128]{2,1,0:T(8,128)S(1)}, f32[56,8,128]{2,1,0:T(8,128)S(1)}, u32[]{:S(2)}, u32[]{:S(2)}) collective-permute-start(f32[56,8,128]{2,1,0:T(8,128)S(1)} %get-tuple-element.64), channel_id=1, source_target_pairs={{0,1},{1,0},{2,3},{3,2},{4,5},{5,4},{6,7},{7,6},{8,9},{9,8},{10,11... | collective-permute-start | bytes 688136 | tf_op jit(solution)/shard_map/ppermute | solution.py:503
  35.0 6.3 %collective-permute-start.9 = (f32[32,16,128]{2,1,0:T(8,128)S(1)}, f32[32,16,128]{2,1,0:T(8,128)S(1)}, u32[]{:S(2)}, u32[]{:S(2)}) collective-permute-start(f32[32,16,128]{2,1,0:T(8,128)S(1)} %get-tuple-element.78), channel_id=1, source_target_pairs={{0,16},{16,0},{1,17},{17,1},{2,18},{18,2},{3,19},{19,3},{4,20},{20... | collective-permute-start | bytes 786440 | tf_op jit(solution)/shard_map/ppermute | solution.py:503
  35.1 11.5 %collective-permute-start.10 = (f32[24,16,128]{2,1,0:T(8,128)S(1)}, f32[24,16,128]{2,1,0:T(8,128)S(1)}, u32[]{:S(2)}, u32[]{:S(2)}) collective-permute-start(f32[24,16,128]{2,1,0:T(8,128)S(1)} %get-tuple-element.73.refs_1_), channel_id=1, source_target_pairs={{0,2},{2,0},{4,6},{6,4},{8,10},{10,8},{12,14},{14,12},{1,3},{3,1},... | collective-permute-start | bytes 589832 | tf_op jit(solution)/shard_map/ppermute | solution.py:497
  35.7 10.9 %collective-permute-start.11 = (f32[24,16,128]{2,1,0:T(8,128)S(1)}, f32[24,16,128]{2,1,0:T(8,128)S(1)}, u32[]{:S(2)}, u32[]{:S(2)}) collective-permute-start(f32[24,16,128]{2,1,0:T(8,128)S(1)} %get-tuple-element.74.refs_2_), channel_id=1, source_target_pairs={{2,4},{18,20},{3,5},{19,21},{4,2},{20,18},{5,3},{21,19},{6,8},{22,... | collective-permute-start | bytes 589832 | tf_op jit(solution)/shard_map/ppermute | solution.py:500
  35.7 5.6 %collective-permute-start.8 = (f32[32,8,128]{2,1,0:T(8,128)S(1)}, f32[32,8,128]{2,1,0:T(8,128)S(1)}, u32[]{:S(2)}, u32[]{:S(2)}) collective-permute-start(f32[32,8,128]{2,1,0:T(8,128)S(1)} %get-tuple-element.77), channel_id=1, source_target_pairs={{0,1},{1,0},{2,3},{3,2},{4,5},{5,4},{6,7},{7,6},{8,9},{9,8},{10,11... | collective-permute-start | bytes 393224 | tf_op jit(solution)/shard_map/ppermute | solution.py:503
  43.1 12.6 %copy-start.3 = (bf16[2,1152,256]{2,1,0:T(8,128)(2,1)S(1)}, bf16[2,1152,256]{2,1,0:T(8,128)(2,1)}, u32[]{:S(2)}) copy-start(bf16[2,1152,256]{2,1,0:T(8,128)(2,1)} %constant.5.clone.refs_7_) | copy-start | bytes 3538948
  46.9 8.8 %collective-permute-start.13 = (f32[64,16,128]{2,1,0:T(8,128)S(1)}, f32[64,16,128]{2,1,0:T(8,128)S(1)}, u32[]{:S(2)}, u32[]{:S(2)}) collective-permute-start(f32[64,16,128]{2,1,0:T(8,128)S(1)} %get-tuple-element.85), channel_id=1, source_target_pairs={{0,16},{16,0},{1,17},{17,1},{2,18},{18,2},{3,19},{19,3},{4,20},{20... | collective-permute-start | bytes 1572872 | tf_op jit(solution)/shard_map/ppermute | solution.py:503
  47.0 8.7 %collective-permute-start.12 = (f32[64,8,128]{2,1,0:T(8,128)S(1)}, f32[64,8,128]{2,1,0:T(8,128)S(1)}, u32[]{:S(2)}, u32[]{:S(2)}) collective-permute-start(f32[64,8,128]{2,1,0:T(8,128)S(1)} %get-tuple-element.84), channel_id=1, source_target_pairs={{0,1},{1,0},{2,3},{3,2},{4,5},{5,4},{6,7},{7,6},{8,9},{9,8},{10,11... | collective-permute-start | bytes 786440 | tf_op jit(solution)/shard_map/ppermute | solution.py:503
  47.5 12.0 %collective-permute-start.14 = (f32[24,16,128]{2,1,0:T(8,128)S(1)}, f32[24,16,128]{2,1,0:T(8,128)S(1)}, u32[]{:S(2)}, u32[]{:S(2)}) collective-permute-start(f32[24,16,128]{2,1,0:T(8,128)S(1)} %get-tuple-element.80.refs_1_), channel_id=1, source_target_pairs={{0,2},{2,0},{4,6},{6,4},{8,10},{10,8},{12,14},{14,12},{1,3},{3,1},... | collective-permute-start | bytes 589832 | tf_op jit(solution)/shard_map/ppermute | solution.py:497
  48.1 11.4 %collective-permute-start.15 = (f32[24,16,128]{2,1,0:T(8,128)S(1)}, f32[24,16,128]{2,1,0:T(8,128)S(1)}, u32[]{:S(2)}, u32[]{:S(2)}) collective-permute-start(f32[24,16,128]{2,1,0:T(8,128)S(1)} %get-tuple-element.81.refs_2_), channel_id=1, source_target_pairs={{2,4},{18,20},{3,5},{19,21},{4,2},{20,18},{5,3},{21,19},{6,8},{22,... | collective-permute-start | bytes 589832 | tf_op jit(solution)/shard_map/ppermute | solution.py:500
  48.1 14.9 %collective-permute-start.16 = (f32[24,16,128]{2,1,0:T(8,128)S(1)}, f32[24,16,128]{2,1,0:T(8,128)S(1)}, u32[]{:S(2)}, u32[]{:S(2)}) collective-permute-start(f32[24,16,128]{2,1,0:T(8,128)S(1)} %get-tuple-element.87), channel_id=1, source_target_pairs={{0,2},{2,0},{4,6},{6,4},{8,10},{10,8},{12,14},{14,12},{1,3},{3,1},... | collective-permute-start | bytes 589832 | tf_op jit(solution)/shard_map/ppermute | solution.py:497
  59.6 8.5 %collective-permute-start.18 = (f32[32,16,128]{2,1,0:T(8,128)S(1)}, f32[32,16,128]{2,1,0:T(8,128)S(1)}, u32[]{:S(2)}, u32[]{:S(2)}) collective-permute-start(f32[32,16,128]{2,1,0:T(8,128)S(1)} %get-tuple-element.91), channel_id=1, source_target_pairs={{0,16},{16,0},{1,17},{17,1},{2,18},{18,2},{3,19},{19,3},{4,20},{20... | collective-permute-start | bytes 786440 | tf_op jit(solution)/shard_map/ppermute | solution.py:503
  59.7 10.0 %collective-permute-start.21 = (f32[24,16,128]{2,1,0:T(8,128)S(1)}, f32[24,16,128]{2,1,0:T(8,128)S(1)}, u32[]{:S(2)}, u32[]{:S(2)}) collective-permute-start(f32[24,16,128]{2,1,0:T(8,128)S(1)} %get-tuple-element.95), channel_id=1, source_target_pairs={{2,4},{18,20},{3,5},{19,21},{4,2},{20,18},{5,3},{21,19},{6,8},{22,... | collective-permute-start | bytes 589832 | tf_op jit(solution)/shard_map/ppermute | solution.py:500
  59.8 16.6 %collective-permute-start.19 = (f32[24,16,128]{2,1,0:T(8,128)S(1)}, f32[24,16,128]{2,1,0:T(8,128)S(1)}, u32[]{:S(2)}, u32[]{:S(2)}) collective-permute-start(f32[24,16,128]{2,1,0:T(8,128)S(1)} %get-tuple-element.88.refs_1_), channel_id=1, source_target_pairs={{0,2},{2,0},{4,6},{6,4},{8,10},{10,8},{12,14},{14,12},{1,3},{3,1},... | collective-permute-start | bytes 589832 | tf_op jit(solution)/shard_map/ppermute | solution.py:497
  62.8 13.6 %collective-permute-start.20 = (f32[24,16,128]{2,1,0:T(8,128)S(1)}, f32[24,16,128]{2,1,0:T(8,128)S(1)}, u32[]{:S(2)}, u32[]{:S(2)}) collective-permute-start(f32[24,16,128]{2,1,0:T(8,128)S(1)} %get-tuple-element.89.refs_2_), channel_id=1, source_target_pairs={{2,4},{18,20},{3,5},{19,21},{4,2},{20,18},{5,3},{21,19},{6,8},{22,... | collective-permute-start | bytes 589832 | tf_op jit(solution)/shard_map/ppermute | solution.py:500
  62.9 5.2 %collective-permute-start.17 = (f32[32,8,128]{2,1,0:T(8,128)S(1)}, f32[32,8,128]{2,1,0:T(8,128)S(1)}, u32[]{:S(2)}, u32[]{:S(2)}) collective-permute-start(f32[32,8,128]{2,1,0:T(8,128)S(1)} %get-tuple-element.90), channel_id=1, source_target_pairs={{0,1},{1,0},{2,3},{3,2},{4,5},{5,4},{6,7},{7,6},{8,9},{9,8},{10,11... | collective-permute-start | bytes 393224 | tf_op jit(solution)/shard_map/ppermute | solution.py:503
  76.5 6.3 %collective-permute-start.23 = (f32[32,16,128]{2,1,0:T(8,128)S(1)}, f32[32,16,128]{2,1,0:T(8,128)S(1)}, u32[]{:S(2)}, u32[]{:S(2)}) collective-permute-start(f32[32,16,128]{2,1,0:T(8,128)S(1)} %get-tuple-element.101), channel_id=1, source_target_pairs={{0,16},{16,0},{1,17},{17,1},{2,18},{18,2},{3,19},{19,3},{4,20},{20... | collective-permute-start | bytes 786440 | tf_op jit(solution)/shard_map/ppermute | solution.py:503
  76.7 11.5 %collective-permute-start.24 = (f32[24,16,128]{2,1,0:T(8,128)S(1)}, f32[24,16,128]{2,1,0:T(8,128)S(1)}, u32[]{:S(2)}, u32[]{:S(2)}) collective-permute-start(f32[24,16,128]{2,1,0:T(8,128)S(1)} %get-tuple-element.96.refs_1_), channel_id=1, source_target_pairs={{0,2},{2,0},{4,6},{6,4},{8,10},{10,8},{12,14},{14,12},{1,3},{3,1},... | collective-permute-start | bytes 589832 | tf_op jit(solution)/shard_map/ppermute | solution.py:497
  77.2 10.9 %collective-permute-start.25 = (f32[24,16,128]{2,1,0:T(8,128)S(1)}, f32[24,16,128]{2,1,0:T(8,128)S(1)}, u32[]{:S(2)}, u32[]{:S(2)}) collective-permute-start(f32[24,16,128]{2,1,0:T(8,128)S(1)} %get-tuple-element.97.refs_2_), channel_id=1, source_target_pairs={{2,4},{18,20},{3,5},{19,21},{4,2},{20,18},{5,3},{21,19},{6,8},{22,... | collective-permute-start | bytes 589832 | tf_op jit(solution)/shard_map/ppermute | solution.py:500
  77.2 5.6 %collective-permute-start.22 = (f32[32,8,128]{2,1,0:T(8,128)S(1)}, f32[32,8,128]{2,1,0:T(8,128)S(1)}, u32[]{:S(2)}, u32[]{:S(2)}) collective-permute-start(f32[32,8,128]{2,1,0:T(8,128)S(1)} %get-tuple-element.100), channel_id=1, source_target_pairs={{0,1},{1,0},{2,3},{3,2},{4,5},{5,4},{6,7},{7,6},{8,9},{9,8},{10,11... | collective-permute-start | bytes 393224 | tf_op jit(solution)/shard_map/ppermute | solution.py:503
  88.4 8.8 %collective-permute-start.27 = (f32[64,16,128]{2,1,0:T(8,128)S(1)}, f32[64,16,128]{2,1,0:T(8,128)S(1)}, u32[]{:S(2)}, u32[]{:S(2)}) collective-permute-start(f32[64,16,128]{2,1,0:T(8,128)S(1)} %get-tuple-element.108), channel_id=1, source_target_pairs={{0,16},{16,0},{1,17},{17,1},{2,18},{18,2},{3,19},{19,3},{4,20},{20... | collective-permute-start | bytes 1572872 | tf_op jit(solution)/shard_map/ppermute | solution.py:503
  88.5 8.7 %collective-permute-start.26 = (f32[64,8,128]{2,1,0:T(8,128)S(1)}, f32[64,8,128]{2,1,0:T(8,128)S(1)}, u32[]{:S(2)}, u32[]{:S(2)}) collective-permute-start(f32[64,8,128]{2,1,0:T(8,128)S(1)} %get-tuple-element.107), channel_id=1, source_target_pairs={{0,1},{1,0},{2,3},{3,2},{4,5},{5,4},{6,7},{7,6},{8,9},{9,8},{10,11... | collective-permute-start | bytes 786440 | tf_op jit(solution)/shard_map/ppermute | solution.py:503
  90.1 11.2 %collective-permute-start.28 = (f32[24,16,128]{2,1,0:T(8,128)S(1)}, f32[24,16,128]{2,1,0:T(8,128)S(1)}, u32[]{:S(2)}, u32[]{:S(2)}) collective-permute-start(f32[24,16,128]{2,1,0:T(8,128)S(1)} %get-tuple-element.103.refs_1_), channel_id=1, source_target_pairs={{0,2},{2,0},{4,6},{6,4},{8,10},{10,8},{12,14},{14,12},{1,3},{3,1},... | collective-permute-start | bytes 589832 | tf_op jit(solution)/shard_map/ppermute | solution.py:497
  90.6 10.7 %collective-permute-start.29 = (f32[24,16,128]{2,1,0:T(8,128)S(1)}, f32[24,16,128]{2,1,0:T(8,128)S(1)}, u32[]{:S(2)}, u32[]{:S(2)}) collective-permute-start(f32[24,16,128]{2,1,0:T(8,128)S(1)} %get-tuple-element.104.refs_2_), channel_id=1, source_target_pairs={{2,4},{18,20},{3,5},{19,21},{4,2},{20,18},{5,3},{21,19},{6,8},{22,... | collective-permute-start | bytes 589832 | tf_op jit(solution)/shard_map/ppermute | solution.py:500
